TPU v7x, 32 devices: a whole 2x2x4 slice. The times are simulated.
32 devices in a mesh: group: 4 (over y, x), replica: 8 (over z, core).
Axes of the slice: x: 2, y: 2, z: 4, core: 2. Of those that a mesh axis runs over, the one named last changes fastest.
Arguments:
- latents: bfloat16 [64, 256, 384], P(('group', 'replica')), may hold values from -6 to 6
- condition: float32 [64, 384], P(('group', 'replica')), may hold values from -6 to 6
- cotangent: bfloat16 [64, 256, 384], P(('group', 'replica')), may hold values from -6 to 6
- live_counts: int32 [32], P(('group', 'replica')), may hold values from 1 to 2, 41 in all
- modulation: bfloat16 [384, 2304], P('group'), may hold values from -0.3125 to 0.3125
- attending: bfloat16 [384, 1152], P('group'), may hold values from -0.3125 to 0.3125
- projection: bfloat16 [384, 384], P('group'), may hold values from -1.25 to 1.25
- expand: bfloat16 [384, 1536], P(None, 'group'), may hold values from -0.3125 to 0.3125
- contract: bfloat16 [1536, 384], P('group'), may hold values from -0.15625 to 0.15625
- biases: bfloat16 [14, 384], P(None, 'group'), may hold values from -1.1953125 to 1.1953125
- modulation_mean: bfloat16 [384, 2304], P('group'), may hold values from -20 to 20
- attending_mean: bfloat16 [384, 1152], P('group'), may hold values from -20 to 20
- projection_mean: bfloat16 [384, 384], P('group'), may hold values from -10 to 10
- expand_mean: bfloat16 [384, 1536], P(None, 'group'), may hold values from -12 to 12
- contract_mean: bfloat16 [1536, 384], P('group'), may hold values from -32 to 32
- biases_mean: bfloat16 [14, 384], P(None, 'group'), may hold values from -20 to 20
- modulation_square: bfloat16 [384, 2304], P('group'), may hold values from 0.47070312 to 7.53125
- attending_square: bfloat16 [384, 1152], P('group'), may hold values from 0.47070312 to 7.53125
- projection_square: bfloat16 [384, 384], P('group'), may hold values from 0.11767578 to 1.8828125
- expand_square: bfloat16 [384, 1536], P(None, 'group'), may hold values from 0.16992188 to 2.71875
- contract_square: bfloat16 [1536, 384], P('group'), may hold values from 1.0625 to 17
- biases_square: bfloat16 [14, 384], P(None, 'group'), may hold values from 0.47070312 to 7.53125
Outputs:
- out_latents: bfloat16 [64, 256, 384], P(('group', 'replica'))
- grad_latents: bfloat16 [64, 256, 384], P(('group', 'replica'))
- grad_condition: float32 [64, 384], P(('group', 'replica'))
- modulation_updated: float32 [384, 2304], P('group')
- attending_updated: float32 [384, 1152], P('group')
- projection_updated: float32 [384, 384], P('group')
- expand_updated: float32 [384, 1536], P(None, 'group')
- contract_updated: float32 [1536, 384], P('group')
- biases_updated: float32 [14, 384], P(None, 'group')
- modulation_momentum: float32 [384, 2304], P('group')
- attending_momentum: float32 [384, 1152], P('group')
- projection_momentum: float32 [384, 384], P('group')
- expand_momentum: float32 [384, 1536], P(None, 'group')
- contract_momentum: float32 [1536, 384], P('group')
- biases_momentum: float32 [14, 384], P(None, 'group')
- modulation_variance: float32 [384, 2304], P('group')
- attending_variance: float32 [384, 1152], P('group')
- projection_variance: float32 [384, 384], P('group')
- expand_variance: float32 [384, 1536], P(None, 'group')
- contract_variance: float32 [1536, 384], P('group')
- biases_variance: float32 [14, 384], P(None, 'group')
Inputs may be any that keep to these rules, and one draw needn't show every extreme that they name: A device's first live_counts slots are live, the rest are not; the entries add up to 41 and some device has all 2 slots live.
All inputs are finite; a program needn't handle non-finite values.
Results may differ from a plain program's by a relative error of at most 0.019.
Values may be sent and summed in bfloat16 or wider, within the bound.
No kernel may reach another device: no remote copies, remote signals or barrier semaphores. Data moves between devices by JAX's collectives and lax.ppermute only.
A program may use at most 128 MiB of HBM per device.

v0:
```python
import jax
import jax.numpy as jnp
from jax import lax
from jax.sharding import PartitionSpec as P

HEADS = 6
HEAD_DIM = 64
FF = 1536
STEP = 10


NORM_EPS = 1e-06
ADAM_EPS = 1e-08
BETA_FIRST = 0.9
BETA_SECOND = 0.999
DECAY_RATE = 0.1
LEARN_RATES = (0.05, 0.05, 0.2, 0.05, 0.025, 0.1)
DECAY_FLAGS = (1.0, 1.0, 1.0, 1.0, 1.0, 0.0)
GELU_COEF = 0.7978845608028654


def layer_norm_parts(values):
    centred = values - jnp.mean(values, axis=-1, keepdims=True)
    inverse = lax.rsqrt(jnp.mean(centred * centred, axis=-1, keepdims=True) + NORM_EPS)
    return (centred * inverse, inverse)


def norm_backward(grad_normed, normed, inverse):
    mean_grad = jnp.mean(grad_normed, axis=-1, keepdims=True)
    mean_cross = jnp.mean(grad_normed * normed, axis=-1, keepdims=True)
    return inverse * (grad_normed - mean_grad - normed * mean_cross)


def gelu_slope(before):
    tangent = jnp.tanh(GELU_COEF * (before + 0.044715 * before * before * before))
    return 0.5 * (1.0 + tangent) + 0.5 * before * (1.0 - tangent * tangent) * GELU_COEF * (
        1.0 + 3.0 * 0.044715 * before * before
    )


def dot_first(left_side, right_side):
    return lax.dot_general(
        left_side, right_side, (((0,), (0,)), ((), ())), preferred_element_type=jnp.float32
    )


def dot_last(left_side, right_side):
    return lax.dot_general(
        left_side, right_side, (((1,), (1,)), ((), ())), preferred_element_type=jnp.float32
    )


def adam_update(weight, gradient, mean_old, square_old, step_rate, decay_flag):
    momentum = BETA_FIRST * mean_old + (1.0 - BETA_FIRST) * gradient
    variance = BETA_SECOND * square_old + (1.0 - BETA_SECOND) * gradient * gradient
    mean_hat = momentum / (1.0 - BETA_FIRST**STEP)
    square_hat = variance / (1.0 - BETA_SECOND**STEP)
    updated = weight - step_rate * (
        mean_hat / (jnp.sqrt(square_hat) + ADAM_EPS) + decay_flag * DECAY_RATE * weight
    )
    return (updated, momentum, variance)


def shards(
    latents,
    condition,
    cotangent,
    live_counts,
    modulation,
    attending,
    projection,
    expand,
    contract,
    biases,
    modulation_mean,
    attending_mean,
    projection_mean,
    expand_mean,
    contract_mean,
    biases_mean,
    modulation_square,
    attending_square,
    projection_square,
    expand_square,
    contract_square,
    biases_square,
):
    slot_count, length, model_width = latents.shape
    row_count = slot_count * length
    hidden_rows = FF // model_width
    head_scale = HEAD_DIM ** (-0.5)
    live_mask = (jnp.arange(slot_count) < live_counts[0]).astype(jnp.float32)
    full_mod, full_att, full_proj, full_expand, full_contract, full_bias = (
        lax.all_gather(modulation, "group", axis=0, tiled=True),
        lax.all_gather(attending, "group", axis=0, tiled=True),
        lax.all_gather(projection, "group", axis=0, tiled=True),
        lax.all_gather(expand, "group", axis=1, tiled=True),
        lax.all_gather(contract, "group", axis=0, tiled=True),
        lax.all_gather(biases, "group", axis=1, tiled=True),
    )
    bias_rows = full_bias.astype(jnp.float32)
    mod_bias = bias_rows[0:6].reshape(6 * model_width)
    joined_bias = jnp.concatenate([bias_rows[6], jnp.zeros_like(bias_rows[6]), bias_rows[7]])
    proj_bias = bias_rows[8]
    expand_bias = bias_rows[9 : 9 + hidden_rows].reshape(FF)
    contract_bias = bias_rows[9 + hidden_rows]
    cond_low = jax.nn.silu(condition).astype(jnp.bfloat16)
    modulated = jnp.dot(cond_low, full_mod, preferred_element_type=jnp.float32) + mod_bias
    pieces = modulated.reshape(slot_count, 6, 1, model_width)
    shift_att, scale_att, gate_att = (pieces[:, 0], pieces[:, 1], pieces[:, 2])
    shift_ffn, scale_ffn, gate_ffn = (pieces[:, 3], pieces[:, 4], pieces[:, 5])
    tokens = latents.astype(jnp.float32)
    normed_one, inverse_one = layer_norm_parts(tokens)
    first_in = (
        (normed_one * (1.0 + scale_att) + shift_att)
        .astype(jnp.bfloat16)
        .reshape(row_count, model_width)
    )
    joined = (jnp.dot(first_in, full_att, preferred_element_type=jnp.float32) + joined_bias).astype(
        jnp.bfloat16
    )
    joined = joined.reshape(slot_count, length, 3, HEADS, HEAD_DIM)
    query_vectors = joined[:, :, 0]
    key_vectors = joined[:, :, 1]
    value_vectors = joined[:, :, 2]
    scores = (
        jnp.einsum(
            "sqhe,skhe->shqk", query_vectors, key_vectors, preferred_element_type=jnp.float32
        )
        * head_scale
    )
    top_score = jnp.max(scores, axis=-1, keepdims=True)
    log_total = top_score + jnp.log(jnp.sum(jnp.exp(scores - top_score), axis=-1, keepdims=True))
    soft_low = jnp.exp(scores - log_total).astype(jnp.bfloat16)
    mixed_heads = jnp.einsum(
        "shqk,skhe->sqhe", soft_low, value_vectors, preferred_element_type=jnp.float32
    )
    mixed_low = mixed_heads.astype(jnp.bfloat16).reshape(row_count, model_width)
    branch = (
        jnp.dot(mixed_low, full_proj, preferred_element_type=jnp.float32) + proj_bias
    ).reshape(slot_count, length, model_width)
    middle = tokens + gate_att * branch
    normed_two, inverse_two = layer_norm_parts(middle)
    second_in = (
        (normed_two * (1.0 + scale_ffn) + shift_ffn)
        .astype(jnp.bfloat16)
        .reshape(row_count, model_width)
    )
    before = jnp.dot(second_in, full_expand, preferred_element_type=jnp.float32) + expand_bias
    activated = jax.nn.gelu(before, approximate=True).astype(jnp.bfloat16)
    feed_out = jnp.dot(activated, full_contract, preferred_element_type=jnp.float32) + contract_bias
    feed_out = feed_out.reshape(slot_count, length, model_width)
    result = middle + gate_ffn * feed_out
    out_latents = (result * live_mask[:, None, None]).astype(jnp.bfloat16)
    grad_out = cotangent.astype(jnp.float32) * live_mask[:, None, None]
    grad_gate_ffn = jnp.sum(grad_out * feed_out, axis=1)
    grad_feed = (gate_ffn * grad_out).astype(jnp.bfloat16).reshape(row_count, model_width)
    contract_bias_grad = jnp.sum(grad_feed, axis=0, dtype=jnp.float32)
    grad_contract = dot_first(activated, grad_feed)
    grad_before = (dot_last(grad_feed, full_contract) * gelu_slope(before)).astype(jnp.bfloat16)
    grad_expand = dot_first(second_in, grad_before)
    expand_bias_grad = jnp.sum(grad_before, axis=0, dtype=jnp.float32)
    grad_second = dot_last(grad_before, full_expand)
    grad_second = grad_second.reshape(slot_count, length, model_width)
    grad_shift_ffn = jnp.sum(grad_second, axis=1)
    grad_scale_ffn = jnp.sum(grad_second * normed_two, axis=1)
    grad_middle = grad_out + norm_backward(grad_second * (1.0 + scale_ffn), normed_two, inverse_two)
    grad_gate_att = jnp.sum(grad_middle * branch, axis=1)
    grad_branch = (gate_att * grad_middle).astype(jnp.bfloat16).reshape(row_count, model_width)
    proj_bias_grad = jnp.sum(grad_branch, axis=0, dtype=jnp.float32)
    grad_proj = dot_first(mixed_low, grad_branch)
    grad_mixed = (
        dot_last(grad_branch, full_proj)
        .astype(jnp.bfloat16)
        .reshape(slot_count, length, HEADS, HEAD_DIM)
    )
    again = (
        jnp.einsum(
            "sqhe,skhe->shqk", query_vectors, key_vectors, preferred_element_type=jnp.float32
        )
        * head_scale
    )
    soft_full = jnp.exp(again - log_total)
    soft_again = soft_full.astype(jnp.bfloat16)
    grad_soft = jnp.einsum(
        "sqhe,skhe->shqk", grad_mixed, value_vectors, preferred_element_type=jnp.float32
    )
    grad_values = jnp.einsum(
        "shqk,sqhe->skhe", soft_again, grad_mixed, preferred_element_type=jnp.float32
    )
    row_inner = jnp.sum(soft_full * grad_soft, axis=-1, keepdims=True)
    grad_scores = (soft_full * (grad_soft - row_inner)).astype(jnp.bfloat16)
    grad_query = (
        jnp.einsum("shqk,skhe->sqhe", grad_scores, key_vectors, preferred_element_type=jnp.float32)
        * head_scale
    )
    grad_keys = (
        jnp.einsum(
            "shqk,sqhe->skhe", grad_scores, query_vectors, preferred_element_type=jnp.float32
        )
        * head_scale
    )
    grad_joined = (
        jnp.stack([grad_query, grad_keys, grad_values], axis=2)
        .astype(jnp.bfloat16)
        .reshape(row_count, 3 * model_width)
    )
    query_bias_grad = jnp.sum(grad_joined[:, :model_width], axis=0, dtype=jnp.float32)
    value_bias_grad = jnp.sum(grad_joined[:, 2 * model_width :], axis=0, dtype=jnp.float32)
    grad_attending = dot_first(first_in, grad_joined)
    grad_first = dot_last(grad_joined, full_att).reshape(slot_count, length, model_width)
    grad_shift_att = jnp.sum(grad_first, axis=1)
    grad_scale_att = jnp.sum(grad_first * normed_one, axis=1)
    grad_tokens = grad_middle + norm_backward(
        grad_first * (1.0 + scale_att), normed_one, inverse_one
    )
    grad_latents = grad_tokens.astype(jnp.bfloat16)
    grad_modulated = (
        jnp.stack(
            [
                grad_shift_att,
                grad_scale_att,
                grad_gate_att,
                grad_shift_ffn,
                grad_scale_ffn,
                grad_gate_ffn,
            ],
            axis=1,
        )
        .astype(jnp.bfloat16)
        .reshape(slot_count, 6 * model_width)
    )
    grad_mod = dot_first(cond_low, grad_modulated)
    mod_bias_grad = jnp.sum(grad_modulated, axis=0, dtype=jnp.float32)
    sigmoid_cond = jax.nn.sigmoid(condition)
    grad_condition = (
        dot_last(grad_modulated, full_mod) * sigmoid_cond * (1.0 + condition * (1.0 - sigmoid_cond))
    )
    bias_grad = jnp.concatenate(
        [
            mod_bias_grad.reshape(6, model_width),
            query_bias_grad[None],
            value_bias_grad[None],
            proj_bias_grad[None],
            expand_bias_grad.reshape(hidden_rows, model_width),
            contract_bias_grad[None],
        ],
        axis=0,
    )
    owned = (
        lax.psum_scatter(
            grad_mod.astype(jnp.bfloat16), "group", scatter_dimension=0, tiled=True
        ).astype(jnp.float32),
        lax.psum_scatter(
            grad_attending.astype(jnp.bfloat16), "group", scatter_dimension=0, tiled=True
        ).astype(jnp.float32),
        lax.psum_scatter(
            grad_proj.astype(jnp.bfloat16), "group", scatter_dimension=0, tiled=True
        ).astype(jnp.float32),
        lax.psum_scatter(
            grad_expand.astype(jnp.bfloat16), "group", scatter_dimension=1, tiled=True
        ).astype(jnp.float32),
        lax.psum_scatter(
            grad_contract.astype(jnp.bfloat16), "group", scatter_dimension=0, tiled=True
        ).astype(jnp.float32),
        lax.psum_scatter(
            bias_grad.astype(jnp.bfloat16), "group", scatter_dimension=1, tiled=True
        ).astype(jnp.float32),
    )
    totals = lax.psum((owned[0], owned[1], owned[2], owned[3], owned[4], owned[5]), "replica")
    stored = (modulation, attending, projection, expand, contract, biases)
    means = (
        modulation_mean,
        attending_mean,
        projection_mean,
        expand_mean,
        contract_mean,
        biases_mean,
    )
    squares = (
        modulation_square,
        attending_square,
        projection_square,
        expand_square,
        contract_square,
        biases_square,
    )
    results = [
        adam_update(
            stored[kind].astype(jnp.float32),
            totals[kind],
            means[kind].astype(jnp.float32),
            squares[kind].astype(jnp.float32),
            LEARN_RATES[kind],
            DECAY_FLAGS[kind],
        )
        for kind in range(6)
    ]
    return (
        out_latents,
        grad_latents,
        grad_condition,
        results[0][0],
        results[1][0],
        results[2][0],
        results[3][0],
        results[4][0],
        results[5][0],
        results[0][1],
        results[1][1],
        results[2][1],
        results[3][1],
        results[4][1],
        results[5][1],
        results[0][2],
        results[1][2],
        results[2][2],
        results[3][2],
        results[4][2],
        results[5][2],
    )


def solution(mesh):
    return jax.shard_map(
        shards,
        mesh=mesh,
        in_specs=(
            P(("group", "replica"), None, None),
            P(("group", "replica"), None),
            P(("group", "replica"), None, None),
            P(("group", "replica")),
            P("group", None),
            P("group", None),
            P("group", None),
            P(None, "group"),
            P("group", None),
            P(None, "group"),
            P("group", None),
            P("group", None),
            P("group", None),
            P(None, "group"),
            P("group", None),
            P(None, "group"),
            P("group", None),
            P("group", None),
            P("group", None),
            P(None, "group"),
            P("group", None),
            P(None, "group"),
        ),
        out_specs=(
            P(("group", "replica"), None, None),
            P(("group", "replica"), None, None),
            P(("group", "replica"), None),
            P("group", None),
            P("group", None),
            P("group", None),
            P(None, "group"),
            P("group", None),
            P(None, "group"),
            P("group", None),
            P("group", None),
            P("group", None),
            P(None, "group"),
            P("group", None),
            P(None, "group"),
            P("group", None),
            P("group", None),
            P("group", None),
            P(None, "group"),
            P("group", None),
            P(None, "group"),
        ),
        check_vma=False,
    )
```

profile of v0, /device:TPU:0, one launch (start us, length us, event | category | flops | bytes accessed | tf_op | source)
XLA Modules:
  0.0 411.4 jit_solution(7953411237953184427)
XLA Ops:
  7.3 0.7 all-gather.5.cloned.1.call-update
  8.0 0.7 all-gather.7.cloned.1.call-update
  8.7 0.7 all-gather.9.cloned.1.call-update
  9.5 9.7 %all-gather = bf16[4,96,14]{1,2,0:T(8,128)(2,1)S(1)} all-gather(bf16[1,96,14]{1,2,0:T(8,128)(2,1)} %bitcast.169), channel_id=1, replica_groups=mesh['group'=4,'replica'=8] {'group'}, dimensions={0}, use_global_device_ids=true | all-gather | bytes 13440 | tf_op jit(solution)/shard_map/all_gather | solution.py:99
  19.3 0.6 slice_reduce_fusion.2
  21.1 1.1 convert_reduce_fusion
  22.3 1.3 fusion.39
  23.5 0.6 add.285
  24.2 9.7 %all_gather.21 = bf16[384,384]{1,0:T(8,128)(2,1)} all-gather(bf16[96,384]{1,0:T(8,128)(2,1)} %param.28), channel_id=1, replica_groups=mesh['group'=4,'replica'=8] {'group'}, dimensions={0}, use_global_device_ids=true | all-gather | bytes 368640 | tf_op jit(solution)/shard_map/all_gather | solution.py:96
  33.9 18.0 %all_gather.20 = bf16[384,1152]{1,0:T(8,128)(2,1)S(1)} all-gather(bf16[96,1152]{1,0:T(8,128)(2,1)} %param.27), channel_id=1, replica_groups=mesh['group'=4,'replica'=8] {'group'}, dimensions={0}, use_global_device_ids=true | all-gather | bytes 1105920 | tf_op jit(solution)/shard_map/all_gather | solution.py:95
  51.9 2.1 convolution_add_fusion.2
  56.1 0.7 copy-done.30
  56.8 0.8 fusion.13
  57.6 0.6 copy.85
  58.8 0.8 fusion.76
  59.6 0.7 copy-done.13
  60.3 0.6 multiply_reduce_fusion.1
  61.6 0.7 fusion.18
  63.5 0.6 copy-done.4
  64.7 1.5 fusion.73
  66.3 1.0 add_convert_fusion
  67.2 13.2 %all-gather.7.cloned.1.call-done = bf16[384,1536]{1,0:T(8,128)(2,1)} async-done(((bf16[384,384]{1,0:T(8,128)(2,1)}), bf16[384,1536]{1,0:T(8,128)(2,1)}) %all-gather.7.cloned.1.call-update) | async-done | bytes 1179664 | tf_op jit(solution)/shard_map/all_gather | solution.py:97
  80.5 4.0 convolution_add_fusion.1
  84.4 25.7 %all-gather.9.cloned.1.call-done = bf16[1536,384]{1,0:T(8,128)(2,1)} async-done(((bf16[384,384]{1,0:T(8,128)(2,1)}), bf16[1536,384]{1,0:T(8,128)(2,1)}) %all-gather.9.cloned.1.call-update) | async-done | bytes 1179664 | tf_op jit(solution)/shard_map/all_gather | solution.py:98
  110.1 5.5 %fusion.78 = (bf16[1536]{0:T(1024)(128)(2,1)}, bf16[512,1536]{1,0:T(8,128)(2,1)S(1)}) fusion(f32[512,1536]{1,0:T(8,128)} %convolution_add_fusion.1, bf16[512,384]{1,0:T(8,128)(2,1)} %bitcast.153, bf16[1536,384]{1,0:T(8,128)(2,1)} %all-gather.9.cloned.1.call-done), kind=kOutput, calls=%fused_computation.172 | convolution fusion | flops 619706880 | bytes 6294528 | tf_op jit(solution)/shard_map/dot_general | solution.py:48
  115.5 1.2 copy-done.24
  116.8 1.9 fusion.40
  119.2 1.3 div.115
  120.6 3.6 convolution_add_fusion.3
  124.3 1.8 fusion.41
  126.1 1.9 fusion.74
  128.0 0.7 copy-done.11
  128.7 1.2 convolution_convert_fusion.5
  129.9 1.9 copy.91
  131.8 1.8 reshape.196
  133.6 1.7 convolution_bitcast_fusion
  135.4 1.2 multiply_reduce_fusion
  136.6 0.7 multiply_convert_fusion
  138.8 1.2 copy.99
  141.3 2.5 fusion.38
  144.4 1.2 multiply_reduce_fusion.3
  145.8 0.8 copy.107
  146.7 1.1 convolution_convert_fusion.6
  147.8 1.6 convolution_convert_fusion.3
  149.6 2.2 convolution_convert_fusion.2
  151.8 1.4 copy.105
  153.3 4.3 %convolution_convert_fusion.1 = bf16[1536,384]{1,0:T(8,128)(2,1)} fusion(bf16[512,384]{1,0:T(8,128)(2,1)S(1)} %bitcast.154, f32[512,1536]{1,0:T(8,128)} %convolution_add_fusion.1), kind=kOutput, calls=%fused_computation.27 | convolution fusion | flops 611647488 | bytes 4718592 | tf_op jit(solution)/shard_map/dot_general | solution.py:42
  157.7 1.9 convolution_convert_fusion
  159.7 1.2 fusion.19
  160.9 9.7 %reduce-scatter.21.cloned.1.call-done = bf16[96,14]{1,0:T(8,128)(2,1)} async-done(((bf16[384,14]{1,0:T(8,128)(2,1)}), bf16[96,14]{1,0:T(8,128)(2,1)}) %reduce-scatter.21.cloned.1.call-update) | async-done | bytes 2704
  170.6 0.8 copy.108
  171.3 26.9 %reduce-scatter.15.cloned.1.call-done = bf16[96,384]{1,0:T(8,128)(2,1)} async-done(((bf16[384,384]{1,0:T(8,128)(2,1)}), bf16[96,384]{1,0:T(8,128)(2,1)}) %reduce-scatter.15.cloned.1.call-update) | async-done | bytes 73744 | tf_op jit(solution)/shard_map/reduce_scatter | solution.py:257
  198.2 30.4 %reduce-scatter.13.cloned.1.call-done = bf16[96,1152]{1,0:T(8,128)(2,1)} async-done(((bf16[384,1152]{1,0:T(8,128)(2,1)}), bf16[96,1152]{1,0:T(8,128)(2,1)}) %reduce-scatter.13.cloned.1.call-update) | async-done | bytes 221200 | tf_op jit(solution)/shard_map/reduce_scatter | solution.py:254
  228.6 31.7 %reduce-scatter.19.cloned.1.call-done = bf16[384,384]{1,0:T(8,128)(2,1)} async-done(((bf16[1536,384]{1,0:T(8,128)(2,1)}), bf16[384,384]{1,0:T(8,128)(2,1)}) %reduce-scatter.19.cloned.1.call-update) | async-done | bytes 294928
  260.3 1.2 copy.106
  261.5 30.6 %reduce-scatter.17.cloned.1.call-done = bf16[384,384]{1,0:T(8,128)(2,1)} async-done(((bf16[1536,384]{1,0:T(8,128)(2,1)}), bf16[384,384]{1,0:T(8,128)(2,1)}) %reduce-scatter.17.cloned.1.call-update) | async-done | bytes 294928 | tf_op jit(solution)/shard_map/reduce_scatter | solution.py:263
  292.1 35.8 %reduce-scatter.11.cloned.1.call-done = bf16[96,2304]{1,0:T(8,128)(2,1)} async-done(((bf16[384,2304]{1,0:T(8,128)(2,1)}), bf16[96,2304]{1,0:T(8,128)(2,1)}) %reduce-scatter.11.cloned.1.call-update) | async-done | bytes 442384 | tf_op jit(solution)/shard_map/reduce_scatter | solution.py:251
  327.9 65.8 %all-reduce.2 = (f32[96,2304]{1,0:T(8,128)S(1)}, f32[96,1152]{1,0:T(8,128)}, f32[96,384]{1,0:T(8,128)S(1)}, f32[384,384]{1,0:T(8,128)S(1)}, f32[384,384]{1,0:T(8,128)S(1)}, /*index=5*/f32[14,96]{1,0:T(8,128)S(1)}) all-reduce(bf16[96,2304]{1,0:T(8,128)(2,1)} %reduce-scatter.11.cloned.1.call-don, ...), channel_id=1, replica_groups=mesh['group'=4,'replica'=8] {'replica'}, use_global_device_ids=true, to_apply=%region_18.19 | all-reduce | flops 664896 | bytes 3989376 | tf_op jit(solution)/shard_map/psum | solution.py:270
  393.7 0.6 convert_subtract_fusion.6
  394.4 1.7 convert_subtract_fusion.5
  396.1 2.5 convert_subtract_fusion.4
  398.7 3.2 convert_subtract_fusion.1
  401.9 1.5 convert_subtract_fusion.3
  403.4 1.5 convert_subtract_fusion.2
  (215 shorter events, 10.0 us)
Async XLA Ops:
  7.2 48.6 %copy-start.3 = (bf16[2,256,384]{2,1,0:T(8,128)(2,1)S(1)}, bf16[2,256,384]{2,1,0:T(8,128)(2,1)}, u32[]{:S(2)}) copy-start(bf16[2,256,384]{2,1,0:T(8,128)(2,1)} %param.22) | copy-start | bytes 1179652
  7.2 44.7 %copy-start.53 = (f32[2,384]{1,0:T(2,128)S(1)}, f32[2,384]{1,0:T(2,128)}, u32[]{:S(2)}) copy-start(f32[2,384]{1,0:T(2,128)} %param.23) | copy-start | bytes 9220
  7.2 44.7 %all-gather.5.cloned.1.call-start = ((), (), s32[]{:S(2)}) async-start(), calls=%async_computation.6 | async-start | bytes 2211840 | tf_op jit(solution)/shard_map/all_gather | solution.py:94
  7.9 72.5 %all-gather.7.cloned.1.call-start = ((), (), s32[]{:S(2)}) async-start(), calls=%async_computation.7 | async-start | bytes 1474560 | tf_op jit(solution)/shard_map/all_gather | solution.py:97
  8.7 101.4 %all-gather.9.cloned.1.call-start = ((), (), s32[]{:S(2)}) async-start(), calls=%async_computation.8 | async-start | bytes 1474560 | tf_op jit(solution)/shard_map/all_gather | solution.py:98
  9.4 161.1 %reduce-scatter.21.cloned.1.call-start = ((), (), s32[]{:S(2)}) async-start(), calls=%async_computation.14 | async-start | bytes 122880
  22.3 33.8 %copy-start.45 = (f32[2,256]{1,0:T(2,128)}, f32[2,256]{1,0:T(2,128)S(1)}, u32[]{:S(2)}) copy-start(f32[2,256]{1,0:T(2,128)S(1)} %broadcast_multiply_fusion.5) | copy-start | bytes 6148
  23.5 32.5 %copy-start.57 = (f32[2,256]{1,0:T(2,128)}, f32[2,256]{1,0:T(2,128)S(1)}, u32[]{:S(2)}) copy-start(f32[2,256]{1,0:T(2,128)S(1)} %add_rsqrt_fusion.1) | copy-start | bytes 6148
  51.8 4.2 %copy-start.29 = (bf16[384,1152]{1,0:T(8,128)(2,1)}, bf16[384,1152]{1,0:T(8,128)(2,1)S(1)}, u32[]{:S(2)}) copy-start(bf16[384,1152]{1,0:T(8,128)(2,1)S(1)} %all_gather.20) | copy-start | bytes 2654212
  59.6 2.0 copy-start.17
  61.6 2.6 copy-start.49
  62.3 2.4 copy-start.61
  62.3 2.4 copy-start.62
  62.3 2.4 copy-start.9
  62.3 2.4 copy-start.70
  62.3 3.9 copy-start.60
  64.3 1.9 copy-start
  64.4 1.9 copy-start.43
  110.1 6.7 %copy-start.27 = (bf16[384,1536]{1,0:T(8,128)(2,1)S(1)}, bf16[384,1536]{1,0:T(8,128)(2,1)}, u32[]{:S(2)}) copy-start(bf16[384,1536]{1,0:T(8,128)(2,1)} %all-gather.7.cloned.1.call-done) | copy-start | bytes 3538948
  110.1 6.7 %copy-start.40 = (f32[2,384]{1,0:T(2,128)S(1)}, f32[2,384]{1,0:T(2,128)}, u32[]{:S(2)}) copy-start(f32[2,384]{1,0:T(2,128)} %copy-done.39) | copy-start | bytes 9220
  120.5 3.7 copy-start.1
  120.5 3.7 copy-start.2
  120.5 3.7 copy-start.10
  120.5 3.7 copy-start.41
  120.5 3.7 copy-start.44
  120.5 3.7 copy-start.48
  120.5 3.7 copy-start.52
  120.5 3.7 copy-start.71
  124.1 1.9 copy-start.50
  124.2 1.9 copy-start.64
  124.3 4.5 %copy-start.22 = (bf16[384,384]{1,0:T(8,128)(2,1)S(1)}, bf16[384,384]{1,0:T(8,128)(2,1)}, u32[]{:S(2)}) copy-start(bf16[384,384]{1,0:T(8,128)(2,1)} %all_gather.21) | copy-start | bytes 884740
  138.6 2.1 copy-start.74
  138.6 2.1 copy-start.73
  138.6 2.7 copy-start.46
  138.6 2.7 copy-start.56
  138.6 2.7 copy-start.58
  141.3 3.1 copy-start.5
  141.3 3.1 copy-start.20
  143.8 1.9 copy-start.65
  143.8 2.8 copy-start.8
  143.8 2.8 copy-start.12
  144.1 3.7 copy-start.31
  145.6 4.0 copy-start.33
  146.6 51.6 %reduce-scatter.15.cloned.1.call-start = ((), (), s32[]{:S(2)}) async-start(), calls=%async_computation.11 | async-start | bytes 368640 | tf_op jit(solution)/shard_map/reduce_scatter | solution.py:257
  147.8 80.8 %reduce-scatter.13.cloned.1.call-start = ((), (), s32[]{:S(2)}) async-start(), calls=%async_computation.10 | async-start | bytes 1105920 | tf_op jit(solution)/shard_map/reduce_scatter | solution.py:254
  149.5 3.8 copy-start.32
  149.5 110.8 %reduce-scatter.19.cloned.1.call-start = ((), (), s32[]{:S(2)}) async-start(), calls=%async_computation.13 | async-start | bytes 1474560
  153.2 4.4 %copy-start.54 = (f32[2,384]{1,0:T(2,128)S(1)}, f32[2,384]{1,0:T(2,128)}, u32[]{:S(2)}) copy-start(f32[2,384]{1,0:T(2,128)} %param.23) | copy-start | bytes 9220
  153.2 138.8 %reduce-scatter.17.cloned.1.call-start = ((), (), s32[]{:S(2)}) async-start(), calls=%async_computation.12 | async-start | bytes 1474560 | tf_op jit(solution)/shard_map/reduce_scatter | solution.py:263
  157.6 2.1 copy-start.6
  157.6 170.3 %reduce-scatter.11.cloned.1.call-start = ((), (), s32[]{:S(2)}) async-start(), calls=%async_computation.9 | async-start | bytes 2211840 | tf_op jit(solution)/shard_map/reduce_scatter | solution.py:251
  159.6 234.1 %copy-start.59 = (bf16[14,96]{1,0:T(8,128)(2,1)S(1)}, bf16[14,96]{1,0:T(8,128)(2,1)}, u32[]{:S(2)}) copy-start(bf16[14,96]{1,0:T(8,128)(2,1)} %param.31) | copy-start | bytes 8068
  159.6 234.1 %copy-start.75 = (bf16[14,96]{1,0:T(8,128)(2,1)S(1)}, bf16[14,96]{1,0:T(8,128)(2,1)}, u32[]{:S(2)}) copy-start(bf16[14,96]{1,0:T(8,128)(2,1)} %param.37) | copy-start | bytes 8068
  159.6 234.1 %copy-start.76 = (bf16[14,96]{1,0:T(8,128)(2,1)S(1)}, bf16[14,96]{1,0:T(8,128)(2,1)}, u32[]{:S(2)}) copy-start(bf16[14,96]{1,0:T(8,128)(2,1)} %param.43) | copy-start | bytes 8068
  159.6 234.8 %copy-start.38 = (bf16[96,384]{1,0:T(8,128)(2,1)S(1)}, bf16[96,384]{1,0:T(8,128)(2,1)}, u32[]{:S(2)}) copy-start(bf16[96,384]{1,0:T(8,128)(2,1)} %param.28) | copy-start | bytes 221188
  159.6 234.8 %copy-start.42 = (bf16[96,384]{1,0:T(8,128)(2,1)S(1)}, bf16[96,384]{1,0:T(8,128)(2,1)}, u32[]{:S(2)}) copy-start(bf16[96,384]{1,0:T(8,128)(2,1)} %param.34) | copy-start | bytes 221188
  159.6 236.5 %copy-start.28 = (bf16[96,1152]{1,0:T(8,128)(2,1)S(1)}, bf16[96,1152]{1,0:T(8,128)(2,1)}, u32[]{:S(2)}) copy-start(bf16[96,1152]{1,0:T(8,128)(2,1)} %param.27) | copy-start | bytes 663556
  159.7 239.0 %copy-start.23 = (bf16[96,2304]{1,0:T(8,128)(2,1)S(1)}, bf16[96,2304]{1,0:T(8,128)(2,1)}, u32[]{:S(2)}) copy-start(bf16[96,2304]{1,0:T(8,128)(2,1)} %param.26) | copy-start | bytes 1327108
  396.1 5.7 %copy-start.25 = (bf16[384,384]{1,0:T(8,128)(2,1)S(1)}, bf16[384,384]{1,0:T(8,128)(2,1)}, u32[]{:S(2)}) copy-start(bf16[384,384]{1,0:T(8,128)(2,1)} %param.29) | copy-start | bytes 884740
  396.1 5.7 %copy-start.34 = (bf16[384,384]{1,0:T(8,128)(2,1)S(1)}, bf16[384,384]{1,0:T(8,128)(2,1)}, u32[]{:S(2)}) copy-start(bf16[384,384]{1,0:T(8,128)(2,1)} %param.35) | copy-start | bytes 884740
  396.1 5.7 %copy-start.35 = (bf16[384,384]{1,0:T(8,128)(2,1)S(1)}, bf16[384,384]{1,0:T(8,128)(2,1)}, u32[]{:S(2)}) copy-start(bf16[384,384]{1,0:T(8,128)(2,1)} %param.41) | copy-start | bytes 884740
  398.7 4.7 %copy-start.26 = (bf16[384,384]{1,0:T(8,128)(2,1)S(1)}, bf16[384,384]{1,0:T(8,128)(2,1)}, u32[]{:S(2)}) copy-start(bf16[384,384]{1,0:T(8,128)(2,1)} %param.30) | copy-start | bytes 884740
  398.7 4.7 %copy-start.36 = (bf16[384,384]{1,0:T(8,128)(2,1)S(1)}, bf16[384,384]{1,0:T(8,128)(2,1)}, u32[]{:S(2)}) copy-start(bf16[384,384]{1,0:T(8,128)(2,1)} %param.36) | copy-start | bytes 884740
  398.7 4.7 %copy-start.37 = (bf16[384,384]{1,0:T(8,128)(2,1)S(1)}, bf16[384,384]{1,0:T(8,128)(2,1)}, u32[]{:S(2)}) copy-start(bf16[384,384]{1,0:T(8,128)(2,1)} %param.42) | copy-start | bytes 884740
  (22 other events, 29.7 us)
Sparse Core Ops, SparseCore 0:
  9.9 41.0 all-gather.4
  52.8 27.6 all-gather.6
  82.3 27.7 all-gather.8
  146.7 23.8 reduce-scatter.20
  174.0 24.1 reduce-scatter.14
  201.8 26.6 reduce-scatter.12
  231.7 28.5 reduce-scatter.18
  263.5 28.5 reduce-scatter.16
  295.4 32.4 reduce-scatter.10
where the time goes:
time: 412 us; the launch traced here: 411 us
  waiting for transfers between devices  206 us (50%)
  blocking collectives  103 us (25%)
  matrix products  39.4 us (10%)
  other arithmetic  24.9 us (6%)
  local copies, waits for them, and re-layouts  21.8 us (5%)
  between operations  15.6 us (4%)
    psum x1, blocking collectives, shards(): lax.psum((owned[0], owned[1], owned[2], owned[3], owned[4], owned[5]), 'r...  65.8 us
    unnamed x11, waiting for transfers between devices  43.6 us
    reduce_scatter x1, waiting for transfers between devices, shards(): lax.psum_scatter(grad_mod.astype(jnp.bfloat16), 'group', scatter_dimensio...  35.8 us
    reduce_scatter x1, waiting for transfers between devices, shards(): lax.psum_scatter(grad_contract.astype(jnp.bfloat16), 'group', scatter_dim...  30.6 us
    reduce_scatter x1, waiting for transfers between devices, shards(): lax.psum_scatter(grad_attending.astype(jnp.bfloat16), 'group', scatter_di...  30.4 us
    reduce_scatter x1, waiting for transfers between devices, shards(): lax.psum_scatter(grad_proj.astype(jnp.bfloat16), 'group', scatter_dimensi...  26.9 us
    all_gather x1, waiting for transfers between devices, shards(): lax.all_gather(contract, 'group', axis=0, tiled=True)  25.7 us
    all_gather x1, blocking collectives, shards(): lax.all_gather(attending, 'group', axis=0, tiled=True)  18 us
  transfers between devices with their start and end apart: 9, of which 8 were waited for; matrix products, arithmetic and copies ran while one was open for 9% of the time, Pallas kernels for 0%

commit v1 on v0

v1 whole, which is shorter than its diff:
```python
import functools

import jax
import jax.numpy as jnp
from jax import lax
from jax.experimental import pallas as pl
from jax.experimental.pallas import tpu as pltpu
from jax.sharding import PartitionSpec as P

HEADS = 6
HEAD_DIM = 64
FF = 1536
STEP = 10


NORM_EPS = 1e-06
ADAM_EPS = 1e-08
BETA_FIRST = 0.9
BETA_SECOND = 0.999
DECAY_RATE = 0.1
LEARN_RATES = (0.05, 0.05, 0.2, 0.05, 0.025, 0.1)
DECAY_FLAGS = (1.0, 1.0, 1.0, 1.0, 1.0, 0.0)
GELU_COEF = 0.7978845608028654
BIAS_ROWS = 14
D = 384
SEQ = 256
QUARTER = D // 4
VMEM_BYTES = 48 * 1024 * 1024
LOW = jnp.bfloat16
SMALL = 32
WIDE = jnp.float32


def dot_plain(left_side, right_side):
    return jnp.dot(left_side, right_side, preferred_element_type=WIDE)


def dot_first(left_side, right_side):
    return lax.dot_general(
        left_side, right_side, (((0,), (0,)), ((), ())), preferred_element_type=WIDE
    )


def dot_last(left_side, right_side):
    return lax.dot_general(
        left_side, right_side, (((1,), (1,)), ((), ())), preferred_element_type=WIDE
    )


def adam_update(weight, gradient, mean_old, square_old, step_rate, decay_flag):
    momentum = BETA_FIRST * mean_old + (1.0 - BETA_FIRST) * gradient
    variance = BETA_SECOND * square_old + (1.0 - BETA_SECOND) * gradient * gradient
    mean_hat = momentum / (1.0 - BETA_FIRST**STEP)
    square_hat = variance / (1.0 - BETA_SECOND**STEP)
    updated = weight - step_rate * (
        mean_hat / (jnp.sqrt(square_hat) + ADAM_EPS) + decay_flag * DECAY_RATE * weight
    )
    return (updated, momentum, variance)


def replica_stages(count):
    stages, low_bit = [(0, 2)], 1
    while (1 << low_bit) < count:
        radix = min(4, count >> low_bit)
        stages.append((low_bit, radix))
        low_bit += radix.bit_length() - 1
    return stages


def swap_group(value, k):
    if k == 0:
        return value
    return lax.ppermute(value, "group", [(i, i ^ k) for i in range(lax.axis_size("group"))])


def swap_replica(value, k):
    if k == 0:
        return value
    return lax.ppermute(value, "replica", [(i, i ^ k) for i in range(lax.axis_size("replica"))])


def pick(blocks, index):
    return lax.dynamic_index_in_dim(blocks, index, axis=0, keepdims=False)


def in_order(blocks, digit):
    ordered = []
    for place in range(len(blocks)):
        chosen = blocks[0]
        for k in range(1, len(blocks)):
            chosen = jnp.where((digit ^ k) == place, blocks[k], chosen)
        ordered.append(chosen)
    return jnp.stack(ordered)


def wide_sum(blocks):
    total = blocks[0].astype(jnp.float32)
    for block in blocks[1:]:
        total = total + block.astype(jnp.float32)
    return total


def scatter_stage(value, digit, low_bit, radix):
    rows = value.shape[-2] // radix
    parts = [
        lax.dynamic_slice_in_dim(value, (digit ^ k) * rows, rows, value.ndim - 2)
        for k in range(radix)
    ]
    received = [swap_replica(parts[k], k << low_bit) for k in range(radix)]
    return wide_sum(received).astype(jnp.bfloat16)


def reduce_replicas(value, copy, stages):
    core = copy % 2
    for low_bit, radix in stages[1:]:
        value = scatter_stage(value, (copy >> low_bit) % radix, low_bit, radix)
    for low_bit, radix in reversed(stages[1:]):
        blocks = [swap_replica(value, k << low_bit) for k in range(radix)]
        value = in_order(blocks, (copy >> low_bit) % radix)
        value = value.reshape(-1, value.shape[-1])
    other = swap_replica(value, 1)
    return (
        jnp.where(core == 0, value, other).astype(jnp.float32),
        jnp.where(core == 0, other, value).astype(jnp.float32),
    )


def layer_norm_parts(values):
    centred = values - jnp.mean(values, axis=-1, keepdims=True)
    inverse = lax.rsqrt(jnp.mean(centred * centred, axis=-1, keepdims=True) + NORM_EPS)
    return (centred * inverse, inverse)


def norm_backward(grad_normed, normed, inverse):
    mean_grad = jnp.mean(grad_normed, axis=-1, keepdims=True)
    mean_cross = jnp.mean(grad_normed * normed, axis=-1, keepdims=True)
    return inverse * (grad_normed - mean_grad - normed * mean_cross)


def column_sum(values):
    return jnp.sum(values, axis=0, keepdims=True)


def head_mask(shape, which):
    lane = lax.broadcasted_iota(jnp.int32, shape, 1)
    return (lane < HEAD_DIM) if which == 0 else (lane >= HEAD_DIM)


def place_rows(target, lanes, block, owner):
    start = pl.multiple_of(owner * QUARTER, 32)
    target[pl.ds(start, QUARTER), lanes] = block


def neighbours(where):
    rank, core = where[0], where[1]
    return (rank ^ (1 + core), rank ^ (2 - core), rank ^ 3)


def payload_kernel(where, condition, attending, projection, biases, out):
    @pl.when(where[1] == 0)
    def _():
        out[0:QUARTER, :] = attending[:, 0:D]
        out[QUARTER : 2 * QUARTER, :] = attending[:, D : 2 * D]

    @pl.when(where[1] != 0)
    def _():
        out[0:QUARTER, :] = attending[:, 2 * D : 3 * D]
        out[QUARTER : 2 * QUARTER, :] = projection[...]

    cond = condition[...]
    active = cond / (1.0 + jnp.exp(-cond))
    padded = jnp.concatenate(
        [biases[...].astype(WIDE), jnp.zeros((BIAS_ROWS, D - QUARTER), WIDE)], axis=1
    )
    out[2 * QUARTER :, :] = jnp.concatenate([active, padded], axis=0).astype(LOW)


def modulation_kernel(
    where, own, first, second, last, weight, expand, contract, stay, go, bias_out, feed_part
):
    rank = where[0]
    owners = (rank,) + neighbours(where)
    rows = [block[...].astype(WIDE) for block in (own, first, second, last)]
    conds = jnp.concatenate([rows[0][0:2], rows[2][0:2], rows[1][0:2], rows[3][0:2]], axis=0)
    columns = conds[:, :QUARTER]
    for place in range(1, 4):
        lanes = slice(place * QUARTER, (place + 1) * QUARTER)
        columns = jnp.where(rank == place, conds[:, lanes], columns)
    partial = dot_plain(columns.astype(LOW), weight[...])
    stay[...] = partial[:4]
    go[...] = partial[4:]
    lanes = []
    for place in range(4):
        chosen = rows[0][:, :QUARTER]
        for k in range(1, 4):
            chosen = jnp.where(owners[k] == place, rows[k][:, :QUARTER], chosen)
        lanes.append(chosen)
    bias_out[...] = jnp.concatenate(lanes, axis=1)

    @pl.when(where[1] == 0)
    def _():
        feed_part[...] = expand[...]

    @pl.when(where[1] != 0)
    def _():
        feed_part[...] = contract[...]


def attention_forward_kernel(
    where, tokens, stay, arrived, bias, own_att, own_proj, n1, n2, n3, f1, f2, f3,
    joined_out, soft_out, mixed_out, mod_out, att, proj,
):
    slot = pl.program_id(0)
    rank = where[0]

    core = where[1]

    def assemble(lows, highs):
        for k, block in zip((1, 2, 3), lows):
            place_rows(att, slice(0, D), block[0:QUARTER, :], rank ^ k)
            place_rows(att, slice(D, 2 * D), block[QUARTER : 2 * QUARTER, :], rank ^ k)
        for k, block in zip((2, 1, 3), highs):
            place_rows(att, slice(2 * D, 3 * D), block[0:QUARTER, :], rank ^ k)
            place_rows(proj, slice(0, D), block[QUARTER : 2 * QUARTER, :], rank ^ k)

    @pl.when(slot == 0)
    def _():
        place_rows(att, slice(0, 3 * D), own_att[...], rank)
        place_rows(proj, slice(0, D), own_proj[...], rank)

        @pl.when(core == 0)
        def _():
            assemble((n1, n2, n3), (f1, f2, f3))

        @pl.when(core != 0)
        def _():
            assemble((f1, f2, f3), (n1, n2, n3))

    summed = stay[0:2, :] + arrived[...]
    row = jnp.where(slot == 0, summed[0:1], summed[1:2])
    pieces = [row[:, j * D : (j + 1) * D] + bias[2 + j : 3 + j, :] for j in range(6)]
    mod_out[0] = jnp.concatenate(pieces, axis=0)
    normed, _ = layer_norm_parts(tokens[0].astype(WIDE))
    first_in = (normed * (1.0 + pieces[1]) + pieces[0]).astype(LOW)
    thirds = []
    for third in range(3):
        part = dot_plain(first_in, att[:, third * D : (third + 1) * D])
        if third == 0:
            part = part + bias[8:9, :]
        if third == 2:
            part = part + bias[9:10, :]
        part = part.astype(LOW)
        joined_out[0, :, third * D : (third + 1) * D] = part
        thirds.append(part)
    first_half = head_mask((SEQ, 128), 0)
    scale = jnp.asarray(HEAD_DIM ** (-0.5), LOW)
    zero = jnp.zeros((SEQ, 128), LOW)
    for pair in range(HEADS // 2):
        lanes = slice(pair * 128, (pair + 1) * 128)
        query, key, value = (part[:, lanes] for part in thirds)
        query = query * scale
        outs = []
        for half in range(2):
            masked = (
                jnp.where(first_half, query, zero)
                if half == 0
                else jnp.where(first_half, zero, query)
            )
            scores = dot_last(masked, key)
            weights = jnp.exp(scores - jnp.max(scores, axis=-1, keepdims=True))
            total = jnp.sum(weights, axis=-1, keepdims=True)
            soft = (weights * (1.0 / total)).astype(LOW)
            soft_out[0, 2 * pair + half] = soft
            outs.append(dot_plain(soft, value))
        mixed_out[0, :, lanes] = jnp.where(first_half, outs[0], outs[1]).astype(LOW)


def feed_kernel(
    where, mixed, tokens, cotangent, mod, bias, proj, own_expand, own_contract, n1, n2, n3, f1, f2, f3,
    out, grad_middle_out, send_out, keep_out, rows_out,
    expands, contracts, branch, middle, second, normed, inverse, grad_feed, feed, grad_second,
):
    step = pl.program_id(0)
    rank, core, live = where[0], where[1], where[3]

    def assemble(lows, highs):
        for k, block in zip((1, 2, 3), lows):
            expands[k] = block[...]
        for k, block in zip((2, 1, 3), highs):
            contracts[k] = block[...]

    slots = [slice(s * SEQ, (s + 1) * SEQ) for s in range(2)]

    @pl.when(step == 0)
    def _():
        expands[0] = own_expand[...]
        contracts[0] = own_contract[...]

        @pl.when(core == 0)
        def _():
            assemble((n1, n2, n3), (f1, f2, f3))

        @pl.when(core != 0)
        def _():
            assemble((f1, f2, f3), (n1, n2, n3))

        for s, rows in enumerate(slots):
            pieces = mod[s]
            value = dot_plain(mixed[s], proj[...]) + bias[10:11, :]
            branch[rows, :] = value
            centre = tokens[s].astype(WIDE) + pieces[2:3] * value
            middle[rows, :] = centre
            unit, spread = layer_norm_parts(centre)
            normed[rows, :] = unit
            inverse[rows, :] = jnp.broadcast_to(spread, (SEQ, 128))
            second[rows, :] = (unit * (1.0 + pieces[4:5]) + pieces[3:4]).astype(LOW)
            alive = jnp.where(s < live, 1.0, 0.0)
            grad_feed[rows, :] = (
                pieces[5:6] * (cotangent[s].astype(WIDE) * alive)
            ).astype(LOW)
        rows_out[...] = jnp.zeros_like(rows_out)
        rows_out[12:13, :] = column_sum(grad_feed[...].astype(WIDE))

    hidden_bias = bias[pl.ds(11 + (rank ^ step), 1), :]
    expand, contract = expands[step], contracts[step]
    before = dot_plain(second[...], expand) + hidden_bias
    square = before * before
    tangent = jnp.tanh(before * (GELU_COEF + (GELU_COEF * 0.044715) * square))
    half_up = 0.5 + 0.5 * tangent
    activated = (before * half_up).astype(LOW)
    slope = half_up + (0.5 * before) * (1.0 - tangent * tangent) * (
        GELU_COEF + (GELU_COEF * 3.0 * 0.044715) * square
    )
    grad_before_wide = dot_last(grad_feed[...], contract) * slope
    grad_before = grad_before_wide.astype(LOW)
    feed_term = dot_plain(activated, contract)
    second_term = dot_last(grad_before, expand)
    grad_expand = dot_first(second[...], grad_before).astype(LOW)
    grad_contract = dot_first(activated, grad_feed[...]).astype(LOW)
    rows_out[pl.ds(8 + (rank ^ step), 1), :] = column_sum(grad_before.astype(WIDE))

    @pl.when(core == 0)
    def _():
        send_out[0] = grad_contract
        keep_out[0] = grad_expand

    @pl.when(core != 0)
    def _():
        send_out[0] = grad_expand
        keep_out[0] = grad_contract

    @pl.when(step == 0)
    def _():
        feed[...] = feed_term
        grad_second[...] = second_term

    @pl.when(step > 0)
    def _():
        feed[...] += feed_term
        grad_second[...] += second_term

    @pl.when(step == 3)
    def _():
        for s, rows in enumerate(slots):
            pieces = mod[s]
            alive = jnp.where(s < live, 1.0, 0.0)
            feed_out = feed[rows, :] + bias[15:16, :]
            grad_out = cotangent[s].astype(WIDE) * alive
            out[s] = ((middle[rows, :] + pieces[5:6] * feed_out) * alive).astype(LOW)
            grad = grad_second[rows, :]
            unit = normed[rows, :]
            grad_middle = grad_out + norm_backward(
                grad * (1.0 + pieces[4:5]), unit, inverse[rows, 0:1]
            )
            grad_middle_out[s] = grad_middle
            rows_out[4 * s : 4 * s + 1, :] = column_sum(grad_middle * branch[rows, :])
            rows_out[4 * s + 1 : 4 * s + 2, :] = column_sum(grad)
            rows_out[4 * s + 2 : 4 * s + 3, :] = column_sum(grad * unit)
            rows_out[4 * s + 3 : 4 * s + 4, :] = column_sum(grad_out * feed_out)


def attention_backward_kernel(
    slot, where, tokens, grad_middle_in, joined, soft_in, mixed, mod, feed_rows, cond, att, proj, *refs
):
    rank, core = where[0], where[1]
    if slot == 0:
        grad_tokens_out, grad_att, grad_proj, rows, grad_joined = refs
    else:
        before_att, before_proj, before_rows, _, _ = refs[:5]
        grad_tokens_out, send_out, keep_out, rows_out = refs[5:9]
        grad_joined, grad_att, grad_proj, rows = refs[9:]

    if slot == 0:
        rows[...] = jnp.zeros_like(rows)
        rows[12:14, :] = cond[...]
        rows[17:22, :] = feed_rows[8:13, :]
    else:
        rows[...] = before_rows[...]

    pieces = mod[0]
    grad_middle = grad_middle_in[0]
    grad_branch = (pieces[2:3] * grad_middle).astype(LOW)
    rows[16:17, :] += column_sum(grad_branch.astype(WIDE))
    proj_term = dot_first(mixed[0], grad_branch)
    grad_proj[...] = proj_term if slot == 0 else before_proj[...] + proj_term
    grad_mixed = dot_last(grad_branch, proj[...]).astype(LOW)
    first_half = head_mask((SEQ, 128), 0)
    zero = jnp.zeros((SEQ, 128), LOW)
    scale = HEAD_DIM ** (-0.5)
    for pair in range(HEADS // 2):
        lanes = slice(pair * 128, (pair + 1) * 128)
        query = joined[0, :, pair * 128 : (pair + 1) * 128]
        key = joined[0, :, D + pair * 128 : D + (pair + 1) * 128]
        value = joined[0, :, 2 * D + pair * 128 : 2 * D + (pair + 1) * 128]
        grads = grad_mixed[:, lanes]
        results = []
        for half in range(2):
            soft = soft_in[0, 2 * pair + half]
            masked = (
                jnp.where(first_half, grads, zero)
                if half == 0
                else jnp.where(first_half, zero, grads)
            )
            grad_soft = dot_last(masked, value)
            grad_values = dot_first(soft, grads)
            soft_wide = soft.astype(WIDE)
            weighted = soft_wide * grad_soft
            inner = jnp.sum(weighted, axis=-1, keepdims=True)
            grad_scores = (weighted - soft_wide * inner).astype(LOW)
            results.append(
                (dot_plain(grad_scores, key), dot_first(grad_scores, query), grad_values)
            )
        for third in range(3):
            merged = jnp.where(first_half, results[0][third], results[1][third])
            if third < 2:
                merged = merged * scale
            grad_joined[:, third * D + pair * 128 : third * D + (pair + 1) * 128] = merged.astype(LOW)
    grads = grad_joined[...]
    sums = column_sum(grads.astype(WIDE))
    rows[14:15, :] += sums[:, :D]
    rows[15:16, :] += sums[:, 2 * D :]
    normed, inverse = layer_norm_parts(tokens[0].astype(WIDE))
    first_in = (normed * (1.0 + pieces[1:2]) + pieces[0:1]).astype(LOW)
    att_term = dot_first(first_in, grads)
    grad_att[...] = att_term if slot == 0 else before_att[...] + att_term
    grad_first = dot_last(grads, att[...])
    grad_tokens_out[0] = (
        grad_middle + norm_backward(grad_first * (1.0 + pieces[1:2]), normed, inverse)
    ).astype(LOW)
    own_rows = jnp.concatenate(
        [
            column_sum(grad_first),
            column_sum(grad_first * normed),
        ],
        axis=0,
    )

    rows[6 * slot : 6 * slot + 2, :] = own_rows
    rows[6 * slot + 2 : 6 * slot + 6, :] = feed_rows[4 * slot : 4 * slot + 4, :]
    if slot == 0:
        return
    rows_out[...] = rows[...].astype(LOW)
    for k in range(4):
        start = pl.multiple_of((rank ^ k) * QUARTER, 32)
        block = grad_att[pl.ds(start, QUARTER), :].astype(LOW)
        low_part = (block[:, :D], block[:, D : 2 * D])
        high_part = (block[:, 2 * D :], grad_proj[pl.ds(start, QUARTER), :].astype(LOW))
        turned = (0, 2, 1, 3)[k]

        @pl.when(core == 0)
        def _():
            for j in range(2):
                keep_out[turned, j * QUARTER : (j + 1) * QUARTER, :] = low_part[j]
                send_out[k, j * QUARTER : (j + 1) * QUARTER, :] = high_part[j]

        @pl.when(core != 0)
        def _():
            for j in range(2):
                keep_out[k, j * QUARTER : (j + 1) * QUARTER, :] = high_part[j]
                send_out[turned, j * QUARTER : (j + 1) * QUARTER, :] = low_part[j]


def half_of(where):
    return (where[2] >> where[1]) & 1


def rows_at(index, count):
    return pl.ds(pl.multiple_of(index * count, 32), count)


def step0_kernel(
    where, att_keep, att_in, feed_keep, feed_in, small, att_stay, att_go, feed_stay, message, total
):
    half = half_of(where)
    att_stay[...] = att_keep[0:2].astype(WIDE) + att_in[0:2].astype(WIDE)
    att_go[...] = (att_keep[2:4].astype(WIDE) + att_in[2:4].astype(WIDE)).astype(LOW)
    total[...] = feed_keep[0] + feed_in[0].astype(WIDE)
    count = D // 2
    feed_stay[...] = total[rows_at(half, count), :]
    message[0:count, :] = total[rows_at(1 - half, count), :].astype(LOW)
    message[count:, :] = small[...]


def step1_kernel(
    where, att_keep, att_in, feed_keep, own, feed_in, att_stay, att_go, message
):
    count = D // 2
    att_stay[...] = att_keep[0] + att_in[0].astype(WIDE)
    att_go[...] = (att_keep[1] + att_in[1].astype(WIDE)).astype(LOW)
    message[0:count, :] = (feed_keep[...] + feed_in[0:count, :].astype(WIDE)).astype(LOW)
    message[count : count + SMALL, :] = own[count:, :]
    message[count + SMALL :, :] = feed_in[count:, :]


def step2_kernel(
    where, att_keep, att_in, own, feed_in, att_stay, att_go, feed_half, small, total
):
    half = half_of(where)
    count = D // 2
    total[...] = att_keep[...] + att_in[...].astype(WIDE)
    att_stay[...] = total[rows_at(half, QUARTER), :]
    att_go[...] = total[rows_at(1 - half, QUARTER), :].astype(LOW)
    feed_half[...] = (own[0:count, :].astype(WIDE) + feed_in[0:count, :].astype(WIDE)).astype(LOW)
    small[0 : 2 * SMALL, :] = own[count:, :]
    small[2 * SMALL :, :] = feed_in[count:, :]


def step3_kernel(
    where, att_keep, att_in, feed_half, feed_in, small, small_in, att_half, feed_part, small_out
):
    half = half_of(where)
    count = D // 2
    att_half[...] = (att_keep[...] + att_in[...].astype(WIDE)).astype(LOW)
    feed_part[rows_at(half, count), :] = feed_half[...]
    feed_part[rows_at(1 - half, count), :] = feed_in[...]
    small_out[0 : 4 * SMALL, :] = small[...]
    small_out[4 * SMALL :, :] = small_in[...]


def step4_kernel(
    where, att_half, att_in, small, small_in, weight, att_sum, small_out, cond_keep, cond_go
):
    att_sum[...] = (att_half[...].astype(WIDE) + att_in[...].astype(WIDE)).astype(LOW)
    small_out[0 : 8 * SMALL, :] = small[...]
    small_out[8 * SMALL :, :] = small_in[...]
    rows = [
        block[start : start + SMALL, :].astype(WIDE)
        for block in (small, small_in)
        for start in (0, 4 * SMALL)
    ]
    total = None
    for j in range(6):
        lines = [row[6 * slot + j : 6 * slot + j + 1] for row in rows for slot in range(2)]
        term = dot_last(
            jnp.concatenate(lines, axis=0).astype(LOW), weight[:, j * D : (j + 1) * D]
        )
        total = term if total is None else total + term
    padded = jnp.concatenate([total, jnp.zeros((8, 128 - QUARTER), WIDE)], axis=1)
    blank = jnp.zeros((4, 128), WIDE)
    cond_keep[...] = jnp.concatenate([padded[0:4], blank], axis=0)
    cond_go[...] = jnp.concatenate([padded[4:8], blank], axis=0)


def step5_kernel(where, att_sum, att_in, cond_keep, cond_in, _, __, att_part, cond_go):
    half = half_of(where)
    att_part[rows_at(half, QUARTER), :] = att_sum[...]
    att_part[rows_at(1 - half, QUARTER), :] = att_in[...]
    blank = jnp.zeros((4, 128), WIDE)
    cond_go[...] = jnp.concatenate([cond_keep[2:4], cond_in[2:4], blank], axis=0)


def modulation_update_kernel(
    where, near, far, weight, mean, square, bias, bias_mean, bias_square,
    weight_out, mean_out, square_out, bias_out, bias_mean_out, bias_square_out, everyone,
):
    rank, core, plane = where[0], where[1], where[2]
    for side, source in enumerate((near, far)):
        here = core ^ side
        first, second = 1 + here, 2 - here
        for index in range(16):
            a, b, c, d = (index & 1, (index >> 1) & 1, (index >> 2) & 1, index >> 3)
            z_at = plane ^ (a * first) ^ (b * second)
            g_at = rank ^ (c * second) ^ (d * first)
            place = (g_at * 4 + z_at) * 2 + here
            block = source[index * SMALL : (index + 1) * SMALL, :].astype(WIDE)
            for third in range(3):
                everyone[third, rows_at(place, SMALL), :] = block[
                    :, third * 128 : (third + 1) * 128
                ]

    def line(at):
        parts = [everyone[third, pl.ds(at, 32, stride=SMALL), :] for third in range(3)]
        return jnp.concatenate(parts, axis=1)

    def both(at, other):
        return jnp.concatenate([line(at), line(other)], axis=0)

    def own_lanes(values):
        chosen = values[:, :QUARTER]
        for place in range(1, 4):
            lanes = slice(place * QUARTER, (place + 1) * QUARTER)
            chosen = jnp.where(rank == place, values[:, lanes], chosen)
        return chosen

    cond = own_lanes(both(12, 13)).astype(LOW)
    sums = []
    for j in range(6):
        lanes = slice(j * D, (j + 1) * D)
        grads = both(j, 6 + j)
        sums.append(column_sum(grads))
        gradient = dot_first(cond, grads.astype(LOW))
        updated, momentum, variance = adam_update(
            weight[:, lanes].astype(WIDE),
            gradient,
            mean[:, lanes].astype(WIDE),
            square[:, lanes].astype(WIDE),
            LEARN_RATES[0],
            DECAY_FLAGS[0],
        )
        weight_out[:, lanes] = updated
        mean_out[:, lanes] = momentum
        square_out[:, lanes] = variance
    for at in range(14, 22):
        sums.append(column_sum(line(at)))
    gradient = own_lanes(jnp.concatenate(sums, axis=0))
    updated, momentum, variance = adam_update(
        bias[...].astype(WIDE),
        gradient,
        bias_mean[...].astype(WIDE),
        bias_square[...].astype(WIDE),
        LEARN_RATES[5],
        DECAY_FLAGS[5],
    )
    bias_out[...] = updated
    bias_mean_out[...] = momentum
    bias_square_out[...] = variance


def split_kernel(keep, arrived, stay, go):
    half = stay.shape[0]
    stay[...] = keep[:half].astype(WIDE) + arrived[:half].astype(WIDE)
    go[...] = (keep[half:].astype(WIDE) + arrived[half:].astype(WIDE)).astype(LOW)


def whole(shape):
    return pl.BlockSpec(shape, lambda *grid: (0,) * len(shape))


def by_slot(shape):
    return pl.BlockSpec((1,) + shape, lambda s: (s,) + (0,) * len(shape))


def shape_of(shape, dtype):
    return jax.ShapeDtypeStruct(shape, dtype)


SMEM_SPEC = pl.BlockSpec(memory_space=pltpu.SMEM)
PARAMS = pltpu.CompilerParams(vmem_limit_bytes=VMEM_BYTES)


ANY_SPEC = pl.BlockSpec(memory_space=pl.ANY)


def small_call(kernel, name, outs, where, *operands, scratch=(), after=()):
    return pl.pallas_call(
        kernel,
        grid=(1,),
        in_specs=[SMEM_SPEC]
        + [whole(item.shape) for item in operands]
        + [ANY_SPEC] * len(after),
        out_specs=[whole(shape) for shape, _ in outs],
        out_shape=[shape_of(*item) for item in outs],
        scratch_shapes=[pltpu.VMEM(*item) for item in scratch],
        compiler_params=PARAMS,
        name=name,
    )(where, *operands, *after)


def run_payload(where, condition, attending, projection, biases):
    return small_call(
        payload_kernel,
        "own_payload",
        [((2 * QUARTER + 16, D), LOW)],
        where,
        condition,
        attending,
        projection,
        biases,
    )[0]


def run_modulation(where, blocks, weight, expand, contract):
    message = pl.BlockSpec((16, D), lambda s: (2 * QUARTER // 16, 0))
    return pl.pallas_call(
        modulation_kernel,
        grid=(1,),
        in_specs=[SMEM_SPEC] + [message] * 4 + [whole((QUARTER, 6 * D))] + [whole((D, D))] * 2,
        out_specs=[whole((4, 6 * D))] * 2 + [whole((16, D)), whole((D, D))],
        out_shape=[shape_of((4, 6 * D), WIDE)] * 2
        + [shape_of((16, D), WIDE), shape_of((D, D), LOW)],
        compiler_params=PARAMS,
        cost_estimate=pl.CostEstimate(flops=10**7, bytes_accessed=10**6, transcendentals=0),
        name="modulation_partials",
    )(where, *blocks, weight, expand, contract)


def run_attention_forward(where, tokens, stay, arrived, bias, own_att, own_proj, nears, fars):
    part = whole((2 * QUARTER + 16, D))
    return pl.pallas_call(
        attention_forward_kernel,
        grid=(2,),
        in_specs=[
            SMEM_SPEC,
            by_slot((SEQ, D)),
            whole((4, 6 * D)),
            whole((2, 6 * D)),
            whole((16, D)),
            whole((QUARTER, 3 * D)),
            whole((QUARTER, D)),
        ]
        + [part] * 6,
        out_specs=[
            by_slot((SEQ, 3 * D)),
            by_slot((HEADS, SEQ, SEQ)),
            by_slot((SEQ, D)),
            by_slot((6, D)),
            whole((D, 3 * D)),
            whole((D, D)),
        ],
        out_shape=[
            shape_of((2, SEQ, 3 * D), LOW),
            shape_of((2, HEADS, SEQ, SEQ), LOW),
            shape_of((2, SEQ, D), LOW),
            shape_of((2, 6, D), WIDE),
            shape_of((D, 3 * D), LOW),
            shape_of((D, D), LOW),
        ],
        compiler_params=PARAMS,
        cost_estimate=pl.CostEstimate(
            flops=3 * 10**9, bytes_accessed=6 * 10**6, transcendentals=10**6
        ),
        name="attention_forward",
    )(where, tokens, stay, arrived, bias, own_att, own_proj, *nears, *fars)


def run_feed(where, mixed, tokens, cotangent, mod, bias, proj, own_expand, own_contract, nears, fars):
    rows = 2 * SEQ

    def turned(step):
        return jnp.where(step == 1, 2, jnp.where(step == 2, 1, step))

    def keep_place(step, where):
        return (jnp.where(where[1] == 0, turned(step), step), 0, 0)

    def send_place(step, where):
        return (jnp.where(where[1] == 0, step, turned(step)), 0, 0)

    return pl.pallas_call(
        feed_kernel,
        grid_spec=pltpu.PrefetchScalarGridSpec(
            num_scalar_prefetch=1,
            grid=(4,),
            in_specs=[whole((2, SEQ, D))] * 3
            + [whole((2, 6, D)), whole((16, D))]
            + [whole((D, D))] * 9,
            out_specs=[
                whole((2, SEQ, D)),
                whole((2, SEQ, D)),
                pl.BlockSpec((1, D, D), send_place),
                pl.BlockSpec((1, D, D), keep_place),
                whole((16, D)),
            ],
            scratch_shapes=[
                pltpu.VMEM((4, D, D), LOW),
                pltpu.VMEM((4, D, D), LOW),
                pltpu.VMEM((rows, D), WIDE),
                pltpu.VMEM((rows, D), WIDE),
                pltpu.VMEM((rows, D), LOW),
                pltpu.VMEM((rows, D), WIDE),
                pltpu.VMEM((rows, 128), WIDE),
                pltpu.VMEM((rows, D), LOW),
                pltpu.VMEM((rows, D), WIDE),
                pltpu.VMEM((rows, D), WIDE),
            ],
        ),
        out_shape=[
            shape_of((2, SEQ, D), LOW),
            shape_of((2, SEQ, D), WIDE),
            shape_of((4, D, D), LOW),
            shape_of((4, D, D), LOW),
            shape_of((16, D), WIDE),
        ],
        compiler_params=PARAMS,
        cost_estimate=pl.CostEstimate(
            flops=8 * 10**9, bytes_accessed=10**7, transcendentals=10**6
        ),
        name="feed_forward_and_back",
    )(where, mixed, tokens, cotangent, mod, bias, proj, own_expand, own_contract, *nears, *fars)


def run_attention_backward(
    slot, where, tokens, grad_middle, joined, soft, mixed, mod, feed_rows, cond, att, proj, earlier=()
):
    def at_slot(shape):
        return pl.BlockSpec((1,) + shape, lambda i: (slot,) + (0,) * len(shape))

    sums = [((D, 3 * D), WIDE), ((D, D), WIDE), ((SMALL, D), WIDE)]
    in_specs = [
        SMEM_SPEC,
        at_slot((SEQ, D)),
        at_slot((SEQ, D)),
        at_slot((SEQ, 3 * D)),
        at_slot((HEADS, SEQ, SEQ)),
        at_slot((SEQ, D)),
        at_slot((6, D)),
        whole((16, D)),
        whole((2, D)),
        whole((D, 3 * D)),
        whole((D, D)),
    ]
    out_specs = [at_slot((SEQ, D))]
    out_shape = [shape_of((2, SEQ, D), LOW)]
    scratch = [pltpu.VMEM((SEQ, 3 * D), LOW)]
    aliases = {}
    if slot == 0:
        out_specs += [whole(shape) for shape, _ in sums]
        out_shape += [shape_of(*item) for item in sums]
    else:
        in_specs += [whole(shape) for shape, _ in sums] + [ANY_SPEC, ANY_SPEC]
        aliases = {14: 0}
        out_specs += [whole((4, 2 * QUARTER, D))] * 2 + [whole((SMALL, D))]
        out_shape += [shape_of((4, 2 * QUARTER, D), LOW)] * 2 + [shape_of((SMALL, D), LOW)]
        scratch += [pltpu.VMEM(*item) for item in sums]
    return pl.pallas_call(
        functools.partial(attention_backward_kernel, slot),
        grid=(1,),
        in_specs=in_specs,
        out_specs=out_specs,
        out_shape=out_shape,
        scratch_shapes=scratch,
        input_output_aliases=aliases,
        compiler_params=PARAMS,
        cost_estimate=pl.CostEstimate(
            flops=4 * 10**9, bytes_accessed=8 * 10**6, transcendentals=0
        ),
        name="attention_backward",
    )(where, tokens, grad_middle, joined, soft, mixed, mod, feed_rows, cond, att, proj, *earlier)


def run_split(keep, arrived):
    count, rest = keep.shape[0], keep.shape[1:]
    half = (count // 2,) + rest
    return pl.pallas_call(
        split_kernel,
        grid=(1,),
        in_specs=[whole(keep.shape)] * 2,
        out_specs=[whole(half)] * 2,
        out_shape=[shape_of(half, WIDE), shape_of(half, LOW)],
        compiler_params=PARAMS,
        name="sum_and_split",
    )(keep, arrived)


def swap_plane(value, which):
    pairs = [(r, r ^ ((1 + ((r + which) & 1)) << 1)) for r in range(lax.axis_size("replica"))]
    return lax.ppermute(value, "replica", pairs)


def swap_pair(value, which):
    groups, copies = lax.axis_size("group"), lax.axis_size("replica")
    pairs = []
    for g in range(groups):
        for r in range(copies):
            other = g ^ (1 if (r + which) % 2 == 0 else 2)
            pairs.append((g * copies + r, other * copies + r))
    return lax.ppermute(value, ("group", "replica"), pairs)


def gather_pair(value):
    first = swap_pair(value, 0)
    second = swap_pair(value, 1)
    return (first, second, swap_pair(first, 1))


def update_all(stored, gradients, means, squares, kinds):
    return [
        adam_update(
            stored[kind].astype(jnp.float32),
            gradient,
            means[kind].astype(jnp.float32),
            squares[kind].astype(jnp.float32),
            LEARN_RATES[kind],
            DECAY_FLAGS[kind],
        )
        for kind, gradient in zip(kinds, gradients)
    ]


def by_core(core, own, other):
    return (
        jnp.where(core == 0, own, other).astype(jnp.float32),
        jnp.where(core == 0, other, own).astype(jnp.float32),
    )


def attention_shards(totals):
    joined = jnp.concatenate(
        [totals[0][:QUARTER], totals[0][QUARTER:], totals[1][:QUARTER]], axis=1
    )
    return (joined, totals[1][QUARTER:])


def tail_in_step(
    where, copy, stages, condition, ffn_halves, att_parts, small_rows, stored, means, squares
):
    core = where[1]
    (feed_stay, feed_go), (att_send, att_keep) = ffn_halves, att_parts
    half, third = (D // 2, D), (2 * QUARTER, D)
    att_stay, att_go, feed_stay, message = small_call(
        step0_kernel, "step_0",
        [((2,) + third, WIDE), ((2,) + third, LOW), (half, WIDE), ((D // 2 + SMALL, D), LOW)],
        where, att_keep, swap_replica(att_send, 1), feed_stay, swap_pair(feed_go, 1), small_rows,
        scratch=[((D, D), WIDE)],
    )
    att_stay, att_go, message = small_call(
        step1_kernel, "step_1",
        [(third, WIDE), (third, LOW), ((D // 2 + 2 * SMALL, D), LOW)],
        where, att_stay, swap_pair(att_go, 0), feed_stay, message, swap_plane(message, 0),
    )
    quarter = (QUARTER, D)
    att_stay, att_go, feed_half, small = small_call(
        step2_kernel, "step_2",
        [(quarter, WIDE), (quarter, LOW), (half, LOW), ((4 * SMALL, D), LOW)],
        where, att_stay, swap_pair(att_go, 1), message, swap_plane(message, 1),
        scratch=[(third, WIDE)],
    )
    att_half, feed_part, small = small_call(
        step3_kernel, "step_3",
        [(quarter, LOW), ((D, D), LOW), ((8 * SMALL, D), LOW)],
        where, att_stay, swap_plane(att_go, 0), feed_half, swap_plane(feed_half, 0),
        small, swap_pair(small, 1),
    )
    feed_totals = by_core(core, feed_part, swap_replica(feed_part, 1))
    att_sum, small, cond_keep, cond_go = small_call(
        step4_kernel, "step_4",
        [(quarter, LOW), ((16 * SMALL, D), LOW), ((8, 128), WIDE), ((8, 128), WIDE)],
        where, att_half, swap_plane(att_half, 1), small, swap_pair(small, 0), stored[0],
    )
    cond_in = swap_pair(cond_go, 0)
    feed_updates = update_all(stored, feed_totals, means, squares, (3, 4))
    att_part, cond_go = small_call(
        step5_kernel, "step_5",
        [(third, LOW), ((8, 128), WIDE)],
        where, att_sum, swap_plane(att_sum, 0), cond_keep, cond_in,
        after=(feed_updates[0][1], feed_updates[1][1]),
    )
    shard = [((QUARTER, 6 * D), WIDE)] * 3 + [((BIAS_ROWS, QUARTER), WIDE)] * 3
    updates = small_call(
        modulation_update_kernel, "modulation_update", shard,
        where, small, swap_replica(small, 1), stored[0], means[0], squares[0],
        stored[5], means[5], squares[5],
        scratch=[((3, 32 * SMALL, 128), WIDE)],
    )
    cond_last = swap_pair(cond_go, 1)
    att_totals = by_core(core, att_part, swap_replica(att_part, 1))
    blocks = [
        block[:, :QUARTER] for block in (cond_keep[:2], cond_in[:2], cond_last[:2], cond_last[2:4])
    ]
    owners = (where[0],) + neighbours(where)
    lanes = []
    for place in range(4):
        chosen = blocks[0]
        for k in range(1, 4):
            chosen = jnp.where(owners[k] == place, blocks[k], chosen)
        lanes.append(chosen)
    sigmoid_cond = jax.nn.sigmoid(condition)
    grad_condition = (
        jnp.concatenate(lanes, axis=1) * sigmoid_cond * (1.0 + condition * (1.0 - sigmoid_cond))
    )
    att_updates = update_all(stored, attention_shards(att_totals), means, squares, (1, 2))
    return grad_condition, [updates[:3]] + att_updates + feed_updates + [updates[3:]]


def tail_in_turn(
    where, copy, stages, condition, ffn_halves, att_parts, small_rows, stored, means, squares
):
    rank, core = where[0], where[1]
    slot_count, model_width = condition.shape
    modulation, cond_low = stored[0], jax.nn.silu(condition).astype(jnp.bfloat16)
    (ffn_stay, ffn_go), (att_send, att_keep) = ffn_halves, att_parts
    ffn_totals = reduce_replicas(
        wide_sum([ffn_stay[0], swap_pair(ffn_go[0], 1)]).astype(LOW), copy, stages
    )
    att_stay, att_go = run_split(att_keep, swap_replica(att_send, 1))
    att_stay, att_go = run_split(att_stay, swap_pair(att_go, 0))
    att_totals = reduce_replicas(
        wide_sum([att_stay[0], swap_pair(att_go[0], 1)]).astype(LOW), copy, stages
    )
    row_total = small_rows.shape[0]
    gathered = small_rows[None]
    for low_bit, radix in stages[1:]:
        digit = (copy >> low_bit) % radix
        gathered = in_order(
            [swap_replica(gathered, k << low_bit) for k in range(radix)], digit
        ).reshape(-1, row_total, model_width)
    gathered = in_order([swap_group(gathered, k) for k in range(4)], rank)
    own_plane = lax.dynamic_index_in_dim(gathered, copy >> 1, axis=1, keepdims=False)
    group_mod = own_plane[:, : 6 * slot_count].reshape(4 * slot_count, 6 * model_width)
    grad_cond_columns = dot_last(group_mod, modulation).reshape(4, slot_count, model_width // 4)
    cond_back = in_order(
        [swap_group(pick(grad_cond_columns, rank ^ k), k) for k in range(4)], rank
    )
    sigmoid_cond = jax.nn.sigmoid(condition)
    grad_condition = (
        jnp.swapaxes(cond_back, 0, 1).reshape(slot_count, model_width)
        * sigmoid_cond
        * (1.0 + condition * (1.0 - sigmoid_cond))
    )
    everyone = in_order([swap_replica(gathered, k) for k in range(2)], core).reshape(
        -1, row_total, model_width
    )
    all_mod = everyone[:, : 6 * slot_count].reshape(-1, 6 * model_width)
    all_cond = everyone[:, 6 * slot_count : 7 * slot_count].reshape(-1, model_width)
    cond_own = lax.dynamic_slice_in_dim(all_cond, rank * (model_width // 4), model_width // 4, 1)
    grad_mod = dot_first(cond_own, all_mod)
    mod_bias_grad = jnp.sum(all_mod, axis=0, dtype=jnp.float32).reshape(6, model_width)
    rest_bias_grad = jnp.sum(everyone[:, 7 * slot_count : 22], axis=0, dtype=jnp.float32)
    bias_grad = lax.dynamic_slice_in_dim(
        jnp.concatenate([mod_bias_grad, rest_bias_grad], axis=0),
        rank * (model_width // 4),
        model_width // 4,
        1,
    )
    grad_att_own = jnp.concatenate(
        [att_totals[0][:QUARTER], att_totals[0][QUARTER:], att_totals[1][:QUARTER]], axis=1
    )
    totals = (
        grad_mod,
        grad_att_own,
        att_totals[1][QUARTER:],
        ffn_totals[0],
        ffn_totals[1],
        bias_grad,
    )
    return grad_condition, update_all(stored, totals, means, squares, range(6))


def shards(
    latents,
    condition,
    cotangent,
    live_counts,
    modulation,
    attending,
    projection,
    expand,
    contract,
    biases,
    modulation_mean,
    attending_mean,
    projection_mean,
    expand_mean,
    contract_mean,
    biases_mean,
    modulation_square,
    attending_square,
    projection_square,
    expand_square,
    contract_square,
    biases_square,
):
    slot_count, length, model_width = latents.shape
    rank = lax.axis_index("group")
    copy = lax.axis_index("replica")
    core = copy % 2
    stages = replica_stages(lax.axis_size("replica"))
    where = jnp.stack([rank, core, copy >> 1, live_counts[0]]).astype(jnp.int32)

    cond_low = jax.nn.silu(condition).astype(LOW)
    payload = run_payload(where, condition, attending, projection, biases)
    nears = gather_pair(payload)
    fars = [swap_replica(item, 1) for item in nears]
    stay, go, bias, feed_part = run_modulation(
        where, (payload,) + nears, modulation, expand, contract
    )
    feed_nears = gather_pair(feed_part)
    feed_fars = [swap_replica(item, 1) for item in feed_nears]
    stay = stay + swap_pair(go, 0)
    arrived = swap_pair(stay[slot_count:], 1)

    joined, soft, mixed, mod, att, proj = run_attention_forward(
        where, latents, stay, arrived, bias, attending, projection, nears, fars
    )
    out_latents, grad_middle, ffn_send, ffn_keep, feed_rows = run_feed(
        where, mixed, latents, cotangent, mod, bias, proj, expand, contract, feed_nears, feed_fars
    )
    cond_wide = cond_low.astype(WIDE)
    ffn_stay, ffn_go = run_split(ffn_keep, swap_replica(ffn_send, 1))
    half_tokens, half_att, half_proj, half_rows = run_attention_backward(
        0, where, latents, grad_middle, joined, soft, mixed, mod, feed_rows, cond_wide, att, proj
    )
    ffn_stay, ffn_go = run_split(ffn_stay, swap_pair(ffn_go, 0))
    grad_latents, att_send, att_keep, small_rows = run_attention_backward(
        1, where, latents, grad_middle, joined, soft, mixed, mod, feed_rows, cond_wide, att, proj,
        (half_att, half_proj, half_rows, half_tokens, ffn_go),
    )
    tail = tail_in_step if lax.axis_size("replica") == 8 else tail_in_turn
    grad_condition, results = tail(
        where, copy, stages, condition, (ffn_stay, ffn_go), (att_send, att_keep), small_rows,
        (modulation, attending, projection, expand, contract, biases),
        (
            modulation_mean, attending_mean, projection_mean,
            expand_mean, contract_mean, biases_mean,
        ),
        (
            modulation_square, attending_square, projection_square,
            expand_square, contract_square, biases_square,
        ),
    )
    return (
        out_latents,
        grad_latents,
        grad_condition,
        results[0][0],
        results[1][0],
        results[2][0],
        results[3][0],
        results[4][0],
        results[5][0],
        results[0][1],
        results[1][1],
        results[2][1],
        results[3][1],
        results[4][1],
        results[5][1],
        results[0][2],
        results[1][2],
        results[2][2],
        results[3][2],
        results[4][2],
        results[5][2],
    )


def solution(mesh):
    return jax.shard_map(
        shards,
        mesh=mesh,
        in_specs=(
            P(("group", "replica"), None, None),
            P(("group", "replica"), None),
            P(("group", "replica"), None, None),
            P(("group", "replica")),
            P("group", None),
            P("group", None),
            P("group", None),
            P(None, "group"),
            P("group", None),
            P(None, "group"),
            P("group", None),
            P("group", None),
            P("group", None),
            P(None, "group"),
            P("group", None),
            P(None, "group"),
            P("group", None),
            P("group", None),
            P("group", None),
            P(None, "group"),
            P("group", None),
            P(None, "group"),
        ),
        out_specs=(
            P(("group", "replica"), None, None),
            P(("group", "replica"), None, None),
            P(("group", "replica"), None),
            P("group", None),
            P("group", None),
            P("group", None),
            P(None, "group"),
            P("group", None),
            P(None, "group"),
            P("group", None),
            P("group", None),
            P("group", None),
            P(None, "group"),
            P("group", None),
            P(None, "group"),
            P("group", None),
            P("group", None),
            P("group", None),
            P(None, "group"),
            P("group", None),
            P(None, "group"),
        ),
        check_vma=False,
    )
```

time: 412 us -> 135 us (0.33)
  waiting for transfers between devices: 206 us -> 44.4 us
  blocking collectives: 103 us -> 0 us
  matrix products: 39.4 us -> 0 us
  starting transfers between devices: 0.36 us -> 38.8 us
  Pallas kernels: 0 us -> 35.1 us
  other arithmetic: 24.9 us -> 6.38 us
  local copies, waits for them, and re-layouts: 21.8 us -> 7.65 us
  between operations: 15.6 us -> 1.67 us
    reduce_scatter x4 -> x0, waiting for transfers between devices: 124 us -> none  [the longest x1 35.8 us: shards(): lax.psum_scatter(grad_mod.astype(jnp.bfloat16), 'group', scatter_dimensio...]
    psum x1 -> x0, blocking collectives: 65.8 us -> none  [shards(): lax.psum((owned[0], owned[1], owned[2], owned[3], owned[4], owned[5]), 'r...]
    ppermute x0 -> x33, waiting for transfers between devices: none -> 44.4 us  [the longest x16 28.7 us: swap_pair(): return lax.ppermute(value, ('group', 'replica'), pairs)]
    unnamed x11 -> x0, waiting for transfers between devices: 43.6 us -> none
    dot_general x21 -> x0, matrix products: 39.4 us -> none  [the longest x5 12.1 us: dot_last(): lax.dot_general(left_side, right_side, (((1,), (1,)), ((), ())), preferre...]
    all_gather x3 -> x0, waiting for transfers between devices: 38.9 us -> none  [the longest x1 25.7 us: shards(): lax.all_gather(contract, 'group', axis=0, tiled=True)]
    ppermute x0 -> x33, starting transfers between devices: none -> 38.8 us  [the longest x16 27.6 us: swap_pair(): return lax.ppermute(value, ('group', 'replica'), pairs)]
    all_gather x3 -> x0, blocking collectives: 37.4 us -> none  [the longest x1 18 us: shards(): lax.all_gather(attending, 'group', axis=0, tiled=True)]
  transfers between devices with their start and end apart: 9 -> 33, of which waited for: 8 -> 15; matrix products, arithmetic and copies ran while one was open for 9% -> 5% of each run, Pallas kernels for 0% -> 7%
where the time goes in v1:
time: 135 us; the launch traced here: 134 us
  waiting for transfers between devices  44.4 us (33%)
  starting transfers between devices  38.8 us (29%)
  Pallas kernels  35.1 us (26%)
  local copies, waits for them, and re-layouts  7.65 us (6%)
  other arithmetic  6.38 us (5%)
  between operations  1.67 us (1%)
    ppermute x16, waiting for transfers between devices, swap_pair(): return lax.ppermute(value, ('group', 'replica'), pairs)  28.7 us
    ppermute x16, starting transfers between devices, swap_pair(): return lax.ppermute(value, ('group', 'replica'), pairs)  27.6 us
    ppermute x6, waiting for transfers between devices, swap_plane(): return lax.ppermute(value, 'replica', pairs)  12.8 us
    pallas_call x1, Pallas kernels, run_feed(): pl.pallas_call(feed_kernel, grid_spec=pltpu.PrefetchScalarGridSpec(num_sc...  10.7 us
    pallas_call x2, Pallas kernels, run_attention_backward(): pl.pallas_call(functools.partial(attention_backward_kernel, slot), grid=(...  10.7 us
    ppermute x6, starting transfers between devices, swap_plane(): return lax.ppermute(value, 'replica', pairs)  9.18 us
    pallas_call x8, Pallas kernels, small_call(): pl.pallas_call(kernel, grid=(1,), in_specs=[SMEM_SPEC] + [whole(item.shap...  8.43 us
    unnamed x58, local copies, waits for them, and re-layouts  7.61 us
  transfers between devices with their start and end apart: 33, of which 15 were waited for; matrix products, arithmetic and copies ran while one was open for 5% of the time, Pallas kernels for 7%

profile of v1, /device:TPU:0, one launch (start us, length us, event | category | flops | bytes accessed | tf_op | source)
XLA Modules:
  0.0 134.1 jit_solution(3006828819496798079)
XLA Ops:
  1.4 0.9 copy-done.9
  2.3 0.9 copy-done.13
  3.2 0.7 copy-done.15
  3.9 0.7 copy-done.17
  4.6 0.6 own_payload.1.own
  5.2 3.0 %collective-permute-start = (bf16[208,384]{1,0:T(8,128)(2,1)S(1)}, bf16[208,384]{1,0:T(8,128)(2,1)S(1)}, u32[]{:S(2)}, u32[]{:S(2)}) collective-permute-start(bf16[208,384]{1,0:T(8,128)(2,1)S(1)} %own_payload.1.own), channel_id=1, source_target_pairs={{0,8},{1,17},{2,10},{3,19},{4,12},{5,21},{6,14},{7,23},{8,0},{9,25... | collective-permute-start | bytes 479240 | tf_op jit(solution)/shard_map/ppermute | solution.py:876
  8.2 1.5 %collective-permute-start.1 = (bf16[208,384]{1,0:T(8,128)(2,1)S(1)}, bf16[208,384]{1,0:T(8,128)(2,1)S(1)}, u32[]{:S(2)}, u32[]{:S(2)}) collective-permute-start(bf16[208,384]{1,0:T(8,128)(2,1)S(1)} %own_payload.1.own), channel_id=1, source_target_pairs={{0,16},{1,9},{2,18},{3,11},{4,20},{5,13},{6,22},{7,15},{8,24},{9,1... | collective-permute-start | bytes 479240 | tf_op jit(solution)/shard_map/ppermute | solution.py:876
  9.7 2.9 %collective-permute-done.first.n1 = bf16[208,384]{1,0:T(8,128)(2,1)S(1)} collective-permute-done((bf16[208,384]{1,0:T(8,128)(2,1)S(1)}, bf16[208,384]{1,0:T(8,128)(2,1)S(1)}, u32[]{:S(2)}, u32[]{:S(2)}) %collective-permute-start) | collective-permute-done | bytes 159776 | tf_op jit(solution)/shard_map/ppermute | solution.py:876
  12.6 1.6 %collective-permute-start.2 = (bf16[208,384]{1,0:T(8,128)(2,1)S(1)}, bf16[208,384]{1,0:T(8,128)(2,1)S(1)}, u32[]{:S(2)}, u32[]{:S(2)}) collective-permute-start(bf16[208,384]{1,0:T(8,128)(2,1)S(1)} %collective-permute-done.first.n1), channel_id=1, source_target_pairs={{0,16},{1,9},{2,18},{3,11},{4,20},{5,13},{6,22},{7,15},{8,24},{9,1... | collective-permute-start | bytes 479240 | tf_op jit(solution)/shard_map/ppermute | solution.py:876
  14.1 3.7 %collective-permute-done.2.last.n3 = bf16[208,384]{1,0:T(8,128)(2,1)S(1)} collective-permute-done((bf16[208,384]{1,0:T(8,128)(2,1)S(1)}, bf16[208,384]{1,0:T(8,128)(2,1)S(1)}, u32[]{:S(2)}, u32[]{:S(2)}) %collective-permute-start.2) | collective-permute-done | bytes 159776 | tf_op jit(solution)/shard_map/ppermute | solution.py:876
  17.9 1.0 copy-done
  18.9 1.0 copy-done.4
  19.8 1.0 copy-done.6
  20.8 1.0 modulation_partials.1
  21.8 2.5 %collective-permute-start.8 = (bf16[384,384]{1,0:T(8,128)(2,1)S(1)}, bf16[384,384]{1,0:T(8,128)(2,1)S(1)}, u32[]{:S(2)}, u32[]{:S(2)}) collective-permute-start(bf16[384,384]{1,0:T(8,128)(2,1)S(1)} %get-tuple-element.80), channel_id=1, source_target_pairs={{0,8},{1,17},{2,10},{3,19},{4,12},{5,21},{6,14},{7,23},{8,0},{9,25... | collective-permute-start | bytes 884744 | tf_op jit(solution)/shard_map/ppermute | solution.py:876
  24.3 0.7 collective-permute-start.9
  25.1 5.9 %collective-permute-done.8.n1 = bf16[384,384]{1,0:T(8,128)(2,1)S(1)} collective-permute-done((bf16[384,384]{1,0:T(8,128)(2,1)S(1)}, bf16[384,384]{1,0:T(8,128)(2,1)S(1)}, u32[]{:S(2)}, u32[]{:S(2)}) %collective-permute-start.8) | collective-permute-done | bytes 294944 | tf_op jit(solution)/shard_map/ppermute | solution.py:876
  31.0 0.5 collective-permute-start.10
  31.4 1.8 %collective-permute-start.3 = (f32[4,2304]{1,0:T(4,128)S(1)}, f32[4,2304]{1,0:T(4,128)S(1)}, u32[]{:S(2)}, u32[]{:S(2)}) collective-permute-start(f32[4,2304]{1,0:T(4,128)S(1)} %get-tuple-element.75), channel_id=1, source_target_pairs={{0,8},{1,17},{2,10},{3,19},{4,12},{5,21},{6,14},{7,23},{8,0},{9,25... | collective-permute-start | bytes 110600 | tf_op jit(solution)/shard_map/ppermute | solution.py:876
  33.2 0.5 collective-permute-start.6
  33.7 1.7 %collective-permute-done.3 = f32[4,2304]{1,0:T(4,128)S(1)} collective-permute-done((f32[4,2304]{1,0:T(4,128)S(1)}, f32[4,2304]{1,0:T(4,128)S(1)}, u32[]{:S(2)}, u32[]{:S(2)}) %collective-permute-start.3) | collective-permute-done | bytes 36896 | tf_op jit(solution)/shard_map/ppermute | solution.py:876
  35.4 1.6 %collective-permute-start.4 = (f32[2,2304]{1,0:T(2,128)S(1)}, f32[2,2304]{1,0:T(2,128)S(1)}, u32[]{:S(2)}, u32[]{:S(2)}) collective-permute-start(f32[2,2304]{1,0:T(2,128)S(1)} %slice.44), channel_id=1, source_target_pairs={{0,16},{1,9},{2,18},{3,11},{4,20},{5,13},{6,22},{7,15},{8,24},{9,1... | collective-permute-start | bytes 55304 | tf_op jit(solution)/shard_map/ppermute | solution.py:876
  37.1 0.5 collective-permute-start.11
  37.7 0.4 collective-permute-start.13
  38.0 1.2 collective-permute-done.4.arrived
  39.3 3.9 %attention_forward.1 = (bf16[2,256,1152]{2,1,0:T(8,128)(2,1)S(1)}, bf16[2,6,256,256]{3,2,1,0:T(8,128)(2,1)S(1)}, bf16[2,256,384]{2,1,0:T(8,128)(2,1)S(1)}, f32[2...) custom-call(s32[4]{0:T(128)S(1)} %pad_add_fusion.where, ...), custom_call_target="tpu_custom_call" | custom-call | flops 3000000000 | bytes 6000000 | tf_op jit(solution)/shard_map/attention_forward/pallas_call | solution.py:709
  43.3 10.7 %feed_forward_and_back.1 = (bf16[2,256,384]{2,1,0:T(8,128)(2,1)}, f32[2,256,384]{2,1,0:T(8,128)S(1)}, bf16[4,384,384]{2,1,0:T(8,128)(2,1)S(1)}, bf16[4,384,384]{2,1,0:T(8,128)(2,1)}, f32[16,384]{1,0:T(8,128)S(1)}) custom-call(s32[4]{0:T(128)S(1)} %pad_add_fusion.where, bf16[2,256,384]{2,1,0:T(8,128)(2,1)S(1)} %get-tuple-element.77.mixed, ...), custom_call_target="tpu_custom_call" | custom-call | flops 8000000000 | bytes 10000000 | tf_op jit(solution)/shard_map/feed_forward_and_back/pallas_call | solution.py:758
  54.1 2.8 %collective-permute-done.14.arrived = bf16[4,384,384]{2,1,0:T(8,128)(2,1)S(1)} collective-permute-done((bf16[4,384,384]{2,1,0:T(8,128)(2,1)S(1)}, bf16[4,384,384]{2,1,0:T(8,128)(2,1)S(1)}, u32[]{:S(2)}, u32[]{:S(2)}) %collective-permute-start.14) | collective-permute-done | bytes 1179680 | tf_op jit(solution)/shard_map/ppermute | solution.py:79
  56.9 1.3 copy-done.8
  58.2 0.3 sum_and_split.2
  58.4 1.8 %collective-permute-start.15 = (bf16[2,384,384]{2,1,0:T(8,128)(2,1)S(1)}, bf16[2,384,384]{2,1,0:T(8,128)(2,1)S(1)}, u32[]{:S(2)}, u32[]{:S(2)}) collective-permute-start(bf16[2,384,384]{2,1,0:T(8,128)(2,1)S(1)} %get-tuple-element.94), channel_id=1, source_target_pairs={{0,8},{1,17},{2,10},{3,19},{4,12},{5,21},{6,14},{7,23},{8,0},{9,25... | collective-permute-start | bytes 1769480 | tf_op jit(solution)/shard_map/ppermute | solution.py:876
  60.3 4.6 %attention_backward.2 = (bf16[2,256,384]{2,1,0:T(8,128)(2,1)}, f32[384,1152]{1,0:T(8,128)}, f32[384,384]{1,0:T(8,128)S(1)}, f32[32,384]{1,0:T(8,128)S(1)}) custom-call(s32[4]{0:T(128)S(1)} %pad_add_fusion.where, bf16[2,256,384]{2,1,0:T(8,128)(2,1)S(1)} %copy-done.22, f32[2,256,384]{2,1,0:T(8,128)S(1)} %get-tuple-element.82.grad_middle_in, ...), custom_call_target="tpu_custom_call" | custom-call | flops 4000000000 | bytes 8000000 | tf_op jit(solution)/shard_map/attention_backward/pallas_call | solution.py:834
  64.9 3.5 %collective-permute-done.15.arrived = bf16[2,384,384]{2,1,0:T(8,128)(2,1)S(1)} collective-permute-done((bf16[2,384,384]{2,1,0:T(8,128)(2,1)S(1)}, bf16[2,384,384]{2,1,0:T(8,128)(2,1)S(1)}, u32[]{:S(2)}, u32[]{:S(2)}) %collective-permute-start.15) | collective-permute-done | bytes 589856 | tf_op jit(solution)/shard_map/ppermute | solution.py:876
  68.5 6.1 %attention_backward.3 = (bf16[2,256,384]{2,1,0:T(8,128)(2,1)}, bf16[4,192,384]{2,1,0:T(8,128)(2,1)S(1)}, bf16[4,192,384]{2,1,0:T(8,128)(2,1)S(1)}, bf16[32,384]{1,0:T(8,128)(2,1)S(1)}) custom-call(s32[4]{0:T(128)S(1)} %pad_add_fusion.where, bf16[2,256,384]{2,1,0:T(8,128)(2,1)S(1)} %copy-done.22, ...), custom_call_target="tpu_custom_call", output_to_operand_aliasing={{0}: (14, {})} | custom-call | flops 4000000000 | bytes 8000000 | tf_op jit(solution)/shard_map/attention_backward/pallas_call | solution.py:834
  74.6 1.6 %collective-permute-start.17 = (bf16[1,384,384]{2,1,0:T(8,128)(2,1)S(1)}, bf16[1,384,384]{2,1,0:T(8,128)(2,1)S(1)}, u32[]{:S(2)}, u32[]{:S(2)}) collective-permute-start(bf16[1,384,384]{2,1,0:T(8,128)(2,1)S(1)} %get-tuple-element.95.refs_4_), channel_id=1, source_target_pairs={{0,16},{1,9},{2,18},{3,11},{4,20},{5,13},{6,22},{7,15},{8,24},{9,1... | collective-permute-start | bytes 884744 | tf_op jit(solution)/shard_map/ppermute | solution.py:876
  76.2 5.2 %collective-permute-done.17.feed_in = bf16[1,384,384]{2,1,0:T(8,128)(2,1)S(1)} collective-permute-done((bf16[1,384,384]{2,1,0:T(8,128)(2,1)S(1)}, bf16[1,384,384]{2,1,0:T(8,128)(2,1)S(1)}, u32[]{:S(2)}, u32[]{:S(2)}) %collective-permute-start.17) | collective-permute-done | bytes 294944 | tf_op jit(solution)/shard_map/ppermute | solution.py:876
  81.3 0.9 step_0.1
  82.2 1.8 %collective-permute-start.18 = (bf16[2,192,384]{2,1,0:T(8,128)(2,1)S(1)}, bf16[2,192,384]{2,1,0:T(8,128)(2,1)S(1)}, u32[]{:S(2)}, u32[]{:S(2)}) collective-permute-start(bf16[2,192,384]{2,1,0:T(8,128)(2,1)S(1)} %get-tuple-element.102), channel_id=1, source_target_pairs={{0,8},{1,17},{2,10},{3,19},{4,12},{5,21},{6,14},{7,23},{8,0},{9,25... | collective-permute-start | bytes 884744 | tf_op jit(solution)/shard_map/ppermute | solution.py:876
  84.0 1.6 %collective-permute-start.19 = (bf16[224,384]{1,0:T(8,128)(2,1)S(1)}, bf16[224,384]{1,0:T(8,128)(2,1)S(1)}, u32[]{:S(2)}, u32[]{:S(2)}) collective-permute-start(bf16[224,384]{1,0:T(8,128)(2,1)S(1)} %get-tuple-element.104.own), channel_id=1, source_target_pairs={{0,2},{1,5},{2,0},{3,7},{4,6},{5,1},{6,4},{7,3},{8,10},{9,13},{10,... | collective-permute-start | bytes 516104 | tf_op jit(solution)/shard_map/ppermute | solution.py:866
  85.6 5.4 %collective-permute-done.19.feed_in = bf16[224,384]{1,0:T(8,128)(2,1)S(1)} collective-permute-done((bf16[224,384]{1,0:T(8,128)(2,1)S(1)}, bf16[224,384]{1,0:T(8,128)(2,1)S(1)}, u32[]{:S(2)}, u32[]{:S(2)}) %collective-permute-start.19) | collective-permute-done | bytes 172064 | tf_op jit(solution)/shard_map/ppermute | solution.py:866
  91.0 0.6 step_1.1
  91.7 1.9 %collective-permute-start.21 = (bf16[256,384]{1,0:T(8,128)(2,1)S(1)}, bf16[256,384]{1,0:T(8,128)(2,1)S(1)}, u32[]{:S(2)}, u32[]{:S(2)}) collective-permute-start(bf16[256,384]{1,0:T(8,128)(2,1)S(1)} %get-tuple-element.107.own), channel_id=1, source_target_pairs={{0,4},{1,3},{2,6},{3,1},{4,0},{5,7},{6,2},{7,5},{8,12},{9,11},{10,... | collective-permute-start | bytes 589832 | tf_op jit(solution)/shard_map/ppermute | solution.py:866
  93.6 2.1 %collective-permute-start.20 = (bf16[192,384]{1,0:T(8,128)(2,1)S(1)}, bf16[192,384]{1,0:T(8,128)(2,1)S(1)}, u32[]{:S(2)}, u32[]{:S(2)}) collective-permute-start(bf16[192,384]{1,0:T(8,128)(2,1)S(1)} %get-tuple-element.106), channel_id=1, source_target_pairs={{0,16},{1,9},{2,18},{3,11},{4,20},{5,13},{6,22},{7,15},{8,24},{9,1... | collective-permute-start | bytes 442376 | tf_op jit(solution)/shard_map/ppermute | solution.py:876
  95.6 3.1 %collective-permute-done.20.att_in = bf16[192,384]{1,0:T(8,128)(2,1)S(1)} collective-permute-done((bf16[192,384]{1,0:T(8,128)(2,1)S(1)}, bf16[192,384]{1,0:T(8,128)(2,1)S(1)}, u32[]{:S(2)}, u32[]{:S(2)}) %collective-permute-start.20) | collective-permute-done | bytes 147488 | tf_op jit(solution)/shard_map/ppermute | solution.py:876
  98.7 0.5 collective-permute-done.21.feed_in
  99.3 0.7 step_2.1
  99.9 2.1 %collective-permute-start.23 = (bf16[192,384]{1,0:T(8,128)(2,1)S(1)}, bf16[192,384]{1,0:T(8,128)(2,1)S(1)}, u32[]{:S(2)}, u32[]{:S(2)}) collective-permute-start(bf16[192,384]{1,0:T(8,128)(2,1)S(1)} %get-tuple-element.110.feed_half), channel_id=1, source_target_pairs={{0,2},{1,5},{2,0},{3,7},{4,6},{5,1},{6,4},{7,3},{8,10},{9,13},{10,... | collective-permute-start | bytes 442376 | tf_op jit(solution)/shard_map/ppermute | solution.py:866
  102.0 3.3 %collective-permute-start.24 = (bf16[128,384]{1,0:T(8,128)(2,1)S(1)}, bf16[128,384]{1,0:T(8,128)(2,1)S(1)}, u32[]{:S(2)}, u32[]{:S(2)}) collective-permute-start(bf16[128,384]{1,0:T(8,128)(2,1)S(1)} %get-tuple-element.111.small), channel_id=1, source_target_pairs={{0,16},{1,9},{2,18},{3,11},{4,20},{5,13},{6,22},{7,15},{8,24},{9,1... | collective-permute-start | bytes 294920 | tf_op jit(solution)/shard_map/ppermute | solution.py:876
  105.4 4.3 %collective-permute-done.22.att_in = bf16[96,384]{1,0:T(8,128)(2,1)S(1)} collective-permute-done((bf16[96,384]{1,0:T(8,128)(2,1)S(1)}, bf16[96,384]{1,0:T(8,128)(2,1)S(1)}, u32[]{:S(2)}, u32[]{:S(2)}) %collective-permute-start.22) | collective-permute-done | bytes 73760 | tf_op jit(solution)/shard_map/ppermute | solution.py:866
  109.7 0.6 step_3.1
  110.4 3.6 %collective-permute-start.25 = (bf16[96,384]{1,0:T(8,128)(2,1)S(1)}, bf16[96,384]{1,0:T(8,128)(2,1)S(1)}, u32[]{:S(2)}, u32[]{:S(2)}) collective-permute-start(bf16[96,384]{1,0:T(8,128)(2,1)S(1)} %get-tuple-element.112.att_half), channel_id=1, source_target_pairs={{0,4},{1,3},{2,6},{3,1},{4,0},{5,7},{6,2},{7,5},{8,12},{9,11},{10,... | collective-permute-start | bytes 221192 | tf_op jit(solution)/shard_map/ppermute | solution.py:866
  114.0 2.6 %collective-permute-done.25.att_in = bf16[96,384]{1,0:T(8,128)(2,1)S(1)} collective-permute-done((bf16[96,384]{1,0:T(8,128)(2,1)S(1)}, bf16[96,384]{1,0:T(8,128)(2,1)S(1)}, u32[]{:S(2)}, u32[]{:S(2)}) %collective-permute-start.25) | collective-permute-done | bytes 73760 | tf_op jit(solution)/shard_map/ppermute | solution.py:866
  116.7 0.8 step_4.1
  117.5 2.0 %collective-permute-start.28 = (f32[8,128]{1,0:T(8,128)S(1)}, f32[8,128]{1,0:T(8,128)S(1)}, u32[]{:S(2)}, u32[]{:S(2)}) collective-permute-start(f32[8,128]{1,0:T(8,128)S(1)} %get-tuple-element.116), channel_id=1, source_target_pairs={{0,8},{1,17},{2,10},{3,19},{4,12},{5,21},{6,14},{7,23},{8,0},{9,25... | collective-permute-start | bytes 12296 | tf_op jit(solution)/shard_map/ppermute | solution.py:876
  119.5 3.4 %convert_subtract_fusion = (f32[384,384]{1,0:T(8,128)}, f32[384,384]{1,0:T(8,128)}, f32[384,384]{1,0:T(8,128)S(1)}, f32[384,384]{1,0:T(8,128)}, f32[384,384]{1,0:T(8,128)}, /*index=5*/f32[384,384]{1,0:T(8,128)S(1)}) fusion(bf16[384,384]{1,0:T(8,128)(2,1)S(1)} %copy-done.7, bf16[384,384]{1,0:T(8,128)(2,1)} %collective-permute-done.29, ...), kind=kLoop, calls=%fused_computation.2 | loop fusion | flops 5898240 | bytes 5898241 | tf_op jit(solution)/shard_map/sub | solution.py:55
  123.0 0.6 step_5.1
  123.6 1.7 %collective-permute-start.30 = (f32[8,128]{1,0:T(8,128)S(1)}, f32[8,128]{1,0:T(8,128)S(1)}, u32[]{:S(2)}, u32[]{:S(2)}) collective-permute-start(f32[8,128]{1,0:T(8,128)S(1)} %get-tuple-element.118), channel_id=1, source_target_pairs={{0,16},{1,9},{2,18},{3,11},{4,20},{5,13},{6,22},{7,15},{8,24},{9,1... | collective-permute-start | bytes 12296 | tf_op jit(solution)/shard_map/ppermute | solution.py:876
  125.2 0.5 collective-permute-start.32
  125.7 1.5 %collective-permute-done.30 = f32[8,128]{1,0:T(8,128)S(1)} collective-permute-done((f32[8,128]{1,0:T(8,128)S(1)}, f32[8,128]{1,0:T(8,128)S(1)}, u32[]{:S(2)}, u32[]{:S(2)}) %collective-permute-start.30) | collective-permute-done | bytes 4128 | tf_op jit(solution)/shard_map/ppermute | solution.py:876
  127.3 0.7 fusion.14
  128.0 0.8 convert_subtract_fusion.3
  128.9 0.1 copy-done.26
  129.0 1.3 convert_subtract_fusion.2
  130.4 3.7 %modulation_update.1 = (f32[96,2304]{1,0:T(8,128)}, f32[96,2304]{1,0:T(8,128)}, f32[96,2304]{1,0:T(8,128)}, f32[14,96]{1,0:T(8,128)}, f32[14,96]{1,0:T(8,128)}, /*index=5*/f32[14,96]{1,0:T(8,128)}) custom-call(s32[4]{0:T(128)S(1)} %pad_add_fusion.where, bf16[512,384]{1,0:T(8,128)(2,1)S(1)} %get-tuple-element.119.near, ...), custom_call_target="tpu_custom_call" | custom-call | tf_op jit(solution)/shard_map/modulation_update/pallas_call | solution.py:665
  (87 shorter events, 0.8 us)
Async XLA Ops:
  1.4 0.9 copy-start.9
  2.3 0.9 copy-start.13
  3.2 0.7 copy-start.15
  3.9 0.7 copy-start.17
  4.6 34.7 %copy-start.10 = (bf16[96,1152]{1,0:T(8,128)(2,1)S(1)}, bf16[96,1152]{1,0:T(8,128)(2,1)}, u32[]{:S(2)}) copy-start(bf16[96,1152]{1,0:T(8,128)(2,1)} %own_att.1) | copy-start | bytes 663556
  4.6 34.7 %copy-start.14 = (bf16[96,384]{1,0:T(8,128)(2,1)S(1)}, bf16[96,384]{1,0:T(8,128)(2,1)}, u32[]{:S(2)}) copy-start(bf16[96,384]{1,0:T(8,128)(2,1)} %own_proj.1) | copy-start | bytes 221188
  5.2 7.4 %collective-permute-start = (bf16[208,384]{1,0:T(8,128)(2,1)S(1)}, bf16[208,384]{1,0:T(8,128)(2,1)S(1)}, u32[]{:S(2)}, u32[]{:S(2)}) collective-permute-start(bf16[208,384]{1,0:T(8,128)(2,1)S(1)} %own_payload.1.own), channel_id=1, source_target_pairs={{0,8},{1,17},{2,10},{3,19},{4,12},{5,21},{6,14},{7,23},{8,0},{9,25... | collective-permute-start | bytes 479240 | tf_op jit(solution)/shard_map/ppermute | solution.py:876
  8.2 6.0 %collective-permute-start.1 = (bf16[208,384]{1,0:T(8,128)(2,1)S(1)}, bf16[208,384]{1,0:T(8,128)(2,1)S(1)}, u32[]{:S(2)}, u32[]{:S(2)}) collective-permute-start(bf16[208,384]{1,0:T(8,128)(2,1)S(1)} %own_payload.1.own), channel_id=1, source_target_pairs={{0,16},{1,9},{2,18},{3,11},{4,20},{5,13},{6,22},{7,15},{8,24},{9,1... | collective-permute-start | bytes 479240 | tf_op jit(solution)/shard_map/ppermute | solution.py:876
  12.6 5.3 %collective-permute-start.2 = (bf16[208,384]{1,0:T(8,128)(2,1)S(1)}, bf16[208,384]{1,0:T(8,128)(2,1)S(1)}, u32[]{:S(2)}, u32[]{:S(2)}) collective-permute-start(bf16[208,384]{1,0:T(8,128)(2,1)S(1)} %collective-permute-done.first.n1), channel_id=1, source_target_pairs={{0,16},{1,9},{2,18},{3,11},{4,20},{5,13},{6,22},{7,15},{8,24},{9,1... | collective-permute-start | bytes 479240 | tf_op jit(solution)/shard_map/ppermute | solution.py:876
  17.8 1.0 copy-start
  18.9 1.0 copy-start.4
  19.8 1.0 copy-start.6
  20.8 18.5 %copy-start.22 = (bf16[2,256,384]{2,1,0:T(8,128)(2,1)S(1)}, bf16[2,256,384]{2,1,0:T(8,128)(2,1)}, u32[]{:S(2)}) copy-start(bf16[2,256,384]{2,1,0:T(8,128)(2,1)} %tokens.7) | copy-start | bytes 1179652
  21.8 9.2 %collective-permute-start.8 = (bf16[384,384]{1,0:T(8,128)(2,1)S(1)}, bf16[384,384]{1,0:T(8,128)(2,1)S(1)}, u32[]{:S(2)}, u32[]{:S(2)}) collective-permute-start(bf16[384,384]{1,0:T(8,128)(2,1)S(1)} %get-tuple-element.80), channel_id=1, source_target_pairs={{0,8},{1,17},{2,10},{3,19},{4,12},{5,21},{6,14},{7,23},{8,0},{9,25... | collective-permute-start | bytes 884744 | tf_op jit(solution)/shard_map/ppermute | solution.py:876
  24.3 13.2 %collective-permute-start.9 = (bf16[384,384]{1,0:T(8,128)(2,1)S(1)}, bf16[384,384]{1,0:T(8,128)(2,1)S(1)}, u32[]{:S(2)}, u32[]{:S(2)}) collective-permute-start(bf16[384,384]{1,0:T(8,128)(2,1)S(1)} %get-tuple-element.80), channel_id=1, source_target_pairs={{0,16},{1,9},{2,18},{3,11},{4,20},{5,13},{6,22},{7,15},{8,24},{9,1... | collective-permute-start | bytes 884744 | tf_op jit(solution)/shard_map/ppermute | solution.py:876
  31.0 6.7 %collective-permute-start.10 = (bf16[384,384]{1,0:T(8,128)(2,1)S(1)}, bf16[384,384]{1,0:T(8,128)(2,1)S(1)}, u32[]{:S(2)}, u32[]{:S(2)}) collective-permute-start(bf16[384,384]{1,0:T(8,128)(2,1)S(1)} %collective-permute-done.8.n1), channel_id=1, source_target_pairs={{0,16},{1,9},{2,18},{3,11},{4,20},{5,13},{6,22},{7,15},{8,24},{9,1... | collective-permute-start | bytes 884744 | tf_op jit(solution)/shard_map/ppermute | solution.py:876
  31.4 4.0 %collective-permute-start.3 = (f32[4,2304]{1,0:T(4,128)S(1)}, f32[4,2304]{1,0:T(4,128)S(1)}, u32[]{:S(2)}, u32[]{:S(2)}) collective-permute-start(f32[4,2304]{1,0:T(4,128)S(1)} %get-tuple-element.75), channel_id=1, source_target_pairs={{0,8},{1,17},{2,10},{3,19},{4,12},{5,21},{6,14},{7,23},{8,0},{9,25... | collective-permute-start | bytes 110600 | tf_op jit(solution)/shard_map/ppermute | solution.py:876
  33.2 2.2 %collective-permute-start.5 = (bf16[208,384]{1,0:T(8,128)(2,1)S(1)}, bf16[208,384]{1,0:T(8,128)(2,1)S(1)}, u32[]{:S(2)}, u32[]{:S(2)}) collective-permute-start(bf16[208,384]{1,0:T(8,128)(2,1)S(1)} %collective-permute-done.first.n1), channel_id=1, source_target_pairs={{0,1},{1,0},{2,3},{3,2},{4,5},{5,4},{6,7},{7,6},{8,9},{9,8},{10,11... | collective-permute-start | bytes 479240 | tf_op jit(solution)/shard_map/ppermute | solution.py:79
  33.2 3.8 %collective-permute-start.6 = (bf16[208,384]{1,0:T(8,128)(2,1)S(1)}, bf16[208,384]{1,0:T(8,128)(2,1)S(1)}, u32[]{:S(2)}, u32[]{:S(2)}) collective-permute-start(bf16[208,384]{1,0:T(8,128)(2,1)S(1)} %collective-permute-done.1.second.n2), channel_id=1, source_target_pairs={{0,1},{1,0},{2,3},{3,2},{4,5},{5,4},{6,7},{7,6},{8,9},{9,8},{10,11... | collective-permute-start | bytes 479240 | tf_op jit(solution)/shard_map/ppermute | solution.py:79
  35.4 3.9 %collective-permute-start.7 = (bf16[208,384]{1,0:T(8,128)(2,1)S(1)}, bf16[208,384]{1,0:T(8,128)(2,1)S(1)}, u32[]{:S(2)}, u32[]{:S(2)}) collective-permute-start(bf16[208,384]{1,0:T(8,128)(2,1)S(1)} %collective-permute-done.2.last.n3), channel_id=1, source_target_pairs={{0,1},{1,0},{2,3},{3,2},{4,5},{5,4},{6,7},{7,6},{8,9},{9,8},{10,11... | collective-permute-start | bytes 479240 | tf_op jit(solution)/shard_map/ppermute | solution.py:79
  35.4 3.8 %collective-permute-start.4 = (f32[2,2304]{1,0:T(2,128)S(1)}, f32[2,2304]{1,0:T(2,128)S(1)}, u32[]{:S(2)}, u32[]{:S(2)}) collective-permute-start(f32[2,2304]{1,0:T(2,128)S(1)} %slice.44), channel_id=1, source_target_pairs={{0,16},{1,9},{2,18},{3,11},{4,20},{5,13},{6,22},{7,15},{8,24},{9,1... | collective-permute-start | bytes 55304 | tf_op jit(solution)/shard_map/ppermute | solution.py:876
  37.1 6.2 %collective-permute-start.11 = (bf16[384,384]{1,0:T(8,128)(2,1)S(1)}, bf16[384,384]{1,0:T(8,128)(2,1)S(1)}, u32[]{:S(2)}, u32[]{:S(2)}) collective-permute-start(bf16[384,384]{1,0:T(8,128)(2,1)S(1)} %collective-permute-done.8.n1), channel_id=1, source_target_pairs={{0,1},{1,0},{2,3},{3,2},{4,5},{5,4},{6,7},{7,6},{8,9},{9,8},{10,11... | collective-permute-start | bytes 884744 | tf_op jit(solution)/shard_map/ppermute | solution.py:79
  37.5 5.7 %collective-permute-start.12 = (bf16[384,384]{1,0:T(8,128)(2,1)S(1)}, bf16[384,384]{1,0:T(8,128)(2,1)S(1)}, u32[]{:S(2)}, u32[]{:S(2)}) collective-permute-start(bf16[384,384]{1,0:T(8,128)(2,1)S(1)} %collective-permute-done.9.n2), channel_id=1, source_target_pairs={{0,1},{1,0},{2,3},{3,2},{4,5},{5,4},{6,7},{7,6},{8,9},{9,8},{10,11... | collective-permute-start | bytes 884744 | tf_op jit(solution)/shard_map/ppermute | solution.py:79
  37.7 5.6 %collective-permute-start.13 = (bf16[384,384]{1,0:T(8,128)(2,1)S(1)}, bf16[384,384]{1,0:T(8,128)(2,1)S(1)}, u32[]{:S(2)}, u32[]{:S(2)}) collective-permute-start(bf16[384,384]{1,0:T(8,128)(2,1)S(1)} %collective-permute-done.10.n3), channel_id=1, source_target_pairs={{0,1},{1,0},{2,3},{3,2},{4,5},{5,4},{6,7},{7,6},{8,9},{9,8},{10,11... | collective-permute-start | bytes 884744 | tf_op jit(solution)/shard_map/ppermute | solution.py:79
  39.3 4.0 %copy-start.5 = (bf16[384,384]{1,0:T(8,128)(2,1)S(1)}, bf16[384,384]{1,0:T(8,128)(2,1)}, u32[]{:S(2)}) copy-start(bf16[384,384]{1,0:T(8,128)(2,1)} %own_expand.1) | copy-start | bytes 884740
  39.3 4.0 %copy-start.7 = (bf16[384,384]{1,0:T(8,128)(2,1)S(1)}, bf16[384,384]{1,0:T(8,128)(2,1)}, u32[]{:S(2)}) copy-start(bf16[384,384]{1,0:T(8,128)(2,1)} %own_contract.1) | copy-start | bytes 884740
  39.3 4.0 %copy-start.21 = (bf16[2,256,384]{2,1,0:T(8,128)(2,1)S(1)}, bf16[2,256,384]{2,1,0:T(8,128)(2,1)}, u32[]{:S(2)}) copy-start(bf16[2,256,384]{2,1,0:T(8,128)(2,1)} %cotangent.1) | copy-start | bytes 1179652
  43.2 17.1 %copy-start.23 = (bf16[2,6,256,256]{3,2,1,0:T(8,128)(2,1)}, bf16[2,6,256,256]{3,2,1,0:T(8,128)(2,1)S(1)}, u32[]{:S(2)}) copy-start(bf16[2,6,256,256]{3,2,1,0:T(8,128)(2,1)S(1)} %get-tuple-element.84.soft_in) | copy-start | bytes 4718596
  54.1 2.8 %collective-permute-start.14 = (bf16[4,384,384]{2,1,0:T(8,128)(2,1)S(1)}, bf16[4,384,384]{2,1,0:T(8,128)(2,1)S(1)}, u32[]{:S(2)}, u32[]{:S(2)}) collective-permute-start(bf16[4,384,384]{2,1,0:T(8,128)(2,1)S(1)} %get-tuple-element.92), channel_id=1, source_target_pairs={{0,1},{1,0},{2,3},{3,2},{4,5},{5,4},{6,7},{7,6},{8,9},{9,8},{10,11... | collective-permute-start | bytes 3538952 | tf_op jit(solution)/shard_map/ppermute | solution.py:79
  56.9 1.3 copy-start.8
  58.2 2.1 %copy-start.16 = (f32[2,384]{1,0:T(2,128)S(1)}, f32[2,384]{1,0:T(2,128)}, u32[]{:S(2)}) copy-start(f32[2,384]{1,0:T(2,128)} %condition.1) | copy-start | bytes 9220
  58.4 9.9 %collective-permute-start.15 = (bf16[2,384,384]{2,1,0:T(8,128)(2,1)S(1)}, bf16[2,384,384]{2,1,0:T(8,128)(2,1)S(1)}, u32[]{:S(2)}, u32[]{:S(2)}) collective-permute-start(bf16[2,384,384]{2,1,0:T(8,128)(2,1)S(1)} %get-tuple-element.94), channel_id=1, source_target_pairs={{0,8},{1,17},{2,10},{3,19},{4,12},{5,21},{6,14},{7,23},{8,0},{9,25... | collective-permute-start | bytes 1769480 | tf_op jit(solution)/shard_map/ppermute | solution.py:876
  74.6 6.7 %collective-permute-start.16 = (bf16[4,192,384]{2,1,0:T(8,128)(2,1)S(1)}, bf16[4,192,384]{2,1,0:T(8,128)(2,1)S(1)}, u32[]{:S(2)}, u32[]{:S(2)}) collective-permute-start(bf16[4,192,384]{2,1,0:T(8,128)(2,1)S(1)} %get-tuple-element.98), channel_id=1, source_target_pairs={{0,1},{1,0},{2,3},{3,2},{4,5},{5,4},{6,7},{7,6},{8,9},{9,8},{10,11... | collective-permute-start | bytes 1769480 | tf_op jit(solution)/shard_map/ppermute | solution.py:79
  74.6 6.7 %collective-permute-start.17 = (bf16[1,384,384]{2,1,0:T(8,128)(2,1)S(1)}, bf16[1,384,384]{2,1,0:T(8,128)(2,1)S(1)}, u32[]{:S(2)}, u32[]{:S(2)}) collective-permute-start(bf16[1,384,384]{2,1,0:T(8,128)(2,1)S(1)} %get-tuple-element.95.refs_4_), channel_id=1, source_target_pairs={{0,16},{1,9},{2,18},{3,11},{4,20},{5,13},{6,22},{7,15},{8,24},{9,1... | collective-permute-start | bytes 884744 | tf_op jit(solution)/shard_map/ppermute | solution.py:876
  82.2 8.9 %collective-permute-start.18 = (bf16[2,192,384]{2,1,0:T(8,128)(2,1)S(1)}, bf16[2,192,384]{2,1,0:T(8,128)(2,1)S(1)}, u32[]{:S(2)}, u32[]{:S(2)}) collective-permute-start(bf16[2,192,384]{2,1,0:T(8,128)(2,1)S(1)} %get-tuple-element.102), channel_id=1, source_target_pairs={{0,8},{1,17},{2,10},{3,19},{4,12},{5,21},{6,14},{7,23},{8,0},{9,25... | collective-permute-start | bytes 884744 | tf_op jit(solution)/shard_map/ppermute | solution.py:876
  84.0 7.0 %collective-permute-start.19 = (bf16[224,384]{1,0:T(8,128)(2,1)S(1)}, bf16[224,384]{1,0:T(8,128)(2,1)S(1)}, u32[]{:S(2)}, u32[]{:S(2)}) collective-permute-start(bf16[224,384]{1,0:T(8,128)(2,1)S(1)} %get-tuple-element.104.own), channel_id=1, source_target_pairs={{0,2},{1,5},{2,0},{3,7},{4,6},{5,1},{6,4},{7,3},{8,10},{9,13},{10,... | collective-permute-start | bytes 516104 | tf_op jit(solution)/shard_map/ppermute | solution.py:866
  91.0 25.6 %copy-start.1 = (bf16[96,2304]{1,0:T(8,128)(2,1)S(1)}, bf16[96,2304]{1,0:T(8,128)(2,1)}, u32[]{:S(2)}) copy-start(bf16[96,2304]{1,0:T(8,128)(2,1)} %weight.5) | copy-start | bytes 1327108
  91.7 7.6 %collective-permute-start.21 = (bf16[256,384]{1,0:T(8,128)(2,1)S(1)}, bf16[256,384]{1,0:T(8,128)(2,1)S(1)}, u32[]{:S(2)}, u32[]{:S(2)}) collective-permute-start(bf16[256,384]{1,0:T(8,128)(2,1)S(1)} %get-tuple-element.107.own), channel_id=1, source_target_pairs={{0,4},{1,3},{2,6},{3,1},{4,0},{5,7},{6,2},{7,5},{8,12},{9,11},{10,... | collective-permute-start | bytes 589832 | tf_op jit(solution)/shard_map/ppermute | solution.py:866
  93.6 5.2 %collective-permute-start.20 = (bf16[192,384]{1,0:T(8,128)(2,1)S(1)}, bf16[192,384]{1,0:T(8,128)(2,1)S(1)}, u32[]{:S(2)}, u32[]{:S(2)}) collective-permute-start(bf16[192,384]{1,0:T(8,128)(2,1)S(1)} %get-tuple-element.106), channel_id=1, source_target_pairs={{0,16},{1,9},{2,18},{3,11},{4,20},{5,13},{6,22},{7,15},{8,24},{9,1... | collective-permute-start | bytes 442376 | tf_op jit(solution)/shard_map/ppermute | solution.py:876
  99.3 20.3 %copy-start.24 = (bf16[384,384]{1,0:T(8,128)(2,1)S(1)}, bf16[384,384]{1,0:T(8,128)(2,1)}, u32[]{:S(2)}) copy-start(bf16[384,384]{1,0:T(8,128)(2,1)} %param.42) | copy-start | bytes 884740
  99.9 9.8 %collective-permute-start.23 = (bf16[192,384]{1,0:T(8,128)(2,1)S(1)}, bf16[192,384]{1,0:T(8,128)(2,1)S(1)}, u32[]{:S(2)}, u32[]{:S(2)}) collective-permute-start(bf16[192,384]{1,0:T(8,128)(2,1)S(1)} %get-tuple-element.110.feed_half), channel_id=1, source_target_pairs={{0,2},{1,5},{2,0},{3,7},{4,6},{5,1},{6,4},{7,3},{8,10},{9,13},{10,... | collective-permute-start | bytes 442376 | tf_op jit(solution)/shard_map/ppermute | solution.py:866
  102.0 7.7 %collective-permute-start.24 = (bf16[128,384]{1,0:T(8,128)(2,1)S(1)}, bf16[128,384]{1,0:T(8,128)(2,1)S(1)}, u32[]{:S(2)}, u32[]{:S(2)}) collective-permute-start(bf16[128,384]{1,0:T(8,128)(2,1)S(1)} %get-tuple-element.111.small), channel_id=1, source_target_pairs={{0,16},{1,9},{2,18},{3,11},{4,20},{5,13},{6,22},{7,15},{8,24},{9,1... | collective-permute-start | bytes 294920 | tf_op jit(solution)/shard_map/ppermute | solution.py:876
  105.3 4.4 %collective-permute-start.22 = (bf16[96,384]{1,0:T(8,128)(2,1)S(1)}, bf16[96,384]{1,0:T(8,128)(2,1)S(1)}, u32[]{:S(2)}, u32[]{:S(2)}) collective-permute-start(bf16[96,384]{1,0:T(8,128)(2,1)S(1)} %get-tuple-element.109), channel_id=1, source_target_pairs={{0,2},{1,5},{2,0},{3,7},{4,6},{5,1},{6,4},{7,3},{8,10},{9,13},{10,... | collective-permute-start | bytes 221192 | tf_op jit(solution)/shard_map/ppermute | solution.py:866
  110.3 9.2 %collective-permute-start.29 = (bf16[384,384]{1,0:T(8,128)(2,1)S(1)}, bf16[384,384]{1,0:T(8,128)(2,1)}, u32[]{:S(2)}, u32[]{:S(2)}) collective-permute-start(bf16[384,384]{1,0:T(8,128)(2,1)S(1)} %get-tuple-element.117), channel_id=1, source_target_pairs={{0,1},{1,0},{2,3},{3,2},{4,5},{5,4},{6,7},{7,6},{8,9},{9,8},{10,11... | collective-permute-start | bytes 884744 | tf_op jit(solution)/shard_map/ppermute | solution.py:79
  110.4 6.3 %collective-permute-start.26 = (bf16[256,384]{1,0:T(8,128)(2,1)S(1)}, bf16[256,384]{1,0:T(8,128)(2,1)S(1)}, u32[]{:S(2)}, u32[]{:S(2)}) collective-permute-start(bf16[256,384]{1,0:T(8,128)(2,1)S(1)} %get-tuple-element.113.small), channel_id=1, source_target_pairs={{0,8},{1,17},{2,10},{3,19},{4,12},{5,21},{6,14},{7,23},{8,0},{9,25... | collective-permute-start | bytes 589832 | tf_op jit(solution)/shard_map/ppermute | solution.py:876
  110.4 6.2 %collective-permute-start.25 = (bf16[96,384]{1,0:T(8,128)(2,1)S(1)}, bf16[96,384]{1,0:T(8,128)(2,1)S(1)}, u32[]{:S(2)}, u32[]{:S(2)}) collective-permute-start(bf16[96,384]{1,0:T(8,128)(2,1)S(1)} %get-tuple-element.112.att_half), channel_id=1, source_target_pairs={{0,4},{1,3},{2,6},{3,1},{4,0},{5,7},{6,2},{7,5},{8,12},{9,11},{10,... | collective-permute-start | bytes 221192 | tf_op jit(solution)/shard_map/ppermute | solution.py:866
  117.5 5.5 %collective-permute-start.27 = (bf16[96,384]{1,0:T(8,128)(2,1)S(1)}, bf16[96,384]{1,0:T(8,128)(2,1)S(1)}, u32[]{:S(2)}, u32[]{:S(2)}) collective-permute-start(bf16[96,384]{1,0:T(8,128)(2,1)S(1)} %get-tuple-element.114.att_sum), channel_id=1, source_target_pairs={{0,2},{1,5},{2,0},{3,7},{4,6},{5,1},{6,4},{7,3},{8,10},{9,13},{10,... | collective-permute-start | bytes 221192 | tf_op jit(solution)/shard_map/ppermute | solution.py:866
  117.5 5.4 %collective-permute-start.28 = (f32[8,128]{1,0:T(8,128)S(1)}, f32[8,128]{1,0:T(8,128)S(1)}, u32[]{:S(2)}, u32[]{:S(2)}) collective-permute-start(f32[8,128]{1,0:T(8,128)S(1)} %get-tuple-element.116), channel_id=1, source_target_pairs={{0,8},{1,17},{2,10},{3,19},{4,12},{5,21},{6,14},{7,23},{8,0},{9,25... | collective-permute-start | bytes 12296 | tf_op jit(solution)/shard_map/ppermute | solution.py:876
  123.0 5.1 %copy-start.2 = (f32[384,384]{1,0:T(8,128)}, f32[384,384]{1,0:T(8,128)S(1)}, u32[]{:S(2)}) copy-start(f32[384,384]{1,0:T(8,128)S(1)} %get-tuple-element.129.__) | copy-start | bytes 1769476
  123.0 5.1 %copy-start.3 = (f32[384,384]{1,0:T(8,128)}, f32[384,384]{1,0:T(8,128)S(1)}, u32[]{:S(2)}) copy-start(f32[384,384]{1,0:T(8,128)S(1)} %get-tuple-element.141._) | copy-start | bytes 1769476
  123.0 5.1 %copy-start.27 = (bf16[96,384]{1,0:T(8,128)(2,1)S(1)}, bf16[96,384]{1,0:T(8,128)(2,1)}, u32[]{:S(2)}) copy-start(bf16[96,384]{1,0:T(8,128)(2,1)} %param.34) | copy-start | bytes 221188
  123.0 5.0 %copy-start.28 = (bf16[96,384]{1,0:T(8,128)(2,1)S(1)}, bf16[96,384]{1,0:T(8,128)(2,1)}, u32[]{:S(2)}) copy-start(bf16[96,384]{1,0:T(8,128)(2,1)} %param.40) | copy-start | bytes 221188
  123.6 3.7 %collective-permute-start.30 = (f32[8,128]{1,0:T(8,128)S(1)}, f32[8,128]{1,0:T(8,128)S(1)}, u32[]{:S(2)}, u32[]{:S(2)}) collective-permute-start(f32[8,128]{1,0:T(8,128)S(1)} %get-tuple-element.118), channel_id=1, source_target_pairs={{0,16},{1,9},{2,18},{3,11},{4,20},{5,13},{6,22},{7,15},{8,24},{9,1... | collective-permute-start | bytes 12296 | tf_op jit(solution)/shard_map/ppermute | solution.py:876
  125.2 5.1 %collective-permute-start.31 = (bf16[512,384]{1,0:T(8,128)(2,1)S(1)}, bf16[512,384]{1,0:T(8,128)(2,1)S(1)}, u32[]{:S(2)}, u32[]{:S(2)}) collective-permute-start(bf16[512,384]{1,0:T(8,128)(2,1)S(1)} %get-tuple-element.119.near), channel_id=1, source_target_pairs={{0,1},{1,0},{2,3},{3,2},{4,5},{5,4},{6,7},{7,6},{8,9},{9,8},{10,11... | collective-permute-start | bytes 1179656 | tf_op jit(solution)/shard_map/ppermute | solution.py:79
  125.2 2.7 %collective-permute-start.32 = (bf16[192,384]{1,0:T(8,128)(2,1)S(1)}, bf16[192,384]{1,0:T(8,128)(2,1)S(1)}, u32[]{:S(2)}, u32[]{:S(2)}) collective-permute-start(bf16[192,384]{1,0:T(8,128)(2,1)S(1)} %get-tuple-element.121), channel_id=1, source_target_pairs={{0,1},{1,0},{2,3},{3,2},{4,5},{5,4},{6,7},{7,6},{8,9},{9,8},{10,11... | collective-permute-start | bytes 442376 | tf_op jit(solution)/shard_map/ppermute | solution.py:79
  127.9 1.0 copy-start.25
  127.9 1.1 copy-start.26
  129.0 1.3 copy-start.11
  129.0 1.3 copy-start.12
  129.0 1.3 copy-start.18
  129.0 1.3 copy-start.19
  129.0 1.3 %copy-start.20 = (bf16[14,96]{1,0:T(8,128)(2,1)S(1)}, bf16[14,96]{1,0:T(8,128)(2,1)}, u32[]{:S(2)}) copy-start(bf16[14,96]{1,0:T(8,128)(2,1)} %bias_square.1) | copy-start | bytes 8068

commit v2 on v1

--- a/solution.py
+++ b/solution.py
@@ -156,14 +156,16 @@
     return (rank ^ (1 + core), rank ^ (2 - core), rank ^ 3)
 
 
-def payload_kernel(where, condition, attending, projection, biases, out):
+def payload_kernel(where, condition, attending, projection, biases, expand, contract, out, part):
     @pl.when(where[1] == 0)
     def _():
+        part[...] = expand[...]
         out[0:QUARTER, :] = attending[:, 0:D]
         out[QUARTER : 2 * QUARTER, :] = attending[:, D : 2 * D]
 
     @pl.when(where[1] != 0)
     def _():
+        part[...] = contract[...]
         out[0:QUARTER, :] = attending[:, 2 * D : 3 * D]
         out[QUARTER : 2 * QUARTER, :] = projection[...]
 
@@ -176,7 +178,7 @@
 
 
 def modulation_kernel(
-    where, own, first, second, last, weight, expand, contract, stay, go, bias_out, feed_part
+    where, own, first, second, last, weight, stay, go, bias_out
 ):
     rank = where[0]
     owners = (rank,) + neighbours(where)
@@ -197,13 +199,14 @@
         lanes.append(chosen)
     bias_out[...] = jnp.concatenate(lanes, axis=1)
 
-    @pl.when(where[1] == 0)
-    def _():
-        feed_part[...] = expand[...]
-
-    @pl.when(where[1] != 0)
-    def _():
-        feed_part[...] = contract[...]
+
+def relay_kernel(where, keep, arrived, _, stay, go, __):
+    stay[...] = keep[0:2, :] + arrived[0:2, :]
+    go[...] = keep[2:4, :] + arrived[2:4, :]
+
+
+def gate_kernel(*refs):
+    pass
 
 
 def attention_forward_kernel(
@@ -236,7 +239,7 @@
         def _():
             assemble((f1, f2, f3), (n1, n2, n3))
 
-    summed = stay[0:2, :] + arrived[...]
+    summed = stay[...] + arrived[...]
     row = jnp.where(slot == 0, summed[0:1], summed[1:2])
     pieces = [row[:, j * D : (j + 1) * D] + bias[2 + j : 3 + j, :] for j in range(6)]
     mod_out[0] = jnp.concatenate(pieces, axis=0)
@@ -488,58 +491,51 @@
     return pl.ds(pl.multiple_of(index * count, 32), count)
 
 
-def step0_kernel(
-    where, att_keep, att_in, feed_keep, feed_in, small, att_stay, att_go, feed_stay, message, total
+def step1_kernel(
+    where, att_keep, att_in, feed_keep, feed_in, small, small_in,
+    att_stay, att_go, feed_stay, feed_go, small_out, total,
 ):
     half = half_of(where)
-    att_stay[...] = att_keep[0:2].astype(WIDE) + att_in[0:2].astype(WIDE)
-    att_go[...] = (att_keep[2:4].astype(WIDE) + att_in[2:4].astype(WIDE)).astype(LOW)
-    total[...] = feed_keep[0] + feed_in[0].astype(WIDE)
-    count = D // 2
-    feed_stay[...] = total[rows_at(half, count), :]
-    message[0:count, :] = total[rows_at(1 - half, count), :].astype(LOW)
-    message[count:, :] = small[...]
-
-
-def step1_kernel(
-    where, att_keep, att_in, feed_keep, own, feed_in, att_stay, att_go, message
-):
     count = D // 2
     att_stay[...] = att_keep[0] + att_in[0].astype(WIDE)
     att_go[...] = (att_keep[1] + att_in[1].astype(WIDE)).astype(LOW)
-    message[0:count, :] = (feed_keep[...] + feed_in[0:count, :].astype(WIDE)).astype(LOW)
-    message[count : count + SMALL, :] = own[count:, :]
-    message[count + SMALL :, :] = feed_in[count:, :]
+    total[...] = feed_keep[...] + feed_in[...].astype(WIDE)
+    feed_stay[...] = total[rows_at(half, count), :]
+    feed_go[...] = total[rows_at(1 - half, count), :].astype(LOW)
+    small_out[0:SMALL, :] = small[...]
+    small_out[SMALL:, :] = small_in[...]
 
 
 def step2_kernel(
-    where, att_keep, att_in, own, feed_in, att_stay, att_go, feed_half, small, total
+    where, att_keep, att_in, feed_keep, feed_in, small, small_in,
+    att_stay, att_go, feed_half, small_out, total,
+):
+    half = half_of(where)
+    total[...] = att_keep[...] + att_in[...].astype(WIDE)
+    att_stay[...] = total[rows_at(half, QUARTER), :]
+    att_go[...] = total[rows_at(1 - half, QUARTER), :].astype(LOW)
+    feed_half[...] = (feed_keep[...] + feed_in[...].astype(WIDE)).astype(LOW)
+    small_out[0 : 2 * SMALL, :] = small[...]
+    small_out[2 * SMALL :, :] = small_in[...]
+
+
+def step3_kernel(
+    where, att_keep, att_in, feed_half, feed_in, small, small_in, att_half, feed_sum, small_out
+):
+    att_half[...] = (att_keep[...] + att_in[...].astype(WIDE)).astype(LOW)
+    feed_sum[...] = (feed_half[...].astype(WIDE) + feed_in[...].astype(WIDE)).astype(LOW)
+    small_out[0 : 4 * SMALL, :] = small[...]
+    small_out[4 * SMALL :, :] = small_in[...]
+
+
+def step4_kernel(
+    where, att_half, att_in, feed_sum, feed_in, small, small_in, weight,
+    att_sum, feed_part, small_out, cond_keep, cond_go,
 ):
     half = half_of(where)
     count = D // 2
-    total[...] = att_keep[...] + att_in[...].astype(WIDE)
-    att_stay[...] = total[rows_at(half, QUARTER), :]
-    att_go[...] = total[rows_at(1 - half, QUARTER), :].astype(LOW)
-    feed_half[...] = (own[0:count, :].astype(WIDE) + feed_in[0:count, :].astype(WIDE)).astype(LOW)
-    small[0 : 2 * SMALL, :] = own[count:, :]
-    small[2 * SMALL :, :] = feed_in[count:, :]
-
-
-def step3_kernel(
-    where, att_keep, att_in, feed_half, feed_in, small, small_in, att_half, feed_part, small_out
-):
-    half = half_of(where)
-    count = D // 2
-    att_half[...] = (att_keep[...] + att_in[...].astype(WIDE)).astype(LOW)
-    feed_part[rows_at(half, count), :] = feed_half[...]
+    feed_part[rows_at(half, count), :] = feed_sum[...]
     feed_part[rows_at(1 - half, count), :] = feed_in[...]
-    small_out[0 : 4 * SMALL, :] = small[...]
-    small_out[4 * SMALL :, :] = small_in[...]
-
-
-def step4_kernel(
-    where, att_half, att_in, small, small_in, weight, att_sum, small_out, cond_keep, cond_go
-):
     att_sum[...] = (att_half[...].astype(WIDE) + att_in[...].astype(WIDE)).astype(LOW)
     small_out[0 : 8 * SMALL, :] = small[...]
     small_out[8 * SMALL :, :] = small_in[...]
@@ -561,7 +557,7 @@
     cond_go[...] = jnp.concatenate([padded[4:8], blank], axis=0)
 
 
-def step5_kernel(where, att_sum, att_in, cond_keep, cond_in, _, __, att_part, cond_go):
+def step5_kernel(where, att_sum, att_in, cond_keep, cond_in, att_part, cond_go):
     half = half_of(where)
     att_part[rows_at(half, QUARTER), :] = att_sum[...]
     att_part[rows_at(1 - half, QUARTER), :] = att_in[...]
@@ -661,47 +657,56 @@
 ANY_SPEC = pl.BlockSpec(memory_space=pl.ANY)
 
 
-def small_call(kernel, name, outs, where, *operands, scratch=(), after=()):
+def small_call(kernel, name, outs, where, *operands, scratch=(), params=PARAMS):
     return pl.pallas_call(
         kernel,
         grid=(1,),
-        in_specs=[SMEM_SPEC]
-        + [whole(item.shape) for item in operands]
-        + [ANY_SPEC] * len(after),
+        in_specs=[SMEM_SPEC] + [whole(item.shape) for item in operands],
         out_specs=[whole(shape) for shape, _ in outs],
         out_shape=[shape_of(*item) for item in outs],
         scratch_shapes=[pltpu.VMEM(*item) for item in scratch],
+        compiler_params=params,
+        name=name,
+    )(where, *operands)
+
+
+def run_gate(value, *after):
+    return pl.pallas_call(
+        gate_kernel,
+        in_specs=[ANY_SPEC] * (1 + len(after)),
+        out_specs=ANY_SPEC,
+        out_shape=shape_of(value.shape, value.dtype),
+        input_output_aliases={0: 0},
+        name="in_order",
+    )(value, *after)
+
+
+def run_relay(where, keep, arrived, passing):
+    two = (2, keep.shape[1])
+    return pl.pallas_call(
+        relay_kernel,
+        grid=(1,),
+        in_specs=[SMEM_SPEC, whole(keep.shape), whole(arrived.shape), ANY_SPEC],
+        out_specs=[whole(two), whole(two), ANY_SPEC],
+        out_shape=[shape_of(two, WIDE)] * 2 + [shape_of(passing.shape, passing.dtype)],
+        input_output_aliases={3: 2},
         compiler_params=PARAMS,
-        name=name,
-    )(where, *operands, *after)
-
-
-def run_payload(where, condition, attending, projection, biases):
-    return small_call(
-        payload_kernel,
-        "own_payload",
-        [((2 * QUARTER + 16, D), LOW)],
-        where,
-        condition,
-        attending,
-        projection,
-        biases,
-    )[0]
-
-
-def run_modulation(where, blocks, weight, expand, contract):
+        name="relay",
+    )(where, keep, arrived, passing)
+
+
+def run_modulation(where, blocks, weight):
     message = pl.BlockSpec((16, D), lambda s: (2 * QUARTER // 16, 0))
     return pl.pallas_call(
         modulation_kernel,
         grid=(1,),
-        in_specs=[SMEM_SPEC] + [message] * 4 + [whole((QUARTER, 6 * D))] + [whole((D, D))] * 2,
-        out_specs=[whole((4, 6 * D))] * 2 + [whole((16, D)), whole((D, D))],
-        out_shape=[shape_of((4, 6 * D), WIDE)] * 2
-        + [shape_of((16, D), WIDE), shape_of((D, D), LOW)],
+        in_specs=[SMEM_SPEC] + [message] * 4 + [whole((QUARTER, 6 * D))],
+        out_specs=[whole((4, 6 * D))] * 2 + [whole((16, D))],
+        out_shape=[shape_of((4, 6 * D), WIDE)] * 2 + [shape_of((16, D), WIDE)],
         compiler_params=PARAMS,
         cost_estimate=pl.CostEstimate(flops=10**7, bytes_accessed=10**6, transcendentals=0),
         name="modulation_partials",
-    )(where, *blocks, weight, expand, contract)
+    )(where, *blocks, weight)
 
 
 def run_attention_forward(where, tokens, stay, arrived, bias, own_att, own_proj, nears, fars):
@@ -712,7 +717,7 @@
         in_specs=[
             SMEM_SPEC,
             by_slot((SEQ, D)),
-            whole((4, 6 * D)),
+            whole((2, 6 * D)),
             whole((2, 6 * D)),
             whole((16, D)),
             whole((QUARTER, 3 * D)),
@@ -914,45 +919,44 @@
     where, copy, stages, condition, ffn_halves, att_parts, small_rows, stored, means, squares
 ):
     core = where[1]
-    (feed_stay, feed_go), (att_send, att_keep) = ffn_halves, att_parts
-    half, third = (D // 2, D), (2 * QUARTER, D)
-    att_stay, att_go, feed_stay, message = small_call(
-        step0_kernel, "step_0",
-        [((2,) + third, WIDE), ((2,) + third, LOW), (half, WIDE), ((D // 2 + SMALL, D), LOW)],
-        where, att_keep, swap_replica(att_send, 1), feed_stay, swap_pair(feed_go, 1), small_rows,
+    (feed_stay, feed_in), (att_send, att_keep) = ffn_halves, att_parts
+    half, third, quarter = (D // 2, D), (2 * QUARTER, D), (QUARTER, D)
+    att_stay, att_go = run_split(att_keep, swap_replica(att_send, 1))
+    feed_stay, feed_go = run_split(feed_stay, feed_in)
+    feed_stay, feed_go = feed_stay[0], feed_go[0]
+    att_stay, att_go, feed_stay, feed_go, small = small_call(
+        step1_kernel, "step_1",
+        [(third, WIDE), (third, LOW), (half, WIDE), (half, LOW), ((2 * SMALL, D), LOW)],
+        where, att_stay, swap_pair(att_go, 0), feed_stay, swap_pair(feed_go, 1),
+        small_rows, swap_plane(small_rows, 0),
         scratch=[((D, D), WIDE)],
     )
-    att_stay, att_go, message = small_call(
-        step1_kernel, "step_1",
-        [(third, WIDE), (third, LOW), ((D // 2 + 2 * SMALL, D), LOW)],
-        where, att_stay, swap_pair(att_go, 0), feed_stay, message, swap_plane(message, 0),
-    )
-    quarter = (QUARTER, D)
     att_stay, att_go, feed_half, small = small_call(
         step2_kernel, "step_2",
         [(quarter, WIDE), (quarter, LOW), (half, LOW), ((4 * SMALL, D), LOW)],
-        where, att_stay, swap_pair(att_go, 1), message, swap_plane(message, 1),
+        where, att_stay, swap_pair(att_go, 1), feed_stay, swap_plane(feed_go, 0),
+        small, swap_plane(small, 1),
         scratch=[(third, WIDE)],
     )
-    att_half, feed_part, small = small_call(
+    att_half, feed_sum, small = small_call(
         step3_kernel, "step_3",
-        [(quarter, LOW), ((D, D), LOW), ((8 * SMALL, D), LOW)],
-        where, att_stay, swap_plane(att_go, 0), feed_half, swap_plane(feed_half, 0),
+        [(quarter, LOW), (half, LOW), ((8 * SMALL, D), LOW)],
+        where, att_stay, swap_plane(att_go, 0), feed_half, swap_plane(feed_half, 1),
         small, swap_pair(small, 1),
     )
+    att_sum, feed_part, small, cond_keep, cond_go = small_call(
+        step4_kernel, "step_4",
+        [(quarter, LOW), ((D, D), LOW), ((16 * SMALL, D), LOW), ((8, 128), WIDE), ((8, 128), WIDE)],
+        where, att_half, swap_plane(att_half, 1), feed_sum, swap_plane(feed_sum, 0),
+        small, swap_pair(small, 0), stored[0],
+    )
     feed_totals = by_core(core, feed_part, swap_replica(feed_part, 1))
-    att_sum, small, cond_keep, cond_go = small_call(
-        step4_kernel, "step_4",
-        [(quarter, LOW), ((16 * SMALL, D), LOW), ((8, 128), WIDE), ((8, 128), WIDE)],
-        where, att_half, swap_plane(att_half, 1), small, swap_pair(small, 0), stored[0],
-    )
     cond_in = swap_pair(cond_go, 0)
     feed_updates = update_all(stored, feed_totals, means, squares, (3, 4))
     att_part, cond_go = small_call(
         step5_kernel, "step_5",
         [(third, LOW), ((8, 128), WIDE)],
         where, att_sum, swap_plane(att_sum, 0), cond_keep, cond_in,
-        after=(feed_updates[0][1], feed_updates[1][1]),
     )
     shard = [((QUARTER, 6 * D), WIDE)] * 3 + [((BIAS_ROWS, QUARTER), WIDE)] * 3
     updates = small_call(
@@ -987,7 +991,8 @@
     rank, core = where[0], where[1]
     slot_count, model_width = condition.shape
     modulation, cond_low = stored[0], jax.nn.silu(condition).astype(jnp.bfloat16)
-    (ffn_stay, ffn_go), (att_send, att_keep) = ffn_halves, att_parts
+    (ffn_stay, ffn_in), (att_send, att_keep) = ffn_halves, att_parts
+    ffn_stay, ffn_go = run_split(ffn_stay, ffn_in)
     ffn_totals = reduce_replicas(
         wide_sum([ffn_stay[0], swap_pair(ffn_go[0], 1)]).astype(LOW), copy, stages
     )
@@ -1077,16 +1082,22 @@
     where = jnp.stack([rank, core, copy >> 1, live_counts[0]]).astype(jnp.int32)
 
     cond_low = jax.nn.silu(condition).astype(LOW)
-    payload = run_payload(where, condition, attending, projection, biases)
-    nears = gather_pair(payload)
+    payload, feed_part = small_call(
+        payload_kernel, "own_payload",
+        [((2 * QUARTER + 16, model_width), LOW), ((model_width, model_width), LOW)],
+        where, condition, attending, projection, biases, expand, contract,
+        params=pltpu.CompilerParams(vmem_limit_bytes=60 * 1024 * 1024),
+    )
+    first, second = swap_pair(payload, 0), swap_pair(payload, 1)
+    feed_part = run_gate(feed_part, first, second)
+    nears = (first, second, swap_pair(first, 1))
     fars = [swap_replica(item, 1) for item in nears]
-    stay, go, bias, feed_part = run_modulation(
-        where, (payload,) + nears, modulation, expand, contract
-    )
-    feed_nears = gather_pair(feed_part)
+    feed_first, feed_second = swap_pair(feed_part, 0), swap_pair(feed_part, 1)
+    stay, go, bias = run_modulation(where, (payload,) + nears, modulation)
+    stay, go, feed_first = run_relay(where, stay, swap_pair(go, 0), feed_first)
+    arrived = swap_pair(go, 1)
+    feed_nears = (feed_first, feed_second, swap_pair(feed_first, 1))
     feed_fars = [swap_replica(item, 1) for item in feed_nears]
-    stay = stay + swap_pair(go, 0)
-    arrived = swap_pair(stay[slot_count:], 1)
 
     joined, soft, mixed, mod, att, proj = run_attention_forward(
         where, latents, stay, arrived, bias, attending, projection, nears, fars
@@ -1099,14 +1110,14 @@
     half_tokens, half_att, half_proj, half_rows = run_attention_backward(
         0, where, latents, grad_middle, joined, soft, mixed, mod, feed_rows, cond_wide, att, proj
     )
-    ffn_stay, ffn_go = run_split(ffn_stay, swap_pair(ffn_go, 0))
+    ffn_in = swap_pair(ffn_go, 0)
     grad_latents, att_send, att_keep, small_rows = run_attention_backward(
         1, where, latents, grad_middle, joined, soft, mixed, mod, feed_rows, cond_wide, att, proj,
         (half_att, half_proj, half_rows, half_tokens, ffn_go),
     )
     tail = tail_in_step if lax.axis_size("replica") == 8 else tail_in_turn
     grad_condition, results = tail(
-        where, copy, stages, condition, (ffn_stay, ffn_go), (att_send, att_keep), small_rows,
+        where, copy, stages, condition, (ffn_stay, ffn_in), (att_send, att_keep), small_rows,
         (modulation, attending, projection, expand, contract, biases),
         (
             modulation_mean, attending_mean, projection_mean,

time: 135 us -> 124 us (0.919)
  waiting for transfers between devices: 44.4 us -> 39.2 us
  local copies, waits for them, and re-layouts: 7.65 us -> 3.97 us
  starting transfers between devices: 38.8 us -> 36 us
  Pallas kernels: 35.1 us -> 36.7 us
    ppermute x16, starting transfers between devices: 27.6 us -> 20.1 us  [swap_pair(): return lax.ppermute(value, ('group', 'replica'), pairs)]
    ppermute x6 -> x8, starting transfers between devices: 9.18 us -> 14.3 us  [swap_plane(): return lax.ppermute(value, 'replica', pairs)]
    unnamed x58 -> x68, local copies, waits for them, and re-layouts: 7.61 us -> 3.95 us
    ppermute x16, waiting for transfers between devices: 28.7 us -> 25.2 us  [swap_pair(): return lax.ppermute(value, ('group', 'replica'), pairs)]
    ppermute x11, waiting for transfers between devices: 2.87 us -> 0.83 us  [swap_replica(): lax.ppermute(value, 'replica', [(i, i ^ k) for i in range(lax.axis_size('...]
    pallas_call x8 -> x7, Pallas kernels: 8.43 us -> 9.15 us  [small_call(): pl.pallas_call(kernel, grid=(1,), in_specs=[SMEM_SPEC] + [whole(item.shap...]
    ppermute x6 -> x8, waiting for transfers between devices: 12.8 us -> 13.2 us  [swap_plane(): return lax.ppermute(value, 'replica', pairs)]
  transfers between devices with their start and end apart: 33 -> 35, of which waited for: 15 -> 20; matrix products, arithmetic and copies ran while one was open for 5% -> 4% of each run, Pallas kernels for 7% -> 13%
where the time goes in v2:
time: 124 us
  waiting for transfers between devices  39.2 us (32%)
  Pallas kernels  36.7 us (30%)
  starting transfers between devices  36 us (29%)
  other arithmetic  6.08 us (5%)
  local copies, waits for them, and re-layouts  3.97 us (3%)
  between operations  1.73 us (1%)
    ppermute x16, waiting for transfers between devices, swap_pair(): return lax.ppermute(value, ('group', 'replica'), pairs)  25.2 us
    ppermute x16, starting transfers between devices, swap_pair(): return lax.ppermute(value, ('group', 'replica'), pairs)  20.1 us
    ppermute x8, starting transfers between devices, swap_plane(): return lax.ppermute(value, 'replica', pairs)  14.3 us
    ppermute x8, waiting for transfers between devices, swap_plane(): return lax.ppermute(value, 'replica', pairs)  13.2 us
    pallas_call x2, Pallas kernels, run_attention_backward(): pl.pallas_call(functools.partial(attention_backward_kernel, slot), grid=(...  10.8 us
    pallas_call x1, Pallas kernels, run_feed(): pl.pallas_call(feed_kernel, grid_spec=pltpu.PrefetchScalarGridSpec(num_sc...  10.7 us
    pallas_call x7, Pallas kernels, small_call(): pl.pallas_call(kernel, grid=(1,), in_specs=[SMEM_SPEC] + [whole(item.shap...  9.15 us
    sub x3, other arithmetic, adam_update(): weight - step_rate * (mean_hat / (jnp.sqrt(square_hat) + ADAM_EPS) + deca...  4.76 us
  transfers between devices with their start and end apart: 35, of which 20 were waited for; matrix products, arithmetic and copies ran while one was open for 4% of the time, Pallas kernels for 13%

profile of v2, /device:TPU:0, one launch (start us, length us, event | category | flops | bytes accessed | tf_op | source)
XLA Modules:
  0.0 123.7 jit_solution(15061444813781428087)
XLA Ops:
  1.4 0.6 pad_add_fusion.where
  2.0 2.1 %own_payload.1 = (bf16[208,384]{1,0:T(8,128)(2,1)}, bf16[384,384]{1,0:T(8,128)(2,1)}) custom-call(s32[4]{0:T(128)} %pad_add_fusion.where, f32[2,384]{1,0:T(2,128)} %condition.1, bf16[96,1152]{1,0:T(8,128)(2,1)} %own_att.1, bf16[96,384]{1,0:T(8,128)(2,1)} %own_proj.1, bf16[14,96]{1,0:T(8,128)(2,1)} %bias.1, bf16[384,384]{1,0:T(8,128)(2,1)} %own_expand.1, ...), custom_call_target="tpu_custom_call" | custom-call | tf_op jit(solution)/shard_map/own_payload/pallas_call | solution.py:661
  4.0 2.9 %collective-permute-start = (bf16[208,384]{1,0:T(8,128)(2,1)}, bf16[208,384]{1,0:T(8,128)(2,1)S(1)}, u32[]{:S(2)}, u32[]{:S(2)}) collective-permute-start(bf16[208,384]{1,0:T(8,128)(2,1)} %get-tuple-element.79.own), channel_id=1, source_target_pairs={{0,8},{1,17},{2,10},{3,19},{4,12},{5,21},{6,14},{7,23},{8,0},{9,25... | collective-permute-start | bytes 479240 | tf_op jit(solution)/shard_map/ppermute | solution.py:881
  7.0 1.5 %collective-permute-start.1 = (bf16[208,384]{1,0:T(8,128)(2,1)}, bf16[208,384]{1,0:T(8,128)(2,1)S(1)}, u32[]{:S(2)}, u32[]{:S(2)}) collective-permute-start(bf16[208,384]{1,0:T(8,128)(2,1)} %get-tuple-element.79.own), channel_id=1, source_target_pairs={{0,16},{1,9},{2,18},{3,11},{4,20},{5,13},{6,22},{7,15},{8,24},{9,1... | collective-permute-start | bytes 479240 | tf_op jit(solution)/shard_map/ppermute | solution.py:881
  8.5 3.2 %collective-permute-done.first.refs_1_.n1 = bf16[208,384]{1,0:T(8,128)(2,1)S(1)} collective-permute-done((bf16[208,384]{1,0:T(8,128)(2,1)}, bf16[208,384]{1,0:T(8,128)(2,1)S(1)}, u32[]{:S(2)}, u32[]{:S(2)}) %collective-permute-start) | collective-permute-done | bytes 159776 | tf_op jit(solution)/shard_map/ppermute | solution.py:881
  11.7 0.8 collective-permute-done.1.second.refs_2_.n2
  12.5 0.7 copy-done.8
  13.1 1.7 %collective-permute-start.4 = (bf16[384,384]{1,0:T(8,128)(2,1)}, bf16[384,384]{1,0:T(8,128)(2,1)S(1)}, u32[]{:S(2)}, u32[]{:S(2)}) collective-permute-start(bf16[384,384]{1,0:T(8,128)(2,1)} %in_order.1), channel_id=1, source_target_pairs={{0,8},{1,17},{2,10},{3,19},{4,12},{5,21},{6,14},{7,23},{8,0},{9,25... | collective-permute-start | bytes 884744 | tf_op jit(solution)/shard_map/ppermute | solution.py:881
  14.8 0.7 collective-permute-start.2
  15.6 5.1 %collective-permute-done.2.last.n3 = bf16[208,384]{1,0:T(8,128)(2,1)S(1)} collective-permute-done((bf16[208,384]{1,0:T(8,128)(2,1)}, bf16[208,384]{1,0:T(8,128)(2,1)S(1)}, u32[]{:S(2)}, u32[]{:S(2)}) %collective-permute-start.2) | collective-permute-done | bytes 159776 | tf_op jit(solution)/shard_map/ppermute | solution.py:881
  20.6 0.9 copy-done.6
  21.5 0.9 copy-done.9
  22.5 0.9 copy-done.14
  23.4 1.0 modulation_partials.1
  24.3 1.8 %collective-permute-start.3 = (f32[4,2304]{1,0:T(4,128)S(1)}, f32[4,2304]{1,0:T(4,128)S(1)}, u32[]{:S(2)}, u32[]{:S(2)}) collective-permute-start(f32[4,2304]{1,0:T(4,128)S(1)} %get-tuple-element.81), channel_id=1, source_target_pairs={{0,8},{1,17},{2,10},{3,19},{4,12},{5,21},{6,14},{7,23},{8,0},{9,25... | collective-permute-start | bytes 110600 | tf_op jit(solution)/shard_map/ppermute | solution.py:881
  26.2 0.4 collective-permute-start.9
  26.6 2.1 %collective-permute-done.3.arrived = f32[4,2304]{1,0:T(4,128)S(1)} collective-permute-done((f32[4,2304]{1,0:T(4,128)S(1)}, f32[4,2304]{1,0:T(4,128)S(1)}, u32[]{:S(2)}, u32[]{:S(2)}) %collective-permute-start.3) | collective-permute-done | bytes 36896 | tf_op jit(solution)/shard_map/ppermute | solution.py:881
  28.7 0.6 relay.1
  29.2 0.5 collective-permute-start.10
  29.8 0.5 collective-permute-start.7
  30.3 0.8 collective-permute-done.6.f1
  31.1 1.6 %collective-permute-start.5 = (f32[2,2304]{1,0:T(2,128)S(1)}, f32[2,2304]{1,0:T(2,128)S(1)}, u32[]{:S(2)}, u32[]{:S(2)}) collective-permute-start(f32[2,2304]{1,0:T(2,128)S(1)} %get-tuple-element.84), channel_id=1, source_target_pairs={{0,16},{1,9},{2,18},{3,11},{4,20},{5,13},{6,22},{7,15},{8,24},{9,1... | collective-permute-start | bytes 55304 | tf_op jit(solution)/shard_map/ppermute | solution.py:881
  33.2 3.0 %collective-permute-done.10.n3 = bf16[384,384]{1,0:T(8,128)(2,1)S(1)} collective-permute-done((bf16[384,384]{1,0:T(8,128)(2,1)S(1)}, bf16[384,384]{1,0:T(8,128)(2,1)S(1)}, u32[]{:S(2)}, u32[]{:S(2)}) %collective-permute-start.10) | collective-permute-done | bytes 294944 | tf_op jit(solution)/shard_map/ppermute | solution.py:881
  36.5 3.9 %attention_forward.1 = (bf16[2,256,1152]{2,1,0:T(8,128)(2,1)S(1)}, bf16[2,6,256,256]{3,2,1,0:T(8,128)(2,1)S(1)}, bf16[2,256,384]{2,1,0:T(8,128)(2,1)S(1)}, f32[2...) custom-call(s32[4]{0:T(128)S(1)} %copy-done.15, ...), custom_call_target="tpu_custom_call" | custom-call | flops 3000000000 | bytes 6000000 | tf_op jit(solution)/shard_map/attention_forward/pallas_call | solution.py:714
  40.6 10.7 %feed_forward_and_back.1 = (bf16[2,256,384]{2,1,0:T(8,128)(2,1)}, f32[2,256,384]{2,1,0:T(8,128)S(1)}, bf16[4,384,384]{2,1,0:T(8,128)(2,1)S(1)}, bf16[4,384,384]{2,1,0:T(8,128)(2,1)}, f32[16,384]{1,0:T(8,128)S(1)}) custom-call(s32[4]{0:T(128)S(1)} %copy-done.15, bf16[2,256,384]{2,1,0:T(8,128)(2,1)S(1)} %get-tuple-element.86.mixed, ...), custom_call_target="tpu_custom_call" | custom-call | flops 8000000000 | bytes 10000000 | tf_op jit(solution)/shard_map/feed_forward_and_back/pallas_call | solution.py:763
  51.7 4.6 %attention_backward.2 = (bf16[2,256,384]{2,1,0:T(8,128)(2,1)}, f32[384,1152]{1,0:T(8,128)}, f32[384,384]{1,0:T(8,128)S(1)}, f32[32,384]{1,0:T(8,128)S(1)}) custom-call(s32[4]{0:T(128)S(1)} %copy-done.15, bf16[2,256,384]{2,1,0:T(8,128)(2,1)S(1)} %copy-done.20, f32[2,256,384]{2,1,0:T(8,128)S(1)} %get-tuple-element.91.grad_middle_in, ...), custom_call_target="tpu_custom_call" | custom-call | flops 4000000000 | bytes 8000000 | tf_op jit(solution)/shard_map/attention_backward/pallas_call | solution.py:839
  56.6 1.6 %collective-permute-start.17 = (bf16[2,384,384]{2,1,0:T(8,128)(2,1)S(1)}, bf16[2,384,384]{2,1,0:T(8,128)(2,1)S(1)}, u32[]{:S(2)}, u32[]{:S(2)}) collective-permute-start(bf16[2,384,384]{2,1,0:T(8,128)(2,1)S(1)} %get-tuple-element.102.refs_4_), channel_id=1, source_target_pairs={{0,8},{1,17},{2,10},{3,19},{4,12},{5,21},{6,14},{7,23},{8,0},{9,25... | collective-permute-start | bytes 1769480 | tf_op jit(solution)/shard_map/ppermute | solution.py:881
  58.2 6.3 %attention_backward.3 = (bf16[2,256,384]{2,1,0:T(8,128)(2,1)}, bf16[4,192,384]{2,1,0:T(8,128)(2,1)S(1)}, bf16[4,192,384]{2,1,0:T(8,128)(2,1)S(1)}, bf16[32,384]{1,0:T(8,128)(2,1)S(1)}) custom-call(s32[4]{0:T(128)S(1)} %copy-done.15, bf16[2,256,384]{2,1,0:T(8,128)(2,1)S(1)} %copy-done.20, ...), custom_call_target="tpu_custom_call", output_to_operand_aliasing={{0}: (14, {})} | custom-call | flops 4000000000 | bytes 8000000 | tf_op jit(solution)/shard_map/attention_backward/pallas_call | solution.py:839
  64.5 2.1 %collective-permute-done.17.arrived = bf16[2,384,384]{2,1,0:T(8,128)(2,1)S(1)} collective-permute-done((bf16[2,384,384]{2,1,0:T(8,128)(2,1)S(1)}, bf16[2,384,384]{2,1,0:T(8,128)(2,1)S(1)}, u32[]{:S(2)}, u32[]{:S(2)}) %collective-permute-start.17) | collective-permute-done | bytes 589856 | tf_op jit(solution)/shard_map/ppermute | solution.py:881
  66.6 0.5 collective-permute-start.18
  67.3 1.6 %collective-permute-start.16 = (bf16[2,192,384]{2,1,0:T(8,128)(2,1)S(1)}, bf16[2,192,384]{2,1,0:T(8,128)(2,1)S(1)}, u32[]{:S(2)}, u32[]{:S(2)}) collective-permute-start(bf16[2,192,384]{2,1,0:T(8,128)(2,1)S(1)} %get-tuple-element.107), channel_id=1, source_target_pairs={{0,8},{1,17},{2,10},{3,19},{4,12},{5,21},{6,14},{7,23},{8,0},{9,25... | collective-permute-start | bytes 884744 | tf_op jit(solution)/shard_map/ppermute | solution.py:881
  68.9 1.6 %collective-permute-start.19 = (bf16[32,384]{1,0:T(8,128)(2,1)S(1)}, bf16[32,384]{1,0:T(8,128)(2,1)S(1)}, u32[]{:S(2)}, u32[]{:S(2)}) collective-permute-start(bf16[32,384]{1,0:T(8,128)(2,1)S(1)} %get-tuple-element.111.small), channel_id=1, source_target_pairs={{0,2},{1,5},{2,0},{3,7},{4,6},{5,1},{6,4},{7,3},{8,10},{9,13},{10,... | collective-permute-start | bytes 73736 | tf_op jit(solution)/shard_map/ppermute | solution.py:871
  70.5 2.3 %collective-permute-done.19.small_in = bf16[32,384]{1,0:T(8,128)(2,1)S(1)} collective-permute-done((bf16[32,384]{1,0:T(8,128)(2,1)S(1)}, bf16[32,384]{1,0:T(8,128)(2,1)S(1)}, u32[]{:S(2)}, u32[]{:S(2)}) %collective-permute-start.19) | collective-permute-done | bytes 24608 | tf_op jit(solution)/shard_map/ppermute | solution.py:871
  72.7 3.7 %collective-permute-done.18.feed_in = bf16[384,384]{1,0:T(8,128)(2,1)S(1)} collective-permute-done((bf16[384,384]{1,0:T(8,128)(2,1)S(1)}, bf16[384,384]{1,0:T(8,128)(2,1)S(1)}, u32[]{:S(2)}, u32[]{:S(2)}) %collective-permute-start.18) | collective-permute-done | bytes 294944 | tf_op jit(solution)/shard_map/ppermute | solution.py:881
  76.4 0.7 step_1.1
  77.2 0.5 collective-permute-start.20
  77.6 1.6 %collective-permute-start.21 = (bf16[192,384]{1,0:T(8,128)(2,1)S(1)}, bf16[192,384]{1,0:T(8,128)(2,1)S(1)}, u32[]{:S(2)}, u32[]{:S(2)}) collective-permute-start(bf16[192,384]{1,0:T(8,128)(2,1)S(1)} %get-tuple-element.115), channel_id=1, source_target_pairs={{0,2},{1,5},{2,0},{3,7},{4,6},{5,1},{6,4},{7,3},{8,10},{9,13},{10,... | collective-permute-start | bytes 442376 | tf_op jit(solution)/shard_map/ppermute | solution.py:871
  79.2 2.6 %collective-permute-start.22 = (bf16[64,384]{1,0:T(8,128)(2,1)S(1)}, bf16[64,384]{1,0:T(8,128)(2,1)S(1)}, u32[]{:S(2)}, u32[]{:S(2)}) collective-permute-start(bf16[64,384]{1,0:T(8,128)(2,1)S(1)} %get-tuple-element.116.small), channel_id=1, source_target_pairs={{0,4},{1,3},{2,6},{3,1},{4,0},{5,7},{6,2},{7,5},{8,12},{9,11},{10,... | collective-permute-start | bytes 147464 | tf_op jit(solution)/shard_map/ppermute | solution.py:871
  81.8 2.7 %collective-permute-done.22.small_in = bf16[64,384]{1,0:T(8,128)(2,1)S(1)} collective-permute-done((bf16[64,384]{1,0:T(8,128)(2,1)S(1)}, bf16[64,384]{1,0:T(8,128)(2,1)S(1)}, u32[]{:S(2)}, u32[]{:S(2)}) %collective-permute-start.22) | collective-permute-done | bytes 49184 | tf_op jit(solution)/shard_map/ppermute | solution.py:871
  84.5 0.4 collective-permute-done.21.feed_in
  85.0 0.6 step_2.1
  85.6 2.7 %collective-permute-start.24 = (bf16[192,384]{1,0:T(8,128)(2,1)S(1)}, bf16[192,384]{1,0:T(8,128)(2,1)S(1)}, u32[]{:S(2)}, u32[]{:S(2)}) collective-permute-start(bf16[192,384]{1,0:T(8,128)(2,1)S(1)} %get-tuple-element.119.feed_half), channel_id=1, source_target_pairs={{0,4},{1,3},{2,6},{3,1},{4,0},{5,7},{6,2},{7,5},{8,12},{9,11},{10,... | collective-permute-start | bytes 442376 | tf_op jit(solution)/shard_map/ppermute | solution.py:871
  88.3 0.9 collective-permute-start.25
  89.3 1.9 %collective-permute-start.23 = (bf16[96,384]{1,0:T(8,128)(2,1)S(1)}, bf16[96,384]{1,0:T(8,128)(2,1)S(1)}, u32[]{:S(2)}, u32[]{:S(2)}) collective-permute-start(bf16[96,384]{1,0:T(8,128)(2,1)S(1)} %get-tuple-element.118), channel_id=1, source_target_pairs={{0,2},{1,5},{2,0},{3,7},{4,6},{5,1},{6,4},{7,3},{8,10},{9,13},{10,... | collective-permute-start | bytes 221192 | tf_op jit(solution)/shard_map/ppermute | solution.py:871
  91.1 2.5 %collective-permute-done.23.att_in = bf16[96,384]{1,0:T(8,128)(2,1)S(1)} collective-permute-done((bf16[96,384]{1,0:T(8,128)(2,1)S(1)}, bf16[96,384]{1,0:T(8,128)(2,1)S(1)}, u32[]{:S(2)}, u32[]{:S(2)}) %collective-permute-start.23) | collective-permute-done | bytes 73760 | tf_op jit(solution)/shard_map/ppermute | solution.py:871
  93.6 0.8 collective-permute-done.24.feed_in
  94.4 0.6 step_3.1
  95.0 1.7 %collective-permute-start.28 = (bf16[256,384]{1,0:T(8,128)(2,1)S(1)}, bf16[256,384]{1,0:T(8,128)(2,1)S(1)}, u32[]{:S(2)}, u32[]{:S(2)}) collective-permute-start(bf16[256,384]{1,0:T(8,128)(2,1)S(1)} %get-tuple-element.123.small), channel_id=1, source_target_pairs={{0,8},{1,17},{2,10},{3,19},{4,12},{5,21},{6,14},{7,23},{8,0},{9,25... | collective-permute-start | bytes 589832 | tf_op jit(solution)/shard_map/ppermute | solution.py:881
  97.0 3.4 %collective-permute-start.26 = (bf16[96,384]{1,0:T(8,128)(2,1)S(1)}, bf16[96,384]{1,0:T(8,128)(2,1)S(1)}, u32[]{:S(2)}, u32[]{:S(2)}) collective-permute-start(bf16[96,384]{1,0:T(8,128)(2,1)S(1)} %get-tuple-element.121.att_half), channel_id=1, source_target_pairs={{0,4},{1,3},{2,6},{3,1},{4,0},{5,7},{6,2},{7,5},{8,12},{9,11},{10,... | collective-permute-start | bytes 221192 | tf_op jit(solution)/shard_map/ppermute | solution.py:871
  100.4 3.2 %collective-permute-done.26.att_in = bf16[96,384]{1,0:T(8,128)(2,1)S(1)} collective-permute-done((bf16[96,384]{1,0:T(8,128)(2,1)S(1)}, bf16[96,384]{1,0:T(8,128)(2,1)S(1)}, u32[]{:S(2)}, u32[]{:S(2)}) %collective-permute-start.26) | collective-permute-done | bytes 73760 | tf_op jit(solution)/shard_map/ppermute | solution.py:871
  103.5 1.0 collective-permute-done.27.feed_in
  104.5 0.9 step_4.1
  105.7 0.7 collective-permute-start.30
  106.4 2.9 %collective-permute-done.30.cond_in = f32[8,128]{1,0:T(8,128)S(1)} collective-permute-done((f32[8,128]{1,0:T(8,128)S(1)}, f32[8,128]{1,0:T(8,128)S(1)}, u32[]{:S(2)}, u32[]{:S(2)}) %collective-permute-start.30) | collective-permute-done | bytes 4128 | tf_op jit(solution)/shard_map/ppermute | solution.py:881
  109.3 0.4 collective-permute-done.29.att_in
  109.7 0.6 step_5.1
  110.3 1.4 %collective-permute-start.31 = (f32[8,128]{1,0:T(8,128)S(1)}, f32[8,128]{1,0:T(8,128)S(1)}, u32[]{:S(2)}, u32[]{:S(2)}) collective-permute-start(f32[8,128]{1,0:T(8,128)S(1)} %get-tuple-element.127), channel_id=1, source_target_pairs={{0,16},{1,9},{2,18},{3,11},{4,20},{5,13},{6,22},{7,15},{8,24},{9,1... | collective-permute-start | bytes 12296 | tf_op jit(solution)/shard_map/ppermute | solution.py:881
  111.6 0.5 collective-permute-start.32
  112.2 1.8 %collective-permute-done.31 = f32[8,128]{1,0:T(8,128)S(1)} collective-permute-done((f32[8,128]{1,0:T(8,128)S(1)}, f32[8,128]{1,0:T(8,128)S(1)}, u32[]{:S(2)}, u32[]{:S(2)}) %collective-permute-start.31) | collective-permute-done | bytes 4128 | tf_op jit(solution)/shard_map/ppermute | solution.py:881
  114.0 0.7 fusion.14
  114.7 0.8 convert_subtract_fusion.3
  115.8 1.3 %convert_subtract_fusion.2 = (f32[96,1152]{1,0:T(8,128)}, f32[96,1152]{1,0:T(8,128)}, f32[96,1152]{1,0:T(8,128)}) fusion(bf16[96,1152]{1,0:T(8,128)(2,1)S(1)} %copy-done.4, f32[96,384]{1,0:T(8,128)S(1)} %get-tuple-element.152, f32[96,384]{1,0:T(8,128)S(1)} %get-tuple-element.154, f32[96,384]{1,0:T(8,128)S(1)} %get-tuple-element.153, ...), kind=kLoop, calls=%fused_computation.17 | loop fusion | flops 2211840 | bytes 2433024 | tf_op jit(solution)/shard_map/sub | solution.py:55
  117.4 2.6 %convert_subtract_fusion = (f32[384,384]{1,0:T(8,128)}, f32[384,384]{1,0:T(8,128)}, f32[384,384]{1,0:T(8,128)}, f32[384,384]{1,0:T(8,128)}, f32[384,384]{1,0:T(8,128)}, /*index=5*/f32[384,384]{1,0:T(8,128)}) fusion(bf16[384,384]{1,0:T(8,128)(2,1)S(1)} %copy-done.2, bf16[384,384]{1,0:T(8,128)(2,1)S(1)} %collective-permute-done.34, ...), kind=kLoop, calls=%fused_computation.3 | loop fusion | flops 5898240 | bytes 5898241 | tf_op jit(solution)/shard_map/sub | solution.py:55
  120.0 3.7 %modulation_update.1 = (f32[96,2304]{1,0:T(8,128)}, f32[96,2304]{1,0:T(8,128)}, f32[96,2304]{1,0:T(8,128)}, f32[14,96]{1,0:T(8,128)}, f32[14,96]{1,0:T(8,128)}, /*index=5*/f32[14,96]{1,0:T(8,128)}) custom-call(s32[4]{0:T(128)S(1)} %copy-done.15, bf16[512,384]{1,0:T(8,128)(2,1)S(1)} %get-tuple-element.128.near, ...), custom_call_target="tpu_custom_call" | custom-call | tf_op jit(solution)/shard_map/modulation_update/pallas_call | solution.py:661
  (101 shorter events, 3.0 us)
Async XLA Ops:
  0.7 20.0 %copy-start = (bf16[96,2304]{1,0:T(8,128)(2,1)S(1)}, bf16[96,2304]{1,0:T(8,128)(2,1)}, u32[]{:S(2)}) copy-start(bf16[96,2304]{1,0:T(8,128)(2,1)} %weight.5) | copy-start | bytes 1327108
  2.0 18.7 %copy-start.15 = (s32[4]{0:T(128)S(1)}, s32[4]{0:T(128)}, u32[]{:S(2)}) copy-start(s32[4]{0:T(128)} %pad_add_fusion.where) | copy-start | bytes 52
  4.0 7.7 %collective-permute-start = (bf16[208,384]{1,0:T(8,128)(2,1)}, bf16[208,384]{1,0:T(8,128)(2,1)S(1)}, u32[]{:S(2)}, u32[]{:S(2)}) collective-permute-start(bf16[208,384]{1,0:T(8,128)(2,1)} %get-tuple-element.79.own), channel_id=1, source_target_pairs={{0,8},{1,17},{2,10},{3,19},{4,12},{5,21},{6,14},{7,23},{8,0},{9,25... | collective-permute-start | bytes 479240 | tf_op jit(solution)/shard_map/ppermute | solution.py:881
  7.0 5.5 %collective-permute-start.1 = (bf16[208,384]{1,0:T(8,128)(2,1)}, bf16[208,384]{1,0:T(8,128)(2,1)S(1)}, u32[]{:S(2)}, u32[]{:S(2)}) collective-permute-start(bf16[208,384]{1,0:T(8,128)(2,1)} %get-tuple-element.79.own), channel_id=1, source_target_pairs={{0,16},{1,9},{2,18},{3,11},{4,20},{5,13},{6,22},{7,15},{8,24},{9,1... | collective-permute-start | bytes 479240 | tf_op jit(solution)/shard_map/ppermute | solution.py:881
  13.1 23.4 %copy-start.4 = (bf16[96,1152]{1,0:T(8,128)(2,1)S(1)}, bf16[96,1152]{1,0:T(8,128)(2,1)}, u32[]{:S(2)}) copy-start(bf16[96,1152]{1,0:T(8,128)(2,1)} %own_att.1) | copy-start | bytes 663556
  13.1 23.4 %copy-start.13 = (bf16[96,384]{1,0:T(8,128)(2,1)S(1)}, bf16[96,384]{1,0:T(8,128)(2,1)}, u32[]{:S(2)}) copy-start(bf16[96,384]{1,0:T(8,128)(2,1)} %own_proj.1) | copy-start | bytes 221188
  13.1 23.4 %copy-start.20 = (bf16[2,256,384]{2,1,0:T(8,128)(2,1)S(1)}, bf16[2,256,384]{2,1,0:T(8,128)(2,1)}, u32[]{:S(2)}) copy-start(bf16[2,256,384]{2,1,0:T(8,128)(2,1)} %tokens.7) | copy-start | bytes 1179652
  13.1 15.5 %collective-permute-start.4 = (bf16[384,384]{1,0:T(8,128)(2,1)}, bf16[384,384]{1,0:T(8,128)(2,1)S(1)}, u32[]{:S(2)}, u32[]{:S(2)}) collective-permute-start(bf16[384,384]{1,0:T(8,128)(2,1)} %in_order.1), channel_id=1, source_target_pairs={{0,8},{1,17},{2,10},{3,19},{4,12},{5,21},{6,14},{7,23},{8,0},{9,25... | collective-permute-start | bytes 884744 | tf_op jit(solution)/shard_map/ppermute | solution.py:881
  14.8 5.8 %collective-permute-start.2 = (bf16[208,384]{1,0:T(8,128)(2,1)}, bf16[208,384]{1,0:T(8,128)(2,1)S(1)}, u32[]{:S(2)}, u32[]{:S(2)}) collective-permute-start(bf16[208,384]{1,0:T(8,128)(2,1)} %copy-done.5), channel_id=1, source_target_pairs={{0,16},{1,9},{2,18},{3,11},{4,20},{5,13},{6,22},{7,15},{8,24},{9,1... | collective-permute-start | bytes 479240 | tf_op jit(solution)/shard_map/ppermute | solution.py:881
  23.4 6.4 %copy-start.7 = (bf16[208,384]{1,0:T(8,128)(2,1)S(1)}, bf16[208,384]{1,0:T(8,128)(2,1)}, u32[]{:S(2)}) copy-start(bf16[208,384]{1,0:T(8,128)(2,1)} %copy-done.5) | copy-start | bytes 479236
  23.4 6.4 %copy-start.10 = (bf16[208,384]{1,0:T(8,128)(2,1)S(1)}, bf16[208,384]{1,0:T(8,128)(2,1)}, u32[]{:S(2)}) copy-start(bf16[208,384]{1,0:T(8,128)(2,1)} %copy-done.8) | copy-start | bytes 479236
  24.3 4.3 %collective-permute-start.3 = (f32[4,2304]{1,0:T(4,128)S(1)}, f32[4,2304]{1,0:T(4,128)S(1)}, u32[]{:S(2)}, u32[]{:S(2)}) collective-permute-start(f32[4,2304]{1,0:T(4,128)S(1)} %get-tuple-element.81), channel_id=1, source_target_pairs={{0,8},{1,17},{2,10},{3,19},{4,12},{5,21},{6,14},{7,23},{8,0},{9,25... | collective-permute-start | bytes 110600 | tf_op jit(solution)/shard_map/ppermute | solution.py:881
  26.2 6.9 %collective-permute-start.9 = (bf16[384,384]{1,0:T(8,128)(2,1)}, bf16[384,384]{1,0:T(8,128)(2,1)S(1)}, u32[]{:S(2)}, u32[]{:S(2)}) collective-permute-start(bf16[384,384]{1,0:T(8,128)(2,1)} %in_order.1), channel_id=1, source_target_pairs={{0,16},{1,9},{2,18},{3,11},{4,20},{5,13},{6,22},{7,15},{8,24},{9,1... | collective-permute-start | bytes 884744 | tf_op jit(solution)/shard_map/ppermute | solution.py:881
  29.2 7.0 %collective-permute-start.10 = (bf16[384,384]{1,0:T(8,128)(2,1)S(1)}, bf16[384,384]{1,0:T(8,128)(2,1)S(1)}, u32[]{:S(2)}, u32[]{:S(2)}) collective-permute-start(bf16[384,384]{1,0:T(8,128)(2,1)S(1)} %get-tuple-element.89.n1), channel_id=1, source_target_pairs={{0,16},{1,9},{2,18},{3,11},{4,20},{5,13},{6,22},{7,15},{8,24},{9,1... | collective-permute-start | bytes 884744 | tf_op jit(solution)/shard_map/ppermute | solution.py:881
  29.8 1.4 %collective-permute-start.6 = (bf16[208,384]{1,0:T(8,128)(2,1)S(1)}, bf16[208,384]{1,0:T(8,128)(2,1)S(1)}, u32[]{:S(2)}, u32[]{:S(2)}) collective-permute-start(bf16[208,384]{1,0:T(8,128)(2,1)S(1)} %copy-done.7), channel_id=1, source_target_pairs={{0,1},{1,0},{2,3},{3,2},{4,5},{5,4},{6,7},{7,6},{8,9},{9,8},{10,11... | collective-permute-start | bytes 479240 | tf_op jit(solution)/shard_map/ppermute | solution.py:79
  29.8 3.0 %collective-permute-start.7 = (bf16[208,384]{1,0:T(8,128)(2,1)S(1)}, bf16[208,384]{1,0:T(8,128)(2,1)S(1)}, u32[]{:S(2)}, u32[]{:S(2)}) collective-permute-start(bf16[208,384]{1,0:T(8,128)(2,1)S(1)} %copy-done.10), channel_id=1, source_target_pairs={{0,1},{1,0},{2,3},{3,2},{4,5},{5,4},{6,7},{7,6},{8,9},{9,8},{10,11... | collective-permute-start | bytes 479240 | tf_op jit(solution)/shard_map/ppermute | solution.py:79
  30.3 6.2 %collective-permute-start.8 = (bf16[208,384]{1,0:T(8,128)(2,1)S(1)}, bf16[208,384]{1,0:T(8,128)(2,1)S(1)}, u32[]{:S(2)}, u32[]{:S(2)}) collective-permute-start(bf16[208,384]{1,0:T(8,128)(2,1)S(1)} %collective-permute-done.2.last.n3), channel_id=1, source_target_pairs={{0,1},{1,0},{2,3},{3,2},{4,5},{5,4},{6,7},{7,6},{8,9},{9,8},{10,11... | collective-permute-start | bytes 479240 | tf_op jit(solution)/shard_map/ppermute | solution.py:79
  31.1 5.3 %collective-permute-start.5 = (f32[2,2304]{1,0:T(2,128)S(1)}, f32[2,2304]{1,0:T(2,128)S(1)}, u32[]{:S(2)}, u32[]{:S(2)}) collective-permute-start(f32[2,2304]{1,0:T(2,128)S(1)} %get-tuple-element.84), channel_id=1, source_target_pairs={{0,16},{1,9},{2,18},{3,11},{4,20},{5,13},{6,22},{7,15},{8,24},{9,1... | collective-permute-start | bytes 55304 | tf_op jit(solution)/shard_map/ppermute | solution.py:881
  32.7 7.8 %collective-permute-start.11 = (bf16[384,384]{1,0:T(8,128)(2,1)S(1)}, bf16[384,384]{1,0:T(8,128)(2,1)S(1)}, u32[]{:S(2)}, u32[]{:S(2)}) collective-permute-start(bf16[384,384]{1,0:T(8,128)(2,1)S(1)} %get-tuple-element.89.n1), channel_id=1, source_target_pairs={{0,1},{1,0},{2,3},{3,2},{4,5},{5,4},{6,7},{7,6},{8,9},{9,8},{10,11... | collective-permute-start | bytes 884744 | tf_op jit(solution)/shard_map/ppermute | solution.py:79
  33.1 7.4 %collective-permute-start.12 = (bf16[384,384]{1,0:T(8,128)(2,1)S(1)}, bf16[384,384]{1,0:T(8,128)(2,1)S(1)}, u32[]{:S(2)}, u32[]{:S(2)}) collective-permute-start(bf16[384,384]{1,0:T(8,128)(2,1)S(1)} %collective-permute-done.9.n2), channel_id=1, source_target_pairs={{0,1},{1,0},{2,3},{3,2},{4,5},{5,4},{6,7},{7,6},{8,9},{9,8},{10,11... | collective-permute-start | bytes 884744 | tf_op jit(solution)/shard_map/ppermute | solution.py:79
  36.3 4.2 %collective-permute-start.13 = (bf16[384,384]{1,0:T(8,128)(2,1)S(1)}, bf16[384,384]{1,0:T(8,128)(2,1)S(1)}, u32[]{:S(2)}, u32[]{:S(2)}) collective-permute-start(bf16[384,384]{1,0:T(8,128)(2,1)S(1)} %collective-permute-done.10.n3), channel_id=1, source_target_pairs={{0,1},{1,0},{2,3},{3,2},{4,5},{5,4},{6,7},{7,6},{8,9},{9,8},{10,11... | collective-permute-start | bytes 884744 | tf_op jit(solution)/shard_map/ppermute | solution.py:79
  36.5 4.0 %copy-start.1 = (bf16[384,384]{1,0:T(8,128)(2,1)S(1)}, bf16[384,384]{1,0:T(8,128)(2,1)}, u32[]{:S(2)}) copy-start(bf16[384,384]{1,0:T(8,128)(2,1)} %own_expand.1) | copy-start | bytes 884740
  36.5 4.0 %copy-start.2 = (bf16[384,384]{1,0:T(8,128)(2,1)S(1)}, bf16[384,384]{1,0:T(8,128)(2,1)}, u32[]{:S(2)}) copy-start(bf16[384,384]{1,0:T(8,128)(2,1)} %own_contract.1) | copy-start | bytes 884740
  36.5 4.0 %copy-start.19 = (bf16[2,256,384]{2,1,0:T(8,128)(2,1)S(1)}, bf16[2,256,384]{2,1,0:T(8,128)(2,1)}, u32[]{:S(2)}) copy-start(bf16[2,256,384]{2,1,0:T(8,128)(2,1)} %cotangent.1) | copy-start | bytes 1179652
  40.5 11.2 %copy-start.21 = (bf16[2,6,256,256]{3,2,1,0:T(8,128)(2,1)}, bf16[2,6,256,256]{3,2,1,0:T(8,128)(2,1)S(1)}, u32[]{:S(2)}) copy-start(bf16[2,6,256,256]{3,2,1,0:T(8,128)(2,1)S(1)} %get-tuple-element.93.soft_in) | copy-start | bytes 4718596
  40.5 11.2 %copy-start.22 = (bf16[2,256,1152]{2,1,0:T(8,128)(2,1)}, bf16[2,256,1152]{2,1,0:T(8,128)(2,1)S(1)}, u32[]{:S(2)}) copy-start(bf16[2,256,1152]{2,1,0:T(8,128)(2,1)S(1)} %get-tuple-element.92.joined) | copy-start | bytes 3538948
  40.6 11.1 %copy-start.33 = (f32[2,384]{1,0:T(2,128)S(1)}, f32[2,384]{1,0:T(2,128)}, u32[]{:S(2)}) copy-start(f32[2,384]{1,0:T(2,128)} %condition.1) | copy-start | bytes 9220
  51.3 5.0 %copy-start.23 = (f32[2,256,384]{2,1,0:T(8,128)}, f32[2,256,384]{2,1,0:T(8,128)S(1)}, u32[]{:S(2)}) copy-start(f32[2,256,384]{2,1,0:T(8,128)S(1)} %get-tuple-element.91.grad_middle_in) | copy-start | bytes 2359300
  51.3 5.0 %collective-permute-start.14 = (bf16[4,384,384]{2,1,0:T(8,128)(2,1)S(1)}, bf16[4,384,384]{2,1,0:T(8,128)(2,1)S(1)}, u32[]{:S(2)}, u32[]{:S(2)}) collective-permute-start(bf16[4,384,384]{2,1,0:T(8,128)(2,1)S(1)} %get-tuple-element.101), channel_id=1, source_target_pairs={{0,1},{1,0},{2,3},{3,2},{4,5},{5,4},{6,7},{7,6},{8,9},{9,8},{10,11... | collective-permute-start | bytes 3538952 | tf_op jit(solution)/shard_map/ppermute | solution.py:79
  51.7 4.6 %copy-start.3 = (bf16[4,384,384]{2,1,0:T(8,128)(2,1)S(1)}, bf16[4,384,384]{2,1,0:T(8,128)(2,1)}, u32[]{:S(2)}) copy-start(bf16[4,384,384]{2,1,0:T(8,128)(2,1)} %get-tuple-element.100.keep) | copy-start | bytes 3538948
  56.3 1.9 %copy-start.24 = (f32[2,256,384]{2,1,0:T(8,128)S(1)}, f32[2,256,384]{2,1,0:T(8,128)}, u32[]{:S(2)}) copy-start(f32[2,256,384]{2,1,0:T(8,128)} %copy-done.23) | copy-start | bytes 2359300
  56.6 9.9 %collective-permute-start.17 = (bf16[2,384,384]{2,1,0:T(8,128)(2,1)S(1)}, bf16[2,384,384]{2,1,0:T(8,128)(2,1)S(1)}, u32[]{:S(2)}, u32[]{:S(2)}) collective-permute-start(bf16[2,384,384]{2,1,0:T(8,128)(2,1)S(1)} %get-tuple-element.102.refs_4_), channel_id=1, source_target_pairs={{0,8},{1,17},{2,10},{3,19},{4,12},{5,21},{6,14},{7,23},{8,0},{9,25... | collective-permute-start | bytes 1769480 | tf_op jit(solution)/shard_map/ppermute | solution.py:881
  64.4 2.7 %collective-permute-start.15 = (bf16[4,192,384]{2,1,0:T(8,128)(2,1)S(1)}, bf16[4,192,384]{2,1,0:T(8,128)(2,1)S(1)}, u32[]{:S(2)}, u32[]{:S(2)}) collective-permute-start(bf16[4,192,384]{2,1,0:T(8,128)(2,1)S(1)} %get-tuple-element.105), channel_id=1, source_target_pairs={{0,1},{1,0},{2,3},{3,2},{4,5},{5,4},{6,7},{7,6},{8,9},{9,8},{10,11... | collective-permute-start | bytes 1769480 | tf_op jit(solution)/shard_map/ppermute | solution.py:79
  66.6 9.8 %collective-permute-start.18 = (bf16[384,384]{1,0:T(8,128)(2,1)S(1)}, bf16[384,384]{1,0:T(8,128)(2,1)S(1)}, u32[]{:S(2)}, u32[]{:S(2)}) collective-permute-start(bf16[384,384]{1,0:T(8,128)(2,1)S(1)} %bitcast.6), channel_id=1, source_target_pairs={{0,16},{1,9},{2,18},{3,11},{4,20},{5,13},{6,22},{7,15},{8,24},{9,1... | collective-permute-start | bytes 884744 | tf_op jit(solution)/shard_map/ppermute | solution.py:881
  67.3 9.1 %collective-permute-start.16 = (bf16[2,192,384]{2,1,0:T(8,128)(2,1)S(1)}, bf16[2,192,384]{2,1,0:T(8,128)(2,1)S(1)}, u32[]{:S(2)}, u32[]{:S(2)}) collective-permute-start(bf16[2,192,384]{2,1,0:T(8,128)(2,1)S(1)} %get-tuple-element.107), channel_id=1, source_target_pairs={{0,8},{1,17},{2,10},{3,19},{4,12},{5,21},{6,14},{7,23},{8,0},{9,25... | collective-permute-start | bytes 884744 | tf_op jit(solution)/shard_map/ppermute | solution.py:881
  68.9 3.8 %collective-permute-start.19 = (bf16[32,384]{1,0:T(8,128)(2,1)S(1)}, bf16[32,384]{1,0:T(8,128)(2,1)S(1)}, u32[]{:S(2)}, u32[]{:S(2)}) collective-permute-start(bf16[32,384]{1,0:T(8,128)(2,1)S(1)} %get-tuple-element.111.small), channel_id=1, source_target_pairs={{0,2},{1,5},{2,0},{3,7},{4,6},{5,1},{6,4},{7,3},{8,10},{9,13},{10,... | collective-permute-start | bytes 73736 | tf_op jit(solution)/shard_map/ppermute | solution.py:871
  77.2 7.4 %collective-permute-start.20 = (bf16[192,384]{1,0:T(8,128)(2,1)S(1)}, bf16[192,384]{1,0:T(8,128)(2,1)S(1)}, u32[]{:S(2)}, u32[]{:S(2)}) collective-permute-start(bf16[192,384]{1,0:T(8,128)(2,1)S(1)} %get-tuple-element.113), channel_id=1, source_target_pairs={{0,16},{1,9},{2,18},{3,11},{4,20},{5,13},{6,22},{7,15},{8,24},{9,1... | collective-permute-start | bytes 442376 | tf_op jit(solution)/shard_map/ppermute | solution.py:881
  77.6 7.3 %collective-permute-start.21 = (bf16[192,384]{1,0:T(8,128)(2,1)S(1)}, bf16[192,384]{1,0:T(8,128)(2,1)S(1)}, u32[]{:S(2)}, u32[]{:S(2)}) collective-permute-start(bf16[192,384]{1,0:T(8,128)(2,1)S(1)} %get-tuple-element.115), channel_id=1, source_target_pairs={{0,2},{1,5},{2,0},{3,7},{4,6},{5,1},{6,4},{7,3},{8,10},{9,13},{10,... | collective-permute-start | bytes 442376 | tf_op jit(solution)/shard_map/ppermute | solution.py:871
  79.2 5.3 %collective-permute-start.22 = (bf16[64,384]{1,0:T(8,128)(2,1)S(1)}, bf16[64,384]{1,0:T(8,128)(2,1)S(1)}, u32[]{:S(2)}, u32[]{:S(2)}) collective-permute-start(bf16[64,384]{1,0:T(8,128)(2,1)S(1)} %get-tuple-element.116.small), channel_id=1, source_target_pairs={{0,4},{1,3},{2,6},{3,1},{4,0},{5,7},{6,2},{7,5},{8,12},{9,11},{10,... | collective-permute-start | bytes 147464 | tf_op jit(solution)/shard_map/ppermute | solution.py:871
  85.6 8.8 %collective-permute-start.24 = (bf16[192,384]{1,0:T(8,128)(2,1)S(1)}, bf16[192,384]{1,0:T(8,128)(2,1)S(1)}, u32[]{:S(2)}, u32[]{:S(2)}) collective-permute-start(bf16[192,384]{1,0:T(8,128)(2,1)S(1)} %get-tuple-element.119.feed_half), channel_id=1, source_target_pairs={{0,4},{1,3},{2,6},{3,1},{4,0},{5,7},{6,2},{7,5},{8,12},{9,11},{10,... | collective-permute-start | bytes 442376 | tf_op jit(solution)/shard_map/ppermute | solution.py:871
  88.3 5.3 %collective-permute-start.25 = (bf16[128,384]{1,0:T(8,128)(2,1)S(1)}, bf16[128,384]{1,0:T(8,128)(2,1)S(1)}, u32[]{:S(2)}, u32[]{:S(2)}) collective-permute-start(bf16[128,384]{1,0:T(8,128)(2,1)S(1)} %get-tuple-element.120.small), channel_id=1, source_target_pairs={{0,16},{1,9},{2,18},{3,11},{4,20},{5,13},{6,22},{7,15},{8,24},{9,1... | collective-permute-start | bytes 294920 | tf_op jit(solution)/shard_map/ppermute | solution.py:881
  89.3 4.4 %collective-permute-start.23 = (bf16[96,384]{1,0:T(8,128)(2,1)S(1)}, bf16[96,384]{1,0:T(8,128)(2,1)S(1)}, u32[]{:S(2)}, u32[]{:S(2)}) collective-permute-start(bf16[96,384]{1,0:T(8,128)(2,1)S(1)} %get-tuple-element.118), channel_id=1, source_target_pairs={{0,2},{1,5},{2,0},{3,7},{4,6},{5,1},{6,4},{7,3},{8,10},{9,13},{10,... | collective-permute-start | bytes 221192 | tf_op jit(solution)/shard_map/ppermute | solution.py:871
  95.0 9.5 %collective-permute-start.28 = (bf16[256,384]{1,0:T(8,128)(2,1)S(1)}, bf16[256,384]{1,0:T(8,128)(2,1)S(1)}, u32[]{:S(2)}, u32[]{:S(2)}) collective-permute-start(bf16[256,384]{1,0:T(8,128)(2,1)S(1)} %get-tuple-element.123.small), channel_id=1, source_target_pairs={{0,8},{1,17},{2,10},{3,19},{4,12},{5,21},{6,14},{7,23},{8,0},{9,25... | collective-permute-start | bytes 589832 | tf_op jit(solution)/shard_map/ppermute | solution.py:881
  96.7 7.8 %collective-permute-start.27 = (bf16[192,384]{1,0:T(8,128)(2,1)S(1)}, bf16[192,384]{1,0:T(8,128)(2,1)S(1)}, u32[]{:S(2)}, u32[]{:S(2)}) collective-permute-start(bf16[192,384]{1,0:T(8,128)(2,1)S(1)} %get-tuple-element.122.feed_sum), channel_id=1, source_target_pairs={{0,2},{1,5},{2,0},{3,7},{4,6},{5,1},{6,4},{7,3},{8,10},{9,13},{10,... | collective-permute-start | bytes 442376 | tf_op jit(solution)/shard_map/ppermute | solution.py:871
  97.0 17.7 %copy-start.31 = (bf16[96,384]{1,0:T(8,128)(2,1)S(1)}, bf16[96,384]{1,0:T(8,128)(2,1)}, u32[]{:S(2)}) copy-start(bf16[96,384]{1,0:T(8,128)(2,1)} %param.34) | copy-start | bytes 221188
  97.0 17.7 %copy-start.32 = (bf16[96,384]{1,0:T(8,128)(2,1)S(1)}, bf16[96,384]{1,0:T(8,128)(2,1)}, u32[]{:S(2)}) copy-start(bf16[96,384]{1,0:T(8,128)(2,1)} %param.40) | copy-start | bytes 221188
  97.0 6.5 %collective-permute-start.26 = (bf16[96,384]{1,0:T(8,128)(2,1)S(1)}, bf16[96,384]{1,0:T(8,128)(2,1)S(1)}, u32[]{:S(2)}, u32[]{:S(2)}) collective-permute-start(bf16[96,384]{1,0:T(8,128)(2,1)S(1)} %get-tuple-element.121.att_half), channel_id=1, source_target_pairs={{0,4},{1,3},{2,6},{3,1},{4,0},{5,7},{6,2},{7,5},{8,12},{9,11},{10,... | collective-permute-start | bytes 221192 | tf_op jit(solution)/shard_map/ppermute | solution.py:871
  105.3 4.4 %collective-permute-start.29 = (bf16[96,384]{1,0:T(8,128)(2,1)S(1)}, bf16[96,384]{1,0:T(8,128)(2,1)S(1)}, u32[]{:S(2)}, u32[]{:S(2)}) collective-permute-start(bf16[96,384]{1,0:T(8,128)(2,1)S(1)} %get-tuple-element.124.att_sum), channel_id=1, source_target_pairs={{0,2},{1,5},{2,0},{3,7},{4,6},{5,1},{6,4},{7,3},{8,10},{9,13},{10,... | collective-permute-start | bytes 221192 | tf_op jit(solution)/shard_map/ppermute | solution.py:871
  105.7 3.6 %collective-permute-start.30 = (f32[8,128]{1,0:T(8,128)S(1)}, f32[8,128]{1,0:T(8,128)S(1)}, u32[]{:S(2)}, u32[]{:S(2)}) collective-permute-start(f32[8,128]{1,0:T(8,128)S(1)} %get-tuple-element.126), channel_id=1, source_target_pairs={{0,8},{1,17},{2,10},{3,19},{4,12},{5,21},{6,14},{7,23},{8,0},{9,25... | collective-permute-start | bytes 12296 | tf_op jit(solution)/shard_map/ppermute | solution.py:881
  110.3 3.7 %collective-permute-start.31 = (f32[8,128]{1,0:T(8,128)S(1)}, f32[8,128]{1,0:T(8,128)S(1)}, u32[]{:S(2)}, u32[]{:S(2)}) collective-permute-start(f32[8,128]{1,0:T(8,128)S(1)} %get-tuple-element.127), channel_id=1, source_target_pairs={{0,16},{1,9},{2,18},{3,11},{4,20},{5,13},{6,22},{7,15},{8,24},{9,1... | collective-permute-start | bytes 12296 | tf_op jit(solution)/shard_map/ppermute | solution.py:881
  111.6 5.5 %collective-permute-start.34 = (bf16[384,384]{1,0:T(8,128)(2,1)S(1)}, bf16[384,384]{1,0:T(8,128)(2,1)S(1)}, u32[]{:S(2)}, u32[]{:S(2)}) collective-permute-start(bf16[384,384]{1,0:T(8,128)(2,1)S(1)} %get-tuple-element.131), channel_id=1, source_target_pairs={{0,1},{1,0},{2,3},{3,2},{4,5},{5,4},{6,7},{7,6},{8,9},{9,8},{10,11... | collective-permute-start | bytes 884744 | tf_op jit(solution)/shard_map/ppermute | solution.py:79
  111.6 8.4 %collective-permute-start.32 = (bf16[512,384]{1,0:T(8,128)(2,1)S(1)}, bf16[512,384]{1,0:T(8,128)(2,1)S(1)}, u32[]{:S(2)}, u32[]{:S(2)}) collective-permute-start(bf16[512,384]{1,0:T(8,128)(2,1)S(1)} %get-tuple-element.128.near), channel_id=1, source_target_pairs={{0,1},{1,0},{2,3},{3,2},{4,5},{5,4},{6,7},{7,6},{8,9},{9,8},{10,11... | collective-permute-start | bytes 1179656 | tf_op jit(solution)/shard_map/ppermute | solution.py:79
  112.2 2.5 %collective-permute-start.33 = (bf16[192,384]{1,0:T(8,128)(2,1)S(1)}, bf16[192,384]{1,0:T(8,128)(2,1)S(1)}, u32[]{:S(2)}, u32[]{:S(2)}) collective-permute-start(bf16[192,384]{1,0:T(8,128)(2,1)S(1)} %get-tuple-element.130), channel_id=1, source_target_pairs={{0,1},{1,0},{2,3},{3,2},{4,5},{5,4},{6,7},{7,6},{8,9},{9,8},{10,11... | collective-permute-start | bytes 442376 | tf_op jit(solution)/shard_map/ppermute | solution.py:79
  114.6 0.9 copy-start.29
  114.6 1.1 copy-start.30
  115.8 1.3 %copy-start.25 = (bf16[384,384]{1,0:T(8,128)(2,1)S(1)}, bf16[384,384]{1,0:T(8,128)(2,1)}, u32[]{:S(2)}) copy-start(bf16[384,384]{1,0:T(8,128)(2,1)} %param.36) | copy-start | bytes 884740
  115.8 1.4 %copy-start.26 = (bf16[384,384]{1,0:T(8,128)(2,1)S(1)}, bf16[384,384]{1,0:T(8,128)(2,1)}, u32[]{:S(2)}) copy-start(bf16[384,384]{1,0:T(8,128)(2,1)} %param.42) | copy-start | bytes 884740
  115.8 1.4 %copy-start.27 = (bf16[384,384]{1,0:T(8,128)(2,1)S(1)}, bf16[384,384]{1,0:T(8,128)(2,1)}, u32[]{:S(2)}) copy-start(bf16[384,384]{1,0:T(8,128)(2,1)} %param.41) | copy-start | bytes 884740
  115.8 1.6 %copy-start.28 = (bf16[384,384]{1,0:T(8,128)(2,1)S(1)}, bf16[384,384]{1,0:T(8,128)(2,1)}, u32[]{:S(2)}) copy-start(bf16[384,384]{1,0:T(8,128)(2,1)} %param.35) | copy-start | bytes 884740
  117.1 2.9 %copy-start.11 = (bf16[96,2304]{1,0:T(8,128)(2,1)S(1)}, bf16[96,2304]{1,0:T(8,128)(2,1)}, u32[]{:S(2)}) copy-start(bf16[96,2304]{1,0:T(8,128)(2,1)} %mean.1) | copy-start | bytes 1327108
  117.1 2.9 %copy-start.12 = (bf16[96,2304]{1,0:T(8,128)(2,1)S(1)}, bf16[96,2304]{1,0:T(8,128)(2,1)}, u32[]{:S(2)}) copy-start(bf16[96,2304]{1,0:T(8,128)(2,1)} %square.1) | copy-start | bytes 1327108
  117.1 2.9 %copy-start.16 = (bf16[14,96]{1,0:T(8,128)(2,1)S(1)}, bf16[14,96]{1,0:T(8,128)(2,1)}, u32[]{:S(2)}) copy-start(bf16[14,96]{1,0:T(8,128)(2,1)} %bias.1) | copy-start | bytes 8068
  117.1 3.0 %copy-start.17 = (bf16[14,96]{1,0:T(8,128)(2,1)S(1)}, bf16[14,96]{1,0:T(8,128)(2,1)}, u32[]{:S(2)}) copy-start(bf16[14,96]{1,0:T(8,128)(2,1)} %bias_mean.1) | copy-start | bytes 8068
  117.1 3.0 %copy-start.18 = (bf16[14,96]{1,0:T(8,128)(2,1)S(1)}, bf16[14,96]{1,0:T(8,128)(2,1)}, u32[]{:S(2)}) copy-start(bf16[14,96]{1,0:T(8,128)(2,1)} %bias_square.1) | copy-start | bytes 8068
  (5 other events, 4.2 us)

commit v3 on v2

--- a/solution.py
+++ b/solution.py
@@ -49,12 +49,11 @@
 
 def adam_update(weight, gradient, mean_old, square_old, step_rate, decay_flag):
     momentum = BETA_FIRST * mean_old + (1.0 - BETA_FIRST) * gradient
-    variance = BETA_SECOND * square_old + (1.0 - BETA_SECOND) * gradient * gradient
-    mean_hat = momentum / (1.0 - BETA_FIRST**STEP)
-    square_hat = variance / (1.0 - BETA_SECOND**STEP)
-    updated = weight - step_rate * (
-        mean_hat / (jnp.sqrt(square_hat) + ADAM_EPS) + decay_flag * DECAY_RATE * weight
-    )
+    variance = BETA_SECOND * square_old + ((1.0 - BETA_SECOND) * gradient) * gradient
+    root = variance * lax.rsqrt(variance)
+    bottom = root * (1.0 - BETA_SECOND**STEP) ** (-0.5) + ADAM_EPS
+    change = momentum * (step_rate / (1.0 - BETA_FIRST**STEP)) / bottom
+    updated = weight * (1.0 - step_rate * decay_flag * DECAY_RATE) - change
     return (updated, momentum, variance)
 
 
@@ -156,6 +155,15 @@
     return (rank ^ (1 + core), rank ^ (2 - core), rank ^ 3)
 
 
+def own_message(condition, biases):
+    cond = condition[...]
+    active = cond / (1.0 + jnp.exp(-cond))
+    padded = jnp.concatenate(
+        [biases[...].astype(WIDE), jnp.zeros((BIAS_ROWS, D - QUARTER), WIDE)], axis=1
+    )
+    return jnp.concatenate([active, padded], axis=0)
+
+
 def payload_kernel(where, condition, attending, projection, biases, expand, contract, out, part):
     @pl.when(where[1] == 0)
     def _():
@@ -169,20 +177,16 @@
         out[0:QUARTER, :] = attending[:, 2 * D : 3 * D]
         out[QUARTER : 2 * QUARTER, :] = projection[...]
 
-    cond = condition[...]
-    active = cond / (1.0 + jnp.exp(-cond))
-    padded = jnp.concatenate(
-        [biases[...].astype(WIDE), jnp.zeros((BIAS_ROWS, D - QUARTER), WIDE)], axis=1
-    )
-    out[2 * QUARTER :, :] = jnp.concatenate([active, padded], axis=0).astype(LOW)
+    out[2 * QUARTER :, :] = own_message(condition, biases).astype(LOW)
 
 
 def modulation_kernel(
-    where, own, first, second, last, weight, stay, go, bias_out
+    where, condition, biases, first, second, last, weight, stay, go, bias_out
 ):
     rank = where[0]
     owners = (rank,) + neighbours(where)
-    rows = [block[...].astype(WIDE) for block in (own, first, second, last)]
+    rows = [own_message(condition, biases)]
+    rows += [block[...].astype(WIDE) for block in (first, second, last)]
     conds = jnp.concatenate([rows[0][0:2], rows[2][0:2], rows[1][0:2], rows[3][0:2]], axis=0)
     columns = conds[:, :QUARTER]
     for place in range(1, 4):
@@ -288,16 +292,16 @@
 
     def assemble(lows, highs):
         for k, block in zip((1, 2, 3), lows):
-            expands[k] = block[...]
+            expands[k // 2, :, (k % 2) * D : (k % 2 + 1) * D] = block[...]
         for k, block in zip((2, 1, 3), highs):
-            contracts[k] = block[...]
+            contracts[k // 2, (k % 2) * D : (k % 2 + 1) * D, :] = block[...]
 
     slots = [slice(s * SEQ, (s + 1) * SEQ) for s in range(2)]
 
     @pl.when(step == 0)
     def _():
-        expands[0] = own_expand[...]
-        contracts[0] = own_contract[...]
+        expands[0, :, 0:D] = own_expand[...]
+        contracts[0, 0:D, :] = own_contract[...]
 
         @pl.when(core == 0)
         def _():
@@ -324,7 +328,8 @@
         rows_out[...] = jnp.zeros_like(rows_out)
         rows_out[12:13, :] = column_sum(grad_feed[...].astype(WIDE))
 
-    hidden_bias = bias[pl.ds(11 + (rank ^ step), 1), :]
+    owners = (rank ^ (2 * step), rank ^ (2 * step + 1))
+    hidden_bias = jnp.concatenate([bias[pl.ds(11 + owner, 1), :] for owner in owners], axis=1)
     expand, contract = expands[step], contracts[step]
     before = dot_plain(second[...], expand) + hidden_bias
     square = before * before
@@ -340,17 +345,21 @@
     second_term = dot_last(grad_before, expand)
     grad_expand = dot_first(second[...], grad_before).astype(LOW)
     grad_contract = dot_first(activated, grad_feed[...]).astype(LOW)
-    rows_out[pl.ds(8 + (rank ^ step), 1), :] = column_sum(grad_before.astype(WIDE))
+    sums = column_sum(grad_before.astype(WIDE))
+    for k, owner in enumerate(owners):
+        rows_out[pl.ds(8 + owner, 1), :] = sums[:, k * D : (k + 1) * D]
 
     @pl.when(core == 0)
     def _():
-        send_out[0] = grad_contract
-        keep_out[0] = grad_expand
+        for k in range(2):
+            send_out[k] = grad_contract[k * D : (k + 1) * D, :]
+            keep_out[k] = grad_expand[:, k * D : (k + 1) * D]
 
     @pl.when(core != 0)
     def _():
-        send_out[0] = grad_expand
-        keep_out[0] = grad_contract
+        for k in range(2):
+            send_out[k] = grad_expand[:, k * D : (k + 1) * D]
+            keep_out[k] = grad_contract[k * D : (k + 1) * D, :]
 
     @pl.when(step == 0)
     def _():
@@ -362,7 +371,7 @@
         feed[...] += feed_term
         grad_second[...] += second_term
 
-    @pl.when(step == 3)
+    @pl.when(step == 1)
     def _():
         for s, rows in enumerate(slots):
             pieces = mod[s]
@@ -387,11 +396,11 @@
 ):
     rank, core = where[0], where[1]
     if slot == 0:
-        grad_tokens_out, grad_att, grad_proj, rows, grad_joined = refs
+        grad_tokens_out, grad_joined, first_out, branch_out, rows = refs
     else:
-        before_att, before_proj, before_rows, _, _ = refs[:5]
-        grad_tokens_out, send_out, keep_out, rows_out = refs[5:9]
-        grad_joined, grad_att, grad_proj, rows = refs[9:]
+        before_joined, before_first, before_branch, before_rows, _, _ = refs[:6]
+        grad_tokens_out, send_out, keep_out, rows_out = refs[6:10]
+        grad_joined, grad_att, grad_proj, rows = refs[10:]
 
     if slot == 0:
         rows[...] = jnp.zeros_like(rows)
@@ -404,8 +413,12 @@
     grad_middle = grad_middle_in[0]
     grad_branch = (pieces[2:3] * grad_middle).astype(LOW)
     rows[16:17, :] += column_sum(grad_branch.astype(WIDE))
-    proj_term = dot_first(mixed[0], grad_branch)
-    grad_proj[...] = proj_term if slot == 0 else before_proj[...] + proj_term
+    if slot == 0:
+        branch_out[...] = grad_branch
+    else:
+        grad_proj[...] = (
+            dot_first(mixed[0], before_branch[...]) + dot_first(mixed[1], grad_branch)
+        ).astype(LOW)
     grad_mixed = dot_last(grad_branch, proj[...]).astype(LOW)
     first_half = head_mask((SEQ, 128), 0)
     zero = jnp.zeros((SEQ, 128), LOW)
@@ -444,8 +457,15 @@
     rows[15:16, :] += sums[:, 2 * D :]
     normed, inverse = layer_norm_parts(tokens[0].astype(WIDE))
     first_in = (normed * (1.0 + pieces[1:2]) + pieces[0:1]).astype(LOW)
-    att_term = dot_first(first_in, grads)
-    grad_att[...] = att_term if slot == 0 else before_att[...] + att_term
+    if slot == 0:
+        first_out[...] = first_in
+    else:
+        for third in range(3):
+            lanes = slice(third * D, (third + 1) * D)
+            grad_att[:, lanes] = (
+                dot_first(before_first[...], before_joined[:, lanes])
+                + dot_first(first_in, grad_joined[:, lanes])
+            ).astype(LOW)
     grad_first = dot_last(grads, att[...])
     grad_tokens_out[0] = (
         grad_middle + norm_backward(grad_first * (1.0 + pieces[1:2]), normed, inverse)
@@ -465,9 +485,9 @@
     rows_out[...] = rows[...].astype(LOW)
     for k in range(4):
         start = pl.multiple_of((rank ^ k) * QUARTER, 32)
-        block = grad_att[pl.ds(start, QUARTER), :].astype(LOW)
+        block = grad_att[pl.ds(start, QUARTER), :]
         low_part = (block[:, :D], block[:, D : 2 * D])
-        high_part = (block[:, 2 * D :], grad_proj[pl.ds(start, QUARTER), :].astype(LOW))
+        high_part = (block[:, 2 * D :], grad_proj[pl.ds(start, QUARTER), :])
         turned = (0, 2, 1, 3)[k]
 
         @pl.when(core == 0)
@@ -483,8 +503,8 @@
                 send_out[turned, j * QUARTER : (j + 1) * QUARTER, :] = low_part[j]
 
 
-def half_of(where):
-    return (where[2] >> where[1]) & 1
+def half_of(where, which):
+    return (where[2] >> (where[1] ^ which)) & 1
 
 
 def rows_at(index, count):
@@ -495,7 +515,7 @@
     where, att_keep, att_in, feed_keep, feed_in, small, small_in,
     att_stay, att_go, feed_stay, feed_go, small_out, total,
 ):
-    half = half_of(where)
+    half = half_of(where, 0)
     count = D // 2
     att_stay[...] = att_keep[0] + att_in[0].astype(WIDE)
     att_go[...] = (att_keep[1] + att_in[1].astype(WIDE)).astype(LOW)
@@ -507,36 +527,36 @@
 
 
 def step2_kernel(
-    where, att_keep, att_in, feed_keep, feed_in, small, small_in,
-    att_stay, att_go, feed_half, small_out, total,
+    where, att_keep, att_in, feed_keep, feed_in, small, small_in, att_stay, message, small_out, total
 ):
-    half = half_of(where)
+    half = half_of(where, 1)
+    count = D // 2
     total[...] = att_keep[...] + att_in[...].astype(WIDE)
     att_stay[...] = total[rows_at(half, QUARTER), :]
-    att_go[...] = total[rows_at(1 - half, QUARTER), :].astype(LOW)
-    feed_half[...] = (feed_keep[...] + feed_in[...].astype(WIDE)).astype(LOW)
+    message[0:count, :] = (feed_keep[...] + feed_in[...].astype(WIDE)).astype(LOW)
+    message[count:, :] = total[rows_at(1 - half, QUARTER), :].astype(LOW)
     small_out[0 : 2 * SMALL, :] = small[...]
     small_out[2 * SMALL :, :] = small_in[...]
 
 
-def step3_kernel(
-    where, att_keep, att_in, feed_half, feed_in, small, small_in, att_half, feed_sum, small_out
-):
-    att_half[...] = (att_keep[...] + att_in[...].astype(WIDE)).astype(LOW)
-    feed_sum[...] = (feed_half[...].astype(WIDE) + feed_in[...].astype(WIDE)).astype(LOW)
+def step3_kernel(where, att_keep, own, arrived, small, small_in, message, small_out):
+    count = D // 2
+    message[0:count, :] = (
+        own[0:count, :].astype(WIDE) + arrived[0:count, :].astype(WIDE)
+    ).astype(LOW)
+    message[count:, :] = (att_keep[...] + arrived[count:, :].astype(WIDE)).astype(LOW)
     small_out[0 : 4 * SMALL, :] = small[...]
     small_out[4 * SMALL :, :] = small_in[...]
 
 
 def step4_kernel(
-    where, att_half, att_in, feed_sum, feed_in, small, small_in, weight,
-    att_sum, feed_part, small_out, cond_keep, cond_go,
+    where, own, arrived, small, small_in, weight, att_sum, feed_part, small_out, cond_keep, cond_go
 ):
-    half = half_of(where)
+    half = half_of(where, 0)
     count = D // 2
-    feed_part[rows_at(half, count), :] = feed_sum[...]
-    feed_part[rows_at(1 - half, count), :] = feed_in[...]
-    att_sum[...] = (att_half[...].astype(WIDE) + att_in[...].astype(WIDE)).astype(LOW)
+    feed_part[rows_at(half, count), :] = own[0:count, :]
+    feed_part[rows_at(1 - half, count), :] = arrived[0:count, :]
+    att_sum[...] = (own[count:, :].astype(WIDE) + arrived[count:, :].astype(WIDE)).astype(LOW)
     small_out[0 : 8 * SMALL, :] = small[...]
     small_out[8 * SMALL :, :] = small_in[...]
     rows = [
@@ -557,8 +577,8 @@
     cond_go[...] = jnp.concatenate([padded[4:8], blank], axis=0)
 
 
-def step5_kernel(where, att_sum, att_in, cond_keep, cond_in, att_part, cond_go):
-    half = half_of(where)
+def step5_kernel(where, att_sum, att_in, cond_keep, cond_in, _, att_part, cond_go):
+    half = half_of(where, 1)
     att_part[rows_at(half, QUARTER), :] = att_sum[...]
     att_part[rows_at(1 - half, QUARTER), :] = att_in[...]
     blank = jnp.zeros((4, 128), WIDE)
@@ -567,7 +587,7 @@
 
 def modulation_update_kernel(
     where, near, far, weight, mean, square, bias, bias_mean, bias_square,
-    weight_out, mean_out, square_out, bias_out, bias_mean_out, bias_square_out, everyone,
+    weight_out, mean_out, square_out, bias_out, bias_mean_out, bias_square_out, mark, everyone,
 ):
     rank, core, plane = where[0], where[1], where[2]
     for side, source in enumerate((near, far)):
@@ -630,6 +650,7 @@
     bias_out[...] = updated
     bias_mean_out[...] = momentum
     bias_square_out[...] = variance
+    mark[...] = jnp.zeros_like(mark)
 
 
 def split_kernel(keep, arrived, stay, go):
@@ -657,26 +678,29 @@
 ANY_SPEC = pl.BlockSpec(memory_space=pl.ANY)
 
 
-def small_call(kernel, name, outs, where, *operands, scratch=(), params=PARAMS):
+def small_call(kernel, name, outs, where, *operands, scratch=(), after=(), params=PARAMS):
     return pl.pallas_call(
         kernel,
         grid=(1,),
-        in_specs=[SMEM_SPEC] + [whole(item.shape) for item in operands],
+        in_specs=[SMEM_SPEC]
+        + [whole(item.shape) for item in operands]
+        + [ANY_SPEC] * len(after),
         out_specs=[whole(shape) for shape, _ in outs],
         out_shape=[shape_of(*item) for item in outs],
         scratch_shapes=[pltpu.VMEM(*item) for item in scratch],
         compiler_params=params,
         name=name,
-    )(where, *operands)
-
-
-def run_gate(value, *after):
+    )(where, *operands, *after)
+
+
+def run_gate(value, *after, space=ANY_SPEC):
     return pl.pallas_call(
         gate_kernel,
-        in_specs=[ANY_SPEC] * (1 + len(after)),
-        out_specs=ANY_SPEC,
+        in_specs=[space] + [ANY_SPEC] * len(after),
+        out_specs=space,
         out_shape=shape_of(value.shape, value.dtype),
         input_output_aliases={0: 0},
+        compiler_params=pltpu.CompilerParams(vmem_limit_bytes=1024 * 1024),
         name="in_order",
     )(value, *after)
 
@@ -695,18 +719,20 @@
     )(where, keep, arrived, passing)
 
 
-def run_modulation(where, blocks, weight):
+def run_modulation(where, condition, biases, blocks, weight):
     message = pl.BlockSpec((16, D), lambda s: (2 * QUARTER // 16, 0))
     return pl.pallas_call(
         modulation_kernel,
         grid=(1,),
-        in_specs=[SMEM_SPEC] + [message] * 4 + [whole((QUARTER, 6 * D))],
+        in_specs=[SMEM_SPEC, whole((2, D)), whole((BIAS_ROWS, QUARTER))]
+        + [message] * 3
+        + [whole((QUARTER, 6 * D))],
         out_specs=[whole((4, 6 * D))] * 2 + [whole((16, D))],
         out_shape=[shape_of((4, 6 * D), WIDE)] * 2 + [shape_of((16, D), WIDE)],
         compiler_params=PARAMS,
         cost_estimate=pl.CostEstimate(flops=10**7, bytes_accessed=10**6, transcendentals=0),
         name="modulation_partials",
-    )(where, *blocks, weight)
+    )(where, condition, biases, *blocks, weight)
 
 
 def run_attention_forward(where, tokens, stay, arrived, bias, own_att, own_proj, nears, fars):
@@ -751,43 +777,32 @@
 def run_feed(where, mixed, tokens, cotangent, mod, bias, proj, own_expand, own_contract, nears, fars):
     rows = 2 * SEQ
 
-    def turned(step):
-        return jnp.where(step == 1, 2, jnp.where(step == 2, 1, step))
-
-    def keep_place(step, where):
-        return (jnp.where(where[1] == 0, turned(step), step), 0, 0)
-
-    def send_place(step, where):
-        return (jnp.where(where[1] == 0, step, turned(step)), 0, 0)
-
     return pl.pallas_call(
         feed_kernel,
-        grid_spec=pltpu.PrefetchScalarGridSpec(
-            num_scalar_prefetch=1,
-            grid=(4,),
-            in_specs=[whole((2, SEQ, D))] * 3
-            + [whole((2, 6, D)), whole((16, D))]
-            + [whole((D, D))] * 9,
-            out_specs=[
-                whole((2, SEQ, D)),
-                whole((2, SEQ, D)),
-                pl.BlockSpec((1, D, D), send_place),
-                pl.BlockSpec((1, D, D), keep_place),
-                whole((16, D)),
-            ],
-            scratch_shapes=[
-                pltpu.VMEM((4, D, D), LOW),
-                pltpu.VMEM((4, D, D), LOW),
-                pltpu.VMEM((rows, D), WIDE),
-                pltpu.VMEM((rows, D), WIDE),
-                pltpu.VMEM((rows, D), LOW),
-                pltpu.VMEM((rows, D), WIDE),
-                pltpu.VMEM((rows, 128), WIDE),
-                pltpu.VMEM((rows, D), LOW),
-                pltpu.VMEM((rows, D), WIDE),
-                pltpu.VMEM((rows, D), WIDE),
-            ],
-        ),
+        grid=(2,),
+        in_specs=[SMEM_SPEC]
+        + [whole((2, SEQ, D))] * 3
+        + [whole((2, 6, D)), whole((16, D))]
+        + [whole((D, D))] * 9,
+        out_specs=[
+            whole((2, SEQ, D)),
+            whole((2, SEQ, D)),
+            pl.BlockSpec((2, D, D), lambda i: (i, 0, 0)),
+            pl.BlockSpec((2, D, D), lambda i: (i, 0, 0)),
+            whole((16, D)),
+        ],
+        scratch_shapes=[
+            pltpu.VMEM((2, D, 2 * D), LOW),
+            pltpu.VMEM((2, 2 * D, D), LOW),
+            pltpu.VMEM((rows, D), WIDE),
+            pltpu.VMEM((rows, D), WIDE),
+            pltpu.VMEM((rows, D), LOW),
+            pltpu.VMEM((rows, D), WIDE),
+            pltpu.VMEM((rows, 128), WIDE),
+            pltpu.VMEM((rows, D), LOW),
+            pltpu.VMEM((rows, D), WIDE),
+            pltpu.VMEM((rows, D), WIDE),
+        ],
         out_shape=[
             shape_of((2, SEQ, D), LOW),
             shape_of((2, SEQ, D), WIDE),
@@ -809,14 +824,14 @@
     def at_slot(shape):
         return pl.BlockSpec((1,) + shape, lambda i: (slot,) + (0,) * len(shape))
 
-    sums = [((D, 3 * D), WIDE), ((D, D), WIDE), ((SMALL, D), WIDE)]
+    passed = [((SEQ, 3 * D), LOW), ((SEQ, D), LOW), ((SEQ, D), LOW), ((SMALL, D), WIDE)]
     in_specs = [
         SMEM_SPEC,
         at_slot((SEQ, D)),
         at_slot((SEQ, D)),
         at_slot((SEQ, 3 * D)),
         at_slot((HEADS, SEQ, SEQ)),
-        at_slot((SEQ, D)),
+        whole((2, SEQ, D)),
         at_slot((6, D)),
         whole((16, D)),
         whole((2, D)),
@@ -825,17 +840,18 @@
     ]
     out_specs = [at_slot((SEQ, D))]
     out_shape = [shape_of((2, SEQ, D), LOW)]
-    scratch = [pltpu.VMEM((SEQ, 3 * D), LOW)]
+    scratch = []
     aliases = {}
     if slot == 0:
-        out_specs += [whole(shape) for shape, _ in sums]
-        out_shape += [shape_of(*item) for item in sums]
+        out_specs += [whole(shape) for shape, _ in passed]
+        out_shape += [shape_of(*item) for item in passed]
     else:
-        in_specs += [whole(shape) for shape, _ in sums] + [ANY_SPEC, ANY_SPEC]
-        aliases = {14: 0}
+        in_specs += [whole(shape) for shape, _ in passed] + [ANY_SPEC, ANY_SPEC]
+        aliases = {15: 0}
         out_specs += [whole((4, 2 * QUARTER, D))] * 2 + [whole((SMALL, D))]
         out_shape += [shape_of((4, 2 * QUARTER, D), LOW)] * 2 + [shape_of((SMALL, D), LOW)]
-        scratch += [pltpu.VMEM(*item) for item in sums]
+        sums = [((D, 3 * D), LOW), ((D, D), LOW)]
+        scratch = [pltpu.VMEM(*item) for item in (passed[0], *sums, passed[3])]
     return pl.pallas_call(
         functools.partial(attention_backward_kernel, slot),
         grid=(1,),
@@ -850,6 +866,14 @@
         ),
         name="attention_backward",
     )(where, tokens, grad_middle, joined, soft, mixed, mod, feed_rows, cond, att, proj, *earlier)
+
+
+def turn_split_kernel(where, keep, arrived, stay, go):
+    core = where[1]
+    for place, block in enumerate((0, 2 - core)):
+        stay[place] = keep[block].astype(WIDE) + arrived[block].astype(WIDE)
+    for place, block in enumerate((1 + core, 3)):
+        go[place] = (keep[block].astype(WIDE) + arrived[block].astype(WIDE)).astype(LOW)
 
 
 def run_split(keep, arrived):
@@ -931,39 +955,38 @@
         small_rows, swap_plane(small_rows, 0),
         scratch=[((D, D), WIDE)],
     )
-    att_stay, att_go, feed_half, small = small_call(
+    att_stay, message, small = small_call(
         step2_kernel, "step_2",
-        [(quarter, WIDE), (quarter, LOW), (half, LOW), ((4 * SMALL, D), LOW)],
+        [(quarter, WIDE), ((3 * QUARTER, D), LOW), ((4 * SMALL, D), LOW)],
         where, att_stay, swap_pair(att_go, 1), feed_stay, swap_plane(feed_go, 0),
         small, swap_plane(small, 1),
         scratch=[(third, WIDE)],
     )
-    att_half, feed_sum, small = small_call(
+    message, small = small_call(
         step3_kernel, "step_3",
-        [(quarter, LOW), (half, LOW), ((8 * SMALL, D), LOW)],
-        where, att_stay, swap_plane(att_go, 0), feed_half, swap_plane(feed_half, 1),
-        small, swap_pair(small, 1),
+        [((3 * QUARTER, D), LOW), ((8 * SMALL, D), LOW)],
+        where, att_stay, message, swap_plane(message, 1), small, swap_pair(small, 1),
     )
     att_sum, feed_part, small, cond_keep, cond_go = small_call(
         step4_kernel, "step_4",
         [(quarter, LOW), ((D, D), LOW), ((16 * SMALL, D), LOW), ((8, 128), WIDE), ((8, 128), WIDE)],
-        where, att_half, swap_plane(att_half, 1), feed_sum, swap_plane(feed_sum, 0),
-        small, swap_pair(small, 0), stored[0],
+        where, message, swap_plane(message, 0), small, swap_pair(small, 0), stored[0],
+    )
+    shard = [((QUARTER, 6 * D), WIDE)] * 3 + [((BIAS_ROWS, QUARTER), WIDE)] * 3
+    *updates, mark = small_call(
+        modulation_update_kernel, "modulation_update", shard + [((8, 128), WIDE)],
+        where, small, swap_replica(small, 1), stored[0], means[0], squares[0],
+        stored[5], means[5], squares[5],
+        scratch=[((3, 32 * SMALL, 128), WIDE)],
     )
     feed_totals = by_core(core, feed_part, swap_replica(feed_part, 1))
+    feed_updates = update_all(stored, feed_totals, means, squares, (3, 4))
     cond_in = swap_pair(cond_go, 0)
-    feed_updates = update_all(stored, feed_totals, means, squares, (3, 4))
     att_part, cond_go = small_call(
         step5_kernel, "step_5",
         [(third, LOW), ((8, 128), WIDE)],
-        where, att_sum, swap_plane(att_sum, 0), cond_keep, cond_in,
-    )
-    shard = [((QUARTER, 6 * D), WIDE)] * 3 + [((BIAS_ROWS, QUARTER), WIDE)] * 3
-    updates = small_call(
-        modulation_update_kernel, "modulation_update", shard,
-        where, small, swap_replica(small, 1), stored[0], means[0], squares[0],
-        stored[5], means[5], squares[5],
-        scratch=[((3, 32 * SMALL, 128), WIDE)],
+        where, att_sum, swap_plane(att_sum, 1), cond_keep, cond_in,
+        after=(mark,),
     )
     cond_last = swap_pair(cond_go, 1)
     att_totals = by_core(core, att_part, swap_replica(att_part, 1))
@@ -1089,31 +1112,38 @@
         params=pltpu.CompilerParams(vmem_limit_bytes=60 * 1024 * 1024),
     )
     first, second = swap_pair(payload, 0), swap_pair(payload, 1)
-    feed_part = run_gate(feed_part, first, second)
-    nears = (first, second, swap_pair(first, 1))
-    fars = [swap_replica(item, 1) for item in nears]
+    last, first_far = swap_pair(first, 1), swap_replica(first, 1)
+    feed_part = run_gate(
+        feed_part, first_far, second, space=pl.BlockSpec(memory_space=pltpu.HBM)
+    )
+    nears = (first, second, last)
+    fars = [first_far, swap_replica(second, 1), swap_replica(last, 1)]
     feed_first, feed_second = swap_pair(feed_part, 0), swap_pair(feed_part, 1)
-    stay, go, bias = run_modulation(where, (payload,) + nears, modulation)
+    stay, go, bias = run_modulation(where, condition, biases, nears, modulation)
     stay, go, feed_first = run_relay(where, stay, swap_pair(go, 0), feed_first)
     arrived = swap_pair(go, 1)
-    feed_nears = (feed_first, feed_second, swap_pair(feed_first, 1))
-    feed_fars = [swap_replica(item, 1) for item in feed_nears]
-
+    feed_last = swap_pair(feed_first, 1)
     joined, soft, mixed, mod, att, proj = run_attention_forward(
         where, latents, stay, arrived, bias, attending, projection, nears, fars
     )
+    feed_nears = (feed_first, feed_second, run_gate(feed_last, mod))
+    feed_fars = [swap_replica(item, 1) for item in feed_nears]
     out_latents, grad_middle, ffn_send, ffn_keep, feed_rows = run_feed(
         where, mixed, latents, cotangent, mod, bias, proj, expand, contract, feed_nears, feed_fars
     )
     cond_wide = cond_low.astype(WIDE)
-    ffn_stay, ffn_go = run_split(ffn_keep, swap_replica(ffn_send, 1))
-    half_tokens, half_att, half_proj, half_rows = run_attention_backward(
+    two_blocks = (2, model_width, model_width)
+    ffn_stay, ffn_go = small_call(
+        turn_split_kernel, "sum_and_split", [(two_blocks, WIDE), (two_blocks, LOW)],
+        where, ffn_keep, swap_replica(ffn_send, 1),
+    )
+    earlier = run_attention_backward(
         0, where, latents, grad_middle, joined, soft, mixed, mod, feed_rows, cond_wide, att, proj
     )
     ffn_in = swap_pair(ffn_go, 0)
     grad_latents, att_send, att_keep, small_rows = run_attention_backward(
         1, where, latents, grad_middle, joined, soft, mixed, mod, feed_rows, cond_wide, att, proj,
-        (half_att, half_proj, half_rows, half_tokens, ffn_go),
+        (*earlier[1:], earlier[0], ffn_go),
     )
     tail = tail_in_step if lax.axis_size("replica") == 8 else tail_in_turn
     grad_condition, results = tail(

time: 124 us -> 118 us (0.952)
  waiting for transfers between devices: 39.2 us -> 32.9 us
  starting transfers between devices: 36 us -> 37.9 us
    ppermute x8 -> x6, waiting for transfers between devices: 13.2 us -> 6.59 us  [swap_plane(): return lax.ppermute(value, 'replica', pairs)]
    ppermute x8 -> x6, starting transfers between devices: 14.3 us -> 15.9 us  [swap_plane(): return lax.ppermute(value, 'replica', pairs)]
    ppermute x11, waiting for transfers between devices: 0.83 us -> 2.23 us  [swap_replica(): lax.ppermute(value, 'replica', [(i, i ^ k) for i in range(lax.axis_size('...]
    unnamed x68 -> x54, local copies, waits for them, and re-layouts: 3.95 us -> 2.94 us
    pallas_call x3 -> x4, Pallas kernels: 11.7 us -> 10.8 us  [the longest x1 9.83 us: run_feed(): pl.pallas_call(feed_kernel, grid=(2,), in_specs=[SMEM_SPEC] + [whole((2,...]
    pallas_call x7 -> x8, Pallas kernels: 9.15 us -> 9.78 us  [small_call(): pl.pallas_call(kernel, grid=(1,), in_specs=[SMEM_SPEC] + [whole(item.shap...]
  transfers between devices with their start and end apart: 35 -> 33, of which waited for: 20 -> 12; matrix products, arithmetic and copies ran while one was open for 4% -> 3% of each run, Pallas kernels for 13% -> 17%
where the time goes in v3:
time: 118 us
  starting transfers between devices  37.9 us (32%)
  Pallas kernels  35.9 us (30%)
  waiting for transfers between devices  32.9 us (28%)
  other arithmetic  6.63 us (6%)
  local copies, waits for them, and re-layouts  2.96 us (3%)
  between operations  1.74 us (1%)
    ppermute x16, waiting for transfers between devices, swap_pair(): return lax.ppermute(value, ('group', 'replica'), pairs)  24 us
    ppermute x16, starting transfers between devices, swap_pair(): return lax.ppermute(value, ('group', 'replica'), pairs)  20.4 us
    ppermute x6, starting transfers between devices, swap_plane(): return lax.ppermute(value, 'replica', pairs)  15.9 us
    pallas_call x2, Pallas kernels, run_attention_backward(): pl.pallas_call(functools.partial(attention_backward_kernel, slot), grid=(...  10.5 us
    pallas_call x1, Pallas kernels, run_feed(): pl.pallas_call(feed_kernel, grid=(2,), in_specs=[SMEM_SPEC] + [whole((2,...  9.83 us
    pallas_call x8, Pallas kernels, small_call(): pl.pallas_call(kernel, grid=(1,), in_specs=[SMEM_SPEC] + [whole(item.shap...  9.78 us
    ppermute x6, waiting for transfers between devices, swap_plane(): return lax.ppermute(value, 'replica', pairs)  6.59 us
    sub x3, other arithmetic, adam_update(): updated = weight * (1.0 - step_rate * decay_flag * DECAY_RATE) - change  5.31 us
  transfers between devices with their start and end apart: 33, of which 12 were waited for; matrix products, arithmetic and copies ran while one was open for 3% of the time, Pallas kernels for 17%

profile of v3, /device:TPU:0, one launch (start us, length us, event | category | flops | bytes accessed | tf_op | source)
XLA Modules:
  0.0 118.0 jit_solution(8600947018313678253)
XLA Ops:
  1.4 0.6 pad_add_fusion.where
  2.0 2.1 %own_payload.1 = (bf16[208,384]{1,0:T(8,128)(2,1)}, bf16[384,384]{1,0:T(8,128)(2,1)}) custom-call(s32[4]{0:T(128)} %pad_add_fusion.where, f32[2,384]{1,0:T(2,128)} %condition.3, bf16[96,1152]{1,0:T(8,128)(2,1)} %own_att.1, bf16[96,384]{1,0:T(8,128)(2,1)} %own_proj.1, bf16[14,96]{1,0:T(8,128)(2,1)} %bias.1, bf16[384,384]{1,0:T(8,128)(2,1)} %own_expand.1, ...), custom_call_target="tpu_custom_call" | custom-call | tf_op jit(solution)/shard_map/own_payload/pallas_call | solution.py:682
  4.1 2.9 %collective-permute-start = (bf16[208,384]{1,0:T(8,128)(2,1)}, bf16[208,384]{1,0:T(8,128)(2,1)S(1)}, u32[]{:S(2)}, u32[]{:S(2)}) collective-permute-start(bf16[208,384]{1,0:T(8,128)(2,1)} %get-tuple-element.79), channel_id=1, source_target_pairs={{0,8},{1,17},{2,10},{3,19},{4,12},{5,21},{6,14},{7,23},{8,0},{9,25... | collective-permute-start | bytes 479240 | tf_op jit(solution)/shard_map/ppermute | solution.py:905
  7.0 1.5 %collective-permute-start.1 = (bf16[208,384]{1,0:T(8,128)(2,1)}, bf16[208,384]{1,0:T(8,128)(2,1)S(1)}, u32[]{:S(2)}, u32[]{:S(2)}) collective-permute-start(bf16[208,384]{1,0:T(8,128)(2,1)} %get-tuple-element.79), channel_id=1, source_target_pairs={{0,16},{1,9},{2,18},{3,11},{4,20},{5,13},{6,22},{7,15},{8,24},{9,1... | collective-permute-start | bytes 479240 | tf_op jit(solution)/shard_map/ppermute | solution.py:905
  8.6 3.2 %collective-permute-done.first.n1 = bf16[208,384]{1,0:T(8,128)(2,1)S(1)} collective-permute-done((bf16[208,384]{1,0:T(8,128)(2,1)}, bf16[208,384]{1,0:T(8,128)(2,1)S(1)}, u32[]{:S(2)}, u32[]{:S(2)}) %collective-permute-start) | collective-permute-done | bytes 159776 | tf_op jit(solution)/shard_map/ppermute | solution.py:905
  11.8 1.5 %collective-permute-start.2 = (bf16[208,384]{1,0:T(8,128)(2,1)S(1)}, bf16[208,384]{1,0:T(8,128)(2,1)S(1)}, u32[]{:S(2)}, u32[]{:S(2)}) collective-permute-start(bf16[208,384]{1,0:T(8,128)(2,1)S(1)} %collective-permute-done.first.n1), channel_id=1, source_target_pairs={{0,16},{1,9},{2,18},{3,11},{4,20},{5,13},{6,22},{7,15},{8,24},{9,1... | collective-permute-start | bytes 479240 | tf_op jit(solution)/shard_map/ppermute | solution.py:905
  13.2 1.0 copy-done.7
  14.2 0.7 copy-done.8
  14.9 2.3 %collective-permute-start.5 = (bf16[384,384]{1,0:T(8,128)(2,1)}, bf16[384,384]{1,0:T(8,128)(2,1)S(1)}, u32[]{:S(2)}, u32[]{:S(2)}) collective-permute-start(bf16[384,384]{1,0:T(8,128)(2,1)} %copy-done.8), channel_id=1, source_target_pairs={{0,8},{1,17},{2,10},{3,19},{4,12},{5,21},{6,14},{7,23},{8,0},{9,25... | collective-permute-start | bytes 884744 | tf_op jit(solution)/shard_map/ppermute | solution.py:905
  17.2 0.7 collective-permute-start.9
  17.9 0.5 collective-permute-start.8
  18.4 1.0 modulation_partials.1
  19.4 1.1 collective-permute-start.3
  20.5 5.2 %collective-permute-done.3.arrived = f32[4,2304]{1,0:T(4,128)S(1)} collective-permute-done((f32[4,2304]{1,0:T(4,128)S(1)}, f32[4,2304]{1,0:T(4,128)S(1)}, u32[]{:S(2)}, u32[]{:S(2)}) %collective-permute-start.3) | collective-permute-done | bytes 36896 | tf_op jit(solution)/shard_map/ppermute | solution.py:905
  25.7 0.6 relay.1
  26.2 1.1 collective-permute-start.6
  27.3 1.0 collective-permute-start.10
  28.3 0.5 collective-permute-start.12
  28.8 1.2 %collective-permute-done.6.arrived = f32[2,2304]{1,0:T(2,128)S(1)} collective-permute-done((f32[2,2304]{1,0:T(2,128)S(1)}, f32[2,2304]{1,0:T(2,128)S(1)}, u32[]{:S(2)}, u32[]{:S(2)}) %collective-permute-start.6) | collective-permute-done | bytes 18464 | tf_op jit(solution)/shard_map/ppermute | solution.py:905
  30.1 0.0 copy-start.1
  30.1 3.9 %attention_forward.1 = (bf16[2,256,1152]{2,1,0:T(8,128)(2,1)S(1)}, bf16[2,6,256,256]{3,2,1,0:T(8,128)(2,1)S(1)}, bf16[2,256,384]{2,1,0:T(8,128)(2,1)S(1)}, f32[2...) custom-call(s32[4]{0:T(128)S(1)} %copy-done.10, ...), custom_call_target="tpu_custom_call" | custom-call | flops 3000000000 | bytes 6000000 | tf_op jit(solution)/shard_map/attention_forward/pallas_call | solution.py:740
  34.0 1.1 copy-done.17
  35.2 1.6 %collective-permute-done.13.f3 = bf16[384,384]{1,0:T(8,128)(2,1)S(1)} collective-permute-done((bf16[384,384]{1,0:T(8,128)(2,1)S(1)}, bf16[384,384]{1,0:T(8,128)(2,1)S(1)}, u32[]{:S(2)}, u32[]{:S(2)}) %collective-permute-start.13) | collective-permute-done | bytes 294944 | tf_op jit(solution)/shard_map/ppermute | solution.py:78
  36.8 9.8 %feed_forward_and_back.1 = (bf16[2,256,384]{2,1,0:T(8,128)(2,1)}, f32[2,256,384]{2,1,0:T(8,128)S(1)}, bf16[4,384,384]{2,1,0:T(8,128)(2,1)S(1)}, bf16[4,384,384]{2,1,0:T(8,128)(2,1)}, f32[16,384]{1,0:T(8,128)S(1)}) custom-call(s32[4]{0:T(128)S(1)} %copy-done.10, bf16[2,256,384]{2,1,0:T(8,128)(2,1)S(1)} %get-tuple-element.86.mixed, ...), custom_call_target="tpu_custom_call" | custom-call | flops 8000000000 | bytes 10000000 | tf_op jit(solution)/shard_map/feed_forward_and_back/pallas_call | solution.py:780
  46.6 0.1 collective-permute-start.14
  46.8 4.7 %attention_backward.2 = (bf16[2,256,384]{2,1,0:T(8,128)(2,1)}, bf16[256,1152]{1,0:T(8,128)(2,1)S(1)}, bf16[256,384]{1,0:T(8,128)(2,1)S(1)}, bf16[256,384]{1,0:T(8,128)(2,1)S(1)}, f32[32,384]{1,0:T(8,128)S(1)}) custom-call(s32[4]{0:T(128)S(1)} %copy-done.10, bf16[2,256,384]{2,1,0:T(8,128)(2,1)S(1)} %copy-done.16, ...), custom_call_target="tpu_custom_call" | custom-call | flops 4000000000 | bytes 8000000 | tf_op jit(solution)/shard_map/attention_backward/pallas_call | solution.py:855
  51.5 0.8 sum_and_split.3
  52.3 1.7 %collective-permute-start.17 = (bf16[2,384,384]{2,1,0:T(8,128)(2,1)S(1)}, bf16[2,384,384]{2,1,0:T(8,128)(2,1)S(1)}, u32[]{:S(2)}, u32[]{:S(2)}) collective-permute-start(bf16[2,384,384]{2,1,0:T(8,128)(2,1)S(1)} %get-tuple-element.103.refs_5_), channel_id=1, source_target_pairs={{0,8},{1,17},{2,10},{3,19},{4,12},{5,21},{6,14},{7,23},{8,0},{9,25... | collective-permute-start | bytes 1769480 | tf_op jit(solution)/shard_map/ppermute | solution.py:905
  54.0 5.8 %attention_backward.3 = (bf16[2,256,384]{2,1,0:T(8,128)(2,1)}, bf16[4,192,384]{2,1,0:T(8,128)(2,1)S(1)}, bf16[4,192,384]{2,1,0:T(8,128)(2,1)S(1)}, bf16[32,384]{1,0:T(8,128)(2,1)S(1)}) custom-call(s32[4]{0:T(128)S(1)} %copy-done.10, bf16[2,256,384]{2,1,0:T(8,128)(2,1)S(1)} %copy-done.16, ...), custom_call_target="tpu_custom_call", output_to_operand_aliasing={{0}: (15, {})} | custom-call | flops 4000000000 | bytes 8000000 | tf_op jit(solution)/shard_map/attention_backward/pallas_call | solution.py:855
  59.8 2.4 %collective-permute-done.17.arrived = bf16[2,384,384]{2,1,0:T(8,128)(2,1)S(1)} collective-permute-done((bf16[2,384,384]{2,1,0:T(8,128)(2,1)S(1)}, bf16[2,384,384]{2,1,0:T(8,128)(2,1)S(1)}, u32[]{:S(2)}, u32[]{:S(2)}) %collective-permute-start.17) | collective-permute-done | bytes 589856 | tf_op jit(solution)/shard_map/ppermute | solution.py:905
  62.3 0.1 sum_and_split.5
  62.4 1.1 collective-permute-start.18
  63.4 0.1 sum_and_split.4
  63.6 1.8 %collective-permute-start.16 = (bf16[2,192,384]{2,1,0:T(8,128)(2,1)S(1)}, bf16[2,192,384]{2,1,0:T(8,128)(2,1)S(1)}, u32[]{:S(2)}, u32[]{:S(2)}) collective-permute-start(bf16[2,192,384]{2,1,0:T(8,128)(2,1)S(1)} %get-tuple-element.108), channel_id=1, source_target_pairs={{0,8},{1,17},{2,10},{3,19},{4,12},{5,21},{6,14},{7,23},{8,0},{9,25... | collective-permute-start | bytes 884744 | tf_op jit(solution)/shard_map/ppermute | solution.py:905
  65.4 1.6 %collective-permute-start.19 = (bf16[32,384]{1,0:T(8,128)(2,1)S(1)}, bf16[32,384]{1,0:T(8,128)(2,1)S(1)}, u32[]{:S(2)}, u32[]{:S(2)}) collective-permute-start(bf16[32,384]{1,0:T(8,128)(2,1)S(1)} %get-tuple-element.112.small), channel_id=1, source_target_pairs={{0,2},{1,5},{2,0},{3,7},{4,6},{5,1},{6,4},{7,3},{8,10},{9,13},{10,... | collective-permute-start | bytes 73736 | tf_op jit(solution)/shard_map/ppermute | solution.py:895
  66.9 2.2 %collective-permute-done.19.small_in = bf16[32,384]{1,0:T(8,128)(2,1)S(1)} collective-permute-done((bf16[32,384]{1,0:T(8,128)(2,1)S(1)}, bf16[32,384]{1,0:T(8,128)(2,1)S(1)}, u32[]{:S(2)}, u32[]{:S(2)}) %collective-permute-start.19) | collective-permute-done | bytes 24608 | tf_op jit(solution)/shard_map/ppermute | solution.py:895
  69.2 3.0 %collective-permute-done.18.feed_in = bf16[384,384]{1,0:T(8,128)(2,1)S(1)} collective-permute-done((bf16[384,384]{1,0:T(8,128)(2,1)S(1)}, bf16[384,384]{1,0:T(8,128)(2,1)S(1)}, u32[]{:S(2)}, u32[]{:S(2)}) %collective-permute-start.18) | collective-permute-done | bytes 294944 | tf_op jit(solution)/shard_map/ppermute | solution.py:905
  72.2 0.7 step_1.1
  72.9 1.0 collective-permute-start.20
  73.9 2.0 %collective-permute-start.21 = (bf16[192,384]{1,0:T(8,128)(2,1)S(1)}, bf16[192,384]{1,0:T(8,128)(2,1)S(1)}, u32[]{:S(2)}, u32[]{:S(2)}) collective-permute-start(bf16[192,384]{1,0:T(8,128)(2,1)S(1)} %get-tuple-element.116), channel_id=1, source_target_pairs={{0,2},{1,5},{2,0},{3,7},{4,6},{5,1},{6,4},{7,3},{8,10},{9,13},{10,... | collective-permute-start | bytes 442376 | tf_op jit(solution)/shard_map/ppermute | solution.py:895
  75.9 2.6 %collective-permute-start.22 = (bf16[64,384]{1,0:T(8,128)(2,1)S(1)}, bf16[64,384]{1,0:T(8,128)(2,1)S(1)}, u32[]{:S(2)}, u32[]{:S(2)}) collective-permute-start(bf16[64,384]{1,0:T(8,128)(2,1)S(1)} %get-tuple-element.117.small), channel_id=1, source_target_pairs={{0,4},{1,3},{2,6},{3,1},{4,0},{5,7},{6,2},{7,5},{8,12},{9,11},{10,... | collective-permute-start | bytes 147464 | tf_op jit(solution)/shard_map/ppermute | solution.py:895
  78.5 2.4 %collective-permute-done.22.small_in = bf16[64,384]{1,0:T(8,128)(2,1)S(1)} collective-permute-done((bf16[64,384]{1,0:T(8,128)(2,1)S(1)}, bf16[64,384]{1,0:T(8,128)(2,1)S(1)}, u32[]{:S(2)}, u32[]{:S(2)}) %collective-permute-start.22) | collective-permute-done | bytes 49184 | tf_op jit(solution)/shard_map/ppermute | solution.py:895
  80.9 0.6 step_2.1
  81.6 0.0 copy-start.5
  81.6 0.0 copy-start.6
  81.6 2.7 %collective-permute-start.23 = (bf16[288,384]{1,0:T(8,128)(2,1)S(1)}, bf16[288,384]{1,0:T(8,128)(2,1)S(1)}, u32[]{:S(2)}, u32[]{:S(2)}) collective-permute-start(bf16[288,384]{1,0:T(8,128)(2,1)S(1)} %get-tuple-element.119.own), channel_id=1, source_target_pairs={{0,4},{1,3},{2,6},{3,1},{4,0},{5,7},{6,2},{7,5},{8,12},{9,11},{10,... | collective-permute-start | bytes 663560 | tf_op jit(solution)/shard_map/ppermute | solution.py:895
  84.3 1.3 %collective-permute-start.24 = (bf16[128,384]{1,0:T(8,128)(2,1)S(1)}, bf16[128,384]{1,0:T(8,128)(2,1)S(1)}, u32[]{:S(2)}, u32[]{:S(2)}) collective-permute-start(bf16[128,384]{1,0:T(8,128)(2,1)S(1)} %get-tuple-element.120.small), channel_id=1, source_target_pairs={{0,16},{1,9},{2,18},{3,11},{4,20},{5,13},{6,22},{7,15},{8,24},{9,1... | collective-permute-start | bytes 294920 | tf_op jit(solution)/shard_map/ppermute | solution.py:905
  85.6 3.3 %collective-permute-done.24.small_in = bf16[128,384]{1,0:T(8,128)(2,1)S(1)} collective-permute-done((bf16[128,384]{1,0:T(8,128)(2,1)S(1)}, bf16[128,384]{1,0:T(8,128)(2,1)S(1)}, u32[]{:S(2)}, u32[]{:S(2)}) %collective-permute-start.24) | collective-permute-done | bytes 98336 | tf_op jit(solution)/shard_map/ppermute | solution.py:905
  88.9 1.9 %collective-permute-done.23.arrived = bf16[288,384]{1,0:T(8,128)(2,1)S(1)} collective-permute-done((bf16[288,384]{1,0:T(8,128)(2,1)S(1)}, bf16[288,384]{1,0:T(8,128)(2,1)S(1)}, u32[]{:S(2)}, u32[]{:S(2)}) %collective-permute-start.23) | collective-permute-done | bytes 221216 | tf_op jit(solution)/shard_map/ppermute | solution.py:895
  90.9 0.6 step_3.1
  91.5 3.4 %collective-permute-start.25 = (bf16[288,384]{1,0:T(8,128)(2,1)S(1)}, bf16[288,384]{1,0:T(8,128)(2,1)S(1)}, u32[]{:S(2)}, u32[]{:S(2)}) collective-permute-start(bf16[288,384]{1,0:T(8,128)(2,1)S(1)} %get-tuple-element.121.own), channel_id=1, source_target_pairs={{0,2},{1,5},{2,0},{3,7},{4,6},{5,1},{6,4},{7,3},{8,10},{9,13},{10,... | collective-permute-start | bytes 663560 | tf_op jit(solution)/shard_map/ppermute | solution.py:895
  94.9 5.7 %collective-permute-done.26.small_in = bf16[256,384]{1,0:T(8,128)(2,1)S(1)} collective-permute-done((bf16[256,384]{1,0:T(8,128)(2,1)S(1)}, bf16[256,384]{1,0:T(8,128)(2,1)S(1)}, u32[]{:S(2)}, u32[]{:S(2)}) %collective-permute-start.26) | collective-permute-done | bytes 196640 | tf_op jit(solution)/shard_map/ppermute | solution.py:905
  100.6 0.9 step_4.1
  101.5 0.5 collective-permute-start.32
  102.0 3.5 %collective-permute-start.27 = (bf16[96,384]{1,0:T(8,128)(2,1)S(1)}, bf16[96,384]{1,0:T(8,128)(2,1)S(1)}, u32[]{:S(2)}, u32[]{:S(2)}) collective-permute-start(bf16[96,384]{1,0:T(8,128)(2,1)S(1)} %get-tuple-element.123.att_sum), channel_id=1, source_target_pairs={{0,4},{1,3},{2,6},{3,1},{4,0},{5,7},{6,2},{7,5},{8,12},{9,11},{10,... | collective-permute-start | bytes 221192 | tf_op jit(solution)/shard_map/ppermute | solution.py:895
  105.6 3.5 %modulation_update.1 = (f32[96,2304]{1,0:T(8,128)}, f32[96,2304]{1,0:T(8,128)}, f32[96,2304]{1,0:T(8,128)}, f32[14,96]{1,0:T(8,128)}, f32[14,96]{1,0:T(8,128)}, /*index=5*/f32[14,96]{1,0:T(8,128)}, f32[8,128]{1,0:T(8,128)S(1)}) custom-call(s32[4]{0:T(128)S(1)} %copy-done.10, bf16[512,384]{1,0:T(8,128)(2,1)S(1)} %get-tuple-element.126.near, ...), custom_call_target="tpu_custom_call" | custom-call | tf_op jit(solution)/shard_map/modulation_update/pallas_call | solution.py:682
  109.1 0.0 collective-permute-done.28.cond_in
  109.1 0.6 step_5.1
  109.7 1.4 %collective-permute-start.30 = (f32[8,128]{1,0:T(8,128)S(1)}, f32[8,128]{1,0:T(8,128)S(1)}, u32[]{:S(2)}, u32[]{:S(2)}) collective-permute-start(f32[8,128]{1,0:T(8,128)S(1)} %get-tuple-element.128), channel_id=1, source_target_pairs={{0,16},{1,9},{2,18},{3,11},{4,20},{5,13},{6,22},{7,15},{8,24},{9,1... | collective-permute-start | bytes 12296 | tf_op jit(solution)/shard_map/ppermute | solution.py:905
  111.2 3.3 %fusion.11 = (f32[384,384]{1,0:T(8,128)}, f32[384,384]{1,0:T(8,128)}, f32[384,384]{1,0:T(8,128)}, f32[384,384]{1,0:T(8,128)}, f32[384,384]{1,0:T(8,128)}, /*index=5*/f32[384,384]{1,0:T(8,128)}) fusion(bf16[384,384]{1,0:T(8,128)(2,1)S(1)} %copy-done.2, bf16[384,384]{1,0:T(8,128)(2,1)} %collective-permute-done.32, bf16[384,384]{1,0:T(8,128)(2,1)S(1)} %get-tuple-element.131, ...), kind=kLoop, calls=%fused_computation.19 | loop fusion | flops 5603328 | bytes 5898241 | tf_op jit(solution)/shard_map/sub | solution.py:56
  114.5 0.7 fusion.22
  115.2 0.7 collective-permute-done.31
  115.9 0.8 fusion.21
  116.8 1.2 %fusion.16 = (f32[96,1152]{1,0:T(8,128)}, f32[96,1152]{1,0:T(8,128)}, f32[96,1152]{1,0:T(8,128)}) fusion(bf16[96,1152]{1,0:T(8,128)(2,1)S(1)} %copy-done.4, f32[96,384]{1,0:T(8,128)S(1)} %get-tuple-element.152, f32[96,384]{1,0:T(8,128)S(1)} %get-tuple-element.154, f32[96,384]{1,0:T(8,128)S(1)} %get-tuple-element.153, bf16[96,1152]{1,0:T(8,128)(2,1)S(1)} %copy-done.23, ...), kind=kLoop, calls=%fused_computation.24 | loop fusion | flops 2101248 | bytes 2433024 | tf_op jit(solution)/shard_map/sub | solution.py:56
  (84 shorter events, 0.3 us)
Async XLA Ops:
  0.7 17.8 %copy-start.11 = (f32[2,384]{1,0:T(2,128)S(1)}, f32[2,384]{1,0:T(2,128)}, u32[]{:S(2)}) copy-start(f32[2,384]{1,0:T(2,128)} %condition.3) | copy-start | bytes 9220
  0.7 17.8 %copy-start.12 = (bf16[14,96]{1,0:T(8,128)(2,1)S(1)}, bf16[14,96]{1,0:T(8,128)(2,1)}, u32[]{:S(2)}) copy-start(bf16[14,96]{1,0:T(8,128)(2,1)} %bias.1) | copy-start | bytes 8068
  0.7 17.8 %copy-start = (bf16[96,2304]{1,0:T(8,128)(2,1)S(1)}, bf16[96,2304]{1,0:T(8,128)(2,1)}, u32[]{:S(2)}) copy-start(bf16[96,2304]{1,0:T(8,128)(2,1)} %weight.5) | copy-start | bytes 1327108
  2.0 16.5 %copy-start.10 = (s32[4]{0:T(128)S(1)}, s32[4]{0:T(128)}, u32[]{:S(2)}) copy-start(s32[4]{0:T(128)} %pad_add_fusion.where) | copy-start | bytes 52
  2.0 28.1 %copy-start.9 = (bf16[96,384]{1,0:T(8,128)(2,1)S(1)}, bf16[96,384]{1,0:T(8,128)(2,1)}, u32[]{:S(2)}) copy-start(bf16[96,384]{1,0:T(8,128)(2,1)} %own_proj.1) | copy-start | bytes 221188
  2.0 28.1 %copy-start.16 = (bf16[2,256,384]{2,1,0:T(8,128)(2,1)S(1)}, bf16[2,256,384]{2,1,0:T(8,128)(2,1)}, u32[]{:S(2)}) copy-start(bf16[2,256,384]{2,1,0:T(8,128)(2,1)} %tokens.7) | copy-start | bytes 1179652
  4.1 26.0 %copy-start.4 = (bf16[96,1152]{1,0:T(8,128)(2,1)S(1)}, bf16[96,1152]{1,0:T(8,128)(2,1)}, u32[]{:S(2)}) copy-start(bf16[96,1152]{1,0:T(8,128)(2,1)} %own_att.1) | copy-start | bytes 663556
  4.1 7.7 %collective-permute-start = (bf16[208,384]{1,0:T(8,128)(2,1)}, bf16[208,384]{1,0:T(8,128)(2,1)S(1)}, u32[]{:S(2)}, u32[]{:S(2)}) collective-permute-start(bf16[208,384]{1,0:T(8,128)(2,1)} %get-tuple-element.79), channel_id=1, source_target_pairs={{0,8},{1,17},{2,10},{3,19},{4,12},{5,21},{6,14},{7,23},{8,0},{9,25... | collective-permute-start | bytes 479240 | tf_op jit(solution)/shard_map/ppermute | solution.py:905
  7.0 6.2 %collective-permute-start.1 = (bf16[208,384]{1,0:T(8,128)(2,1)}, bf16[208,384]{1,0:T(8,128)(2,1)S(1)}, u32[]{:S(2)}, u32[]{:S(2)}) collective-permute-start(bf16[208,384]{1,0:T(8,128)(2,1)} %get-tuple-element.79), channel_id=1, source_target_pairs={{0,16},{1,9},{2,18},{3,11},{4,20},{5,13},{6,22},{7,15},{8,24},{9,1... | collective-permute-start | bytes 479240 | tf_op jit(solution)/shard_map/ppermute | solution.py:905
  11.8 1.5 %collective-permute-start.4 = (bf16[208,384]{1,0:T(8,128)(2,1)S(1)}, bf16[208,384]{1,0:T(8,128)(2,1)S(1)}, u32[]{:S(2)}, u32[]{:S(2)}) collective-permute-start(bf16[208,384]{1,0:T(8,128)(2,1)S(1)} %collective-permute-done.first.n1), channel_id=1, source_target_pairs={{0,1},{1,0},{2,3},{3,2},{4,5},{5,4},{6,7},{7,6},{8,9},{9,8},{10,11... | collective-permute-start | bytes 479240 | tf_op jit(solution)/shard_map/ppermute | solution.py:78
  11.8 6.2 %collective-permute-start.2 = (bf16[208,384]{1,0:T(8,128)(2,1)S(1)}, bf16[208,384]{1,0:T(8,128)(2,1)S(1)}, u32[]{:S(2)}, u32[]{:S(2)}) collective-permute-start(bf16[208,384]{1,0:T(8,128)(2,1)S(1)} %collective-permute-done.first.n1), channel_id=1, source_target_pairs={{0,16},{1,9},{2,18},{3,11},{4,20},{5,13},{6,22},{7,15},{8,24},{9,1... | collective-permute-start | bytes 479240 | tf_op jit(solution)/shard_map/ppermute | solution.py:905
  13.2 1.0 copy-start.7
  14.2 0.7 copy-start.8
  14.9 10.8 %collective-permute-start.5 = (bf16[384,384]{1,0:T(8,128)(2,1)}, bf16[384,384]{1,0:T(8,128)(2,1)S(1)}, u32[]{:S(2)}, u32[]{:S(2)}) collective-permute-start(bf16[384,384]{1,0:T(8,128)(2,1)} %copy-done.8), channel_id=1, source_target_pairs={{0,8},{1,17},{2,10},{3,19},{4,12},{5,21},{6,14},{7,23},{8,0},{9,25... | collective-permute-start | bytes 884744 | tf_op jit(solution)/shard_map/ppermute | solution.py:905
  17.2 11.1 %collective-permute-start.9 = (bf16[384,384]{1,0:T(8,128)(2,1)}, bf16[384,384]{1,0:T(8,128)(2,1)S(1)}, u32[]{:S(2)}, u32[]{:S(2)}) collective-permute-start(bf16[384,384]{1,0:T(8,128)(2,1)} %copy-done.8), channel_id=1, source_target_pairs={{0,16},{1,9},{2,18},{3,11},{4,20},{5,13},{6,22},{7,15},{8,24},{9,1... | collective-permute-start | bytes 884744 | tf_op jit(solution)/shard_map/ppermute | solution.py:905
  17.9 10.4 %collective-permute-start.7 = (bf16[208,384]{1,0:T(8,128)(2,1)S(1)}, bf16[208,384]{1,0:T(8,128)(2,1)S(1)}, u32[]{:S(2)}, u32[]{:S(2)}) collective-permute-start(bf16[208,384]{1,0:T(8,128)(2,1)S(1)} %collective-permute-done.1.second.refs_2_.n2), channel_id=1, source_target_pairs={{0,1},{1,0},{2,3},{3,2},{4,5},{5,4},{6,7},{7,6},{8,9},{9,8},{10,11... | collective-permute-start | bytes 479240 | tf_op jit(solution)/shard_map/ppermute | solution.py:78
  17.9 10.9 %collective-permute-start.8 = (bf16[208,384]{1,0:T(8,128)(2,1)S(1)}, bf16[208,384]{1,0:T(8,128)(2,1)S(1)}, u32[]{:S(2)}, u32[]{:S(2)}) collective-permute-start(bf16[208,384]{1,0:T(8,128)(2,1)S(1)} %collective-permute-done.2.last.n3), channel_id=1, source_target_pairs={{0,1},{1,0},{2,3},{3,2},{4,5},{5,4},{6,7},{7,6},{8,9},{9,8},{10,11... | collective-permute-start | bytes 479240 | tf_op jit(solution)/shard_map/ppermute | solution.py:78
  19.4 6.2 %collective-permute-start.3 = (f32[4,2304]{1,0:T(4,128)S(1)}, f32[4,2304]{1,0:T(4,128)S(1)}, u32[]{:S(2)}, u32[]{:S(2)}) collective-permute-start(f32[4,2304]{1,0:T(4,128)S(1)} %get-tuple-element.81), channel_id=1, source_target_pairs={{0,8},{1,17},{2,10},{3,19},{4,12},{5,21},{6,14},{7,23},{8,0},{9,25... | collective-permute-start | bytes 110600 | tf_op jit(solution)/shard_map/ppermute | solution.py:905
  26.2 3.8 %collective-permute-start.6 = (f32[2,2304]{1,0:T(2,128)S(1)}, f32[2,2304]{1,0:T(2,128)S(1)}, u32[]{:S(2)}, u32[]{:S(2)}) collective-permute-start(f32[2,2304]{1,0:T(2,128)S(1)} %get-tuple-element.84), channel_id=1, source_target_pairs={{0,16},{1,9},{2,18},{3,11},{4,20},{5,13},{6,22},{7,15},{8,24},{9,1... | collective-permute-start | bytes 55304 | tf_op jit(solution)/shard_map/ppermute | solution.py:905
  27.3 7.9 %collective-permute-start.10 = (bf16[384,384]{1,0:T(8,128)(2,1)S(1)}, bf16[384,384]{1,0:T(8,128)(2,1)S(1)}, u32[]{:S(2)}, u32[]{:S(2)}) collective-permute-start(bf16[384,384]{1,0:T(8,128)(2,1)S(1)} %get-tuple-element.89.n1), channel_id=1, source_target_pairs={{0,16},{1,9},{2,18},{3,11},{4,20},{5,13},{6,22},{7,15},{8,24},{9,1... | collective-permute-start | bytes 884744 | tf_op jit(solution)/shard_map/ppermute | solution.py:905
  28.3 6.9 %collective-permute-start.11 = (bf16[384,384]{1,0:T(8,128)(2,1)S(1)}, bf16[384,384]{1,0:T(8,128)(2,1)S(1)}, u32[]{:S(2)}, u32[]{:S(2)}) collective-permute-start(bf16[384,384]{1,0:T(8,128)(2,1)S(1)} %get-tuple-element.89.n1), channel_id=1, source_target_pairs={{0,1},{1,0},{2,3},{3,2},{4,5},{5,4},{6,7},{7,6},{8,9},{9,8},{10,11... | collective-permute-start | bytes 884744 | tf_op jit(solution)/shard_map/ppermute | solution.py:78
  28.3 6.9 %collective-permute-start.12 = (bf16[384,384]{1,0:T(8,128)(2,1)S(1)}, bf16[384,384]{1,0:T(8,128)(2,1)S(1)}, u32[]{:S(2)}, u32[]{:S(2)}) collective-permute-start(bf16[384,384]{1,0:T(8,128)(2,1)S(1)} %collective-permute-done.9.n2), channel_id=1, source_target_pairs={{0,1},{1,0},{2,3},{3,2},{4,5},{5,4},{6,7},{7,6},{8,9},{9,8},{10,11... | collective-permute-start | bytes 884744 | tf_op jit(solution)/shard_map/ppermute | solution.py:78
  30.1 6.7 %copy-start.1 = (bf16[384,384]{1,0:T(8,128)(2,1)S(1)}, bf16[384,384]{1,0:T(8,128)(2,1)}, u32[]{:S(2)}) copy-start(bf16[384,384]{1,0:T(8,128)(2,1)} %own_expand.1) | copy-start | bytes 884740
  30.1 6.7 %copy-start.2 = (bf16[384,384]{1,0:T(8,128)(2,1)S(1)}, bf16[384,384]{1,0:T(8,128)(2,1)}, u32[]{:S(2)}) copy-start(bf16[384,384]{1,0:T(8,128)(2,1)} %own_contract.1) | copy-start | bytes 884740
  30.1 6.7 %copy-start.15 = (bf16[2,256,384]{2,1,0:T(8,128)(2,1)S(1)}, bf16[2,256,384]{2,1,0:T(8,128)(2,1)}, u32[]{:S(2)}) copy-start(bf16[2,256,384]{2,1,0:T(8,128)(2,1)} %cotangent.1) | copy-start | bytes 1179652
  34.0 1.2 copy-start.17
  35.2 11.6 %copy-start.18 = (bf16[2,256,1152]{2,1,0:T(8,128)(2,1)}, bf16[2,256,1152]{2,1,0:T(8,128)(2,1)S(1)}, u32[]{:S(2)}) copy-start(bf16[2,256,1152]{2,1,0:T(8,128)(2,1)S(1)} %get-tuple-element.92.joined) | copy-start | bytes 3538948
  35.2 1.6 %collective-permute-start.13 = (bf16[384,384]{1,0:T(8,128)(2,1)S(1)}, bf16[384,384]{1,0:T(8,128)(2,1)S(1)}, u32[]{:S(2)}, u32[]{:S(2)}) collective-permute-start(bf16[384,384]{1,0:T(8,128)(2,1)S(1)} %in_order.3.n3), channel_id=1, source_target_pairs={{0,1},{1,0},{2,3},{3,2},{4,5},{5,4},{6,7},{7,6},{8,9},{9,8},{10,11... | collective-permute-start | bytes 884744 | tf_op jit(solution)/shard_map/ppermute | solution.py:78
  46.6 4.9 %collective-permute-start.14 = (bf16[4,384,384]{2,1,0:T(8,128)(2,1)S(1)}, bf16[4,384,384]{2,1,0:T(8,128)(2,1)S(1)}, u32[]{:S(2)}, u32[]{:S(2)}) collective-permute-start(bf16[4,384,384]{2,1,0:T(8,128)(2,1)S(1)} %get-tuple-element.102), channel_id=1, source_target_pairs={{0,1},{1,0},{2,3},{3,2},{4,5},{5,4},{6,7},{7,6},{8,9},{9,8},{10,11... | collective-permute-start | bytes 3538952 | tf_op jit(solution)/shard_map/ppermute | solution.py:78
  46.8 4.7 %copy-start.3 = (bf16[4,384,384]{2,1,0:T(8,128)(2,1)S(1)}, bf16[4,384,384]{2,1,0:T(8,128)(2,1)}, u32[]{:S(2)}) copy-start(bf16[4,384,384]{2,1,0:T(8,128)(2,1)} %get-tuple-element.101.keep) | copy-start | bytes 3538948
  52.3 9.9 %collective-permute-start.17 = (bf16[2,384,384]{2,1,0:T(8,128)(2,1)S(1)}, bf16[2,384,384]{2,1,0:T(8,128)(2,1)S(1)}, u32[]{:S(2)}, u32[]{:S(2)}) collective-permute-start(bf16[2,384,384]{2,1,0:T(8,128)(2,1)S(1)} %get-tuple-element.103.refs_5_), channel_id=1, source_target_pairs={{0,8},{1,17},{2,10},{3,19},{4,12},{5,21},{6,14},{7,23},{8,0},{9,25... | collective-permute-start | bytes 1769480 | tf_op jit(solution)/shard_map/ppermute | solution.py:905
  59.8 3.6 %collective-permute-start.15 = (bf16[4,192,384]{2,1,0:T(8,128)(2,1)S(1)}, bf16[4,192,384]{2,1,0:T(8,128)(2,1)S(1)}, u32[]{:S(2)}, u32[]{:S(2)}) collective-permute-start(bf16[4,192,384]{2,1,0:T(8,128)(2,1)S(1)} %get-tuple-element.106), channel_id=1, source_target_pairs={{0,1},{1,0},{2,3},{3,2},{4,5},{5,4},{6,7},{7,6},{8,9},{9,8},{10,11... | collective-permute-start | bytes 1769480 | tf_op jit(solution)/shard_map/ppermute | solution.py:78
  62.4 9.8 %collective-permute-start.18 = (bf16[384,384]{1,0:T(8,128)(2,1)S(1)}, bf16[384,384]{1,0:T(8,128)(2,1)S(1)}, u32[]{:S(2)}, u32[]{:S(2)}) collective-permute-start(bf16[384,384]{1,0:T(8,128)(2,1)S(1)} %bitcast.6), channel_id=1, source_target_pairs={{0,16},{1,9},{2,18},{3,11},{4,20},{5,13},{6,22},{7,15},{8,24},{9,1... | collective-permute-start | bytes 884744 | tf_op jit(solution)/shard_map/ppermute | solution.py:905
  63.6 8.6 %collective-permute-start.16 = (bf16[2,192,384]{2,1,0:T(8,128)(2,1)S(1)}, bf16[2,192,384]{2,1,0:T(8,128)(2,1)S(1)}, u32[]{:S(2)}, u32[]{:S(2)}) collective-permute-start(bf16[2,192,384]{2,1,0:T(8,128)(2,1)S(1)} %get-tuple-element.108), channel_id=1, source_target_pairs={{0,8},{1,17},{2,10},{3,19},{4,12},{5,21},{6,14},{7,23},{8,0},{9,25... | collective-permute-start | bytes 884744 | tf_op jit(solution)/shard_map/ppermute | solution.py:905
  65.4 3.8 %collective-permute-start.19 = (bf16[32,384]{1,0:T(8,128)(2,1)S(1)}, bf16[32,384]{1,0:T(8,128)(2,1)S(1)}, u32[]{:S(2)}, u32[]{:S(2)}) collective-permute-start(bf16[32,384]{1,0:T(8,128)(2,1)S(1)} %get-tuple-element.112.small), channel_id=1, source_target_pairs={{0,2},{1,5},{2,0},{3,7},{4,6},{5,1},{6,4},{7,3},{8,10},{9,13},{10,... | collective-permute-start | bytes 73736 | tf_op jit(solution)/shard_map/ppermute | solution.py:895
  72.9 8.0 %collective-permute-start.20 = (bf16[192,384]{1,0:T(8,128)(2,1)S(1)}, bf16[192,384]{1,0:T(8,128)(2,1)S(1)}, u32[]{:S(2)}, u32[]{:S(2)}) collective-permute-start(bf16[192,384]{1,0:T(8,128)(2,1)S(1)} %get-tuple-element.114), channel_id=1, source_target_pairs={{0,16},{1,9},{2,18},{3,11},{4,20},{5,13},{6,22},{7,15},{8,24},{9,1... | collective-permute-start | bytes 442376 | tf_op jit(solution)/shard_map/ppermute | solution.py:905
  73.9 7.0 %collective-permute-start.21 = (bf16[192,384]{1,0:T(8,128)(2,1)S(1)}, bf16[192,384]{1,0:T(8,128)(2,1)S(1)}, u32[]{:S(2)}, u32[]{:S(2)}) collective-permute-start(bf16[192,384]{1,0:T(8,128)(2,1)S(1)} %get-tuple-element.116), channel_id=1, source_target_pairs={{0,2},{1,5},{2,0},{3,7},{4,6},{5,1},{6,4},{7,3},{8,10},{9,13},{10,... | collective-permute-start | bytes 442376 | tf_op jit(solution)/shard_map/ppermute | solution.py:895
  75.9 5.0 %collective-permute-start.22 = (bf16[64,384]{1,0:T(8,128)(2,1)S(1)}, bf16[64,384]{1,0:T(8,128)(2,1)S(1)}, u32[]{:S(2)}, u32[]{:S(2)}) collective-permute-start(bf16[64,384]{1,0:T(8,128)(2,1)S(1)} %get-tuple-element.117.small), channel_id=1, source_target_pairs={{0,4},{1,3},{2,6},{3,1},{4,0},{5,7},{6,2},{7,5},{8,12},{9,11},{10,... | collective-permute-start | bytes 147464 | tf_op jit(solution)/shard_map/ppermute | solution.py:895
  81.6 24.0 %copy-start.5 = (bf16[96,2304]{1,0:T(8,128)(2,1)S(1)}, bf16[96,2304]{1,0:T(8,128)(2,1)}, u32[]{:S(2)}) copy-start(bf16[96,2304]{1,0:T(8,128)(2,1)} %mean.1) | copy-start | bytes 1327108
  81.6 24.0 %copy-start.6 = (bf16[96,2304]{1,0:T(8,128)(2,1)S(1)}, bf16[96,2304]{1,0:T(8,128)(2,1)}, u32[]{:S(2)}) copy-start(bf16[96,2304]{1,0:T(8,128)(2,1)} %square.1) | copy-start | bytes 1327108
  81.6 24.0 %copy-start.13 = (bf16[14,96]{1,0:T(8,128)(2,1)S(1)}, bf16[14,96]{1,0:T(8,128)(2,1)}, u32[]{:S(2)}) copy-start(bf16[14,96]{1,0:T(8,128)(2,1)} %bias_mean.1) | copy-start | bytes 8068
  81.6 24.0 %copy-start.14 = (bf16[14,96]{1,0:T(8,128)(2,1)S(1)}, bf16[14,96]{1,0:T(8,128)(2,1)}, u32[]{:S(2)}) copy-start(bf16[14,96]{1,0:T(8,128)(2,1)} %bias_square.1) | copy-start | bytes 8068
  81.6 9.3 %collective-permute-start.23 = (bf16[288,384]{1,0:T(8,128)(2,1)S(1)}, bf16[288,384]{1,0:T(8,128)(2,1)S(1)}, u32[]{:S(2)}, u32[]{:S(2)}) collective-permute-start(bf16[288,384]{1,0:T(8,128)(2,1)S(1)} %get-tuple-element.119.own), channel_id=1, source_target_pairs={{0,4},{1,3},{2,6},{3,1},{4,0},{5,7},{6,2},{7,5},{8,12},{9,11},{10,... | collective-permute-start | bytes 663560 | tf_op jit(solution)/shard_map/ppermute | solution.py:895
  84.3 4.6 %collective-permute-start.24 = (bf16[128,384]{1,0:T(8,128)(2,1)S(1)}, bf16[128,384]{1,0:T(8,128)(2,1)S(1)}, u32[]{:S(2)}, u32[]{:S(2)}) collective-permute-start(bf16[128,384]{1,0:T(8,128)(2,1)S(1)} %get-tuple-element.120.small), channel_id=1, source_target_pairs={{0,16},{1,9},{2,18},{3,11},{4,20},{5,13},{6,22},{7,15},{8,24},{9,1... | collective-permute-start | bytes 294920 | tf_op jit(solution)/shard_map/ppermute | solution.py:905
  91.5 9.1 %collective-permute-start.25 = (bf16[288,384]{1,0:T(8,128)(2,1)S(1)}, bf16[288,384]{1,0:T(8,128)(2,1)S(1)}, u32[]{:S(2)}, u32[]{:S(2)}) collective-permute-start(bf16[288,384]{1,0:T(8,128)(2,1)S(1)} %get-tuple-element.121.own), channel_id=1, source_target_pairs={{0,2},{1,5},{2,0},{3,7},{4,6},{5,1},{6,4},{7,3},{8,10},{9,13},{10,... | collective-permute-start | bytes 663560 | tf_op jit(solution)/shard_map/ppermute | solution.py:895
  94.9 5.7 %collective-permute-start.26 = (bf16[256,384]{1,0:T(8,128)(2,1)S(1)}, bf16[256,384]{1,0:T(8,128)(2,1)S(1)}, u32[]{:S(2)}, u32[]{:S(2)}) collective-permute-start(bf16[256,384]{1,0:T(8,128)(2,1)S(1)} %get-tuple-element.122.small), channel_id=1, source_target_pairs={{0,8},{1,17},{2,10},{3,19},{4,12},{5,21},{6,14},{7,23},{8,0},{9,25... | collective-permute-start | bytes 589832 | tf_op jit(solution)/shard_map/ppermute | solution.py:905
  101.5 4.1 %collective-permute-start.29 = (bf16[512,384]{1,0:T(8,128)(2,1)S(1)}, bf16[512,384]{1,0:T(8,128)(2,1)S(1)}, u32[]{:S(2)}, u32[]{:S(2)}) collective-permute-start(bf16[512,384]{1,0:T(8,128)(2,1)S(1)} %get-tuple-element.126.near), channel_id=1, source_target_pairs={{0,1},{1,0},{2,3},{3,2},{4,5},{5,4},{6,7},{7,6},{8,9},{9,8},{10,11... | collective-permute-start | bytes 1179656 | tf_op jit(solution)/shard_map/ppermute | solution.py:78
  101.5 9.7 %collective-permute-start.32 = (bf16[384,384]{1,0:T(8,128)(2,1)S(1)}, bf16[384,384]{1,0:T(8,128)(2,1)}, u32[]{:S(2)}, u32[]{:S(2)}) collective-permute-start(bf16[384,384]{1,0:T(8,128)(2,1)S(1)} %get-tuple-element.131), channel_id=1, source_target_pairs={{0,1},{1,0},{2,3},{3,2},{4,5},{5,4},{6,7},{7,6},{8,9},{9,8},{10,11... | collective-permute-start | bytes 884744 | tf_op jit(solution)/shard_map/ppermute | solution.py:78
  102.0 7.1 %collective-permute-start.27 = (bf16[96,384]{1,0:T(8,128)(2,1)S(1)}, bf16[96,384]{1,0:T(8,128)(2,1)S(1)}, u32[]{:S(2)}, u32[]{:S(2)}) collective-permute-start(bf16[96,384]{1,0:T(8,128)(2,1)S(1)} %get-tuple-element.123.att_sum), channel_id=1, source_target_pairs={{0,4},{1,3},{2,6},{3,1},{4,0},{5,7},{6,2},{7,5},{8,12},{9,11},{10,... | collective-permute-start | bytes 221192 | tf_op jit(solution)/shard_map/ppermute | solution.py:895
  105.5 3.6 %collective-permute-start.28 = (f32[8,128]{1,0:T(8,128)S(1)}, f32[8,128]{1,0:T(8,128)S(1)}, u32[]{:S(2)}, u32[]{:S(2)}) collective-permute-start(f32[8,128]{1,0:T(8,128)S(1)} %get-tuple-element.125), channel_id=1, source_target_pairs={{0,8},{1,17},{2,10},{3,19},{4,12},{5,21},{6,14},{7,23},{8,0},{9,25... | collective-permute-start | bytes 12296 | tf_op jit(solution)/shard_map/ppermute | solution.py:905
  105.5 5.6 %copy-start.19 = (bf16[384,384]{1,0:T(8,128)(2,1)S(1)}, bf16[384,384]{1,0:T(8,128)(2,1)}, u32[]{:S(2)}) copy-start(bf16[384,384]{1,0:T(8,128)(2,1)} %param.36) | copy-start | bytes 884740
  105.5 5.6 %copy-start.20 = (bf16[384,384]{1,0:T(8,128)(2,1)S(1)}, bf16[384,384]{1,0:T(8,128)(2,1)}, u32[]{:S(2)}) copy-start(bf16[384,384]{1,0:T(8,128)(2,1)} %param.42) | copy-start | bytes 884740
  105.5 5.6 %copy-start.21 = (bf16[384,384]{1,0:T(8,128)(2,1)S(1)}, bf16[384,384]{1,0:T(8,128)(2,1)}, u32[]{:S(2)}) copy-start(bf16[384,384]{1,0:T(8,128)(2,1)} %param.41) | copy-start | bytes 884740
  105.5 5.6 %copy-start.22 = (bf16[384,384]{1,0:T(8,128)(2,1)S(1)}, bf16[384,384]{1,0:T(8,128)(2,1)}, u32[]{:S(2)}) copy-start(bf16[384,384]{1,0:T(8,128)(2,1)} %param.35) | copy-start | bytes 884740
  109.7 4.8 %collective-permute-start.30 = (f32[8,128]{1,0:T(8,128)S(1)}, f32[8,128]{1,0:T(8,128)S(1)}, u32[]{:S(2)}, u32[]{:S(2)}) collective-permute-start(f32[8,128]{1,0:T(8,128)S(1)} %get-tuple-element.128), channel_id=1, source_target_pairs={{0,16},{1,9},{2,18},{3,11},{4,20},{5,13},{6,22},{7,15},{8,24},{9,1... | collective-permute-start | bytes 12296 | tf_op jit(solution)/shard_map/ppermute | solution.py:905
  114.5 1.5 %copy-start.25 = (bf16[96,384]{1,0:T(8,128)(2,1)S(1)}, bf16[96,384]{1,0:T(8,128)(2,1)}, u32[]{:S(2)}) copy-start(bf16[96,384]{1,0:T(8,128)(2,1)} %param.34) | copy-start | bytes 221188
  114.5 1.5 %copy-start.26 = (bf16[96,384]{1,0:T(8,128)(2,1)S(1)}, bf16[96,384]{1,0:T(8,128)(2,1)}, u32[]{:S(2)}) copy-start(bf16[96,384]{1,0:T(8,128)(2,1)} %param.40) | copy-start | bytes 221188
  114.5 1.4 %collective-permute-start.31 = (bf16[192,384]{1,0:T(8,128)(2,1)S(1)}, bf16[192,384]{1,0:T(8,128)(2,1)S(1)}, u32[]{:S(2)}, u32[]{:S(2)}) collective-permute-start(bf16[192,384]{1,0:T(8,128)(2,1)S(1)} %get-tuple-element.130), channel_id=1, source_target_pairs={{0,1},{1,0},{2,3},{3,2},{4,5},{5,4},{6,7},{7,6},{8,9},{9,8},{10,11... | collective-permute-start | bytes 442376 | tf_op jit(solution)/shard_map/ppermute | solution.py:78
  115.2 1.6 %copy-start.23 = (bf16[96,1152]{1,0:T(8,128)(2,1)S(1)}, bf16[96,1152]{1,0:T(8,128)(2,1)}, u32[]{:S(2)}) copy-start(bf16[96,1152]{1,0:T(8,128)(2,1)} %param.33) | copy-start | bytes 663556
  115.2 1.6 %copy-start.24 = (bf16[96,1152]{1,0:T(8,128)(2,1)S(1)}, bf16[96,1152]{1,0:T(8,128)(2,1)}, u32[]{:S(2)}) copy-start(bf16[96,1152]{1,0:T(8,128)(2,1)} %param.39) | copy-start | bytes 663556

commit v4 on v3

--- a/solution.py
+++ b/solution.py
@@ -28,6 +28,7 @@
 VMEM_BYTES = 48 * 1024 * 1024
 LOW = jnp.bfloat16
 SMALL = 32
+BLOCK = 16
 WIDE = jnp.float32
 
 
@@ -405,14 +406,14 @@
     if slot == 0:
         rows[...] = jnp.zeros_like(rows)
         rows[12:14, :] = cond[...]
-        rows[17:22, :] = feed_rows[8:13, :]
+        rows[19:24, :] = feed_rows[8:13, :]
     else:
         rows[...] = before_rows[...]
 
     pieces = mod[0]
     grad_middle = grad_middle_in[0]
     grad_branch = (pieces[2:3] * grad_middle).astype(LOW)
-    rows[16:17, :] += column_sum(grad_branch.astype(WIDE))
+    rows[18:19, :] += column_sum(grad_branch.astype(WIDE))
     if slot == 0:
         branch_out[...] = grad_branch
     else:
@@ -453,8 +454,8 @@
             grad_joined[:, third * D + pair * 128 : third * D + (pair + 1) * 128] = merged.astype(LOW)
     grads = grad_joined[...]
     sums = column_sum(grads.astype(WIDE))
-    rows[14:15, :] += sums[:, :D]
-    rows[15:16, :] += sums[:, 2 * D :]
+    rows[16:17, :] += sums[:, :D]
+    rows[17:18, :] += sums[:, 2 * D :]
     normed, inverse = layer_norm_parts(tokens[0].astype(WIDE))
     first_in = (normed * (1.0 + pieces[1:2]) + pieces[0:1]).astype(LOW)
     if slot == 0:
@@ -508,7 +509,16 @@
 
 
 def rows_at(index, count):
-    return pl.ds(pl.multiple_of(index * count, 32), count)
+    return pl.ds(pl.multiple_of(index * count, 16), count)
+
+
+def merge_small(out, own, arrived):
+    count = own.shape[0] - BLOCK
+    out[0:count, :] = own[0:count, :]
+    out[count : 2 * count, :] = arrived[0:count, :]
+    out[2 * count :, :] = (
+        own[count:, :].astype(WIDE) + arrived[count:, :].astype(WIDE)
+    ).astype(LOW)
 
 
 def step1_kernel(
@@ -522,47 +532,34 @@
     total[...] = feed_keep[...] + feed_in[...].astype(WIDE)
     feed_stay[...] = total[rows_at(half, count), :]
     feed_go[...] = total[rows_at(1 - half, count), :].astype(LOW)
-    small_out[0:SMALL, :] = small[...]
-    small_out[SMALL:, :] = small_in[...]
-
-
-def step2_kernel(
-    where, att_keep, att_in, feed_keep, feed_in, small, small_in, att_stay, message, small_out, total
-):
-    half = half_of(where, 1)
+    merge_small(small_out, small, small_in)
+
+
+def step2_kernel(where, att_keep, att_in, feed_keep, feed_in, small, small_in, message, small_out):
     count = D // 2
-    total[...] = att_keep[...] + att_in[...].astype(WIDE)
-    att_stay[...] = total[rows_at(half, QUARTER), :]
     message[0:count, :] = (feed_keep[...] + feed_in[...].astype(WIDE)).astype(LOW)
-    message[count:, :] = total[rows_at(1 - half, QUARTER), :].astype(LOW)
-    small_out[0 : 2 * SMALL, :] = small[...]
-    small_out[2 * SMALL :, :] = small_in[...]
-
-
-def step3_kernel(where, att_keep, own, arrived, small, small_in, message, small_out):
-    count = D // 2
-    message[0:count, :] = (
-        own[0:count, :].astype(WIDE) + arrived[0:count, :].astype(WIDE)
-    ).astype(LOW)
-    message[count:, :] = (att_keep[...] + arrived[count:, :].astype(WIDE)).astype(LOW)
-    small_out[0 : 4 * SMALL, :] = small[...]
-    small_out[4 * SMALL :, :] = small_in[...]
+    message[count:, :] = (att_keep[...] + att_in[...].astype(WIDE)).astype(LOW)
+    merge_small(small_out, small, small_in)
+
+
+def step3_kernel(where, own, arrived, small, small_in, message, small_out):
+    message[...] = (own[...].astype(WIDE) + arrived[...].astype(WIDE)).astype(LOW)
+    merge_small(small_out, small, small_in)
 
 
 def step4_kernel(
-    where, own, arrived, small, small_in, weight, att_sum, feed_part, small_out, cond_keep, cond_go
+    where, own, arrived, small, small_in, weight, att_part, feed_part, small_out, cond_keep, cond_go
 ):
     half = half_of(where, 0)
     count = D // 2
     feed_part[rows_at(half, count), :] = own[0:count, :]
     feed_part[rows_at(1 - half, count), :] = arrived[0:count, :]
-    att_sum[...] = (own[count:, :].astype(WIDE) + arrived[count:, :].astype(WIDE)).astype(LOW)
-    small_out[0 : 8 * SMALL, :] = small[...]
-    small_out[8 * SMALL :, :] = small_in[...]
+    att_part[...] = (own[count:, :].astype(WIDE) + arrived[count:, :].astype(WIDE)).astype(LOW)
+    merge_small(small_out, small, small_in)
     rows = [
-        block[start : start + SMALL, :].astype(WIDE)
+        block[start : start + BLOCK, :].astype(WIDE)
         for block in (small, small_in)
-        for start in (0, 4 * SMALL)
+        for start in (0, 4 * BLOCK)
     ]
     total = None
     for j in range(6):
@@ -577,10 +574,7 @@
     cond_go[...] = jnp.concatenate([padded[4:8], blank], axis=0)
 
 
-def step5_kernel(where, att_sum, att_in, cond_keep, cond_in, _, att_part, cond_go):
-    half = half_of(where, 1)
-    att_part[rows_at(half, QUARTER), :] = att_sum[...]
-    att_part[rows_at(1 - half, QUARTER), :] = att_in[...]
+def step5_kernel(where, cond_keep, cond_in, _, cond_go):
     blank = jnp.zeros((4, 128), WIDE)
     cond_go[...] = jnp.concatenate([cond_keep[2:4], cond_in[2:4], blank], axis=0)
 
@@ -598,14 +592,14 @@
             z_at = plane ^ (a * first) ^ (b * second)
             g_at = rank ^ (c * second) ^ (d * first)
             place = (g_at * 4 + z_at) * 2 + here
-            block = source[index * SMALL : (index + 1) * SMALL, :].astype(WIDE)
+            block = source[index * BLOCK : (index + 1) * BLOCK, :].astype(WIDE)
             for third in range(3):
-                everyone[third, rows_at(place, SMALL), :] = block[
+                everyone[third, rows_at(place, BLOCK), :] = block[
                     :, third * 128 : (third + 1) * 128
                 ]
 
     def line(at):
-        parts = [everyone[third, pl.ds(at, 32, stride=SMALL), :] for third in range(3)]
+        parts = [everyone[third, pl.ds(at, 32, stride=BLOCK), :] for third in range(3)]
         return jnp.concatenate(parts, axis=1)
 
     def both(at, other):
@@ -636,8 +630,7 @@
         weight_out[:, lanes] = updated
         mean_out[:, lanes] = momentum
         square_out[:, lanes] = variance
-    for at in range(14, 22):
-        sums.append(column_sum(line(at)))
+    sums.append(near[16 * BLOCK :, :].astype(WIDE)[0:8] + far[16 * BLOCK :, :].astype(WIDE)[0:8])
     gradient = own_lanes(jnp.concatenate(sums, axis=0))
     updated, momentum, variance = adam_update(
         bias[...].astype(WIDE),
@@ -944,32 +937,31 @@
 ):
     core = where[1]
     (feed_stay, feed_in), (att_send, att_keep) = ffn_halves, att_parts
-    half, third, quarter = (D // 2, D), (2 * QUARTER, D), (QUARTER, D)
+    half, third = (D // 2, D), (2 * QUARTER, D)
     att_stay, att_go = run_split(att_keep, swap_replica(att_send, 1))
     feed_stay, feed_go = run_split(feed_stay, feed_in)
     feed_stay, feed_go = feed_stay[0], feed_go[0]
     att_stay, att_go, feed_stay, feed_go, small = small_call(
         step1_kernel, "step_1",
-        [(third, WIDE), (third, LOW), (half, WIDE), (half, LOW), ((2 * SMALL, D), LOW)],
+        [(third, WIDE), (third, LOW), (half, WIDE), (half, LOW), ((3 * BLOCK, D), LOW)],
         where, att_stay, swap_pair(att_go, 0), feed_stay, swap_pair(feed_go, 1),
         small_rows, swap_plane(small_rows, 0),
         scratch=[((D, D), WIDE)],
     )
-    att_stay, message, small = small_call(
+    message, small = small_call(
         step2_kernel, "step_2",
-        [(quarter, WIDE), ((3 * QUARTER, D), LOW), ((4 * SMALL, D), LOW)],
+        [((D, D), LOW), ((5 * BLOCK, D), LOW)],
         where, att_stay, swap_pair(att_go, 1), feed_stay, swap_plane(feed_go, 0),
         small, swap_plane(small, 1),
-        scratch=[(third, WIDE)],
     )
     message, small = small_call(
         step3_kernel, "step_3",
-        [((3 * QUARTER, D), LOW), ((8 * SMALL, D), LOW)],
-        where, att_stay, message, swap_plane(message, 1), small, swap_pair(small, 1),
-    )
-    att_sum, feed_part, small, cond_keep, cond_go = small_call(
+        [((D, D), LOW), ((9 * BLOCK, D), LOW)],
+        where, message, swap_plane(message, 1), small, swap_pair(small, 1),
+    )
+    att_part, feed_part, small, cond_keep, cond_go = small_call(
         step4_kernel, "step_4",
-        [(quarter, LOW), ((D, D), LOW), ((16 * SMALL, D), LOW), ((8, 128), WIDE), ((8, 128), WIDE)],
+        [(third, LOW), ((D, D), LOW), ((17 * BLOCK, D), LOW), ((8, 128), WIDE), ((8, 128), WIDE)],
         where, message, swap_plane(message, 0), small, swap_pair(small, 0), stored[0],
     )
     shard = [((QUARTER, 6 * D), WIDE)] * 3 + [((BIAS_ROWS, QUARTER), WIDE)] * 3
@@ -977,17 +969,14 @@
         modulation_update_kernel, "modulation_update", shard + [((8, 128), WIDE)],
         where, small, swap_replica(small, 1), stored[0], means[0], squares[0],
         stored[5], means[5], squares[5],
-        scratch=[((3, 32 * SMALL, 128), WIDE)],
+        scratch=[((3, 32 * BLOCK, 128), WIDE)],
     )
     feed_totals = by_core(core, feed_part, swap_replica(feed_part, 1))
     feed_updates = update_all(stored, feed_totals, means, squares, (3, 4))
     cond_in = swap_pair(cond_go, 0)
-    att_part, cond_go = small_call(
-        step5_kernel, "step_5",
-        [(third, LOW), ((8, 128), WIDE)],
-        where, att_sum, swap_plane(att_sum, 1), cond_keep, cond_in,
-        after=(mark,),
-    )
+    cond_go = small_call(
+        step5_kernel, "step_5", [((8, 128), WIDE)], where, cond_keep, cond_in, after=(mark,)
+    )[0]
     cond_last = swap_pair(cond_go, 1)
     att_totals = by_core(core, att_part, swap_replica(att_part, 1))
     blocks = [
@@ -1052,7 +1041,7 @@
     cond_own = lax.dynamic_slice_in_dim(all_cond, rank * (model_width // 4), model_width // 4, 1)
     grad_mod = dot_first(cond_own, all_mod)
     mod_bias_grad = jnp.sum(all_mod, axis=0, dtype=jnp.float32).reshape(6, model_width)
-    rest_bias_grad = jnp.sum(everyone[:, 7 * slot_count : 22], axis=0, dtype=jnp.float32)
+    rest_bias_grad = jnp.sum(everyone[:, BLOCK : BLOCK + 8], axis=0, dtype=jnp.float32)
     bias_grad = lax.dynamic_slice_in_dim(
         jnp.concatenate([mod_bias_grad, rest_bias_grad], axis=0),
         rank * (model_width // 4),

time: 118 us -> 115 us (0.975)
  waiting for transfers between devices: 32.9 us -> 36.6 us
  starting transfers between devices: 37.9 us -> 34.5 us
  local copies, waits for them, and re-layouts: 2.96 us -> 1.29 us
    ppermute x6 -> x5, waiting for transfers between devices: 6.59 us -> 11.9 us  [swap_plane(): return lax.ppermute(value, 'replica', pairs)]
    ppermute x6 -> x5, starting transfers between devices: 15.9 us -> 11 us  [swap_plane(): return lax.ppermute(value, 'replica', pairs)]
    ppermute x16, starting transfers between devices: 20.4 us -> 22.1 us  [swap_pair(): return lax.ppermute(value, ('group', 'replica'), pairs)]
    unnamed x54 -> x50, local copies, waits for them, and re-layouts: 2.94 us -> 1.27 us
    ppermute x16, waiting for transfers between devices: 24 us -> 22.4 us  [swap_pair(): return lax.ppermute(value, ('group', 'replica'), pairs)]
  transfers between devices with their start and end apart: 33 -> 32, of which waited for: 12 -> 14; matrix products, arithmetic and copies ran while one was open for 3% -> 2% of each run, Pallas kernels for 17% -> 17%
where the time goes in v4:
time: 115 us
  waiting for transfers between devices  36.6 us (32%)
  Pallas kernels  35.4 us (31%)
  starting transfers between devices  34.5 us (30%)
  other arithmetic  5.69 us (5%)
  between operations  1.74 us (2%)
  local copies, waits for them, and re-layouts  1.29 us (1%)
    ppermute x16, waiting for transfers between devices, swap_pair(): return lax.ppermute(value, ('group', 'replica'), pairs)  22.4 us
    ppermute x16, starting transfers between devices, swap_pair(): return lax.ppermute(value, ('group', 'replica'), pairs)  22.1 us
    ppermute x5, waiting for transfers between devices, swap_plane(): return lax.ppermute(value, 'replica', pairs)  11.9 us
    ppermute x5, starting transfers between devices, swap_plane(): return lax.ppermute(value, 'replica', pairs)  11 us
    pallas_call x2, Pallas kernels, run_attention_backward(): pl.pallas_call(functools.partial(attention_backward_kernel, slot), grid=(...  10.6 us
    pallas_call x1, Pallas kernels, run_feed(): pl.pallas_call(feed_kernel, grid=(2,), in_specs=[SMEM_SPEC] + [whole((2,...  9.83 us
    pallas_call x8, Pallas kernels, small_call(): pl.pallas_call(kernel, grid=(1,), in_specs=[SMEM_SPEC] + [whole(item.shap...  9.32 us
    sub x3, other arithmetic, adam_update(): updated = weight * (1.0 - step_rate * decay_flag * DECAY_RATE) - change  4.37 us
  transfers between devices with their start and end apart: 32, of which 14 were waited for; matrix products, arithmetic and copies ran while one was open for 2% of the time, Pallas kernels for 17%

profile of v4, /device:TPU:0, one launch (start us, length us, event | category | flops | bytes accessed | tf_op | source)
XLA Modules:
  0.0 115.3 jit_solution(14075899630817257398)
XLA Ops:
  0.7 0.0 copy-start.10
  1.4 0.6 pad_add_fusion.where
  2.0 2.1 %own_payload.1 = (bf16[208,384]{1,0:T(8,128)(2,1)}, bf16[384,384]{1,0:T(8,128)(2,1)}) custom-call(s32[4]{0:T(128)} %pad_add_fusion.where, f32[2,384]{1,0:T(2,128)} %condition.3, bf16[96,1152]{1,0:T(8,128)(2,1)} %own_att.1, bf16[96,384]{1,0:T(8,128)(2,1)} %own_proj.1, bf16[14,96]{1,0:T(8,128)(2,1)} %bias.1, bf16[384,384]{1,0:T(8,128)(2,1)} %own_expand.1, ...), custom_call_target="tpu_custom_call" | custom-call | tf_op jit(solution)/shard_map/own_payload/pallas_call | solution.py:675
  4.1 0.0 copy-start.14
  4.1 3.0 %collective-permute-start = (bf16[208,384]{1,0:T(8,128)(2,1)}, bf16[208,384]{1,0:T(8,128)(2,1)S(1)}, u32[]{:S(2)}, u32[]{:S(2)}) collective-permute-start(bf16[208,384]{1,0:T(8,128)(2,1)} %get-tuple-element.76), channel_id=1, source_target_pairs={{0,8},{1,17},{2,10},{3,19},{4,12},{5,21},{6,14},{7,23},{8,0},{9,25... | collective-permute-start | bytes 479240 | tf_op jit(solution)/shard_map/ppermute | solution.py:898
  7.1 1.5 %collective-permute-start.1 = (bf16[208,384]{1,0:T(8,128)(2,1)}, bf16[208,384]{1,0:T(8,128)(2,1)S(1)}, u32[]{:S(2)}, u32[]{:S(2)}) collective-permute-start(bf16[208,384]{1,0:T(8,128)(2,1)} %get-tuple-element.76), channel_id=1, source_target_pairs={{0,16},{1,9},{2,18},{3,11},{4,20},{5,13},{6,22},{7,15},{8,24},{9,1... | collective-permute-start | bytes 479240 | tf_op jit(solution)/shard_map/ppermute | solution.py:898
  8.6 3.2 %collective-permute-done.first.n1 = bf16[208,384]{1,0:T(8,128)(2,1)S(1)} collective-permute-done((bf16[208,384]{1,0:T(8,128)(2,1)}, bf16[208,384]{1,0:T(8,128)(2,1)S(1)}, u32[]{:S(2)}, u32[]{:S(2)}) %collective-permute-start) | collective-permute-done | bytes 159776 | tf_op jit(solution)/shard_map/ppermute | solution.py:898
  11.8 1.5 %collective-permute-start.2 = (bf16[208,384]{1,0:T(8,128)(2,1)S(1)}, bf16[208,384]{1,0:T(8,128)(2,1)S(1)}, u32[]{:S(2)}, u32[]{:S(2)}) collective-permute-start(bf16[208,384]{1,0:T(8,128)(2,1)S(1)} %collective-permute-done.first.n1), channel_id=1, source_target_pairs={{0,16},{1,9},{2,18},{3,11},{4,20},{5,13},{6,22},{7,15},{8,24},{9,1... | collective-permute-start | bytes 479240 | tf_op jit(solution)/shard_map/ppermute | solution.py:898
  13.3 2.3 %collective-permute-start.5 = (bf16[384,384]{1,0:T(8,128)(2,1)}, bf16[384,384]{1,0:T(8,128)(2,1)S(1)}, u32[]{:S(2)}, u32[]{:S(2)}) collective-permute-start(bf16[384,384]{1,0:T(8,128)(2,1)} %in_order.2), channel_id=1, source_target_pairs={{0,8},{1,17},{2,10},{3,19},{4,12},{5,21},{6,14},{7,23},{8,0},{9,25... | collective-permute-start | bytes 884744 | tf_op jit(solution)/shard_map/ppermute | solution.py:898
  15.6 0.7 collective-permute-start.9
  16.3 0.8 collective-permute-done.2.last.n3
  17.1 0.1 collective-permute-start.8
  17.2 1.0 modulation_partials.1
  18.2 3.3 %collective-permute-start.3 = (f32[4,2304]{1,0:T(4,128)S(1)}, f32[4,2304]{1,0:T(4,128)S(1)}, u32[]{:S(2)}, u32[]{:S(2)}) collective-permute-start(f32[4,2304]{1,0:T(4,128)S(1)} %get-tuple-element.78), channel_id=1, source_target_pairs={{0,8},{1,17},{2,10},{3,19},{4,12},{5,21},{6,14},{7,23},{8,0},{9,25... | collective-permute-start | bytes 110600 | tf_op jit(solution)/shard_map/ppermute | solution.py:898
  21.5 2.5 %collective-permute-done.3.arrived = f32[4,2304]{1,0:T(4,128)S(1)} collective-permute-done((f32[4,2304]{1,0:T(4,128)S(1)}, f32[4,2304]{1,0:T(4,128)S(1)}, u32[]{:S(2)}, u32[]{:S(2)}) %collective-permute-start.3) | collective-permute-done | bytes 36896 | tf_op jit(solution)/shard_map/ppermute | solution.py:898
  24.0 0.6 relay.1
  24.6 1.1 collective-permute-start.6
  25.7 1.0 collective-permute-start.10
  26.7 0.5 collective-permute-start.12
  27.2 1.2 %collective-permute-done.6.arrived = f32[2,2304]{1,0:T(2,128)S(1)} collective-permute-done((f32[2,2304]{1,0:T(2,128)S(1)}, f32[2,2304]{1,0:T(2,128)S(1)}, u32[]{:S(2)}, u32[]{:S(2)}) %collective-permute-start.6) | collective-permute-done | bytes 18464 | tf_op jit(solution)/shard_map/ppermute | solution.py:898
  28.4 0.0 copy-start.1
  28.5 3.9 %attention_forward.1 = (bf16[2,256,1152]{2,1,0:T(8,128)(2,1)S(1)}, bf16[2,6,256,256]{3,2,1,0:T(8,128)(2,1)S(1)}, bf16[2,256,384]{2,1,0:T(8,128)(2,1)S(1)}, f32[2...) custom-call(s32[4]{0:T(128)S(1)} %copy-done.8, ...), custom_call_target="tpu_custom_call" | custom-call | flops 3000000000 | bytes 6000000 | tf_op jit(solution)/shard_map/attention_forward/pallas_call | solution.py:733
  32.4 1.1 copy-done.15
  33.6 1.6 %collective-permute-done.13.f3 = bf16[384,384]{1,0:T(8,128)(2,1)S(1)} collective-permute-done((bf16[384,384]{1,0:T(8,128)(2,1)S(1)}, bf16[384,384]{1,0:T(8,128)(2,1)S(1)}, u32[]{:S(2)}, u32[]{:S(2)}) %collective-permute-start.13) | collective-permute-done | bytes 294944 | tf_op jit(solution)/shard_map/ppermute | solution.py:79
  35.2 9.8 %feed_forward_and_back.1 = (bf16[2,256,384]{2,1,0:T(8,128)(2,1)}, f32[2,256,384]{2,1,0:T(8,128)S(1)}, bf16[4,384,384]{2,1,0:T(8,128)(2,1)S(1)}, bf16[4,384,384]{2,1,0:T(8,128)(2,1)}, f32[16,384]{1,0:T(8,128)S(1)}) custom-call(s32[4]{0:T(128)S(1)} %copy-done.8, bf16[2,256,384]{2,1,0:T(8,128)(2,1)S(1)} %get-tuple-element.83.mixed, ...), custom_call_target="tpu_custom_call" | custom-call | flops 8000000000 | bytes 10000000 | tf_op jit(solution)/shard_map/feed_forward_and_back/pallas_call | solution.py:773
  45.0 0.1 collective-permute-start.14
  45.2 4.7 %attention_backward.2 = (bf16[2,256,384]{2,1,0:T(8,128)(2,1)}, bf16[256,1152]{1,0:T(8,128)(2,1)S(1)}, bf16[256,384]{1,0:T(8,128)(2,1)S(1)}, bf16[256,384]{1,0:T(8,128)(2,1)S(1)}, f32[32,384]{1,0:T(8,128)S(1)}) custom-call(s32[4]{0:T(128)S(1)} %copy-done.8, bf16[2,256,384]{2,1,0:T(8,128)(2,1)S(1)} %copy-done.14, ...), custom_call_target="tpu_custom_call" | custom-call | flops 4000000000 | bytes 8000000 | tf_op jit(solution)/shard_map/attention_backward/pallas_call | solution.py:848
  49.9 0.8 sum_and_split.3
  50.7 1.7 %collective-permute-start.17 = (bf16[2,384,384]{2,1,0:T(8,128)(2,1)S(1)}, bf16[2,384,384]{2,1,0:T(8,128)(2,1)S(1)}, u32[]{:S(2)}, u32[]{:S(2)}) collective-permute-start(bf16[2,384,384]{2,1,0:T(8,128)(2,1)S(1)} %get-tuple-element.100.refs_5_), channel_id=1, source_target_pairs={{0,8},{1,17},{2,10},{3,19},{4,12},{5,21},{6,14},{7,23},{8,0},{9,25... | collective-permute-start | bytes 1769480 | tf_op jit(solution)/shard_map/ppermute | solution.py:898
  52.4 5.8 %attention_backward.3 = (bf16[2,256,384]{2,1,0:T(8,128)(2,1)}, bf16[4,192,384]{2,1,0:T(8,128)(2,1)S(1)}, bf16[4,192,384]{2,1,0:T(8,128)(2,1)S(1)}, bf16[32,384]{1,0:T(8,128)(2,1)S(1)}) custom-call(s32[4]{0:T(128)S(1)} %copy-done.8, bf16[2,256,384]{2,1,0:T(8,128)(2,1)S(1)} %copy-done.14, ...), custom_call_target="tpu_custom_call", output_to_operand_aliasing={{0}: (15, {})} | custom-call | flops 4000000000 | bytes 8000000 | tf_op jit(solution)/shard_map/attention_backward/pallas_call | solution.py:848
  58.3 2.4 %collective-permute-done.17.arrived = bf16[2,384,384]{2,1,0:T(8,128)(2,1)S(1)} collective-permute-done((bf16[2,384,384]{2,1,0:T(8,128)(2,1)S(1)}, bf16[2,384,384]{2,1,0:T(8,128)(2,1)S(1)}, u32[]{:S(2)}, u32[]{:S(2)}) %collective-permute-start.17) | collective-permute-done | bytes 589856 | tf_op jit(solution)/shard_map/ppermute | solution.py:898
  60.7 0.1 sum_and_split.5
  60.8 1.1 collective-permute-start.18
  61.9 0.1 sum_and_split.4
  62.0 1.8 %collective-permute-start.16 = (bf16[2,192,384]{2,1,0:T(8,128)(2,1)S(1)}, bf16[2,192,384]{2,1,0:T(8,128)(2,1)S(1)}, u32[]{:S(2)}, u32[]{:S(2)}) collective-permute-start(bf16[2,192,384]{2,1,0:T(8,128)(2,1)S(1)} %get-tuple-element.105), channel_id=1, source_target_pairs={{0,8},{1,17},{2,10},{3,19},{4,12},{5,21},{6,14},{7,23},{8,0},{9,25... | collective-permute-start | bytes 884744 | tf_op jit(solution)/shard_map/ppermute | solution.py:898
  63.8 1.6 %collective-permute-start.19 = (bf16[32,384]{1,0:T(8,128)(2,1)S(1)}, bf16[32,384]{1,0:T(8,128)(2,1)S(1)}, u32[]{:S(2)}, u32[]{:S(2)}) collective-permute-start(bf16[32,384]{1,0:T(8,128)(2,1)S(1)} %get-tuple-element.109.small), channel_id=1, source_target_pairs={{0,2},{1,5},{2,0},{3,7},{4,6},{5,1},{6,4},{7,3},{8,10},{9,13},{10,... | collective-permute-start | bytes 73736 | tf_op jit(solution)/shard_map/ppermute | solution.py:888
  65.4 2.2 %collective-permute-done.19.small_in = bf16[32,384]{1,0:T(8,128)(2,1)S(1)} collective-permute-done((bf16[32,384]{1,0:T(8,128)(2,1)S(1)}, bf16[32,384]{1,0:T(8,128)(2,1)S(1)}, u32[]{:S(2)}, u32[]{:S(2)}) %collective-permute-start.19) | collective-permute-done | bytes 24608 | tf_op jit(solution)/shard_map/ppermute | solution.py:888
  67.6 2.9 %collective-permute-done.18.feed_in = bf16[384,384]{1,0:T(8,128)(2,1)S(1)} collective-permute-done((bf16[384,384]{1,0:T(8,128)(2,1)S(1)}, bf16[384,384]{1,0:T(8,128)(2,1)S(1)}, u32[]{:S(2)}, u32[]{:S(2)}) %collective-permute-start.18) | collective-permute-done | bytes 294944 | tf_op jit(solution)/shard_map/ppermute | solution.py:898
  70.6 0.7 step_1.1
  71.3 1.0 collective-permute-start.20
  72.3 2.0 %collective-permute-start.21 = (bf16[192,384]{1,0:T(8,128)(2,1)S(1)}, bf16[192,384]{1,0:T(8,128)(2,1)S(1)}, u32[]{:S(2)}, u32[]{:S(2)}) collective-permute-start(bf16[192,384]{1,0:T(8,128)(2,1)S(1)} %get-tuple-element.113), channel_id=1, source_target_pairs={{0,2},{1,5},{2,0},{3,7},{4,6},{5,1},{6,4},{7,3},{8,10},{9,13},{10,... | collective-permute-start | bytes 442376 | tf_op jit(solution)/shard_map/ppermute | solution.py:888
  74.3 2.6 %collective-permute-start.22 = (bf16[48,384]{1,0:T(8,128)(2,1)S(1)}, bf16[48,384]{1,0:T(8,128)(2,1)S(1)}, u32[]{:S(2)}, u32[]{:S(2)}) collective-permute-start(bf16[48,384]{1,0:T(8,128)(2,1)S(1)} %get-tuple-element.114.small), channel_id=1, source_target_pairs={{0,4},{1,3},{2,6},{3,1},{4,0},{5,7},{6,2},{7,5},{8,12},{9,11},{10,... | collective-permute-start | bytes 110600 | tf_op jit(solution)/shard_map/ppermute | solution.py:888
  76.9 2.3 %collective-permute-done.22.small_in = bf16[48,384]{1,0:T(8,128)(2,1)S(1)} collective-permute-done((bf16[48,384]{1,0:T(8,128)(2,1)S(1)}, bf16[48,384]{1,0:T(8,128)(2,1)S(1)}, u32[]{:S(2)}, u32[]{:S(2)}) %collective-permute-start.22) | collective-permute-done | bytes 36896 | tf_op jit(solution)/shard_map/ppermute | solution.py:888
  79.2 0.6 step_2.1
  79.8 2.7 %collective-permute-start.23 = (bf16[384,384]{1,0:T(8,128)(2,1)S(1)}, bf16[384,384]{1,0:T(8,128)(2,1)S(1)}, u32[]{:S(2)}, u32[]{:S(2)}) collective-permute-start(bf16[384,384]{1,0:T(8,128)(2,1)S(1)} %get-tuple-element.115.own), channel_id=1, source_target_pairs={{0,4},{1,3},{2,6},{3,1},{4,0},{5,7},{6,2},{7,5},{8,12},{9,11},{10,... | collective-permute-start | bytes 884744 | tf_op jit(solution)/shard_map/ppermute | solution.py:888
  82.5 1.2 %collective-permute-start.24 = (bf16[80,384]{1,0:T(8,128)(2,1)S(1)}, bf16[80,384]{1,0:T(8,128)(2,1)S(1)}, u32[]{:S(2)}, u32[]{:S(2)}) collective-permute-start(bf16[80,384]{1,0:T(8,128)(2,1)S(1)} %get-tuple-element.116.small), channel_id=1, source_target_pairs={{0,16},{1,9},{2,18},{3,11},{4,20},{5,13},{6,22},{7,15},{8,24},{9,1... | collective-permute-start | bytes 184328 | tf_op jit(solution)/shard_map/ppermute | solution.py:898
  83.7 3.0 %collective-permute-done.24.small_in = bf16[80,384]{1,0:T(8,128)(2,1)S(1)} collective-permute-done((bf16[80,384]{1,0:T(8,128)(2,1)S(1)}, bf16[80,384]{1,0:T(8,128)(2,1)S(1)}, u32[]{:S(2)}, u32[]{:S(2)}) %collective-permute-start.24) | collective-permute-done | bytes 61472 | tf_op jit(solution)/shard_map/ppermute | solution.py:898
  86.7 7.4 %collective-permute-done.23.arrived = bf16[384,384]{1,0:T(8,128)(2,1)S(1)} collective-permute-done((bf16[384,384]{1,0:T(8,128)(2,1)S(1)}, bf16[384,384]{1,0:T(8,128)(2,1)S(1)}, u32[]{:S(2)}, u32[]{:S(2)}) %collective-permute-start.23) | collective-permute-done | bytes 294944 | tf_op jit(solution)/shard_map/ppermute | solution.py:888
  94.1 0.6 step_3.1
  94.7 2.2 %collective-permute-start.25 = (bf16[384,384]{1,0:T(8,128)(2,1)S(1)}, bf16[384,384]{1,0:T(8,128)(2,1)S(1)}, u32[]{:S(2)}, u32[]{:S(2)}) collective-permute-start(bf16[384,384]{1,0:T(8,128)(2,1)S(1)} %get-tuple-element.117.own), channel_id=1, source_target_pairs={{0,2},{1,5},{2,0},{3,7},{4,6},{5,1},{6,4},{7,3},{8,10},{9,13},{10,... | collective-permute-start | bytes 884744 | tf_op jit(solution)/shard_map/ppermute | solution.py:888
  96.9 4.7 %collective-permute-done.26.small_in = bf16[144,384]{1,0:T(8,128)(2,1)S(1)} collective-permute-done((bf16[144,384]{1,0:T(8,128)(2,1)S(1)}, bf16[144,384]{1,0:T(8,128)(2,1)S(1)}, u32[]{:S(2)}, u32[]{:S(2)}) %collective-permute-start.26) | collective-permute-done | bytes 110624 | tf_op jit(solution)/shard_map/ppermute | solution.py:898
  101.7 0.9 step_4.1
  102.5 0.5 collective-permute-start.31
  103.1 0.1 collective-permute-start.28
  103.1 0.1 collective-permute-start.27
  103.2 0.7 collective-permute-done.30
  104.0 0.8 fusion.21
  104.9 3.1 %modulation_update.1 = (f32[96,2304]{1,0:T(8,128)}, f32[96,2304]{1,0:T(8,128)}, f32[96,2304]{1,0:T(8,128)}, f32[14,96]{1,0:T(8,128)}, f32[14,96]{1,0:T(8,128)}, /*index=5*/f32[14,96]{1,0:T(8,128)}, f32[8,128]{1,0:T(8,128)S(1)}) custom-call(s32[4]{0:T(128)S(1)} %copy-done.8, bf16[272,384]{1,0:T(8,128)(2,1)S(1)} %get-tuple-element.121.near, ...), custom_call_target="tpu_custom_call" | custom-call | tf_op jit(solution)/shard_map/modulation_update/pallas_call | solution.py:675
  108.0 0.5 step_5.1
  108.5 0.8 collective-permute-start.29
  109.4 1.2 %fusion.16 = (f32[96,1152]{1,0:T(8,128)}, f32[96,1152]{1,0:T(8,128)}, f32[96,1152]{1,0:T(8,128)}) fusion(bf16[96,1152]{1,0:T(8,128)(2,1)S(1)} %copy-done.4, f32[96,384]{1,0:T(8,128)S(1)} %get-tuple-element.146, f32[96,384]{1,0:T(8,128)S(1)} %get-tuple-element.148, f32[96,384]{1,0:T(8,128)S(1)} %get-tuple-element.147, bf16[96,1152]{1,0:T(8,128)(2,1)S(1)} %copy-done.21, ...), kind=kLoop, calls=%fused_computation.24 | loop fusion | flops 2101248 | bytes 2433024 | tf_op jit(solution)/shard_map/sub | solution.py:57
  110.6 1.6 %collective-permute-done.29 = f32[8,128]{1,0:T(8,128)S(1)} collective-permute-done((f32[8,128]{1,0:T(8,128)S(1)}, f32[8,128]{1,0:T(8,128)S(1)}, u32[]{:S(2)}, u32[]{:S(2)}) %collective-permute-start.29) | collective-permute-done | bytes 4128 | tf_op jit(solution)/shard_map/ppermute | solution.py:898
  112.2 0.7 fusion.22
  112.9 2.4 %fusion.11 = (f32[384,384]{1,0:T(8,128)}, f32[384,384]{1,0:T(8,128)}, f32[384,384]{1,0:T(8,128)}, f32[384,384]{1,0:T(8,128)}, f32[384,384]{1,0:T(8,128)}, /*index=5*/f32[384,384]{1,0:T(8,128)}) fusion(bf16[384,384]{1,0:T(8,128)(2,1)S(1)} %copy-done.2, bf16[384,384]{1,0:T(8,128)(2,1)S(1)} %collective-permute-done.31, ...), kind=kLoop, calls=%fused_computation.19 | loop fusion | flops 5603328 | bytes 5898241 | tf_op jit(solution)/shard_map/sub | solution.py:57
  (78 shorter events, 0.3 us)
Async XLA Ops:
  0.7 16.5 %copy-start.9 = (f32[2,384]{1,0:T(2,128)S(1)}, f32[2,384]{1,0:T(2,128)}, u32[]{:S(2)}) copy-start(f32[2,384]{1,0:T(2,128)} %condition.3) | copy-start | bytes 9220
  0.7 16.5 %copy-start.10 = (bf16[14,96]{1,0:T(8,128)(2,1)S(1)}, bf16[14,96]{1,0:T(8,128)(2,1)}, u32[]{:S(2)}) copy-start(bf16[14,96]{1,0:T(8,128)(2,1)} %bias.1) | copy-start | bytes 8068
  0.7 16.5 %copy-start = (bf16[96,2304]{1,0:T(8,128)(2,1)S(1)}, bf16[96,2304]{1,0:T(8,128)(2,1)}, u32[]{:S(2)}) copy-start(bf16[96,2304]{1,0:T(8,128)(2,1)} %weight.5) | copy-start | bytes 1327108
  2.0 15.2 %copy-start.8 = (s32[4]{0:T(128)S(1)}, s32[4]{0:T(128)}, u32[]{:S(2)}) copy-start(s32[4]{0:T(128)} %pad_add_fusion.where) | copy-start | bytes 52
  4.1 24.4 %copy-start.4 = (bf16[96,1152]{1,0:T(8,128)(2,1)S(1)}, bf16[96,1152]{1,0:T(8,128)(2,1)}, u32[]{:S(2)}) copy-start(bf16[96,1152]{1,0:T(8,128)(2,1)} %own_att.1) | copy-start | bytes 663556
  4.1 24.4 %copy-start.7 = (bf16[96,384]{1,0:T(8,128)(2,1)S(1)}, bf16[96,384]{1,0:T(8,128)(2,1)}, u32[]{:S(2)}) copy-start(bf16[96,384]{1,0:T(8,128)(2,1)} %own_proj.1) | copy-start | bytes 221188
  4.1 24.4 %copy-start.14 = (bf16[2,256,384]{2,1,0:T(8,128)(2,1)S(1)}, bf16[2,256,384]{2,1,0:T(8,128)(2,1)}, u32[]{:S(2)}) copy-start(bf16[2,256,384]{2,1,0:T(8,128)(2,1)} %tokens.7) | copy-start | bytes 1179652
  4.1 7.7 %collective-permute-start = (bf16[208,384]{1,0:T(8,128)(2,1)}, bf16[208,384]{1,0:T(8,128)(2,1)S(1)}, u32[]{:S(2)}, u32[]{:S(2)}) collective-permute-start(bf16[208,384]{1,0:T(8,128)(2,1)} %get-tuple-element.76), channel_id=1, source_target_pairs={{0,8},{1,17},{2,10},{3,19},{4,12},{5,21},{6,14},{7,23},{8,0},{9,25... | collective-permute-start | bytes 479240 | tf_op jit(solution)/shard_map/ppermute | solution.py:898
  7.1 6.2 %collective-permute-start.1 = (bf16[208,384]{1,0:T(8,128)(2,1)}, bf16[208,384]{1,0:T(8,128)(2,1)S(1)}, u32[]{:S(2)}, u32[]{:S(2)}) collective-permute-start(bf16[208,384]{1,0:T(8,128)(2,1)} %get-tuple-element.76), channel_id=1, source_target_pairs={{0,16},{1,9},{2,18},{3,11},{4,20},{5,13},{6,22},{7,15},{8,24},{9,1... | collective-permute-start | bytes 479240 | tf_op jit(solution)/shard_map/ppermute | solution.py:898
  11.8 1.5 %collective-permute-start.4 = (bf16[208,384]{1,0:T(8,128)(2,1)S(1)}, bf16[208,384]{1,0:T(8,128)(2,1)S(1)}, u32[]{:S(2)}, u32[]{:S(2)}) collective-permute-start(bf16[208,384]{1,0:T(8,128)(2,1)S(1)} %collective-permute-done.first.n1), channel_id=1, source_target_pairs={{0,1},{1,0},{2,3},{3,2},{4,5},{5,4},{6,7},{7,6},{8,9},{9,8},{10,11... | collective-permute-start | bytes 479240 | tf_op jit(solution)/shard_map/ppermute | solution.py:79
  11.8 5.3 %collective-permute-start.2 = (bf16[208,384]{1,0:T(8,128)(2,1)S(1)}, bf16[208,384]{1,0:T(8,128)(2,1)S(1)}, u32[]{:S(2)}, u32[]{:S(2)}) collective-permute-start(bf16[208,384]{1,0:T(8,128)(2,1)S(1)} %collective-permute-done.first.n1), channel_id=1, source_target_pairs={{0,16},{1,9},{2,18},{3,11},{4,20},{5,13},{6,22},{7,15},{8,24},{9,1... | collective-permute-start | bytes 479240 | tf_op jit(solution)/shard_map/ppermute | solution.py:898
  13.3 10.8 %collective-permute-start.5 = (bf16[384,384]{1,0:T(8,128)(2,1)}, bf16[384,384]{1,0:T(8,128)(2,1)S(1)}, u32[]{:S(2)}, u32[]{:S(2)}) collective-permute-start(bf16[384,384]{1,0:T(8,128)(2,1)} %in_order.2), channel_id=1, source_target_pairs={{0,8},{1,17},{2,10},{3,19},{4,12},{5,21},{6,14},{7,23},{8,0},{9,25... | collective-permute-start | bytes 884744 | tf_op jit(solution)/shard_map/ppermute | solution.py:898
  15.6 11.1 %collective-permute-start.9 = (bf16[384,384]{1,0:T(8,128)(2,1)}, bf16[384,384]{1,0:T(8,128)(2,1)S(1)}, u32[]{:S(2)}, u32[]{:S(2)}) collective-permute-start(bf16[384,384]{1,0:T(8,128)(2,1)} %in_order.2), channel_id=1, source_target_pairs={{0,16},{1,9},{2,18},{3,11},{4,20},{5,13},{6,22},{7,15},{8,24},{9,1... | collective-permute-start | bytes 884744 | tf_op jit(solution)/shard_map/ppermute | solution.py:898
  16.3 10.4 %collective-permute-start.7 = (bf16[208,384]{1,0:T(8,128)(2,1)S(1)}, bf16[208,384]{1,0:T(8,128)(2,1)S(1)}, u32[]{:S(2)}, u32[]{:S(2)}) collective-permute-start(bf16[208,384]{1,0:T(8,128)(2,1)S(1)} %collective-permute-done.1.second.refs_2_.n2), channel_id=1, source_target_pairs={{0,1},{1,0},{2,3},{3,2},{4,5},{5,4},{6,7},{7,6},{8,9},{9,8},{10,11... | collective-permute-start | bytes 479240 | tf_op jit(solution)/shard_map/ppermute | solution.py:79
  17.1 10.1 %collective-permute-start.8 = (bf16[208,384]{1,0:T(8,128)(2,1)S(1)}, bf16[208,384]{1,0:T(8,128)(2,1)S(1)}, u32[]{:S(2)}, u32[]{:S(2)}) collective-permute-start(bf16[208,384]{1,0:T(8,128)(2,1)S(1)} %collective-permute-done.2.last.n3), channel_id=1, source_target_pairs={{0,1},{1,0},{2,3},{3,2},{4,5},{5,4},{6,7},{7,6},{8,9},{9,8},{10,11... | collective-permute-start | bytes 479240 | tf_op jit(solution)/shard_map/ppermute | solution.py:79
  18.2 5.8 %collective-permute-start.3 = (f32[4,2304]{1,0:T(4,128)S(1)}, f32[4,2304]{1,0:T(4,128)S(1)}, u32[]{:S(2)}, u32[]{:S(2)}) collective-permute-start(f32[4,2304]{1,0:T(4,128)S(1)} %get-tuple-element.78), channel_id=1, source_target_pairs={{0,8},{1,17},{2,10},{3,19},{4,12},{5,21},{6,14},{7,23},{8,0},{9,25... | collective-permute-start | bytes 110600 | tf_op jit(solution)/shard_map/ppermute | solution.py:898
  24.6 3.8 %collective-permute-start.6 = (f32[2,2304]{1,0:T(2,128)S(1)}, f32[2,2304]{1,0:T(2,128)S(1)}, u32[]{:S(2)}, u32[]{:S(2)}) collective-permute-start(f32[2,2304]{1,0:T(2,128)S(1)} %get-tuple-element.81), channel_id=1, source_target_pairs={{0,16},{1,9},{2,18},{3,11},{4,20},{5,13},{6,22},{7,15},{8,24},{9,1... | collective-permute-start | bytes 55304 | tf_op jit(solution)/shard_map/ppermute | solution.py:898
  25.7 7.9 %collective-permute-start.10 = (bf16[384,384]{1,0:T(8,128)(2,1)S(1)}, bf16[384,384]{1,0:T(8,128)(2,1)S(1)}, u32[]{:S(2)}, u32[]{:S(2)}) collective-permute-start(bf16[384,384]{1,0:T(8,128)(2,1)S(1)} %get-tuple-element.86.n1), channel_id=1, source_target_pairs={{0,16},{1,9},{2,18},{3,11},{4,20},{5,13},{6,22},{7,15},{8,24},{9,1... | collective-permute-start | bytes 884744 | tf_op jit(solution)/shard_map/ppermute | solution.py:898
  26.7 6.9 %collective-permute-start.11 = (bf16[384,384]{1,0:T(8,128)(2,1)S(1)}, bf16[384,384]{1,0:T(8,128)(2,1)S(1)}, u32[]{:S(2)}, u32[]{:S(2)}) collective-permute-start(bf16[384,384]{1,0:T(8,128)(2,1)S(1)} %get-tuple-element.86.n1), channel_id=1, source_target_pairs={{0,1},{1,0},{2,3},{3,2},{4,5},{5,4},{6,7},{7,6},{8,9},{9,8},{10,11... | collective-permute-start | bytes 884744 | tf_op jit(solution)/shard_map/ppermute | solution.py:79
  26.7 6.9 %collective-permute-start.12 = (bf16[384,384]{1,0:T(8,128)(2,1)S(1)}, bf16[384,384]{1,0:T(8,128)(2,1)S(1)}, u32[]{:S(2)}, u32[]{:S(2)}) collective-permute-start(bf16[384,384]{1,0:T(8,128)(2,1)S(1)} %collective-permute-done.9.n2), channel_id=1, source_target_pairs={{0,1},{1,0},{2,3},{3,2},{4,5},{5,4},{6,7},{7,6},{8,9},{9,8},{10,11... | collective-permute-start | bytes 884744 | tf_op jit(solution)/shard_map/ppermute | solution.py:79
  28.4 6.7 %copy-start.1 = (bf16[384,384]{1,0:T(8,128)(2,1)S(1)}, bf16[384,384]{1,0:T(8,128)(2,1)}, u32[]{:S(2)}) copy-start(bf16[384,384]{1,0:T(8,128)(2,1)} %own_expand.1) | copy-start | bytes 884740
  28.4 6.7 %copy-start.2 = (bf16[384,384]{1,0:T(8,128)(2,1)S(1)}, bf16[384,384]{1,0:T(8,128)(2,1)}, u32[]{:S(2)}) copy-start(bf16[384,384]{1,0:T(8,128)(2,1)} %own_contract.1) | copy-start | bytes 884740
  28.5 6.7 %copy-start.13 = (bf16[2,256,384]{2,1,0:T(8,128)(2,1)S(1)}, bf16[2,256,384]{2,1,0:T(8,128)(2,1)}, u32[]{:S(2)}) copy-start(bf16[2,256,384]{2,1,0:T(8,128)(2,1)} %cotangent.1) | copy-start | bytes 1179652
  32.4 1.2 %copy-start.15 = (bf16[2,6,256,256]{3,2,1,0:T(8,128)(2,1)}, bf16[2,6,256,256]{3,2,1,0:T(8,128)(2,1)S(1)}, u32[]{:S(2)}) copy-start(bf16[2,6,256,256]{3,2,1,0:T(8,128)(2,1)S(1)} %get-tuple-element.90.soft_in) | copy-start | bytes 4718596
  33.6 11.6 %copy-start.16 = (bf16[2,256,1152]{2,1,0:T(8,128)(2,1)}, bf16[2,256,1152]{2,1,0:T(8,128)(2,1)S(1)}, u32[]{:S(2)}) copy-start(bf16[2,256,1152]{2,1,0:T(8,128)(2,1)S(1)} %get-tuple-element.89.joined) | copy-start | bytes 3538948
  33.6 1.6 %collective-permute-start.13 = (bf16[384,384]{1,0:T(8,128)(2,1)S(1)}, bf16[384,384]{1,0:T(8,128)(2,1)S(1)}, u32[]{:S(2)}, u32[]{:S(2)}) collective-permute-start(bf16[384,384]{1,0:T(8,128)(2,1)S(1)} %in_order.3.n3), channel_id=1, source_target_pairs={{0,1},{1,0},{2,3},{3,2},{4,5},{5,4},{6,7},{7,6},{8,9},{9,8},{10,11... | collective-permute-start | bytes 884744 | tf_op jit(solution)/shard_map/ppermute | solution.py:79
  45.0 4.9 %collective-permute-start.14 = (bf16[4,384,384]{2,1,0:T(8,128)(2,1)S(1)}, bf16[4,384,384]{2,1,0:T(8,128)(2,1)S(1)}, u32[]{:S(2)}, u32[]{:S(2)}) collective-permute-start(bf16[4,384,384]{2,1,0:T(8,128)(2,1)S(1)} %get-tuple-element.99), channel_id=1, source_target_pairs={{0,1},{1,0},{2,3},{3,2},{4,5},{5,4},{6,7},{7,6},{8,9},{9,8},{10,11... | collective-permute-start | bytes 3538952 | tf_op jit(solution)/shard_map/ppermute | solution.py:79
  45.1 4.8 %copy-start.3 = (bf16[4,384,384]{2,1,0:T(8,128)(2,1)S(1)}, bf16[4,384,384]{2,1,0:T(8,128)(2,1)}, u32[]{:S(2)}) copy-start(bf16[4,384,384]{2,1,0:T(8,128)(2,1)} %get-tuple-element.98.keep) | copy-start | bytes 3538948
  50.7 9.9 %collective-permute-start.17 = (bf16[2,384,384]{2,1,0:T(8,128)(2,1)S(1)}, bf16[2,384,384]{2,1,0:T(8,128)(2,1)S(1)}, u32[]{:S(2)}, u32[]{:S(2)}) collective-permute-start(bf16[2,384,384]{2,1,0:T(8,128)(2,1)S(1)} %get-tuple-element.100.refs_5_), channel_id=1, source_target_pairs={{0,8},{1,17},{2,10},{3,19},{4,12},{5,21},{6,14},{7,23},{8,0},{9,25... | collective-permute-start | bytes 1769480 | tf_op jit(solution)/shard_map/ppermute | solution.py:898
  58.3 3.6 %collective-permute-start.15 = (bf16[4,192,384]{2,1,0:T(8,128)(2,1)S(1)}, bf16[4,192,384]{2,1,0:T(8,128)(2,1)S(1)}, u32[]{:S(2)}, u32[]{:S(2)}) collective-permute-start(bf16[4,192,384]{2,1,0:T(8,128)(2,1)S(1)} %get-tuple-element.103), channel_id=1, source_target_pairs={{0,1},{1,0},{2,3},{3,2},{4,5},{5,4},{6,7},{7,6},{8,9},{9,8},{10,11... | collective-permute-start | bytes 1769480 | tf_op jit(solution)/shard_map/ppermute | solution.py:79
  60.8 9.8 %collective-permute-start.18 = (bf16[384,384]{1,0:T(8,128)(2,1)S(1)}, bf16[384,384]{1,0:T(8,128)(2,1)S(1)}, u32[]{:S(2)}, u32[]{:S(2)}) collective-permute-start(bf16[384,384]{1,0:T(8,128)(2,1)S(1)} %bitcast.6), channel_id=1, source_target_pairs={{0,16},{1,9},{2,18},{3,11},{4,20},{5,13},{6,22},{7,15},{8,24},{9,1... | collective-permute-start | bytes 884744 | tf_op jit(solution)/shard_map/ppermute | solution.py:898
  62.0 8.6 %collective-permute-start.16 = (bf16[2,192,384]{2,1,0:T(8,128)(2,1)S(1)}, bf16[2,192,384]{2,1,0:T(8,128)(2,1)S(1)}, u32[]{:S(2)}, u32[]{:S(2)}) collective-permute-start(bf16[2,192,384]{2,1,0:T(8,128)(2,1)S(1)} %get-tuple-element.105), channel_id=1, source_target_pairs={{0,8},{1,17},{2,10},{3,19},{4,12},{5,21},{6,14},{7,23},{8,0},{9,25... | collective-permute-start | bytes 884744 | tf_op jit(solution)/shard_map/ppermute | solution.py:898
  63.8 3.8 %collective-permute-start.19 = (bf16[32,384]{1,0:T(8,128)(2,1)S(1)}, bf16[32,384]{1,0:T(8,128)(2,1)S(1)}, u32[]{:S(2)}, u32[]{:S(2)}) collective-permute-start(bf16[32,384]{1,0:T(8,128)(2,1)S(1)} %get-tuple-element.109.small), channel_id=1, source_target_pairs={{0,2},{1,5},{2,0},{3,7},{4,6},{5,1},{6,4},{7,3},{8,10},{9,13},{10,... | collective-permute-start | bytes 73736 | tf_op jit(solution)/shard_map/ppermute | solution.py:888
  71.3 7.9 %collective-permute-start.20 = (bf16[192,384]{1,0:T(8,128)(2,1)S(1)}, bf16[192,384]{1,0:T(8,128)(2,1)S(1)}, u32[]{:S(2)}, u32[]{:S(2)}) collective-permute-start(bf16[192,384]{1,0:T(8,128)(2,1)S(1)} %get-tuple-element.111), channel_id=1, source_target_pairs={{0,16},{1,9},{2,18},{3,11},{4,20},{5,13},{6,22},{7,15},{8,24},{9,1... | collective-permute-start | bytes 442376 | tf_op jit(solution)/shard_map/ppermute | solution.py:898
  72.3 6.9 %collective-permute-start.21 = (bf16[192,384]{1,0:T(8,128)(2,1)S(1)}, bf16[192,384]{1,0:T(8,128)(2,1)S(1)}, u32[]{:S(2)}, u32[]{:S(2)}) collective-permute-start(bf16[192,384]{1,0:T(8,128)(2,1)S(1)} %get-tuple-element.113), channel_id=1, source_target_pairs={{0,2},{1,5},{2,0},{3,7},{4,6},{5,1},{6,4},{7,3},{8,10},{9,13},{10,... | collective-permute-start | bytes 442376 | tf_op jit(solution)/shard_map/ppermute | solution.py:888
  74.3 4.9 %collective-permute-start.22 = (bf16[48,384]{1,0:T(8,128)(2,1)S(1)}, bf16[48,384]{1,0:T(8,128)(2,1)S(1)}, u32[]{:S(2)}, u32[]{:S(2)}) collective-permute-start(bf16[48,384]{1,0:T(8,128)(2,1)S(1)} %get-tuple-element.114.small), channel_id=1, source_target_pairs={{0,4},{1,3},{2,6},{3,1},{4,0},{5,7},{6,2},{7,5},{8,12},{9,11},{10,... | collective-permute-start | bytes 110600 | tf_op jit(solution)/shard_map/ppermute | solution.py:888
  79.8 14.3 %collective-permute-start.23 = (bf16[384,384]{1,0:T(8,128)(2,1)S(1)}, bf16[384,384]{1,0:T(8,128)(2,1)S(1)}, u32[]{:S(2)}, u32[]{:S(2)}) collective-permute-start(bf16[384,384]{1,0:T(8,128)(2,1)S(1)} %get-tuple-element.115.own), channel_id=1, source_target_pairs={{0,4},{1,3},{2,6},{3,1},{4,0},{5,7},{6,2},{7,5},{8,12},{9,11},{10,... | collective-permute-start | bytes 884744 | tf_op jit(solution)/shard_map/ppermute | solution.py:888
  82.5 4.2 %collective-permute-start.24 = (bf16[80,384]{1,0:T(8,128)(2,1)S(1)}, bf16[80,384]{1,0:T(8,128)(2,1)S(1)}, u32[]{:S(2)}, u32[]{:S(2)}) collective-permute-start(bf16[80,384]{1,0:T(8,128)(2,1)S(1)} %get-tuple-element.116.small), channel_id=1, source_target_pairs={{0,16},{1,9},{2,18},{3,11},{4,20},{5,13},{6,22},{7,15},{8,24},{9,1... | collective-permute-start | bytes 184328 | tf_op jit(solution)/shard_map/ppermute | solution.py:898
  94.7 9.3 %copy-start.23 = (bf16[96,384]{1,0:T(8,128)(2,1)S(1)}, bf16[96,384]{1,0:T(8,128)(2,1)}, u32[]{:S(2)}) copy-start(bf16[96,384]{1,0:T(8,128)(2,1)} %param.34) | copy-start | bytes 221188
  94.7 9.3 %copy-start.24 = (bf16[96,384]{1,0:T(8,128)(2,1)S(1)}, bf16[96,384]{1,0:T(8,128)(2,1)}, u32[]{:S(2)}) copy-start(bf16[96,384]{1,0:T(8,128)(2,1)} %param.40) | copy-start | bytes 221188
  94.7 6.9 %collective-permute-start.25 = (bf16[384,384]{1,0:T(8,128)(2,1)S(1)}, bf16[384,384]{1,0:T(8,128)(2,1)S(1)}, u32[]{:S(2)}, u32[]{:S(2)}) collective-permute-start(bf16[384,384]{1,0:T(8,128)(2,1)S(1)} %get-tuple-element.117.own), channel_id=1, source_target_pairs={{0,2},{1,5},{2,0},{3,7},{4,6},{5,1},{6,4},{7,3},{8,10},{9,13},{10,... | collective-permute-start | bytes 884744 | tf_op jit(solution)/shard_map/ppermute | solution.py:888
  96.9 4.7 %collective-permute-start.26 = (bf16[144,384]{1,0:T(8,128)(2,1)S(1)}, bf16[144,384]{1,0:T(8,128)(2,1)S(1)}, u32[]{:S(2)}, u32[]{:S(2)}) collective-permute-start(bf16[144,384]{1,0:T(8,128)(2,1)S(1)} %get-tuple-element.118.small), channel_id=1, source_target_pairs={{0,8},{1,17},{2,10},{3,19},{4,12},{5,21},{6,14},{7,23},{8,0},{9,25... | collective-permute-start | bytes 331784 | tf_op jit(solution)/shard_map/ppermute | solution.py:898
  102.5 1.4 %collective-permute-start.30 = (bf16[192,384]{1,0:T(8,128)(2,1)S(1)}, bf16[192,384]{1,0:T(8,128)(2,1)S(1)}, u32[]{:S(2)}, u32[]{:S(2)}) collective-permute-start(bf16[192,384]{1,0:T(8,128)(2,1)S(1)} %get-tuple-element.124), channel_id=1, source_target_pairs={{0,1},{1,0},{2,3},{3,2},{4,5},{5,4},{6,7},{7,6},{8,9},{9,8},{10,11... | collective-permute-start | bytes 442376 | tf_op jit(solution)/shard_map/ppermute | solution.py:79
  102.5 10.3 %collective-permute-start.31 = (bf16[384,384]{1,0:T(8,128)(2,1)S(1)}, bf16[384,384]{1,0:T(8,128)(2,1)S(1)}, u32[]{:S(2)}, u32[]{:S(2)}) collective-permute-start(bf16[384,384]{1,0:T(8,128)(2,1)S(1)} %get-tuple-element.125), channel_id=1, source_target_pairs={{0,1},{1,0},{2,3},{3,2},{4,5},{5,4},{6,7},{7,6},{8,9},{9,8},{10,11... | collective-permute-start | bytes 884744 | tf_op jit(solution)/shard_map/ppermute | solution.py:79
  103.1 1.8 %collective-permute-start.28 = (bf16[272,384]{1,0:T(8,128)(2,1)S(1)}, bf16[272,384]{1,0:T(8,128)(2,1)S(1)}, u32[]{:S(2)}, u32[]{:S(2)}) collective-permute-start(bf16[272,384]{1,0:T(8,128)(2,1)S(1)} %get-tuple-element.121.near), channel_id=1, source_target_pairs={{0,1},{1,0},{2,3},{3,2},{4,5},{5,4},{6,7},{7,6},{8,9},{9,8},{10,11... | collective-permute-start | bytes 626696 | tf_op jit(solution)/shard_map/ppermute | solution.py:79
  103.1 1.7 %copy-start.5 = (bf16[96,2304]{1,0:T(8,128)(2,1)S(1)}, bf16[96,2304]{1,0:T(8,128)(2,1)}, u32[]{:S(2)}) copy-start(bf16[96,2304]{1,0:T(8,128)(2,1)} %mean.1) | copy-start | bytes 1327108
  103.1 1.7 %copy-start.6 = (bf16[96,2304]{1,0:T(8,128)(2,1)S(1)}, bf16[96,2304]{1,0:T(8,128)(2,1)}, u32[]{:S(2)}) copy-start(bf16[96,2304]{1,0:T(8,128)(2,1)} %square.1) | copy-start | bytes 1327108
  103.1 1.7 %copy-start.11 = (bf16[14,96]{1,0:T(8,128)(2,1)S(1)}, bf16[14,96]{1,0:T(8,128)(2,1)}, u32[]{:S(2)}) copy-start(bf16[14,96]{1,0:T(8,128)(2,1)} %bias_mean.1) | copy-start | bytes 8068
  103.1 1.7 %copy-start.12 = (bf16[14,96]{1,0:T(8,128)(2,1)S(1)}, bf16[14,96]{1,0:T(8,128)(2,1)}, u32[]{:S(2)}) copy-start(bf16[14,96]{1,0:T(8,128)(2,1)} %bias_square.1) | copy-start | bytes 8068
  103.1 4.8 %collective-permute-start.27 = (f32[8,128]{1,0:T(8,128)S(1)}, f32[8,128]{1,0:T(8,128)S(1)}, u32[]{:S(2)}, u32[]{:S(2)}) collective-permute-start(f32[8,128]{1,0:T(8,128)S(1)} %get-tuple-element.120), channel_id=1, source_target_pairs={{0,8},{1,17},{2,10},{3,19},{4,12},{5,21},{6,14},{7,23},{8,0},{9,25... | collective-permute-start | bytes 12296 | tf_op jit(solution)/shard_map/ppermute | solution.py:898
  104.8 4.6 %copy-start.21 = (bf16[96,1152]{1,0:T(8,128)(2,1)S(1)}, bf16[96,1152]{1,0:T(8,128)(2,1)}, u32[]{:S(2)}) copy-start(bf16[96,1152]{1,0:T(8,128)(2,1)} %param.33) | copy-start | bytes 663556
  104.8 4.6 %copy-start.22 = (bf16[96,1152]{1,0:T(8,128)(2,1)S(1)}, bf16[96,1152]{1,0:T(8,128)(2,1)}, u32[]{:S(2)}) copy-start(bf16[96,1152]{1,0:T(8,128)(2,1)} %param.39) | copy-start | bytes 663556
  108.5 3.7 %collective-permute-start.29 = (f32[8,128]{1,0:T(8,128)S(1)}, f32[8,128]{1,0:T(8,128)S(1)}, u32[]{:S(2)}, u32[]{:S(2)}) collective-permute-start(f32[8,128]{1,0:T(8,128)S(1)} %step_5.1), channel_id=1, source_target_pairs={{0,16},{1,9},{2,18},{3,11},{4,20},{5,13},{6,22},{7,15},{8,24},{9,1... | collective-permute-start | bytes 12296 | tf_op jit(solution)/shard_map/ppermute | solution.py:898
  109.4 3.5 %copy-start.17 = (bf16[384,384]{1,0:T(8,128)(2,1)S(1)}, bf16[384,384]{1,0:T(8,128)(2,1)}, u32[]{:S(2)}) copy-start(bf16[384,384]{1,0:T(8,128)(2,1)} %param.36) | copy-start | bytes 884740
  109.4 3.5 %copy-start.18 = (bf16[384,384]{1,0:T(8,128)(2,1)S(1)}, bf16[384,384]{1,0:T(8,128)(2,1)}, u32[]{:S(2)}) copy-start(bf16[384,384]{1,0:T(8,128)(2,1)} %param.42) | copy-start | bytes 884740
  109.4 3.5 %copy-start.19 = (bf16[384,384]{1,0:T(8,128)(2,1)S(1)}, bf16[384,384]{1,0:T(8,128)(2,1)}, u32[]{:S(2)}) copy-start(bf16[384,384]{1,0:T(8,128)(2,1)} %param.41) | copy-start | bytes 884740
  109.4 3.5 %copy-start.20 = (bf16[384,384]{1,0:T(8,128)(2,1)S(1)}, bf16[384,384]{1,0:T(8,128)(2,1)}, u32[]{:S(2)}) copy-start(bf16[384,384]{1,0:T(8,128)(2,1)} %param.35) | copy-start | bytes 884740

commit v5 on v4

--- a/solution.py
+++ b/solution.py
@@ -25,7 +25,7 @@
 D = 384
 SEQ = 256
 QUARTER = D // 4
-VMEM_BYTES = 48 * 1024 * 1024
+VMEM_BYTES = 34 * 1024 * 1024
 LOW = jnp.bfloat16
 SMALL = 32
 BLOCK = 16

time: 115 us -> 113 us (0.983)
  Pallas kernels: 35.4 us -> 33.7 us
  local copies, waits for them, and re-layouts: 1.29 us -> 0.13 us
    pallas_call x2, Pallas kernels: 10.6 us -> 9.1 us  [run_attention_backward(): pl.pallas_call(functools.partial(attention_backward_kernel, slot), grid=(...]
    unnamed x50 -> x44, local copies, waits for them, and re-layouts: 1.27 us -> 0.11 us
  transfers between devices with their start and end apart: 32 -> 32, of which waited for: 14 -> 14; matrix products, arithmetic and copies ran while one was open for 2% -> 2% of each run, Pallas kernels for 17% -> 16%
where the time goes in v5:
time: 113 us
  waiting for transfers between devices  37.3 us (33%)
  starting transfers between devices  34.6 us (31%)
  Pallas kernels  33.7 us (30%)
  other arithmetic  5.69 us (5%)
  between operations  1.73 us (2%)
    ppermute x16, waiting for transfers between devices, swap_pair(): return lax.ppermute(value, ('group', 'replica'), pairs)  23.1 us
    ppermute x16, starting transfers between devices, swap_pair(): return lax.ppermute(value, ('group', 'replica'), pairs)  22.2 us
    ppermute x5, waiting for transfers between devices, swap_plane(): return lax.ppermute(value, 'replica', pairs)  11.9 us
    ppermute x5, starting transfers between devices, swap_plane(): return lax.ppermute(value, 'replica', pairs)  11 us
    pallas_call x1, Pallas kernels, run_feed(): pl.pallas_call(feed_kernel, grid=(2,), in_specs=[SMEM_SPEC] + [whole((2,...  9.6 us
    pallas_call x8, Pallas kernels, small_call(): pl.pallas_call(kernel, grid=(1,), in_specs=[SMEM_SPEC] + [whole(item.shap...  9.32 us
    pallas_call x2, Pallas kernels, run_attention_backward(): pl.pallas_call(functools.partial(attention_backward_kernel, slot), grid=(...  9.1 us
    sub x3, other arithmetic, adam_update(): updated = weight * (1.0 - step_rate * decay_flag * DECAY_RATE) - change  4.37 us
  transfers between devices with their start and end apart: 32, of which 14 were waited for; matrix products, arithmetic and copies ran while one was open for 2% of the time, Pallas kernels for 16%

profile of v5, /device:TPU:0, one launch (start us, length us, event | category | flops | bytes accessed | tf_op | source)
XLA Modules:
  0.0 113.2 jit_solution(622922268887275261)
XLA Ops:
  0.7 0.0 copy-start.8
  1.4 0.6 pad_add_fusion.where
  2.0 2.1 %own_payload.1 = (bf16[208,384]{1,0:T(8,128)(2,1)}, bf16[384,384]{1,0:T(8,128)(2,1)}) custom-call(s32[4]{0:T(128)} %pad_add_fusion.where, f32[2,384]{1,0:T(2,128)} %condition.3, bf16[96,1152]{1,0:T(8,128)(2,1)} %own_att.1, bf16[96,384]{1,0:T(8,128)(2,1)} %own_proj.1, bf16[14,96]{1,0:T(8,128)(2,1)} %bias.1, bf16[384,384]{1,0:T(8,128)(2,1)} %own_expand.1, ...), custom_call_target="tpu_custom_call" | custom-call | tf_op jit(solution)/shard_map/own_payload/pallas_call | solution.py:675
  4.1 3.0 %collective-permute-start = (bf16[208,384]{1,0:T(8,128)(2,1)}, bf16[208,384]{1,0:T(8,128)(2,1)S(1)}, u32[]{:S(2)}, u32[]{:S(2)}) collective-permute-start(bf16[208,384]{1,0:T(8,128)(2,1)} %get-tuple-element.76), channel_id=1, source_target_pairs={{0,8},{1,17},{2,10},{3,19},{4,12},{5,21},{6,14},{7,23},{8,0},{9,25... | collective-permute-start | bytes 479240 | tf_op jit(solution)/shard_map/ppermute | solution.py:898
  7.1 1.5 %collective-permute-start.1 = (bf16[208,384]{1,0:T(8,128)(2,1)}, bf16[208,384]{1,0:T(8,128)(2,1)S(1)}, u32[]{:S(2)}, u32[]{:S(2)}) collective-permute-start(bf16[208,384]{1,0:T(8,128)(2,1)} %get-tuple-element.76), channel_id=1, source_target_pairs={{0,16},{1,9},{2,18},{3,11},{4,20},{5,13},{6,22},{7,15},{8,24},{9,1... | collective-permute-start | bytes 479240 | tf_op jit(solution)/shard_map/ppermute | solution.py:898
  8.6 3.2 %collective-permute-done.first.n1 = bf16[208,384]{1,0:T(8,128)(2,1)S(1)} collective-permute-done((bf16[208,384]{1,0:T(8,128)(2,1)}, bf16[208,384]{1,0:T(8,128)(2,1)S(1)}, u32[]{:S(2)}, u32[]{:S(2)}) %collective-permute-start) | collective-permute-done | bytes 159776 | tf_op jit(solution)/shard_map/ppermute | solution.py:898
  11.8 1.5 %collective-permute-start.2 = (bf16[208,384]{1,0:T(8,128)(2,1)S(1)}, bf16[208,384]{1,0:T(8,128)(2,1)S(1)}, u32[]{:S(2)}, u32[]{:S(2)}) collective-permute-start(bf16[208,384]{1,0:T(8,128)(2,1)S(1)} %collective-permute-done.first.n1), channel_id=1, source_target_pairs={{0,16},{1,9},{2,18},{3,11},{4,20},{5,13},{6,22},{7,15},{8,24},{9,1... | collective-permute-start | bytes 479240 | tf_op jit(solution)/shard_map/ppermute | solution.py:898
  13.3 2.3 %collective-permute-start.5 = (bf16[384,384]{1,0:T(8,128)(2,1)}, bf16[384,384]{1,0:T(8,128)(2,1)S(1)}, u32[]{:S(2)}, u32[]{:S(2)}) collective-permute-start(bf16[384,384]{1,0:T(8,128)(2,1)} %in_order.2), channel_id=1, source_target_pairs={{0,8},{1,17},{2,10},{3,19},{4,12},{5,21},{6,14},{7,23},{8,0},{9,25... | collective-permute-start | bytes 884744 | tf_op jit(solution)/shard_map/ppermute | solution.py:898
  15.6 0.7 collective-permute-start.9
  16.3 0.8 collective-permute-done.2.last.n3
  17.1 0.1 collective-permute-start.8
  17.2 1.0 modulation_partials.1
  18.2 3.3 %collective-permute-start.3 = (f32[4,2304]{1,0:T(4,128)S(1)}, f32[4,2304]{1,0:T(4,128)S(1)}, u32[]{:S(2)}, u32[]{:S(2)}) collective-permute-start(f32[4,2304]{1,0:T(4,128)S(1)} %get-tuple-element.78), channel_id=1, source_target_pairs={{0,8},{1,17},{2,10},{3,19},{4,12},{5,21},{6,14},{7,23},{8,0},{9,25... | collective-permute-start | bytes 110600 | tf_op jit(solution)/shard_map/ppermute | solution.py:898
  21.5 2.5 %collective-permute-done.3.arrived = f32[4,2304]{1,0:T(4,128)S(1)} collective-permute-done((f32[4,2304]{1,0:T(4,128)S(1)}, f32[4,2304]{1,0:T(4,128)S(1)}, u32[]{:S(2)}, u32[]{:S(2)}) %collective-permute-start.3) | collective-permute-done | bytes 36896 | tf_op jit(solution)/shard_map/ppermute | solution.py:898
  24.0 0.6 relay.1
  24.6 1.1 collective-permute-start.6
  25.7 1.0 collective-permute-start.10
  26.7 0.5 collective-permute-start.12
  27.2 1.2 %collective-permute-done.6.arrived = f32[2,2304]{1,0:T(2,128)S(1)} collective-permute-done((f32[2,2304]{1,0:T(2,128)S(1)}, f32[2,2304]{1,0:T(2,128)S(1)}, u32[]{:S(2)}, u32[]{:S(2)}) %collective-permute-start.6) | collective-permute-done | bytes 18464 | tf_op jit(solution)/shard_map/ppermute | solution.py:898
  28.4 0.0 copy-start.1
  28.5 3.9 %attention_forward.1 = (bf16[2,256,1152]{2,1,0:T(8,128)(2,1)S(1)}, bf16[2,6,256,256]{3,2,1,0:T(8,128)(2,1)S(1)}, bf16[2,256,384]{2,1,0:T(8,128)(2,1)S(1)}, f32[2...) custom-call(s32[4]{0:T(128)S(1)} %copy-done.7, ...), custom_call_target="tpu_custom_call" | custom-call | flops 3000000000 | bytes 6000000 | tf_op jit(solution)/shard_map/attention_forward/pallas_call | solution.py:733
  32.4 0.1 collective-permute-start.13
  32.5 1.5 %collective-permute-done.13.f3 = bf16[384,384]{1,0:T(8,128)(2,1)S(1)} collective-permute-done((bf16[384,384]{1,0:T(8,128)(2,1)S(1)}, bf16[384,384]{1,0:T(8,128)(2,1)S(1)}, u32[]{:S(2)}, u32[]{:S(2)}) %collective-permute-start.13) | collective-permute-done | bytes 294944 | tf_op jit(solution)/shard_map/ppermute | solution.py:79
  34.1 9.6 %feed_forward_and_back.1 = (bf16[2,256,384]{2,1,0:T(8,128)(2,1)}, f32[2,256,384]{2,1,0:T(8,128)S(1)}, bf16[4,384,384]{2,1,0:T(8,128)(2,1)S(1)}, bf16[4,384,384]{2,1,0:T(8,128)(2,1)S(1)}, f32[16,384]{1,0:T(8,128)S(1)}) custom-call(s32[4]{0:T(128)S(1)} %copy-done.7, bf16[2,256,384]{2,1,0:T(8,128)(2,1)S(1)} %get-tuple-element.83.mixed, ...), custom_call_target="tpu_custom_call" | custom-call | flops 8000000000 | bytes 10000000 | tf_op jit(solution)/shard_map/feed_forward_and_back/pallas_call | solution.py:773
  43.7 0.1 collective-permute-start.14
  43.8 4.0 %attention_backward.2 = (bf16[2,256,384]{2,1,0:T(8,128)(2,1)}, bf16[256,1152]{1,0:T(8,128)(2,1)S(1)}, bf16[256,384]{1,0:T(8,128)(2,1)S(1)}, bf16[256,384]{1,0:T(8,128)(2,1)S(1)}, f32[32,384]{1,0:T(8,128)S(1)}) custom-call(s32[4]{0:T(128)S(1)} %copy-done.7, bf16[2,256,384]{2,1,0:T(8,128)(2,1)S(1)} %copy-done.13, ...), custom_call_target="tpu_custom_call" | custom-call | flops 4000000000 | bytes 8000000 | tf_op jit(solution)/shard_map/attention_backward/pallas_call | solution.py:848
  47.9 0.8 sum_and_split.3
  48.7 1.7 %collective-permute-start.17 = (bf16[2,384,384]{2,1,0:T(8,128)(2,1)S(1)}, bf16[2,384,384]{2,1,0:T(8,128)(2,1)S(1)}, u32[]{:S(2)}, u32[]{:S(2)}) collective-permute-start(bf16[2,384,384]{2,1,0:T(8,128)(2,1)S(1)} %get-tuple-element.100.refs_5_), channel_id=1, source_target_pairs={{0,8},{1,17},{2,10},{3,19},{4,12},{5,21},{6,14},{7,23},{8,0},{9,25... | collective-permute-start | bytes 1769480 | tf_op jit(solution)/shard_map/ppermute | solution.py:898
  50.4 5.1 %attention_backward.3 = (bf16[2,256,384]{2,1,0:T(8,128)(2,1)}, bf16[4,192,384]{2,1,0:T(8,128)(2,1)S(1)}, bf16[4,192,384]{2,1,0:T(8,128)(2,1)S(1)}, bf16[32,384]{1,0:T(8,128)(2,1)S(1)}) custom-call(s32[4]{0:T(128)S(1)} %copy-done.7, bf16[2,256,384]{2,1,0:T(8,128)(2,1)S(1)} %copy-done.13, ...), custom_call_target="tpu_custom_call", output_to_operand_aliasing={{0}: (15, {})} | custom-call | flops 4000000000 | bytes 8000000 | tf_op jit(solution)/shard_map/attention_backward/pallas_call | solution.py:848
  55.5 3.1 %collective-permute-done.17.arrived = bf16[2,384,384]{2,1,0:T(8,128)(2,1)S(1)} collective-permute-done((bf16[2,384,384]{2,1,0:T(8,128)(2,1)S(1)}, bf16[2,384,384]{2,1,0:T(8,128)(2,1)S(1)}, u32[]{:S(2)}, u32[]{:S(2)}) %collective-permute-start.17) | collective-permute-done | bytes 589856 | tf_op jit(solution)/shard_map/ppermute | solution.py:898
  58.6 0.1 sum_and_split.5
  58.7 1.1 collective-permute-start.18
  59.8 0.1 sum_and_split.4
  60.0 1.8 %collective-permute-start.16 = (bf16[2,192,384]{2,1,0:T(8,128)(2,1)S(1)}, bf16[2,192,384]{2,1,0:T(8,128)(2,1)S(1)}, u32[]{:S(2)}, u32[]{:S(2)}) collective-permute-start(bf16[2,192,384]{2,1,0:T(8,128)(2,1)S(1)} %get-tuple-element.105), channel_id=1, source_target_pairs={{0,8},{1,17},{2,10},{3,19},{4,12},{5,21},{6,14},{7,23},{8,0},{9,25... | collective-permute-start | bytes 884744 | tf_op jit(solution)/shard_map/ppermute | solution.py:898
  61.7 1.6 %collective-permute-start.19 = (bf16[32,384]{1,0:T(8,128)(2,1)S(1)}, bf16[32,384]{1,0:T(8,128)(2,1)S(1)}, u32[]{:S(2)}, u32[]{:S(2)}) collective-permute-start(bf16[32,384]{1,0:T(8,128)(2,1)S(1)} %get-tuple-element.109.small), channel_id=1, source_target_pairs={{0,2},{1,5},{2,0},{3,7},{4,6},{5,1},{6,4},{7,3},{8,10},{9,13},{10,... | collective-permute-start | bytes 73736 | tf_op jit(solution)/shard_map/ppermute | solution.py:888
  63.3 2.2 %collective-permute-done.19.small_in = bf16[32,384]{1,0:T(8,128)(2,1)S(1)} collective-permute-done((bf16[32,384]{1,0:T(8,128)(2,1)S(1)}, bf16[32,384]{1,0:T(8,128)(2,1)S(1)}, u32[]{:S(2)}, u32[]{:S(2)}) %collective-permute-start.19) | collective-permute-done | bytes 24608 | tf_op jit(solution)/shard_map/ppermute | solution.py:888
  65.6 2.9 %collective-permute-done.18.feed_in = bf16[384,384]{1,0:T(8,128)(2,1)S(1)} collective-permute-done((bf16[384,384]{1,0:T(8,128)(2,1)S(1)}, bf16[384,384]{1,0:T(8,128)(2,1)S(1)}, u32[]{:S(2)}, u32[]{:S(2)}) %collective-permute-start.18) | collective-permute-done | bytes 294944 | tf_op jit(solution)/shard_map/ppermute | solution.py:898
  68.5 0.7 step_1.1
  69.2 1.0 collective-permute-start.20
  70.3 2.0 %collective-permute-start.21 = (bf16[192,384]{1,0:T(8,128)(2,1)S(1)}, bf16[192,384]{1,0:T(8,128)(2,1)S(1)}, u32[]{:S(2)}, u32[]{:S(2)}) collective-permute-start(bf16[192,384]{1,0:T(8,128)(2,1)S(1)} %get-tuple-element.113), channel_id=1, source_target_pairs={{0,2},{1,5},{2,0},{3,7},{4,6},{5,1},{6,4},{7,3},{8,10},{9,13},{10,... | collective-permute-start | bytes 442376 | tf_op jit(solution)/shard_map/ppermute | solution.py:888
  72.3 2.6 %collective-permute-start.22 = (bf16[48,384]{1,0:T(8,128)(2,1)S(1)}, bf16[48,384]{1,0:T(8,128)(2,1)S(1)}, u32[]{:S(2)}, u32[]{:S(2)}) collective-permute-start(bf16[48,384]{1,0:T(8,128)(2,1)S(1)} %get-tuple-element.114.small), channel_id=1, source_target_pairs={{0,4},{1,3},{2,6},{3,1},{4,0},{5,7},{6,2},{7,5},{8,12},{9,11},{10,... | collective-permute-start | bytes 110600 | tf_op jit(solution)/shard_map/ppermute | solution.py:888
  74.9 2.3 %collective-permute-done.22.small_in = bf16[48,384]{1,0:T(8,128)(2,1)S(1)} collective-permute-done((bf16[48,384]{1,0:T(8,128)(2,1)S(1)}, bf16[48,384]{1,0:T(8,128)(2,1)S(1)}, u32[]{:S(2)}, u32[]{:S(2)}) %collective-permute-start.22) | collective-permute-done | bytes 36896 | tf_op jit(solution)/shard_map/ppermute | solution.py:888
  77.2 0.6 step_2.1
  77.8 2.6 %collective-permute-start.23 = (bf16[384,384]{1,0:T(8,128)(2,1)S(1)}, bf16[384,384]{1,0:T(8,128)(2,1)S(1)}, u32[]{:S(2)}, u32[]{:S(2)}) collective-permute-start(bf16[384,384]{1,0:T(8,128)(2,1)S(1)} %get-tuple-element.115.own), channel_id=1, source_target_pairs={{0,4},{1,3},{2,6},{3,1},{4,0},{5,7},{6,2},{7,5},{8,12},{9,11},{10,... | collective-permute-start | bytes 884744 | tf_op jit(solution)/shard_map/ppermute | solution.py:888
  80.4 1.2 %collective-permute-start.24 = (bf16[80,384]{1,0:T(8,128)(2,1)S(1)}, bf16[80,384]{1,0:T(8,128)(2,1)S(1)}, u32[]{:S(2)}, u32[]{:S(2)}) collective-permute-start(bf16[80,384]{1,0:T(8,128)(2,1)S(1)} %get-tuple-element.116.small), channel_id=1, source_target_pairs={{0,16},{1,9},{2,18},{3,11},{4,20},{5,13},{6,22},{7,15},{8,24},{9,1... | collective-permute-start | bytes 184328 | tf_op jit(solution)/shard_map/ppermute | solution.py:898
  81.6 3.0 %collective-permute-done.24.small_in = bf16[80,384]{1,0:T(8,128)(2,1)S(1)} collective-permute-done((bf16[80,384]{1,0:T(8,128)(2,1)S(1)}, bf16[80,384]{1,0:T(8,128)(2,1)S(1)}, u32[]{:S(2)}, u32[]{:S(2)}) %collective-permute-start.24) | collective-permute-done | bytes 61472 | tf_op jit(solution)/shard_map/ppermute | solution.py:898
  84.6 7.4 %collective-permute-done.23.arrived = bf16[384,384]{1,0:T(8,128)(2,1)S(1)} collective-permute-done((bf16[384,384]{1,0:T(8,128)(2,1)S(1)}, bf16[384,384]{1,0:T(8,128)(2,1)S(1)}, u32[]{:S(2)}, u32[]{:S(2)}) %collective-permute-start.23) | collective-permute-done | bytes 294944 | tf_op jit(solution)/shard_map/ppermute | solution.py:888
  92.0 0.6 step_3.1
  92.7 0.0 copy-start.21
  92.7 2.1 %collective-permute-start.25 = (bf16[384,384]{1,0:T(8,128)(2,1)S(1)}, bf16[384,384]{1,0:T(8,128)(2,1)S(1)}, u32[]{:S(2)}, u32[]{:S(2)}) collective-permute-start(bf16[384,384]{1,0:T(8,128)(2,1)S(1)} %get-tuple-element.117.own), channel_id=1, source_target_pairs={{0,2},{1,5},{2,0},{3,7},{4,6},{5,1},{6,4},{7,3},{8,10},{9,13},{10,... | collective-permute-start | bytes 884744 | tf_op jit(solution)/shard_map/ppermute | solution.py:888
  94.8 4.7 %collective-permute-done.26.small_in = bf16[144,384]{1,0:T(8,128)(2,1)S(1)} collective-permute-done((bf16[144,384]{1,0:T(8,128)(2,1)S(1)}, bf16[144,384]{1,0:T(8,128)(2,1)S(1)}, u32[]{:S(2)}, u32[]{:S(2)}) %collective-permute-start.26) | collective-permute-done | bytes 110624 | tf_op jit(solution)/shard_map/ppermute | solution.py:898
  99.6 0.9 step_4.1
  100.5 0.5 collective-permute-start.31
  101.0 0.1 collective-permute-start.28
  101.1 0.1 collective-permute-start.27
  101.1 0.7 collective-permute-done.30
  101.9 0.8 fusion.21
  102.8 3.1 %modulation_update.1 = (f32[96,2304]{1,0:T(8,128)}, f32[96,2304]{1,0:T(8,128)}, f32[96,2304]{1,0:T(8,128)}, f32[14,96]{1,0:T(8,128)}, f32[14,96]{1,0:T(8,128)}, /*index=5*/f32[14,96]{1,0:T(8,128)}, f32[8,128]{1,0:T(8,128)S(1)}) custom-call(s32[4]{0:T(128)S(1)} %copy-done.7, bf16[272,384]{1,0:T(8,128)(2,1)S(1)} %get-tuple-element.121.near, ...), custom_call_target="tpu_custom_call" | custom-call | tf_op jit(solution)/shard_map/modulation_update/pallas_call | solution.py:675
  105.9 0.5 step_5.1
  106.5 0.9 collective-permute-start.29
  107.4 1.2 %fusion.16 = (f32[96,1152]{1,0:T(8,128)}, f32[96,1152]{1,0:T(8,128)}, f32[96,1152]{1,0:T(8,128)}) fusion(bf16[96,1152]{1,0:T(8,128)(2,1)S(1)} %copy-done.3, f32[96,384]{1,0:T(8,128)S(1)} %get-tuple-element.146, f32[96,384]{1,0:T(8,128)S(1)} %get-tuple-element.148, f32[96,384]{1,0:T(8,128)S(1)} %get-tuple-element.147, bf16[96,1152]{1,0:T(8,128)(2,1)S(1)} %copy-done.18, ...), kind=kLoop, calls=%fused_computation.24 | loop fusion | flops 2101248 | bytes 2433024 | tf_op jit(solution)/shard_map/sub | solution.py:57
  108.6 1.6 %collective-permute-done.29 = f32[8,128]{1,0:T(8,128)S(1)} collective-permute-done((f32[8,128]{1,0:T(8,128)S(1)}, f32[8,128]{1,0:T(8,128)S(1)}, u32[]{:S(2)}, u32[]{:S(2)}) %collective-permute-start.29) | collective-permute-done | bytes 4128 | tf_op jit(solution)/shard_map/ppermute | solution.py:898
  110.2 0.7 fusion.22
  110.9 2.4 %fusion.11 = (f32[384,384]{1,0:T(8,128)}, f32[384,384]{1,0:T(8,128)}, f32[384,384]{1,0:T(8,128)}, f32[384,384]{1,0:T(8,128)}, f32[384,384]{1,0:T(8,128)}, /*index=5*/f32[384,384]{1,0:T(8,128)}) fusion(bf16[384,384]{1,0:T(8,128)(2,1)S(1)} %copy-done.2, bf16[384,384]{1,0:T(8,128)(2,1)S(1)} %collective-permute-done.31, ...), kind=kLoop, calls=%fused_computation.19 | loop fusion | flops 5603328 | bytes 5898241 | tf_op jit(solution)/shard_map/sub | solution.py:57
  (72 shorter events, 0.2 us)
Async XLA Ops:
  0.7 16.5 %copy-start.8 = (f32[2,384]{1,0:T(2,128)S(1)}, f32[2,384]{1,0:T(2,128)}, u32[]{:S(2)}) copy-start(f32[2,384]{1,0:T(2,128)} %condition.3) | copy-start | bytes 9220
  0.7 16.5 %copy-start.9 = (bf16[14,96]{1,0:T(8,128)(2,1)S(1)}, bf16[14,96]{1,0:T(8,128)(2,1)}, u32[]{:S(2)}) copy-start(bf16[14,96]{1,0:T(8,128)(2,1)} %bias.1) | copy-start | bytes 8068
  0.7 16.5 %copy-start = (bf16[96,2304]{1,0:T(8,128)(2,1)S(1)}, bf16[96,2304]{1,0:T(8,128)(2,1)}, u32[]{:S(2)}) copy-start(bf16[96,2304]{1,0:T(8,128)(2,1)} %weight.5) | copy-start | bytes 1327108
  2.0 15.2 %copy-start.7 = (s32[4]{0:T(128)S(1)}, s32[4]{0:T(128)}, u32[]{:S(2)}) copy-start(s32[4]{0:T(128)} %pad_add_fusion.where) | copy-start | bytes 52
  4.1 24.4 %copy-start.3 = (bf16[96,1152]{1,0:T(8,128)(2,1)S(1)}, bf16[96,1152]{1,0:T(8,128)(2,1)}, u32[]{:S(2)}) copy-start(bf16[96,1152]{1,0:T(8,128)(2,1)} %own_att.1) | copy-start | bytes 663556
  4.1 24.4 %copy-start.6 = (bf16[96,384]{1,0:T(8,128)(2,1)S(1)}, bf16[96,384]{1,0:T(8,128)(2,1)}, u32[]{:S(2)}) copy-start(bf16[96,384]{1,0:T(8,128)(2,1)} %own_proj.1) | copy-start | bytes 221188
  4.1 24.4 %copy-start.13 = (bf16[2,256,384]{2,1,0:T(8,128)(2,1)S(1)}, bf16[2,256,384]{2,1,0:T(8,128)(2,1)}, u32[]{:S(2)}) copy-start(bf16[2,256,384]{2,1,0:T(8,128)(2,1)} %tokens.7) | copy-start | bytes 1179652
  4.1 7.7 %collective-permute-start = (bf16[208,384]{1,0:T(8,128)(2,1)}, bf16[208,384]{1,0:T(8,128)(2,1)S(1)}, u32[]{:S(2)}, u32[]{:S(2)}) collective-permute-start(bf16[208,384]{1,0:T(8,128)(2,1)} %get-tuple-element.76), channel_id=1, source_target_pairs={{0,8},{1,17},{2,10},{3,19},{4,12},{5,21},{6,14},{7,23},{8,0},{9,25... | collective-permute-start | bytes 479240 | tf_op jit(solution)/shard_map/ppermute | solution.py:898
  7.1 6.2 %collective-permute-start.1 = (bf16[208,384]{1,0:T(8,128)(2,1)}, bf16[208,384]{1,0:T(8,128)(2,1)S(1)}, u32[]{:S(2)}, u32[]{:S(2)}) collective-permute-start(bf16[208,384]{1,0:T(8,128)(2,1)} %get-tuple-element.76), channel_id=1, source_target_pairs={{0,16},{1,9},{2,18},{3,11},{4,20},{5,13},{6,22},{7,15},{8,24},{9,1... | collective-permute-start | bytes 479240 | tf_op jit(solution)/shard_map/ppermute | solution.py:898
  11.8 1.5 %collective-permute-start.4 = (bf16[208,384]{1,0:T(8,128)(2,1)S(1)}, bf16[208,384]{1,0:T(8,128)(2,1)S(1)}, u32[]{:S(2)}, u32[]{:S(2)}) collective-permute-start(bf16[208,384]{1,0:T(8,128)(2,1)S(1)} %collective-permute-done.first.n1), channel_id=1, source_target_pairs={{0,1},{1,0},{2,3},{3,2},{4,5},{5,4},{6,7},{7,6},{8,9},{9,8},{10,11... | collective-permute-start | bytes 479240 | tf_op jit(solution)/shard_map/ppermute | solution.py:79
  11.8 5.3 %collective-permute-start.2 = (bf16[208,384]{1,0:T(8,128)(2,1)S(1)}, bf16[208,384]{1,0:T(8,128)(2,1)S(1)}, u32[]{:S(2)}, u32[]{:S(2)}) collective-permute-start(bf16[208,384]{1,0:T(8,128)(2,1)S(1)} %collective-permute-done.first.n1), channel_id=1, source_target_pairs={{0,16},{1,9},{2,18},{3,11},{4,20},{5,13},{6,22},{7,15},{8,24},{9,1... | collective-permute-start | bytes 479240 | tf_op jit(solution)/shard_map/ppermute | solution.py:898
  13.3 10.8 %collective-permute-start.5 = (bf16[384,384]{1,0:T(8,128)(2,1)}, bf16[384,384]{1,0:T(8,128)(2,1)S(1)}, u32[]{:S(2)}, u32[]{:S(2)}) collective-permute-start(bf16[384,384]{1,0:T(8,128)(2,1)} %in_order.2), channel_id=1, source_target_pairs={{0,8},{1,17},{2,10},{3,19},{4,12},{5,21},{6,14},{7,23},{8,0},{9,25... | collective-permute-start | bytes 884744 | tf_op jit(solution)/shard_map/ppermute | solution.py:898
  15.6 11.1 %collective-permute-start.9 = (bf16[384,384]{1,0:T(8,128)(2,1)}, bf16[384,384]{1,0:T(8,128)(2,1)S(1)}, u32[]{:S(2)}, u32[]{:S(2)}) collective-permute-start(bf16[384,384]{1,0:T(8,128)(2,1)} %in_order.2), channel_id=1, source_target_pairs={{0,16},{1,9},{2,18},{3,11},{4,20},{5,13},{6,22},{7,15},{8,24},{9,1... | collective-permute-start | bytes 884744 | tf_op jit(solution)/shard_map/ppermute | solution.py:898
  16.3 10.4 %collective-permute-start.7 = (bf16[208,384]{1,0:T(8,128)(2,1)S(1)}, bf16[208,384]{1,0:T(8,128)(2,1)S(1)}, u32[]{:S(2)}, u32[]{:S(2)}) collective-permute-start(bf16[208,384]{1,0:T(8,128)(2,1)S(1)} %collective-permute-done.1.second.refs_2_.n2), channel_id=1, source_target_pairs={{0,1},{1,0},{2,3},{3,2},{4,5},{5,4},{6,7},{7,6},{8,9},{9,8},{10,11... | collective-permute-start | bytes 479240 | tf_op jit(solution)/shard_map/ppermute | solution.py:79
  17.1 10.1 %collective-permute-start.8 = (bf16[208,384]{1,0:T(8,128)(2,1)S(1)}, bf16[208,384]{1,0:T(8,128)(2,1)S(1)}, u32[]{:S(2)}, u32[]{:S(2)}) collective-permute-start(bf16[208,384]{1,0:T(8,128)(2,1)S(1)} %collective-permute-done.2.last.n3), channel_id=1, source_target_pairs={{0,1},{1,0},{2,3},{3,2},{4,5},{5,4},{6,7},{7,6},{8,9},{9,8},{10,11... | collective-permute-start | bytes 479240 | tf_op jit(solution)/shard_map/ppermute | solution.py:79
  18.2 5.8 %collective-permute-start.3 = (f32[4,2304]{1,0:T(4,128)S(1)}, f32[4,2304]{1,0:T(4,128)S(1)}, u32[]{:S(2)}, u32[]{:S(2)}) collective-permute-start(f32[4,2304]{1,0:T(4,128)S(1)} %get-tuple-element.78), channel_id=1, source_target_pairs={{0,8},{1,17},{2,10},{3,19},{4,12},{5,21},{6,14},{7,23},{8,0},{9,25... | collective-permute-start | bytes 110600 | tf_op jit(solution)/shard_map/ppermute | solution.py:898
  24.6 3.8 %collective-permute-start.6 = (f32[2,2304]{1,0:T(2,128)S(1)}, f32[2,2304]{1,0:T(2,128)S(1)}, u32[]{:S(2)}, u32[]{:S(2)}) collective-permute-start(f32[2,2304]{1,0:T(2,128)S(1)} %get-tuple-element.81), channel_id=1, source_target_pairs={{0,16},{1,9},{2,18},{3,11},{4,20},{5,13},{6,22},{7,15},{8,24},{9,1... | collective-permute-start | bytes 55304 | tf_op jit(solution)/shard_map/ppermute | solution.py:898
  25.7 6.7 %collective-permute-start.10 = (bf16[384,384]{1,0:T(8,128)(2,1)S(1)}, bf16[384,384]{1,0:T(8,128)(2,1)S(1)}, u32[]{:S(2)}, u32[]{:S(2)}) collective-permute-start(bf16[384,384]{1,0:T(8,128)(2,1)S(1)} %get-tuple-element.86.n1), channel_id=1, source_target_pairs={{0,16},{1,9},{2,18},{3,11},{4,20},{5,13},{6,22},{7,15},{8,24},{9,1... | collective-permute-start | bytes 884744 | tf_op jit(solution)/shard_map/ppermute | solution.py:898
  26.7 5.8 %collective-permute-start.11 = (bf16[384,384]{1,0:T(8,128)(2,1)S(1)}, bf16[384,384]{1,0:T(8,128)(2,1)S(1)}, u32[]{:S(2)}, u32[]{:S(2)}) collective-permute-start(bf16[384,384]{1,0:T(8,128)(2,1)S(1)} %get-tuple-element.86.n1), channel_id=1, source_target_pairs={{0,1},{1,0},{2,3},{3,2},{4,5},{5,4},{6,7},{7,6},{8,9},{9,8},{10,11... | collective-permute-start | bytes 884744 | tf_op jit(solution)/shard_map/ppermute | solution.py:79
  26.7 5.8 %collective-permute-start.12 = (bf16[384,384]{1,0:T(8,128)(2,1)S(1)}, bf16[384,384]{1,0:T(8,128)(2,1)S(1)}, u32[]{:S(2)}, u32[]{:S(2)}) collective-permute-start(bf16[384,384]{1,0:T(8,128)(2,1)S(1)} %collective-permute-done.9.n2), channel_id=1, source_target_pairs={{0,1},{1,0},{2,3},{3,2},{4,5},{5,4},{6,7},{7,6},{8,9},{9,8},{10,11... | collective-permute-start | bytes 884744 | tf_op jit(solution)/shard_map/ppermute | solution.py:79
  28.4 5.7 %copy-start.1 = (bf16[384,384]{1,0:T(8,128)(2,1)S(1)}, bf16[384,384]{1,0:T(8,128)(2,1)}, u32[]{:S(2)}) copy-start(bf16[384,384]{1,0:T(8,128)(2,1)} %own_expand.1) | copy-start | bytes 884740
  28.4 5.6 %copy-start.2 = (bf16[384,384]{1,0:T(8,128)(2,1)S(1)}, bf16[384,384]{1,0:T(8,128)(2,1)}, u32[]{:S(2)}) copy-start(bf16[384,384]{1,0:T(8,128)(2,1)} %own_contract.1) | copy-start | bytes 884740
  28.5 5.6 %copy-start.12 = (bf16[2,256,384]{2,1,0:T(8,128)(2,1)S(1)}, bf16[2,256,384]{2,1,0:T(8,128)(2,1)}, u32[]{:S(2)}) copy-start(bf16[2,256,384]{2,1,0:T(8,128)(2,1)} %cotangent.1) | copy-start | bytes 1179652
  32.4 1.6 %collective-permute-start.13 = (bf16[384,384]{1,0:T(8,128)(2,1)S(1)}, bf16[384,384]{1,0:T(8,128)(2,1)S(1)}, u32[]{:S(2)}, u32[]{:S(2)}) collective-permute-start(bf16[384,384]{1,0:T(8,128)(2,1)S(1)} %in_order.3.n3), channel_id=1, source_target_pairs={{0,1},{1,0},{2,3},{3,2},{4,5},{5,4},{6,7},{7,6},{8,9},{9,8},{10,11... | collective-permute-start | bytes 884744 | tf_op jit(solution)/shard_map/ppermute | solution.py:79
  43.7 4.2 %collective-permute-start.14 = (bf16[4,384,384]{2,1,0:T(8,128)(2,1)S(1)}, bf16[4,384,384]{2,1,0:T(8,128)(2,1)S(1)}, u32[]{:S(2)}, u32[]{:S(2)}) collective-permute-start(bf16[4,384,384]{2,1,0:T(8,128)(2,1)S(1)} %get-tuple-element.99), channel_id=1, source_target_pairs={{0,1},{1,0},{2,3},{3,2},{4,5},{5,4},{6,7},{7,6},{8,9},{9,8},{10,11... | collective-permute-start | bytes 3538952 | tf_op jit(solution)/shard_map/ppermute | solution.py:79
  48.7 9.9 %collective-permute-start.17 = (bf16[2,384,384]{2,1,0:T(8,128)(2,1)S(1)}, bf16[2,384,384]{2,1,0:T(8,128)(2,1)S(1)}, u32[]{:S(2)}, u32[]{:S(2)}) collective-permute-start(bf16[2,384,384]{2,1,0:T(8,128)(2,1)S(1)} %get-tuple-element.100.refs_5_), channel_id=1, source_target_pairs={{0,8},{1,17},{2,10},{3,19},{4,12},{5,21},{6,14},{7,23},{8,0},{9,25... | collective-permute-start | bytes 1769480 | tf_op jit(solution)/shard_map/ppermute | solution.py:898
  55.5 4.3 %collective-permute-start.15 = (bf16[4,192,384]{2,1,0:T(8,128)(2,1)S(1)}, bf16[4,192,384]{2,1,0:T(8,128)(2,1)S(1)}, u32[]{:S(2)}, u32[]{:S(2)}) collective-permute-start(bf16[4,192,384]{2,1,0:T(8,128)(2,1)S(1)} %get-tuple-element.103), channel_id=1, source_target_pairs={{0,1},{1,0},{2,3},{3,2},{4,5},{5,4},{6,7},{7,6},{8,9},{9,8},{10,11... | collective-permute-start | bytes 1769480 | tf_op jit(solution)/shard_map/ppermute | solution.py:79
  58.7 9.8 %collective-permute-start.18 = (bf16[384,384]{1,0:T(8,128)(2,1)S(1)}, bf16[384,384]{1,0:T(8,128)(2,1)S(1)}, u32[]{:S(2)}, u32[]{:S(2)}) collective-permute-start(bf16[384,384]{1,0:T(8,128)(2,1)S(1)} %bitcast.6), channel_id=1, source_target_pairs={{0,16},{1,9},{2,18},{3,11},{4,20},{5,13},{6,22},{7,15},{8,24},{9,1... | collective-permute-start | bytes 884744 | tf_op jit(solution)/shard_map/ppermute | solution.py:898
  60.0 8.6 %collective-permute-start.16 = (bf16[2,192,384]{2,1,0:T(8,128)(2,1)S(1)}, bf16[2,192,384]{2,1,0:T(8,128)(2,1)S(1)}, u32[]{:S(2)}, u32[]{:S(2)}) collective-permute-start(bf16[2,192,384]{2,1,0:T(8,128)(2,1)S(1)} %get-tuple-element.105), channel_id=1, source_target_pairs={{0,8},{1,17},{2,10},{3,19},{4,12},{5,21},{6,14},{7,23},{8,0},{9,25... | collective-permute-start | bytes 884744 | tf_op jit(solution)/shard_map/ppermute | solution.py:898
  61.7 3.8 %collective-permute-start.19 = (bf16[32,384]{1,0:T(8,128)(2,1)S(1)}, bf16[32,384]{1,0:T(8,128)(2,1)S(1)}, u32[]{:S(2)}, u32[]{:S(2)}) collective-permute-start(bf16[32,384]{1,0:T(8,128)(2,1)S(1)} %get-tuple-element.109.small), channel_id=1, source_target_pairs={{0,2},{1,5},{2,0},{3,7},{4,6},{5,1},{6,4},{7,3},{8,10},{9,13},{10,... | collective-permute-start | bytes 73736 | tf_op jit(solution)/shard_map/ppermute | solution.py:888
  69.2 7.9 %collective-permute-start.20 = (bf16[192,384]{1,0:T(8,128)(2,1)S(1)}, bf16[192,384]{1,0:T(8,128)(2,1)S(1)}, u32[]{:S(2)}, u32[]{:S(2)}) collective-permute-start(bf16[192,384]{1,0:T(8,128)(2,1)S(1)} %get-tuple-element.111), channel_id=1, source_target_pairs={{0,16},{1,9},{2,18},{3,11},{4,20},{5,13},{6,22},{7,15},{8,24},{9,1... | collective-permute-start | bytes 442376 | tf_op jit(solution)/shard_map/ppermute | solution.py:898
  70.3 6.9 %collective-permute-start.21 = (bf16[192,384]{1,0:T(8,128)(2,1)S(1)}, bf16[192,384]{1,0:T(8,128)(2,1)S(1)}, u32[]{:S(2)}, u32[]{:S(2)}) collective-permute-start(bf16[192,384]{1,0:T(8,128)(2,1)S(1)} %get-tuple-element.113), channel_id=1, source_target_pairs={{0,2},{1,5},{2,0},{3,7},{4,6},{5,1},{6,4},{7,3},{8,10},{9,13},{10,... | collective-permute-start | bytes 442376 | tf_op jit(solution)/shard_map/ppermute | solution.py:888
  72.3 4.9 %collective-permute-start.22 = (bf16[48,384]{1,0:T(8,128)(2,1)S(1)}, bf16[48,384]{1,0:T(8,128)(2,1)S(1)}, u32[]{:S(2)}, u32[]{:S(2)}) collective-permute-start(bf16[48,384]{1,0:T(8,128)(2,1)S(1)} %get-tuple-element.114.small), channel_id=1, source_target_pairs={{0,4},{1,3},{2,6},{3,1},{4,0},{5,7},{6,2},{7,5},{8,12},{9,11},{10,... | collective-permute-start | bytes 110600 | tf_op jit(solution)/shard_map/ppermute | solution.py:888
  77.8 14.3 %collective-permute-start.23 = (bf16[384,384]{1,0:T(8,128)(2,1)S(1)}, bf16[384,384]{1,0:T(8,128)(2,1)S(1)}, u32[]{:S(2)}, u32[]{:S(2)}) collective-permute-start(bf16[384,384]{1,0:T(8,128)(2,1)S(1)} %get-tuple-element.115.own), channel_id=1, source_target_pairs={{0,4},{1,3},{2,6},{3,1},{4,0},{5,7},{6,2},{7,5},{8,12},{9,11},{10,... | collective-permute-start | bytes 884744 | tf_op jit(solution)/shard_map/ppermute | solution.py:888
  80.4 4.2 %collective-permute-start.24 = (bf16[80,384]{1,0:T(8,128)(2,1)S(1)}, bf16[80,384]{1,0:T(8,128)(2,1)S(1)}, u32[]{:S(2)}, u32[]{:S(2)}) collective-permute-start(bf16[80,384]{1,0:T(8,128)(2,1)S(1)} %get-tuple-element.116.small), channel_id=1, source_target_pairs={{0,16},{1,9},{2,18},{3,11},{4,20},{5,13},{6,22},{7,15},{8,24},{9,1... | collective-permute-start | bytes 184328 | tf_op jit(solution)/shard_map/ppermute | solution.py:898
  92.7 9.2 %copy-start.20 = (bf16[96,384]{1,0:T(8,128)(2,1)S(1)}, bf16[96,384]{1,0:T(8,128)(2,1)}, u32[]{:S(2)}) copy-start(bf16[96,384]{1,0:T(8,128)(2,1)} %param.34) | copy-start | bytes 221188
  92.7 9.2 %copy-start.21 = (bf16[96,384]{1,0:T(8,128)(2,1)S(1)}, bf16[96,384]{1,0:T(8,128)(2,1)}, u32[]{:S(2)}) copy-start(bf16[96,384]{1,0:T(8,128)(2,1)} %param.40) | copy-start | bytes 221188
  92.7 6.9 %collective-permute-start.25 = (bf16[384,384]{1,0:T(8,128)(2,1)S(1)}, bf16[384,384]{1,0:T(8,128)(2,1)S(1)}, u32[]{:S(2)}, u32[]{:S(2)}) collective-permute-start(bf16[384,384]{1,0:T(8,128)(2,1)S(1)} %get-tuple-element.117.own), channel_id=1, source_target_pairs={{0,2},{1,5},{2,0},{3,7},{4,6},{5,1},{6,4},{7,3},{8,10},{9,13},{10,... | collective-permute-start | bytes 884744 | tf_op jit(solution)/shard_map/ppermute | solution.py:888
  94.8 4.7 %collective-permute-start.26 = (bf16[144,384]{1,0:T(8,128)(2,1)S(1)}, bf16[144,384]{1,0:T(8,128)(2,1)S(1)}, u32[]{:S(2)}, u32[]{:S(2)}) collective-permute-start(bf16[144,384]{1,0:T(8,128)(2,1)S(1)} %get-tuple-element.118.small), channel_id=1, source_target_pairs={{0,8},{1,17},{2,10},{3,19},{4,12},{5,21},{6,14},{7,23},{8,0},{9,25... | collective-permute-start | bytes 331784 | tf_op jit(solution)/shard_map/ppermute | solution.py:898
  100.5 1.4 %collective-permute-start.30 = (bf16[192,384]{1,0:T(8,128)(2,1)S(1)}, bf16[192,384]{1,0:T(8,128)(2,1)S(1)}, u32[]{:S(2)}, u32[]{:S(2)}) collective-permute-start(bf16[192,384]{1,0:T(8,128)(2,1)S(1)} %get-tuple-element.124), channel_id=1, source_target_pairs={{0,1},{1,0},{2,3},{3,2},{4,5},{5,4},{6,7},{7,6},{8,9},{9,8},{10,11... | collective-permute-start | bytes 442376 | tf_op jit(solution)/shard_map/ppermute | solution.py:79
  100.5 10.3 %collective-permute-start.31 = (bf16[384,384]{1,0:T(8,128)(2,1)S(1)}, bf16[384,384]{1,0:T(8,128)(2,1)S(1)}, u32[]{:S(2)}, u32[]{:S(2)}) collective-permute-start(bf16[384,384]{1,0:T(8,128)(2,1)S(1)} %get-tuple-element.125), channel_id=1, source_target_pairs={{0,1},{1,0},{2,3},{3,2},{4,5},{5,4},{6,7},{7,6},{8,9},{9,8},{10,11... | collective-permute-start | bytes 884744 | tf_op jit(solution)/shard_map/ppermute | solution.py:79
  101.0 1.8 %collective-permute-start.28 = (bf16[272,384]{1,0:T(8,128)(2,1)S(1)}, bf16[272,384]{1,0:T(8,128)(2,1)S(1)}, u32[]{:S(2)}, u32[]{:S(2)}) collective-permute-start(bf16[272,384]{1,0:T(8,128)(2,1)S(1)} %get-tuple-element.121.near), channel_id=1, source_target_pairs={{0,1},{1,0},{2,3},{3,2},{4,5},{5,4},{6,7},{7,6},{8,9},{9,8},{10,11... | collective-permute-start | bytes 626696 | tf_op jit(solution)/shard_map/ppermute | solution.py:79
  101.1 1.7 %copy-start.4 = (bf16[96,2304]{1,0:T(8,128)(2,1)S(1)}, bf16[96,2304]{1,0:T(8,128)(2,1)}, u32[]{:S(2)}) copy-start(bf16[96,2304]{1,0:T(8,128)(2,1)} %mean.1) | copy-start | bytes 1327108
  101.1 1.7 %copy-start.5 = (bf16[96,2304]{1,0:T(8,128)(2,1)S(1)}, bf16[96,2304]{1,0:T(8,128)(2,1)}, u32[]{:S(2)}) copy-start(bf16[96,2304]{1,0:T(8,128)(2,1)} %square.1) | copy-start | bytes 1327108
  101.1 1.7 %copy-start.10 = (bf16[14,96]{1,0:T(8,128)(2,1)S(1)}, bf16[14,96]{1,0:T(8,128)(2,1)}, u32[]{:S(2)}) copy-start(bf16[14,96]{1,0:T(8,128)(2,1)} %bias_mean.1) | copy-start | bytes 8068
  101.1 1.7 %copy-start.11 = (bf16[14,96]{1,0:T(8,128)(2,1)S(1)}, bf16[14,96]{1,0:T(8,128)(2,1)}, u32[]{:S(2)}) copy-start(bf16[14,96]{1,0:T(8,128)(2,1)} %bias_square.1) | copy-start | bytes 8068
  101.1 4.9 %collective-permute-start.27 = (f32[8,128]{1,0:T(8,128)S(1)}, f32[8,128]{1,0:T(8,128)S(1)}, u32[]{:S(2)}, u32[]{:S(2)}) collective-permute-start(f32[8,128]{1,0:T(8,128)S(1)} %get-tuple-element.120), channel_id=1, source_target_pairs={{0,8},{1,17},{2,10},{3,19},{4,12},{5,21},{6,14},{7,23},{8,0},{9,25... | collective-permute-start | bytes 12296 | tf_op jit(solution)/shard_map/ppermute | solution.py:898
  102.7 4.6 %copy-start.18 = (bf16[96,1152]{1,0:T(8,128)(2,1)S(1)}, bf16[96,1152]{1,0:T(8,128)(2,1)}, u32[]{:S(2)}) copy-start(bf16[96,1152]{1,0:T(8,128)(2,1)} %param.33) | copy-start | bytes 663556
  102.7 4.6 %copy-start.19 = (bf16[96,1152]{1,0:T(8,128)(2,1)S(1)}, bf16[96,1152]{1,0:T(8,128)(2,1)}, u32[]{:S(2)}) copy-start(bf16[96,1152]{1,0:T(8,128)(2,1)} %param.39) | copy-start | bytes 663556
  106.5 3.7 %collective-permute-start.29 = (f32[8,128]{1,0:T(8,128)S(1)}, f32[8,128]{1,0:T(8,128)S(1)}, u32[]{:S(2)}, u32[]{:S(2)}) collective-permute-start(f32[8,128]{1,0:T(8,128)S(1)} %step_5.1), channel_id=1, source_target_pairs={{0,16},{1,9},{2,18},{3,11},{4,20},{5,13},{6,22},{7,15},{8,24},{9,1... | collective-permute-start | bytes 12296 | tf_op jit(solution)/shard_map/ppermute | solution.py:898
  107.3 3.5 %copy-start.14 = (bf16[384,384]{1,0:T(8,128)(2,1)S(1)}, bf16[384,384]{1,0:T(8,128)(2,1)}, u32[]{:S(2)}) copy-start(bf16[384,384]{1,0:T(8,128)(2,1)} %param.36) | copy-start | bytes 884740
  107.3 3.5 %copy-start.15 = (bf16[384,384]{1,0:T(8,128)(2,1)S(1)}, bf16[384,384]{1,0:T(8,128)(2,1)}, u32[]{:S(2)}) copy-start(bf16[384,384]{1,0:T(8,128)(2,1)} %param.42) | copy-start | bytes 884740
  107.4 3.5 %copy-start.16 = (bf16[384,384]{1,0:T(8,128)(2,1)S(1)}, bf16[384,384]{1,0:T(8,128)(2,1)}, u32[]{:S(2)}) copy-start(bf16[384,384]{1,0:T(8,128)(2,1)} %param.41) | copy-start | bytes 884740
  107.4 3.5 %copy-start.17 = (bf16[384,384]{1,0:T(8,128)(2,1)S(1)}, bf16[384,384]{1,0:T(8,128)(2,1)}, u32[]{:S(2)}) copy-start(bf16[384,384]{1,0:T(8,128)(2,1)} %param.35) | copy-start | bytes 884740

commit v6 on v5

--- a/solution.py
+++ b/solution.py
@@ -165,20 +165,23 @@
     return jnp.concatenate([active, padded], axis=0)
 
 
-def payload_kernel(where, condition, attending, projection, biases, expand, contract, out, part):
-    @pl.when(where[1] == 0)
+def payload_kernel(condition, attending, projection, biases, expand, contract, out, part, sem):
+    core = lax.axis_index("replica") % 2
+
+    @pl.when(core == 0)
     def _():
-        part[...] = expand[...]
+        pltpu.make_async_copy(expand, part, sem).start()
         out[0:QUARTER, :] = attending[:, 0:D]
         out[QUARTER : 2 * QUARTER, :] = attending[:, D : 2 * D]
 
-    @pl.when(where[1] != 0)
+    @pl.when(core != 0)
     def _():
-        part[...] = contract[...]
+        pltpu.make_async_copy(contract, part, sem).start()
         out[0:QUARTER, :] = attending[:, 2 * D : 3 * D]
         out[QUARTER : 2 * QUARTER, :] = projection[...]
 
     out[2 * QUARTER :, :] = own_message(condition, biases).astype(LOW)
+    pltpu.make_async_copy(expand, part, sem).wait()
 
 
 def modulation_kernel(
@@ -686,6 +689,19 @@
     )(where, *operands, *after)
 
 
+def run_payload(*operands):
+    return pl.pallas_call(
+        payload_kernel,
+        grid=(1,),
+        in_specs=[whole(item.shape) for item in operands[:4]] + [ANY_SPEC] * 2,
+        out_specs=[whole((2 * QUARTER + 16, D)), ANY_SPEC],
+        out_shape=[shape_of((2 * QUARTER + 16, D), LOW), shape_of((D, D), LOW)],
+        scratch_shapes=[pltpu.SemaphoreType.DMA],
+        compiler_params=pltpu.CompilerParams(vmem_limit_bytes=60 * 1024 * 1024),
+        name="own_payload",
+    )(*operands)
+
+
 def run_gate(value, *after, space=ANY_SPEC):
     return pl.pallas_call(
         gate_kernel,
@@ -861,12 +877,34 @@
     )(where, tokens, grad_middle, joined, soft, mixed, mod, feed_rows, cond, att, proj, *earlier)
 
 
-def turn_split_kernel(where, keep, arrived, stay, go):
-    core = where[1]
-    for place, block in enumerate((0, 2 - core)):
-        stay[place] = keep[block].astype(WIDE) + arrived[block].astype(WIDE)
-    for place, block in enumerate((1 + core, 3)):
-        go[place] = (keep[block].astype(WIDE) + arrived[block].astype(WIDE)).astype(LOW)
+def turn_go_kernel(where, keep, last_keep, arrived, last_arrived, go):
+    go[0] = (keep[0].astype(WIDE) + arrived[0].astype(WIDE)).astype(LOW)
+    go[1] = (last_keep[0].astype(WIDE) + last_arrived[0].astype(WIDE)).astype(LOW)
+
+
+def turn_stay_kernel(where, keep, next_keep, swapped, next_swapped, arrived, stay, go):
+    stay[...] = keep[0].astype(WIDE) + swapped[0].astype(WIDE) + arrived[0].astype(WIDE)
+    go[...] = (
+        next_keep[0].astype(WIDE) + next_swapped[0].astype(WIDE) + arrived[1].astype(WIDE)
+    ).astype(LOW)
+
+
+def run_turned(kernel, name, places, outs, where, keep, swapped, *operands):
+    def at(number):
+        return pl.BlockSpec((1, D, D), lambda i, where: (places(where[1])[number], 0, 0))
+
+    return pl.pallas_call(
+        kernel,
+        grid_spec=pltpu.PrefetchScalarGridSpec(
+            num_scalar_prefetch=1,
+            grid=(1,),
+            in_specs=[at(0), at(1), at(0), at(1)] + [whole(item.shape) for item in operands],
+            out_specs=[whole(shape) for shape, _ in outs],
+        ),
+        out_shape=[shape_of(*item) for item in outs],
+        compiler_params=PARAMS,
+        name=name,
+    )(where, keep, keep, swapped, swapped, *operands)
 
 
 def run_split(keep, arrived):
@@ -936,11 +974,9 @@
     where, copy, stages, condition, ffn_halves, att_parts, small_rows, stored, means, squares
 ):
     core = where[1]
-    (feed_stay, feed_in), (att_send, att_keep) = ffn_halves, att_parts
+    (feed_stay, feed_go), (att_send, att_keep) = ffn_halves, att_parts
     half, third = (D // 2, D), (2 * QUARTER, D)
     att_stay, att_go = run_split(att_keep, swap_replica(att_send, 1))
-    feed_stay, feed_go = run_split(feed_stay, feed_in)
-    feed_stay, feed_go = feed_stay[0], feed_go[0]
     att_stay, att_go, feed_stay, feed_go, small = small_call(
         step1_kernel, "step_1",
         [(third, WIDE), (third, LOW), (half, WIDE), (half, LOW), ((3 * BLOCK, D), LOW)],
@@ -977,7 +1013,7 @@
     cond_go = small_call(
         step5_kernel, "step_5", [((8, 128), WIDE)], where, cond_keep, cond_in, after=(mark,)
     )[0]
-    cond_last = swap_pair(cond_go, 1)
+    cond_last = run_gate(swap_pair(cond_go, 1), feed_updates[0][1])
     att_totals = by_core(core, att_part, swap_replica(att_part, 1))
     blocks = [
         block[:, :QUARTER] for block in (cond_keep[:2], cond_in[:2], cond_last[:2], cond_last[2:4])
@@ -1003,10 +1039,9 @@
     rank, core = where[0], where[1]
     slot_count, model_width = condition.shape
     modulation, cond_low = stored[0], jax.nn.silu(condition).astype(jnp.bfloat16)
-    (ffn_stay, ffn_in), (att_send, att_keep) = ffn_halves, att_parts
-    ffn_stay, ffn_go = run_split(ffn_stay, ffn_in)
+    (ffn_stay, ffn_go), (att_send, att_keep) = ffn_halves, att_parts
     ffn_totals = reduce_replicas(
-        wide_sum([ffn_stay[0], swap_pair(ffn_go[0], 1)]).astype(LOW), copy, stages
+        wide_sum([ffn_stay, swap_pair(ffn_go, 1)]).astype(LOW), copy, stages
     )
     att_stay, att_go = run_split(att_keep, swap_replica(att_send, 1))
     att_stay, att_go = run_split(att_stay, swap_pair(att_go, 0))
@@ -1094,11 +1129,8 @@
     where = jnp.stack([rank, core, copy >> 1, live_counts[0]]).astype(jnp.int32)
 
     cond_low = jax.nn.silu(condition).astype(LOW)
-    payload, feed_part = small_call(
-        payload_kernel, "own_payload",
-        [((2 * QUARTER + 16, model_width), LOW), ((model_width, model_width), LOW)],
-        where, condition, attending, projection, biases, expand, contract,
-        params=pltpu.CompilerParams(vmem_limit_bytes=60 * 1024 * 1024),
+    payload, feed_part = run_payload(
+        condition, attending, projection, biases, expand, contract
     )
     first, second = swap_pair(payload, 0), swap_pair(payload, 1)
     last, first_far = swap_pair(first, 1), swap_replica(first, 1)
@@ -1121,11 +1153,12 @@
         where, mixed, latents, cotangent, mod, bias, proj, expand, contract, feed_nears, feed_fars
     )
     cond_wide = cond_low.astype(WIDE)
-    two_blocks = (2, model_width, model_width)
-    ffn_stay, ffn_go = small_call(
-        turn_split_kernel, "sum_and_split", [(two_blocks, WIDE), (two_blocks, LOW)],
-        where, ffn_keep, swap_replica(ffn_send, 1),
-    )
+    block = (model_width, model_width)
+    ffn_other = swap_replica(ffn_send, 1)
+    ffn_go = run_turned(
+        turn_go_kernel, "sum_to_send", lambda core: (1 + core, 3), [((2,) + block, LOW)],
+        where, ffn_keep, ffn_other,
+    )[0]
     earlier = run_attention_backward(
         0, where, latents, grad_middle, joined, soft, mixed, mod, feed_rows, cond_wide, att, proj
     )
@@ -1134,9 +1167,13 @@
         1, where, latents, grad_middle, joined, soft, mixed, mod, feed_rows, cond_wide, att, proj,
         (*earlier[1:], earlier[0], ffn_go),
     )
+    ffn_halves = run_turned(
+        turn_stay_kernel, "sum_and_split", lambda core: (0, 2 - core),
+        [(block, WIDE), (block, LOW)], where, ffn_keep, ffn_other, ffn_in,
+    )
     tail = tail_in_step if lax.axis_size("replica") == 8 else tail_in_turn
     grad_condition, results = tail(
-        where, copy, stages, condition, (ffn_stay, ffn_in), (att_send, att_keep), small_rows,
+        where, copy, stages, condition, ffn_halves, (att_send, att_keep), small_rows,
         (modulation, attending, projection, expand, contract, biases),
         (
             modulation_mean, attending_mean, projection_mean,

time: 113 us -> 121 us (1.071)
  Pallas kernels: 33.7 us -> 43.9 us
  waiting for transfers between devices: 37.3 us -> 35.7 us
    pallas_call x0 -> x3, Pallas kernels: none -> 13.2 us  [the longest x1 11.8 us: run_payload(): pl.pallas_call(payload_kernel, grid=(1,), in_specs=[whole(item.shape) for...]
    pallas_call x8 -> x6, Pallas kernels: 9.32 us -> 6.45 us  [small_call(): pl.pallas_call(kernel, grid=(1,), in_specs=[SMEM_SPEC] + [whole(item.shap...]
    ppermute x16, waiting for transfers between devices: 23.1 us -> 21.4 us  [swap_pair(): return lax.ppermute(value, ('group', 'replica'), pairs)]
  transfers between devices with their start and end apart: 32 -> 32, of which waited for: 14 -> 14; matrix products, arithmetic and copies ran while one was open for 2% -> 4% of each run, Pallas kernels for 16% -> 16%
where the time goes in v6:
time: 121 us
  Pallas kernels  43.9 us (36%)
  waiting for transfers between devices  35.7 us (30%)
  starting transfers between devices  34.6 us (29%)
  other arithmetic  4.98 us (4%)
  between operations  1.67 us (1%)
    ppermute x16, starting transfers between devices, swap_pair(): return lax.ppermute(value, ('group', 'replica'), pairs)  21.8 us
    ppermute x16, waiting for transfers between devices, swap_pair(): return lax.ppermute(value, ('group', 'replica'), pairs)  21.4 us
    ppermute x5, waiting for transfers between devices, swap_plane(): return lax.ppermute(value, 'replica', pairs)  12 us
    pallas_call x1, Pallas kernels, run_payload(): pl.pallas_call(payload_kernel, grid=(1,), in_specs=[whole(item.shape) for...  11.8 us
    ppermute x5, starting transfers between devices, swap_plane(): return lax.ppermute(value, 'replica', pairs)  11 us
    pallas_call x1, Pallas kernels, run_feed(): pl.pallas_call(feed_kernel, grid=(2,), in_specs=[SMEM_SPEC] + [whole((2,...  9.6 us
    pallas_call x2, Pallas kernels, run_attention_backward(): pl.pallas_call(functools.partial(attention_backward_kernel, slot), grid=(...  9.07 us
    pallas_call x6, Pallas kernels, small_call(): pl.pallas_call(kernel, grid=(1,), in_specs=[SMEM_SPEC] + [whole(item.shap...  6.45 us
  transfers between devices with their start and end apart: 32, of which 14 were waited for; matrix products, arithmetic and copies ran while one was open for 4% of the time, Pallas kernels for 16%

profile of v6, /device:TPU:0, one launch (start us, length us, event | category | flops | bytes accessed | tf_op | source)
XLA Modules:
  0.0 121.2 jit_solution(8027791992512649496)
XLA Ops:
  0.7 11.8 %own_payload.1 = (bf16[208,384]{1,0:T(8,128)(2,1)}, bf16[384,384]{1,0:T(8,128)(2,1)}) custom-call(f32[2,384]{1,0:T(2,128)} %condition.3, bf16[96,1152]{1,0:T(8,128)(2,1)} %own_att.1, bf16[96,384]{1,0:T(8,128)(2,1)} %own_proj.1, bf16[14,96]{1,0:T(8,128)(2,1)} %bias.1, bf16[384,384]{1,0:T(8,128)(2,1)} %own_expand.1, bf16[384,384]{1,0:T(8,128)(2,1)} %own_contract.1), custom_call_target="tpu_custom_call" | custom-call | tf_op jit(solution)/shard_map/own_payload/pallas_call | solution.py:693
  12.5 0.0 copy-start.7
  12.5 0.0 copy-start.13
  12.5 3.0 %collective-permute-start = (bf16[208,384]{1,0:T(8,128)(2,1)}, bf16[208,384]{1,0:T(8,128)(2,1)S(1)}, u32[]{:S(2)}, u32[]{:S(2)}) collective-permute-start(bf16[208,384]{1,0:T(8,128)(2,1)} %get-tuple-element.74), channel_id=1, source_target_pairs={{0,8},{1,17},{2,10},{3,19},{4,12},{5,21},{6,14},{7,23},{8,0},{9,25... | collective-permute-start | bytes 479240 | tf_op jit(solution)/shard_map/ppermute | solution.py:936
  15.5 1.5 %collective-permute-start.1 = (bf16[208,384]{1,0:T(8,128)(2,1)}, bf16[208,384]{1,0:T(8,128)(2,1)S(1)}, u32[]{:S(2)}, u32[]{:S(2)}) collective-permute-start(bf16[208,384]{1,0:T(8,128)(2,1)} %get-tuple-element.74), channel_id=1, source_target_pairs={{0,16},{1,9},{2,18},{3,11},{4,20},{5,13},{6,22},{7,15},{8,24},{9,1... | collective-permute-start | bytes 479240 | tf_op jit(solution)/shard_map/ppermute | solution.py:936
  17.0 3.2 %collective-permute-done.first.n1 = bf16[208,384]{1,0:T(8,128)(2,1)S(1)} collective-permute-done((bf16[208,384]{1,0:T(8,128)(2,1)}, bf16[208,384]{1,0:T(8,128)(2,1)S(1)}, u32[]{:S(2)}, u32[]{:S(2)}) %collective-permute-start) | collective-permute-done | bytes 159776 | tf_op jit(solution)/shard_map/ppermute | solution.py:936
  20.2 1.5 %collective-permute-start.2 = (bf16[208,384]{1,0:T(8,128)(2,1)S(1)}, bf16[208,384]{1,0:T(8,128)(2,1)S(1)}, u32[]{:S(2)}, u32[]{:S(2)}) collective-permute-start(bf16[208,384]{1,0:T(8,128)(2,1)S(1)} %collective-permute-done.first.n1), channel_id=1, source_target_pairs={{0,16},{1,9},{2,18},{3,11},{4,20},{5,13},{6,22},{7,15},{8,24},{9,1... | collective-permute-start | bytes 479240 | tf_op jit(solution)/shard_map/ppermute | solution.py:936
  21.7 2.3 %collective-permute-start.5 = (bf16[384,384]{1,0:T(8,128)(2,1)}, bf16[384,384]{1,0:T(8,128)(2,1)S(1)}, u32[]{:S(2)}, u32[]{:S(2)}) collective-permute-start(bf16[384,384]{1,0:T(8,128)(2,1)} %in_order.3), channel_id=1, source_target_pairs={{0,8},{1,17},{2,10},{3,19},{4,12},{5,21},{6,14},{7,23},{8,0},{9,25... | collective-permute-start | bytes 884744 | tf_op jit(solution)/shard_map/ppermute | solution.py:936
  24.0 0.7 collective-permute-start.9
  25.4 0.1 collective-permute-start.7
  25.4 0.1 collective-permute-done.2.last.n3
  25.5 0.4 collective-permute-start.8
  25.9 0.1 pad_add_fusion.where
  26.0 1.0 modulation_partials.1
  27.0 3.0 %collective-permute-start.3 = (f32[4,2304]{1,0:T(4,128)S(1)}, f32[4,2304]{1,0:T(4,128)S(1)}, u32[]{:S(2)}, u32[]{:S(2)}) collective-permute-start(f32[4,2304]{1,0:T(4,128)S(1)} %get-tuple-element.76), channel_id=1, source_target_pairs={{0,8},{1,17},{2,10},{3,19},{4,12},{5,21},{6,14},{7,23},{8,0},{9,25... | collective-permute-start | bytes 110600 | tf_op jit(solution)/shard_map/ppermute | solution.py:936
  30.0 2.5 %collective-permute-done.3.arrived = f32[4,2304]{1,0:T(4,128)S(1)} collective-permute-done((f32[4,2304]{1,0:T(4,128)S(1)}, f32[4,2304]{1,0:T(4,128)S(1)}, u32[]{:S(2)}, u32[]{:S(2)}) %collective-permute-start.3) | collective-permute-done | bytes 36896 | tf_op jit(solution)/shard_map/ppermute | solution.py:936
  32.5 0.6 relay.1
  33.0 1.1 collective-permute-start.6
  34.1 1.0 collective-permute-start.10
  35.1 0.5 collective-permute-start.12
  35.6 1.2 %collective-permute-done.6.arrived = f32[2,2304]{1,0:T(2,128)S(1)} collective-permute-done((f32[2,2304]{1,0:T(2,128)S(1)}, f32[2,2304]{1,0:T(2,128)S(1)}, u32[]{:S(2)}, u32[]{:S(2)}) %collective-permute-start.6) | collective-permute-done | bytes 18464 | tf_op jit(solution)/shard_map/ppermute | solution.py:936
  36.9 3.9 %attention_forward.1 = (bf16[2,256,1152]{2,1,0:T(8,128)(2,1)S(1)}, bf16[2,6,256,256]{3,2,1,0:T(8,128)(2,1)S(1)}, bf16[2,256,384]{2,1,0:T(8,128)(2,1)S(1)}, f32[2...) custom-call(s32[4]{0:T(128)S(1)} %pad_add_fusion.where, ...), custom_call_target="tpu_custom_call" | custom-call | flops 3000000000 | bytes 6000000 | tf_op jit(solution)/shard_map/attention_forward/pallas_call | solution.py:749
  40.9 0.1 collective-permute-start.13
  41.0 1.5 %collective-permute-done.13.f3 = bf16[384,384]{1,0:T(8,128)(2,1)S(1)} collective-permute-done((bf16[384,384]{1,0:T(8,128)(2,1)S(1)}, bf16[384,384]{1,0:T(8,128)(2,1)S(1)}, u32[]{:S(2)}, u32[]{:S(2)}) %collective-permute-start.13) | collective-permute-done | bytes 294944 | tf_op jit(solution)/shard_map/ppermute | solution.py:79
  42.5 9.6 %feed_forward_and_back.1 = (bf16[2,256,384]{2,1,0:T(8,128)(2,1)}, f32[2,256,384]{2,1,0:T(8,128)S(1)}, bf16[4,384,384]{2,1,0:T(8,128)(2,1)S(1)}, bf16[4,384,384]{2,1,0:T(8,128)(2,1)S(1)}, f32[16,384]{1,0:T(8,128)S(1)}) custom-call(s32[4]{0:T(128)S(1)} %pad_add_fusion.where, bf16[2,256,384]{2,1,0:T(8,128)(2,1)S(1)} %get-tuple-element.81.mixed, ...), custom_call_target="tpu_custom_call" | custom-call | flops 8000000000 | bytes 10000000 | tf_op jit(solution)/shard_map/feed_forward_and_back/pallas_call | solution.py:789
  52.1 0.1 collective-permute-start.14
  52.2 4.0 %attention_backward.2 = (bf16[2,256,384]{2,1,0:T(8,128)(2,1)}, bf16[256,1152]{1,0:T(8,128)(2,1)S(1)}, bf16[256,384]{1,0:T(8,128)(2,1)S(1)}, bf16[256,384]{1,0:T(8,128)(2,1)S(1)}, f32[32,384]{1,0:T(8,128)S(1)}) custom-call(s32[4]{0:T(128)S(1)} %pad_add_fusion.where, bf16[2,256,384]{2,1,0:T(8,128)(2,1)S(1)} %copy-done.13, ...), custom_call_target="tpu_custom_call" | custom-call | flops 4000000000 | bytes 8000000 | tf_op jit(solution)/shard_map/attention_backward/pallas_call | solution.py:864
  56.3 0.7 sum_to_send.1.refs_5_
  57.0 1.7 %collective-permute-start.17 = (bf16[2,384,384]{2,1,0:T(8,128)(2,1)S(1)}, bf16[2,384,384]{2,1,0:T(8,128)(2,1)S(1)}, u32[]{:S(2)}, u32[]{:S(2)}) collective-permute-start(bf16[2,384,384]{2,1,0:T(8,128)(2,1)S(1)} %sum_to_send.1.refs_5_), channel_id=1, source_target_pairs={{0,8},{1,17},{2,10},{3,19},{4,12},{5,21},{6,14},{7,23},{8,0},{9,25... | collective-permute-start | bytes 1769480 | tf_op jit(solution)/shard_map/ppermute | solution.py:936
  58.7 5.0 %attention_backward.3 = (bf16[2,256,384]{2,1,0:T(8,128)(2,1)}, bf16[4,192,384]{2,1,0:T(8,128)(2,1)S(1)}, bf16[4,192,384]{2,1,0:T(8,128)(2,1)S(1)}, bf16[32,384]{1,0:T(8,128)(2,1)S(1)}) custom-call(s32[4]{0:T(128)S(1)} %pad_add_fusion.where, bf16[2,256,384]{2,1,0:T(8,128)(2,1)S(1)} %copy-done.13, ...), custom_call_target="tpu_custom_call", output_to_operand_aliasing={{0}: (15, {})} | custom-call | flops 4000000000 | bytes 8000000 | tf_op jit(solution)/shard_map/attention_backward/pallas_call | solution.py:864
  63.7 3.2 %collective-permute-done.17.arrived = bf16[2,384,384]{2,1,0:T(8,128)(2,1)S(1)} collective-permute-done((bf16[2,384,384]{2,1,0:T(8,128)(2,1)S(1)}, bf16[2,384,384]{2,1,0:T(8,128)(2,1)S(1)}, u32[]{:S(2)}, u32[]{:S(2)}) %collective-permute-start.17) | collective-permute-done | bytes 589856 | tf_op jit(solution)/shard_map/ppermute | solution.py:936
  66.9 0.7 sum_and_split.3
  67.7 1.1 collective-permute-start.18
  68.8 0.1 sum_and_split.2
  68.9 1.8 %collective-permute-start.16 = (bf16[2,192,384]{2,1,0:T(8,128)(2,1)S(1)}, bf16[2,192,384]{2,1,0:T(8,128)(2,1)S(1)}, u32[]{:S(2)}, u32[]{:S(2)}) collective-permute-start(bf16[2,192,384]{2,1,0:T(8,128)(2,1)S(1)} %get-tuple-element.102), channel_id=1, source_target_pairs={{0,8},{1,17},{2,10},{3,19},{4,12},{5,21},{6,14},{7,23},{8,0},{9,25... | collective-permute-start | bytes 884744 | tf_op jit(solution)/shard_map/ppermute | solution.py:936
  70.7 1.6 %collective-permute-start.19 = (bf16[32,384]{1,0:T(8,128)(2,1)S(1)}, bf16[32,384]{1,0:T(8,128)(2,1)S(1)}, u32[]{:S(2)}, u32[]{:S(2)}) collective-permute-start(bf16[32,384]{1,0:T(8,128)(2,1)S(1)} %get-tuple-element.105.small), channel_id=1, source_target_pairs={{0,2},{1,5},{2,0},{3,7},{4,6},{5,1},{6,4},{7,3},{8,10},{9,13},{10,... | collective-permute-start | bytes 73736 | tf_op jit(solution)/shard_map/ppermute | solution.py:926
  72.3 2.2 %collective-permute-done.19.small_in = bf16[32,384]{1,0:T(8,128)(2,1)S(1)} collective-permute-done((bf16[32,384]{1,0:T(8,128)(2,1)S(1)}, bf16[32,384]{1,0:T(8,128)(2,1)S(1)}, u32[]{:S(2)}, u32[]{:S(2)}) %collective-permute-start.19) | collective-permute-done | bytes 24608 | tf_op jit(solution)/shard_map/ppermute | solution.py:926
  74.5 2.9 %collective-permute-done.18.feed_in = bf16[384,384]{1,0:T(8,128)(2,1)S(1)} collective-permute-done((bf16[384,384]{1,0:T(8,128)(2,1)S(1)}, bf16[384,384]{1,0:T(8,128)(2,1)S(1)}, u32[]{:S(2)}, u32[]{:S(2)}) %collective-permute-start.18) | collective-permute-done | bytes 294944 | tf_op jit(solution)/shard_map/ppermute | solution.py:936
  77.4 0.7 step_1.1
  78.2 1.0 collective-permute-start.20
  79.2 2.0 %collective-permute-start.21 = (bf16[192,384]{1,0:T(8,128)(2,1)S(1)}, bf16[192,384]{1,0:T(8,128)(2,1)S(1)}, u32[]{:S(2)}, u32[]{:S(2)}) collective-permute-start(bf16[192,384]{1,0:T(8,128)(2,1)S(1)} %get-tuple-element.109), channel_id=1, source_target_pairs={{0,2},{1,5},{2,0},{3,7},{4,6},{5,1},{6,4},{7,3},{8,10},{9,13},{10,... | collective-permute-start | bytes 442376 | tf_op jit(solution)/shard_map/ppermute | solution.py:926
  81.2 2.6 %collective-permute-start.22 = (bf16[48,384]{1,0:T(8,128)(2,1)S(1)}, bf16[48,384]{1,0:T(8,128)(2,1)S(1)}, u32[]{:S(2)}, u32[]{:S(2)}) collective-permute-start(bf16[48,384]{1,0:T(8,128)(2,1)S(1)} %get-tuple-element.110.small), channel_id=1, source_target_pairs={{0,4},{1,3},{2,6},{3,1},{4,0},{5,7},{6,2},{7,5},{8,12},{9,11},{10,... | collective-permute-start | bytes 110600 | tf_op jit(solution)/shard_map/ppermute | solution.py:926
  83.8 2.3 %collective-permute-done.22.small_in = bf16[48,384]{1,0:T(8,128)(2,1)S(1)} collective-permute-done((bf16[48,384]{1,0:T(8,128)(2,1)S(1)}, bf16[48,384]{1,0:T(8,128)(2,1)S(1)}, u32[]{:S(2)}, u32[]{:S(2)}) %collective-permute-start.22) | collective-permute-done | bytes 36896 | tf_op jit(solution)/shard_map/ppermute | solution.py:926
  86.1 0.6 step_2.1
  86.7 2.7 %collective-permute-start.23 = (bf16[384,384]{1,0:T(8,128)(2,1)S(1)}, bf16[384,384]{1,0:T(8,128)(2,1)S(1)}, u32[]{:S(2)}, u32[]{:S(2)}) collective-permute-start(bf16[384,384]{1,0:T(8,128)(2,1)S(1)} %get-tuple-element.111.own), channel_id=1, source_target_pairs={{0,4},{1,3},{2,6},{3,1},{4,0},{5,7},{6,2},{7,5},{8,12},{9,11},{10,... | collective-permute-start | bytes 884744 | tf_op jit(solution)/shard_map/ppermute | solution.py:926
  89.4 1.2 %collective-permute-start.24 = (bf16[80,384]{1,0:T(8,128)(2,1)S(1)}, bf16[80,384]{1,0:T(8,128)(2,1)S(1)}, u32[]{:S(2)}, u32[]{:S(2)}) collective-permute-start(bf16[80,384]{1,0:T(8,128)(2,1)S(1)} %get-tuple-element.112.small), channel_id=1, source_target_pairs={{0,16},{1,9},{2,18},{3,11},{4,20},{5,13},{6,22},{7,15},{8,24},{9,1... | collective-permute-start | bytes 184328 | tf_op jit(solution)/shard_map/ppermute | solution.py:936
  90.6 3.0 %collective-permute-done.24.small_in = bf16[80,384]{1,0:T(8,128)(2,1)S(1)} collective-permute-done((bf16[80,384]{1,0:T(8,128)(2,1)S(1)}, bf16[80,384]{1,0:T(8,128)(2,1)S(1)}, u32[]{:S(2)}, u32[]{:S(2)}) %collective-permute-start.24) | collective-permute-done | bytes 61472 | tf_op jit(solution)/shard_map/ppermute | solution.py:936
  93.6 7.4 %collective-permute-done.23.arrived = bf16[384,384]{1,0:T(8,128)(2,1)S(1)} collective-permute-done((bf16[384,384]{1,0:T(8,128)(2,1)S(1)}, bf16[384,384]{1,0:T(8,128)(2,1)S(1)}, u32[]{:S(2)}, u32[]{:S(2)}) %collective-permute-start.23) | collective-permute-done | bytes 294944 | tf_op jit(solution)/shard_map/ppermute | solution.py:926
  101.0 0.6 step_3.1
  101.6 2.2 %collective-permute-start.25 = (bf16[384,384]{1,0:T(8,128)(2,1)S(1)}, bf16[384,384]{1,0:T(8,128)(2,1)S(1)}, u32[]{:S(2)}, u32[]{:S(2)}) collective-permute-start(bf16[384,384]{1,0:T(8,128)(2,1)S(1)} %get-tuple-element.113.own), channel_id=1, source_target_pairs={{0,2},{1,5},{2,0},{3,7},{4,6},{5,1},{6,4},{7,3},{8,10},{9,13},{10,... | collective-permute-start | bytes 884744 | tf_op jit(solution)/shard_map/ppermute | solution.py:926
  103.8 4.7 %collective-permute-done.26.small_in = bf16[144,384]{1,0:T(8,128)(2,1)S(1)} collective-permute-done((bf16[144,384]{1,0:T(8,128)(2,1)S(1)}, bf16[144,384]{1,0:T(8,128)(2,1)S(1)}, u32[]{:S(2)}, u32[]{:S(2)}) %collective-permute-start.26) | collective-permute-done | bytes 110624 | tf_op jit(solution)/shard_map/ppermute | solution.py:936
  108.6 0.9 step_4.1
  109.4 0.5 collective-permute-start.30
  110.0 0.1 collective-permute-start.28
  110.0 0.8 collective-permute-done.31
  110.9 0.8 fusion.21
  111.8 1.2 fusion.16
  113.0 0.2 copy-done.6
  113.2 3.1 %modulation_update.1 = (f32[96,2304]{1,0:T(8,128)}, f32[96,2304]{1,0:T(8,128)}, f32[96,2304]{1,0:T(8,128)}, f32[14,96]{1,0:T(8,128)}, f32[14,96]{1,0:T(8,128)}, /*index=5*/f32[14,96]{1,0:T(8,128)}, f32[8,128]{1,0:T(8,128)S(1)}) custom-call(s32[4]{0:T(128)S(1)} %pad_add_fusion.where, bf16[272,384]{1,0:T(8,128)(2,1)S(1)} %get-tuple-element.117.near, ...), custom_call_target="tpu_custom_call" | custom-call | tf_op jit(solution)/shard_map/modulation_update/pallas_call | solution.py:678
  116.3 0.5 step_5.1
  116.8 0.8 collective-permute-start.29
  117.7 2.2 %fusion.11 = (f32[384,384]{1,0:T(8,128)}, f32[384,384]{1,0:T(8,128)}, f32[384,384]{1,0:T(8,128)}, f32[384,384]{1,0:T(8,128)}, f32[384,384]{1,0:T(8,128)}, /*index=5*/f32[384,384]{1,0:T(8,128)S(1)}) fusion(bf16[384,384]{1,0:T(8,128)(2,1)S(1)} %copy-done.3, bf16[384,384]{1,0:T(8,128)(2,1)S(1)} %collective-permute-done.30, ...), kind=kLoop, calls=%fused_computation.19 | loop fusion | flops 5603328 | bytes 5898241 | tf_op jit(solution)/shard_map/sub | solution.py:57
  119.9 0.6 collective-permute-done.29.refs_0_
  120.5 0.7 fusion.22
  (73 shorter events, 0.3 us)
Async XLA Ops:
  0.7 25.4 %copy-start.8 = (f32[2,384]{1,0:T(2,128)S(1)}, f32[2,384]{1,0:T(2,128)}, u32[]{:S(2)}) copy-start(f32[2,384]{1,0:T(2,128)} %condition.3) | copy-start | bytes 9220
  0.7 25.4 %copy-start.9 = (bf16[14,96]{1,0:T(8,128)(2,1)S(1)}, bf16[14,96]{1,0:T(8,128)(2,1)}, u32[]{:S(2)}) copy-start(bf16[14,96]{1,0:T(8,128)(2,1)} %bias.1) | copy-start | bytes 8068
  0.7 25.3 %copy-start = (bf16[96,2304]{1,0:T(8,128)(2,1)S(1)}, bf16[96,2304]{1,0:T(8,128)(2,1)}, u32[]{:S(2)}) copy-start(bf16[96,2304]{1,0:T(8,128)(2,1)} %weight.5) | copy-start | bytes 1327108
  12.5 24.4 %copy-start.4 = (bf16[96,1152]{1,0:T(8,128)(2,1)S(1)}, bf16[96,1152]{1,0:T(8,128)(2,1)}, u32[]{:S(2)}) copy-start(bf16[96,1152]{1,0:T(8,128)(2,1)} %own_att.1) | copy-start | bytes 663556
  12.5 24.4 %copy-start.7 = (bf16[96,384]{1,0:T(8,128)(2,1)S(1)}, bf16[96,384]{1,0:T(8,128)(2,1)}, u32[]{:S(2)}) copy-start(bf16[96,384]{1,0:T(8,128)(2,1)} %own_proj.1) | copy-start | bytes 221188
  12.5 24.4 %copy-start.13 = (bf16[2,256,384]{2,1,0:T(8,128)(2,1)S(1)}, bf16[2,256,384]{2,1,0:T(8,128)(2,1)}, u32[]{:S(2)}) copy-start(bf16[2,256,384]{2,1,0:T(8,128)(2,1)} %tokens.7) | copy-start | bytes 1179652
  12.5 7.7 %collective-permute-start = (bf16[208,384]{1,0:T(8,128)(2,1)}, bf16[208,384]{1,0:T(8,128)(2,1)S(1)}, u32[]{:S(2)}, u32[]{:S(2)}) collective-permute-start(bf16[208,384]{1,0:T(8,128)(2,1)} %get-tuple-element.74), channel_id=1, source_target_pairs={{0,8},{1,17},{2,10},{3,19},{4,12},{5,21},{6,14},{7,23},{8,0},{9,25... | collective-permute-start | bytes 479240 | tf_op jit(solution)/shard_map/ppermute | solution.py:936
  15.5 6.2 %collective-permute-start.1 = (bf16[208,384]{1,0:T(8,128)(2,1)}, bf16[208,384]{1,0:T(8,128)(2,1)S(1)}, u32[]{:S(2)}, u32[]{:S(2)}) collective-permute-start(bf16[208,384]{1,0:T(8,128)(2,1)} %get-tuple-element.74), channel_id=1, source_target_pairs={{0,16},{1,9},{2,18},{3,11},{4,20},{5,13},{6,22},{7,15},{8,24},{9,1... | collective-permute-start | bytes 479240 | tf_op jit(solution)/shard_map/ppermute | solution.py:936
  20.2 1.5 %collective-permute-start.4 = (bf16[208,384]{1,0:T(8,128)(2,1)S(1)}, bf16[208,384]{1,0:T(8,128)(2,1)S(1)}, u32[]{:S(2)}, u32[]{:S(2)}) collective-permute-start(bf16[208,384]{1,0:T(8,128)(2,1)S(1)} %collective-permute-done.first.n1), channel_id=1, source_target_pairs={{0,1},{1,0},{2,3},{3,2},{4,5},{5,4},{6,7},{7,6},{8,9},{9,8},{10,11... | collective-permute-start | bytes 479240 | tf_op jit(solution)/shard_map/ppermute | solution.py:79
  20.2 5.3 %collective-permute-start.2 = (bf16[208,384]{1,0:T(8,128)(2,1)S(1)}, bf16[208,384]{1,0:T(8,128)(2,1)S(1)}, u32[]{:S(2)}, u32[]{:S(2)}) collective-permute-start(bf16[208,384]{1,0:T(8,128)(2,1)S(1)} %collective-permute-done.first.n1), channel_id=1, source_target_pairs={{0,16},{1,9},{2,18},{3,11},{4,20},{5,13},{6,22},{7,15},{8,24},{9,1... | collective-permute-start | bytes 479240 | tf_op jit(solution)/shard_map/ppermute | solution.py:936
  21.7 10.8 %collective-permute-start.5 = (bf16[384,384]{1,0:T(8,128)(2,1)}, bf16[384,384]{1,0:T(8,128)(2,1)S(1)}, u32[]{:S(2)}, u32[]{:S(2)}) collective-permute-start(bf16[384,384]{1,0:T(8,128)(2,1)} %in_order.3), channel_id=1, source_target_pairs={{0,8},{1,17},{2,10},{3,19},{4,12},{5,21},{6,14},{7,23},{8,0},{9,25... | collective-permute-start | bytes 884744 | tf_op jit(solution)/shard_map/ppermute | solution.py:936
  24.0 11.1 %collective-permute-start.9 = (bf16[384,384]{1,0:T(8,128)(2,1)}, bf16[384,384]{1,0:T(8,128)(2,1)S(1)}, u32[]{:S(2)}, u32[]{:S(2)}) collective-permute-start(bf16[384,384]{1,0:T(8,128)(2,1)} %in_order.3), channel_id=1, source_target_pairs={{0,16},{1,9},{2,18},{3,11},{4,20},{5,13},{6,22},{7,15},{8,24},{9,1... | collective-permute-start | bytes 884744 | tf_op jit(solution)/shard_map/ppermute | solution.py:936
  25.4 9.7 %collective-permute-start.7 = (bf16[208,384]{1,0:T(8,128)(2,1)S(1)}, bf16[208,384]{1,0:T(8,128)(2,1)S(1)}, u32[]{:S(2)}, u32[]{:S(2)}) collective-permute-start(bf16[208,384]{1,0:T(8,128)(2,1)S(1)} %collective-permute-done.1.second.refs_2_.n2), channel_id=1, source_target_pairs={{0,1},{1,0},{2,3},{3,2},{4,5},{5,4},{6,7},{7,6},{8,9},{9,8},{10,11... | collective-permute-start | bytes 479240 | tf_op jit(solution)/shard_map/ppermute | solution.py:79
  25.5 10.1 %collective-permute-start.8 = (bf16[208,384]{1,0:T(8,128)(2,1)S(1)}, bf16[208,384]{1,0:T(8,128)(2,1)S(1)}, u32[]{:S(2)}, u32[]{:S(2)}) collective-permute-start(bf16[208,384]{1,0:T(8,128)(2,1)S(1)} %collective-permute-done.2.last.n3), channel_id=1, source_target_pairs={{0,1},{1,0},{2,3},{3,2},{4,5},{5,4},{6,7},{7,6},{8,9},{9,8},{10,11... | collective-permute-start | bytes 479240 | tf_op jit(solution)/shard_map/ppermute | solution.py:79
  27.0 5.4 %collective-permute-start.3 = (f32[4,2304]{1,0:T(4,128)S(1)}, f32[4,2304]{1,0:T(4,128)S(1)}, u32[]{:S(2)}, u32[]{:S(2)}) collective-permute-start(f32[4,2304]{1,0:T(4,128)S(1)} %get-tuple-element.76), channel_id=1, source_target_pairs={{0,8},{1,17},{2,10},{3,19},{4,12},{5,21},{6,14},{7,23},{8,0},{9,25... | collective-permute-start | bytes 110600 | tf_op jit(solution)/shard_map/ppermute | solution.py:936
  33.0 3.8 %collective-permute-start.6 = (f32[2,2304]{1,0:T(2,128)S(1)}, f32[2,2304]{1,0:T(2,128)S(1)}, u32[]{:S(2)}, u32[]{:S(2)}) collective-permute-start(f32[2,2304]{1,0:T(2,128)S(1)} %get-tuple-element.79), channel_id=1, source_target_pairs={{0,16},{1,9},{2,18},{3,11},{4,20},{5,13},{6,22},{7,15},{8,24},{9,1... | collective-permute-start | bytes 55304 | tf_op jit(solution)/shard_map/ppermute | solution.py:936
  34.1 6.7 %collective-permute-start.10 = (bf16[384,384]{1,0:T(8,128)(2,1)S(1)}, bf16[384,384]{1,0:T(8,128)(2,1)S(1)}, u32[]{:S(2)}, u32[]{:S(2)}) collective-permute-start(bf16[384,384]{1,0:T(8,128)(2,1)S(1)} %get-tuple-element.84.n1), channel_id=1, source_target_pairs={{0,16},{1,9},{2,18},{3,11},{4,20},{5,13},{6,22},{7,15},{8,24},{9,1... | collective-permute-start | bytes 884744 | tf_op jit(solution)/shard_map/ppermute | solution.py:936
  35.1 5.8 %collective-permute-start.11 = (bf16[384,384]{1,0:T(8,128)(2,1)S(1)}, bf16[384,384]{1,0:T(8,128)(2,1)S(1)}, u32[]{:S(2)}, u32[]{:S(2)}) collective-permute-start(bf16[384,384]{1,0:T(8,128)(2,1)S(1)} %get-tuple-element.84.n1), channel_id=1, source_target_pairs={{0,1},{1,0},{2,3},{3,2},{4,5},{5,4},{6,7},{7,6},{8,9},{9,8},{10,11... | collective-permute-start | bytes 884744 | tf_op jit(solution)/shard_map/ppermute | solution.py:79
  35.1 5.8 %collective-permute-start.12 = (bf16[384,384]{1,0:T(8,128)(2,1)S(1)}, bf16[384,384]{1,0:T(8,128)(2,1)S(1)}, u32[]{:S(2)}, u32[]{:S(2)}) collective-permute-start(bf16[384,384]{1,0:T(8,128)(2,1)S(1)} %collective-permute-done.9.n2), channel_id=1, source_target_pairs={{0,1},{1,0},{2,3},{3,2},{4,5},{5,4},{6,7},{7,6},{8,9},{9,8},{10,11... | collective-permute-start | bytes 884744 | tf_op jit(solution)/shard_map/ppermute | solution.py:79
  36.9 5.7 %copy-start.2 = (bf16[384,384]{1,0:T(8,128)(2,1)S(1)}, bf16[384,384]{1,0:T(8,128)(2,1)}, u32[]{:S(2)}) copy-start(bf16[384,384]{1,0:T(8,128)(2,1)} %own_expand.1) | copy-start | bytes 884740
  36.9 5.7 %copy-start.3 = (bf16[384,384]{1,0:T(8,128)(2,1)S(1)}, bf16[384,384]{1,0:T(8,128)(2,1)}, u32[]{:S(2)}) copy-start(bf16[384,384]{1,0:T(8,128)(2,1)} %own_contract.1) | copy-start | bytes 884740
  36.9 5.6 %copy-start.12 = (bf16[2,256,384]{2,1,0:T(8,128)(2,1)S(1)}, bf16[2,256,384]{2,1,0:T(8,128)(2,1)}, u32[]{:S(2)}) copy-start(bf16[2,256,384]{2,1,0:T(8,128)(2,1)} %cotangent.1) | copy-start | bytes 1179652
  40.9 1.6 %collective-permute-start.13 = (bf16[384,384]{1,0:T(8,128)(2,1)S(1)}, bf16[384,384]{1,0:T(8,128)(2,1)S(1)}, u32[]{:S(2)}, u32[]{:S(2)}) collective-permute-start(bf16[384,384]{1,0:T(8,128)(2,1)S(1)} %in_order.4.n3), channel_id=1, source_target_pairs={{0,1},{1,0},{2,3},{3,2},{4,5},{5,4},{6,7},{7,6},{8,9},{9,8},{10,11... | collective-permute-start | bytes 884744 | tf_op jit(solution)/shard_map/ppermute | solution.py:79
  52.1 4.2 %collective-permute-start.14 = (bf16[4,384,384]{2,1,0:T(8,128)(2,1)S(1)}, bf16[4,384,384]{2,1,0:T(8,128)(2,1)S(1)}, u32[]{:S(2)}, u32[]{:S(2)}) collective-permute-start(bf16[4,384,384]{2,1,0:T(8,128)(2,1)S(1)} %get-tuple-element.97), channel_id=1, source_target_pairs={{0,1},{1,0},{2,3},{3,2},{4,5},{5,4},{6,7},{7,6},{8,9},{9,8},{10,11... | collective-permute-start | bytes 3538952 | tf_op jit(solution)/shard_map/ppermute | solution.py:79
  57.0 9.9 %collective-permute-start.17 = (bf16[2,384,384]{2,1,0:T(8,128)(2,1)S(1)}, bf16[2,384,384]{2,1,0:T(8,128)(2,1)S(1)}, u32[]{:S(2)}, u32[]{:S(2)}) collective-permute-start(bf16[2,384,384]{2,1,0:T(8,128)(2,1)S(1)} %sum_to_send.1.refs_5_), channel_id=1, source_target_pairs={{0,8},{1,17},{2,10},{3,19},{4,12},{5,21},{6,14},{7,23},{8,0},{9,25... | collective-permute-start | bytes 1769480 | tf_op jit(solution)/shard_map/ppermute | solution.py:936
  63.7 5.0 %collective-permute-start.15 = (bf16[4,192,384]{2,1,0:T(8,128)(2,1)S(1)}, bf16[4,192,384]{2,1,0:T(8,128)(2,1)S(1)}, u32[]{:S(2)}, u32[]{:S(2)}) collective-permute-start(bf16[4,192,384]{2,1,0:T(8,128)(2,1)S(1)} %get-tuple-element.100), channel_id=1, source_target_pairs={{0,1},{1,0},{2,3},{3,2},{4,5},{5,4},{6,7},{7,6},{8,9},{9,8},{10,11... | collective-permute-start | bytes 1769480 | tf_op jit(solution)/shard_map/ppermute | solution.py:79
  67.7 9.8 %collective-permute-start.18 = (bf16[384,384]{1,0:T(8,128)(2,1)S(1)}, bf16[384,384]{1,0:T(8,128)(2,1)S(1)}, u32[]{:S(2)}, u32[]{:S(2)}) collective-permute-start(bf16[384,384]{1,0:T(8,128)(2,1)S(1)} %get-tuple-element.104), channel_id=1, source_target_pairs={{0,16},{1,9},{2,18},{3,11},{4,20},{5,13},{6,22},{7,15},{8,24},{9,1... | collective-permute-start | bytes 884744 | tf_op jit(solution)/shard_map/ppermute | solution.py:936
  68.9 8.6 %collective-permute-start.16 = (bf16[2,192,384]{2,1,0:T(8,128)(2,1)S(1)}, bf16[2,192,384]{2,1,0:T(8,128)(2,1)S(1)}, u32[]{:S(2)}, u32[]{:S(2)}) collective-permute-start(bf16[2,192,384]{2,1,0:T(8,128)(2,1)S(1)} %get-tuple-element.102), channel_id=1, source_target_pairs={{0,8},{1,17},{2,10},{3,19},{4,12},{5,21},{6,14},{7,23},{8,0},{9,25... | collective-permute-start | bytes 884744 | tf_op jit(solution)/shard_map/ppermute | solution.py:936
  70.7 3.8 %collective-permute-start.19 = (bf16[32,384]{1,0:T(8,128)(2,1)S(1)}, bf16[32,384]{1,0:T(8,128)(2,1)S(1)}, u32[]{:S(2)}, u32[]{:S(2)}) collective-permute-start(bf16[32,384]{1,0:T(8,128)(2,1)S(1)} %get-tuple-element.105.small), channel_id=1, source_target_pairs={{0,2},{1,5},{2,0},{3,7},{4,6},{5,1},{6,4},{7,3},{8,10},{9,13},{10,... | collective-permute-start | bytes 73736 | tf_op jit(solution)/shard_map/ppermute | solution.py:926
  78.2 7.9 %collective-permute-start.20 = (bf16[192,384]{1,0:T(8,128)(2,1)S(1)}, bf16[192,384]{1,0:T(8,128)(2,1)S(1)}, u32[]{:S(2)}, u32[]{:S(2)}) collective-permute-start(bf16[192,384]{1,0:T(8,128)(2,1)S(1)} %get-tuple-element.107), channel_id=1, source_target_pairs={{0,16},{1,9},{2,18},{3,11},{4,20},{5,13},{6,22},{7,15},{8,24},{9,1... | collective-permute-start | bytes 442376 | tf_op jit(solution)/shard_map/ppermute | solution.py:936
  79.2 6.9 %collective-permute-start.21 = (bf16[192,384]{1,0:T(8,128)(2,1)S(1)}, bf16[192,384]{1,0:T(8,128)(2,1)S(1)}, u32[]{:S(2)}, u32[]{:S(2)}) collective-permute-start(bf16[192,384]{1,0:T(8,128)(2,1)S(1)} %get-tuple-element.109), channel_id=1, source_target_pairs={{0,2},{1,5},{2,0},{3,7},{4,6},{5,1},{6,4},{7,3},{8,10},{9,13},{10,... | collective-permute-start | bytes 442376 | tf_op jit(solution)/shard_map/ppermute | solution.py:926
  81.2 4.9 %collective-permute-start.22 = (bf16[48,384]{1,0:T(8,128)(2,1)S(1)}, bf16[48,384]{1,0:T(8,128)(2,1)S(1)}, u32[]{:S(2)}, u32[]{:S(2)}) collective-permute-start(bf16[48,384]{1,0:T(8,128)(2,1)S(1)} %get-tuple-element.110.small), channel_id=1, source_target_pairs={{0,4},{1,3},{2,6},{3,1},{4,0},{5,7},{6,2},{7,5},{8,12},{9,11},{10,... | collective-permute-start | bytes 110600 | tf_op jit(solution)/shard_map/ppermute | solution.py:926
  86.7 14.3 %collective-permute-start.23 = (bf16[384,384]{1,0:T(8,128)(2,1)S(1)}, bf16[384,384]{1,0:T(8,128)(2,1)S(1)}, u32[]{:S(2)}, u32[]{:S(2)}) collective-permute-start(bf16[384,384]{1,0:T(8,128)(2,1)S(1)} %get-tuple-element.111.own), channel_id=1, source_target_pairs={{0,4},{1,3},{2,6},{3,1},{4,0},{5,7},{6,2},{7,5},{8,12},{9,11},{10,... | collective-permute-start | bytes 884744 | tf_op jit(solution)/shard_map/ppermute | solution.py:926
  89.4 4.2 %collective-permute-start.24 = (bf16[80,384]{1,0:T(8,128)(2,1)S(1)}, bf16[80,384]{1,0:T(8,128)(2,1)S(1)}, u32[]{:S(2)}, u32[]{:S(2)}) collective-permute-start(bf16[80,384]{1,0:T(8,128)(2,1)S(1)} %get-tuple-element.112.small), channel_id=1, source_target_pairs={{0,16},{1,9},{2,18},{3,11},{4,20},{5,13},{6,22},{7,15},{8,24},{9,1... | collective-permute-start | bytes 184328 | tf_op jit(solution)/shard_map/ppermute | solution.py:936
  101.6 6.9 %collective-permute-start.25 = (bf16[384,384]{1,0:T(8,128)(2,1)S(1)}, bf16[384,384]{1,0:T(8,128)(2,1)S(1)}, u32[]{:S(2)}, u32[]{:S(2)}) collective-permute-start(bf16[384,384]{1,0:T(8,128)(2,1)S(1)} %get-tuple-element.113.own), channel_id=1, source_target_pairs={{0,2},{1,5},{2,0},{3,7},{4,6},{5,1},{6,4},{7,3},{8,10},{9,13},{10,... | collective-permute-start | bytes 884744 | tf_op jit(solution)/shard_map/ppermute | solution.py:926
  103.8 7.1 %copy-start.20 = (bf16[96,384]{1,0:T(8,128)(2,1)S(1)}, bf16[96,384]{1,0:T(8,128)(2,1)}, u32[]{:S(2)}) copy-start(bf16[96,384]{1,0:T(8,128)(2,1)} %param.34) | copy-start | bytes 221188
  103.8 7.1 %copy-start.21 = (bf16[96,384]{1,0:T(8,128)(2,1)S(1)}, bf16[96,384]{1,0:T(8,128)(2,1)}, u32[]{:S(2)}) copy-start(bf16[96,384]{1,0:T(8,128)(2,1)} %param.40) | copy-start | bytes 221188
  103.8 4.7 %collective-permute-start.26 = (bf16[144,384]{1,0:T(8,128)(2,1)S(1)}, bf16[144,384]{1,0:T(8,128)(2,1)S(1)}, u32[]{:S(2)}, u32[]{:S(2)}) collective-permute-start(bf16[144,384]{1,0:T(8,128)(2,1)S(1)} %get-tuple-element.114.small), channel_id=1, source_target_pairs={{0,8},{1,17},{2,10},{3,19},{4,12},{5,21},{6,14},{7,23},{8,0},{9,25... | collective-permute-start | bytes 331784 | tf_op jit(solution)/shard_map/ppermute | solution.py:936
  109.4 1.4 %collective-permute-start.31 = (bf16[192,384]{1,0:T(8,128)(2,1)S(1)}, bf16[192,384]{1,0:T(8,128)(2,1)S(1)}, u32[]{:S(2)}, u32[]{:S(2)}) collective-permute-start(bf16[192,384]{1,0:T(8,128)(2,1)S(1)} %get-tuple-element.121), channel_id=1, source_target_pairs={{0,1},{1,0},{2,3},{3,2},{4,5},{5,4},{6,7},{7,6},{8,9},{9,8},{10,11... | collective-permute-start | bytes 442376 | tf_op jit(solution)/shard_map/ppermute | solution.py:79
  109.4 8.2 %collective-permute-start.30 = (bf16[384,384]{1,0:T(8,128)(2,1)S(1)}, bf16[384,384]{1,0:T(8,128)(2,1)S(1)}, u32[]{:S(2)}, u32[]{:S(2)}) collective-permute-start(bf16[384,384]{1,0:T(8,128)(2,1)S(1)} %get-tuple-element.119), channel_id=1, source_target_pairs={{0,1},{1,0},{2,3},{3,2},{4,5},{5,4},{6,7},{7,6},{8,9},{9,8},{10,11... | collective-permute-start | bytes 884744 | tf_op jit(solution)/shard_map/ppermute | solution.py:79
  110.0 3.0 %collective-permute-start.28 = (bf16[272,384]{1,0:T(8,128)(2,1)S(1)}, bf16[272,384]{1,0:T(8,128)(2,1)S(1)}, u32[]{:S(2)}, u32[]{:S(2)}) collective-permute-start(bf16[272,384]{1,0:T(8,128)(2,1)S(1)} %get-tuple-element.117.near), channel_id=1, source_target_pairs={{0,1},{1,0},{2,3},{3,2},{4,5},{5,4},{6,7},{7,6},{8,9},{9,8},{10,11... | collective-permute-start | bytes 626696 | tf_op jit(solution)/shard_map/ppermute | solution.py:79
  110.0 1.7 %copy-start.18 = (bf16[96,1152]{1,0:T(8,128)(2,1)S(1)}, bf16[96,1152]{1,0:T(8,128)(2,1)}, u32[]{:S(2)}) copy-start(bf16[96,1152]{1,0:T(8,128)(2,1)} %param.33) | copy-start | bytes 663556
  110.0 1.7 %copy-start.19 = (bf16[96,1152]{1,0:T(8,128)(2,1)S(1)}, bf16[96,1152]{1,0:T(8,128)(2,1)}, u32[]{:S(2)}) copy-start(bf16[96,1152]{1,0:T(8,128)(2,1)} %param.39) | copy-start | bytes 663556
  110.0 6.3 %collective-permute-start.27 = (f32[8,128]{1,0:T(8,128)S(1)}, f32[8,128]{1,0:T(8,128)S(1)}, u32[]{:S(2)}, u32[]{:S(2)}) collective-permute-start(f32[8,128]{1,0:T(8,128)S(1)} %get-tuple-element.116), channel_id=1, source_target_pairs={{0,8},{1,17},{2,10},{3,19},{4,12},{5,21},{6,14},{7,23},{8,0},{9,25... | collective-permute-start | bytes 12296 | tf_op jit(solution)/shard_map/ppermute | solution.py:936
  111.7 1.3 %copy-start.5 = (bf16[96,2304]{1,0:T(8,128)(2,1)S(1)}, bf16[96,2304]{1,0:T(8,128)(2,1)}, u32[]{:S(2)}) copy-start(bf16[96,2304]{1,0:T(8,128)(2,1)} %mean.1) | copy-start | bytes 1327108
  111.7 1.5 %copy-start.6 = (bf16[96,2304]{1,0:T(8,128)(2,1)S(1)}, bf16[96,2304]{1,0:T(8,128)(2,1)}, u32[]{:S(2)}) copy-start(bf16[96,2304]{1,0:T(8,128)(2,1)} %square.1) | copy-start | bytes 1327108
  111.7 1.4 %copy-start.10 = (bf16[14,96]{1,0:T(8,128)(2,1)S(1)}, bf16[14,96]{1,0:T(8,128)(2,1)}, u32[]{:S(2)}) copy-start(bf16[14,96]{1,0:T(8,128)(2,1)} %bias_mean.1) | copy-start | bytes 8068
  111.8 1.4 %copy-start.11 = (bf16[14,96]{1,0:T(8,128)(2,1)S(1)}, bf16[14,96]{1,0:T(8,128)(2,1)}, u32[]{:S(2)}) copy-start(bf16[14,96]{1,0:T(8,128)(2,1)} %bias_square.1) | copy-start | bytes 8068
  113.0 4.7 %copy-start.14 = (bf16[384,384]{1,0:T(8,128)(2,1)S(1)}, bf16[384,384]{1,0:T(8,128)(2,1)}, u32[]{:S(2)}) copy-start(bf16[384,384]{1,0:T(8,128)(2,1)} %param.36) | copy-start | bytes 884740
  113.0 4.7 %copy-start.15 = (bf16[384,384]{1,0:T(8,128)(2,1)S(1)}, bf16[384,384]{1,0:T(8,128)(2,1)}, u32[]{:S(2)}) copy-start(bf16[384,384]{1,0:T(8,128)(2,1)} %param.42) | copy-start | bytes 884740
  113.0 4.7 %copy-start.16 = (bf16[384,384]{1,0:T(8,128)(2,1)S(1)}, bf16[384,384]{1,0:T(8,128)(2,1)}, u32[]{:S(2)}) copy-start(bf16[384,384]{1,0:T(8,128)(2,1)} %param.41) | copy-start | bytes 884740
  113.0 4.7 %copy-start.17 = (bf16[384,384]{1,0:T(8,128)(2,1)S(1)}, bf16[384,384]{1,0:T(8,128)(2,1)}, u32[]{:S(2)}) copy-start(bf16[384,384]{1,0:T(8,128)(2,1)} %param.35) | copy-start | bytes 884740
  116.8 3.7 %collective-permute-start.29 = (f32[8,128]{1,0:T(8,128)S(1)}, f32[8,128]{1,0:T(8,128)S(1)}, u32[]{:S(2)}, u32[]{:S(2)}) collective-permute-start(f32[8,128]{1,0:T(8,128)S(1)} %step_5.1), channel_id=1, source_target_pairs={{0,16},{1,9},{2,18},{3,11},{4,20},{5,13},{6,22},{7,15},{8,24},{9,1... | collective-permute-start | bytes 12296 | tf_op jit(solution)/shard_map/ppermute | solution.py:936
  119.9 1.3 %copy-start.1 = (f32[384,384]{1,0:T(8,128)}, f32[384,384]{1,0:T(8,128)S(1)}, u32[]{:S(2)}) copy-start(f32[384,384]{1,0:T(8,128)S(1)} %get-tuple-element.141.refs_1_) | copy-start | bytes 1769476

commit v7 on v6

--- a/solution.py
+++ b/solution.py
@@ -690,12 +690,13 @@
 
 
 def run_payload(*operands):
+    outs = [((2 * QUARTER + 16, D), LOW), ((D, D), LOW)]
     return pl.pallas_call(
         payload_kernel,
         grid=(1,),
         in_specs=[whole(item.shape) for item in operands[:4]] + [ANY_SPEC] * 2,
-        out_specs=[whole((2 * QUARTER + 16, D)), ANY_SPEC],
-        out_shape=[shape_of((2 * QUARTER + 16, D), LOW), shape_of((D, D), LOW)],
+        out_specs=[whole(shape) for shape, _ in outs],
+        out_shape=[shape_of(*item) for item in outs],
         scratch_shapes=[pltpu.SemaphoreType.DMA],
         compiler_params=pltpu.CompilerParams(vmem_limit_bytes=60 * 1024 * 1024),
         name="own_payload",
@@ -877,34 +878,24 @@
     )(where, tokens, grad_middle, joined, soft, mixed, mod, feed_rows, cond, att, proj, *earlier)
 
 
-def turn_go_kernel(where, keep, last_keep, arrived, last_arrived, go):
-    go[0] = (keep[0].astype(WIDE) + arrived[0].astype(WIDE)).astype(LOW)
-    go[1] = (last_keep[0].astype(WIDE) + last_arrived[0].astype(WIDE)).astype(LOW)
-
-
-def turn_stay_kernel(where, keep, next_keep, swapped, next_swapped, arrived, stay, go):
-    stay[...] = keep[0].astype(WIDE) + swapped[0].astype(WIDE) + arrived[0].astype(WIDE)
+def turned(where):
+    core = where[1]
+    return (0, 2 - core), (1 + core, 3)
+
+
+def turn_go_kernel(where, keep, arrived, go):
+    for place, block in enumerate(turned(where)[1]):
+        go[place] = (keep[block].astype(WIDE) + arrived[block].astype(WIDE)).astype(LOW)
+
+
+def turn_stay_kernel(where, keep, swapped, arrived, stay, go):
+    own, other = turned(where)[0]
+    stay[...] = (
+        keep[own].astype(WIDE) + swapped[own].astype(WIDE) + arrived[0].astype(WIDE)
+    )
     go[...] = (
-        next_keep[0].astype(WIDE) + next_swapped[0].astype(WIDE) + arrived[1].astype(WIDE)
+        keep[other].astype(WIDE) + swapped[other].astype(WIDE) + arrived[1].astype(WIDE)
     ).astype(LOW)
-
-
-def run_turned(kernel, name, places, outs, where, keep, swapped, *operands):
-    def at(number):
-        return pl.BlockSpec((1, D, D), lambda i, where: (places(where[1])[number], 0, 0))
-
-    return pl.pallas_call(
-        kernel,
-        grid_spec=pltpu.PrefetchScalarGridSpec(
-            num_scalar_prefetch=1,
-            grid=(1,),
-            in_specs=[at(0), at(1), at(0), at(1)] + [whole(item.shape) for item in operands],
-            out_specs=[whole(shape) for shape, _ in outs],
-        ),
-        out_shape=[shape_of(*item) for item in outs],
-        compiler_params=PARAMS,
-        name=name,
-    )(where, keep, keep, swapped, swapped, *operands)
 
 
 def run_split(keep, arrived):
@@ -1155,9 +1146,8 @@
     cond_wide = cond_low.astype(WIDE)
     block = (model_width, model_width)
     ffn_other = swap_replica(ffn_send, 1)
-    ffn_go = run_turned(
-        turn_go_kernel, "sum_to_send", lambda core: (1 + core, 3), [((2,) + block, LOW)],
-        where, ffn_keep, ffn_other,
+    ffn_go = small_call(
+        turn_go_kernel, "sum_to_send", [((2,) + block, LOW)], where, ffn_keep, ffn_other
     )[0]
     earlier = run_attention_backward(
         0, where, latents, grad_middle, joined, soft, mixed, mod, feed_rows, cond_wide, att, proj
@@ -1167,9 +1157,9 @@
         1, where, latents, grad_middle, joined, soft, mixed, mod, feed_rows, cond_wide, att, proj,
         (*earlier[1:], earlier[0], ffn_go),
     )
-    ffn_halves = run_turned(
-        turn_stay_kernel, "sum_and_split", lambda core: (0, 2 - core),
-        [(block, WIDE), (block, LOW)], where, ffn_keep, ffn_other, ffn_in,
+    ffn_halves = small_call(
+        turn_stay_kernel, "sum_and_split", [(block, WIDE), (block, LOW)],
+        where, ffn_keep, ffn_other, ffn_in,
     )
     tail = tail_in_step if lax.axis_size("replica") == 8 else tail_in_turn
     grad_condition, results = tail(

time: 121 us -> 112 us (0.926)
  Pallas kernels: 43.9 us -> 35 us
    pallas_call x1, Pallas kernels: 11.8 us -> 2.8 us  [run_payload(): pl.pallas_call(payload_kernel, grid=(1,), in_specs=[whole(item.shape) for...]
    pallas_call x2 -> x0, Pallas kernels: 1.43 us -> none  [run_turned(): pl.pallas_call(kernel, grid_spec=pltpu.PrefetchScalarGridSpec(num_scalar_...]
    pallas_call x6 -> x8, Pallas kernels: 6.45 us -> 7.88 us  [small_call(): pl.pallas_call(kernel, grid=(1,), in_specs=[SMEM_SPEC] + [whole(item.shap...]
  transfers between devices with their start and end apart: 32 -> 32, of which waited for: 14 -> 14; matrix products, arithmetic and copies ran while one was open for 4% -> 4% of each run, Pallas kernels for 16% -> 17%
where the time goes in v7:
time: 112 us
  waiting for transfers between devices  35.7 us (32%)
  Pallas kernels  35 us (31%)
  starting transfers between devices  34.6 us (31%)
  other arithmetic  4.98 us (4%)
  between operations  1.67 us (1%)
    ppermute x16, starting transfers between devices, swap_pair(): return lax.ppermute(value, ('group', 'replica'), pairs)  21.8 us
    ppermute x16, waiting for transfers between devices, swap_pair(): return lax.ppermute(value, ('group', 'replica'), pairs)  21.4 us
    ppermute x5, waiting for transfers between devices, swap_plane(): return lax.ppermute(value, 'replica', pairs)  12 us
    ppermute x5, starting transfers between devices, swap_plane(): return lax.ppermute(value, 'replica', pairs)  10.9 us
    pallas_call x1, Pallas kernels, run_feed(): pl.pallas_call(feed_kernel, grid=(2,), in_specs=[SMEM_SPEC] + [whole((2,...  9.6 us
    pallas_call x2, Pallas kernels, run_attention_backward(): pl.pallas_call(functools.partial(attention_backward_kernel, slot), grid=(...  9.07 us
    pallas_call x8, Pallas kernels, small_call(): pl.pallas_call(kernel, grid=(1,), in_specs=[SMEM_SPEC] + [whole(item.shap...  7.88 us
    sub x3, other arithmetic, adam_update(): updated = weight * (1.0 - step_rate * decay_flag * DECAY_RATE) - change  4.18 us
  transfers between devices with their start and end apart: 32, of which 14 were waited for; matrix products, arithmetic and copies ran while one was open for 4% of the time, Pallas kernels for 17%

profile of v7, /device:TPU:0, one launch (start us, length us, event | category | flops | bytes accessed | tf_op | source)
XLA Modules:
  0.0 112.2 jit_solution(15231666216403862033)
XLA Ops:
  0.7 2.8 %own_payload.1 = (bf16[208,384]{1,0:T(8,128)(2,1)}, bf16[384,384]{1,0:T(8,128)(2,1)}) custom-call(f32[2,384]{1,0:T(2,128)} %condition.3, bf16[96,1152]{1,0:T(8,128)(2,1)} %own_att.1, bf16[96,384]{1,0:T(8,128)(2,1)} %own_proj.1, bf16[14,96]{1,0:T(8,128)(2,1)} %bias.1, bf16[384,384]{1,0:T(8,128)(2,1)} %own_expand.1, bf16[384,384]{1,0:T(8,128)(2,1)} %own_contract.1), custom_call_target="tpu_custom_call" | custom-call | tf_op jit(solution)/shard_map/own_payload/pallas_call | solution.py:694
  3.5 0.0 copy-start.4
  3.5 3.0 %collective-permute-start = (bf16[208,384]{1,0:T(8,128)(2,1)}, bf16[208,384]{1,0:T(8,128)(2,1)S(1)}, u32[]{:S(2)}, u32[]{:S(2)}) collective-permute-start(bf16[208,384]{1,0:T(8,128)(2,1)} %get-tuple-element.74), channel_id=1, source_target_pairs={{0,8},{1,17},{2,10},{3,19},{4,12},{5,21},{6,14},{7,23},{8,0},{9,25... | collective-permute-start | bytes 479240 | tf_op jit(solution)/shard_map/ppermute | solution.py:927
  6.5 1.5 %collective-permute-start.1 = (bf16[208,384]{1,0:T(8,128)(2,1)}, bf16[208,384]{1,0:T(8,128)(2,1)S(1)}, u32[]{:S(2)}, u32[]{:S(2)}) collective-permute-start(bf16[208,384]{1,0:T(8,128)(2,1)} %get-tuple-element.74), channel_id=1, source_target_pairs={{0,16},{1,9},{2,18},{3,11},{4,20},{5,13},{6,22},{7,15},{8,24},{9,1... | collective-permute-start | bytes 479240 | tf_op jit(solution)/shard_map/ppermute | solution.py:927
  8.1 3.2 %collective-permute-done.first.n1 = bf16[208,384]{1,0:T(8,128)(2,1)S(1)} collective-permute-done((bf16[208,384]{1,0:T(8,128)(2,1)}, bf16[208,384]{1,0:T(8,128)(2,1)S(1)}, u32[]{:S(2)}, u32[]{:S(2)}) %collective-permute-start) | collective-permute-done | bytes 159776 | tf_op jit(solution)/shard_map/ppermute | solution.py:927
  11.3 1.5 %collective-permute-start.2 = (bf16[208,384]{1,0:T(8,128)(2,1)S(1)}, bf16[208,384]{1,0:T(8,128)(2,1)S(1)}, u32[]{:S(2)}, u32[]{:S(2)}) collective-permute-start(bf16[208,384]{1,0:T(8,128)(2,1)S(1)} %collective-permute-done.first.n1), channel_id=1, source_target_pairs={{0,16},{1,9},{2,18},{3,11},{4,20},{5,13},{6,22},{7,15},{8,24},{9,1... | collective-permute-start | bytes 479240 | tf_op jit(solution)/shard_map/ppermute | solution.py:927
  12.7 2.3 %collective-permute-start.5 = (bf16[384,384]{1,0:T(8,128)(2,1)}, bf16[384,384]{1,0:T(8,128)(2,1)S(1)}, u32[]{:S(2)}, u32[]{:S(2)}) collective-permute-start(bf16[384,384]{1,0:T(8,128)(2,1)} %in_order.3), channel_id=1, source_target_pairs={{0,8},{1,17},{2,10},{3,19},{4,12},{5,21},{6,14},{7,23},{8,0},{9,25... | collective-permute-start | bytes 884744 | tf_op jit(solution)/shard_map/ppermute | solution.py:927
  15.0 0.7 collective-permute-start.9
  16.4 0.1 collective-permute-start.7
  16.5 0.1 collective-permute-done.2.last.n3
  16.5 0.4 collective-permute-start.8
  17.0 0.1 pad_add_fusion.where
  17.1 1.0 modulation_partials.1
  18.1 3.0 %collective-permute-start.3 = (f32[4,2304]{1,0:T(4,128)S(1)}, f32[4,2304]{1,0:T(4,128)S(1)}, u32[]{:S(2)}, u32[]{:S(2)}) collective-permute-start(f32[4,2304]{1,0:T(4,128)S(1)} %get-tuple-element.76), channel_id=1, source_target_pairs={{0,8},{1,17},{2,10},{3,19},{4,12},{5,21},{6,14},{7,23},{8,0},{9,25... | collective-permute-start | bytes 110600 | tf_op jit(solution)/shard_map/ppermute | solution.py:927
  21.0 2.5 %collective-permute-done.3.arrived = f32[4,2304]{1,0:T(4,128)S(1)} collective-permute-done((f32[4,2304]{1,0:T(4,128)S(1)}, f32[4,2304]{1,0:T(4,128)S(1)}, u32[]{:S(2)}, u32[]{:S(2)}) %collective-permute-start.3) | collective-permute-done | bytes 36896 | tf_op jit(solution)/shard_map/ppermute | solution.py:927
  23.5 0.6 relay.1
  24.0 1.1 collective-permute-start.6
  25.1 1.0 collective-permute-start.10
  26.2 0.5 collective-permute-start.12
  26.7 1.2 %collective-permute-done.6.arrived = f32[2,2304]{1,0:T(2,128)S(1)} collective-permute-done((f32[2,2304]{1,0:T(2,128)S(1)}, f32[2,2304]{1,0:T(2,128)S(1)}, u32[]{:S(2)}, u32[]{:S(2)}) %collective-permute-start.6) | collective-permute-done | bytes 18464 | tf_op jit(solution)/shard_map/ppermute | solution.py:927
  27.9 0.0 copy-start.2
  27.9 3.9 %attention_forward.1 = (bf16[2,256,1152]{2,1,0:T(8,128)(2,1)S(1)}, bf16[2,6,256,256]{3,2,1,0:T(8,128)(2,1)S(1)}, bf16[2,256,384]{2,1,0:T(8,128)(2,1)S(1)}, f32[2...) custom-call(s32[4]{0:T(128)S(1)} %pad_add_fusion.where, ...), custom_call_target="tpu_custom_call" | custom-call | flops 3000000000 | bytes 6000000 | tf_op jit(solution)/shard_map/attention_forward/pallas_call | solution.py:750
  31.9 0.1 collective-permute-start.13
  32.0 1.5 %collective-permute-done.13.f3 = bf16[384,384]{1,0:T(8,128)(2,1)S(1)} collective-permute-done((bf16[384,384]{1,0:T(8,128)(2,1)S(1)}, bf16[384,384]{1,0:T(8,128)(2,1)S(1)}, u32[]{:S(2)}, u32[]{:S(2)}) %collective-permute-start.13) | collective-permute-done | bytes 294944 | tf_op jit(solution)/shard_map/ppermute | solution.py:79
  33.6 9.6 %feed_forward_and_back.1 = (bf16[2,256,384]{2,1,0:T(8,128)(2,1)}, f32[2,256,384]{2,1,0:T(8,128)S(1)}, bf16[4,384,384]{2,1,0:T(8,128)(2,1)S(1)}, bf16[4,384,384]{2,1,0:T(8,128)(2,1)S(1)}, f32[16,384]{1,0:T(8,128)S(1)}) custom-call(s32[4]{0:T(128)S(1)} %pad_add_fusion.where, bf16[2,256,384]{2,1,0:T(8,128)(2,1)S(1)} %get-tuple-element.81.mixed, ...), custom_call_target="tpu_custom_call" | custom-call | flops 8000000000 | bytes 10000000 | tf_op jit(solution)/shard_map/feed_forward_and_back/pallas_call | solution.py:790
  43.1 0.1 collective-permute-start.14
  43.3 4.0 %attention_backward.2 = (bf16[2,256,384]{2,1,0:T(8,128)(2,1)}, bf16[256,1152]{1,0:T(8,128)(2,1)S(1)}, bf16[256,384]{1,0:T(8,128)(2,1)S(1)}, bf16[256,384]{1,0:T(8,128)(2,1)S(1)}, f32[32,384]{1,0:T(8,128)S(1)}) custom-call(s32[4]{0:T(128)S(1)} %pad_add_fusion.where, bf16[2,256,384]{2,1,0:T(8,128)(2,1)S(1)} %copy-done.13, ...), custom_call_target="tpu_custom_call" | custom-call | flops 4000000000 | bytes 8000000 | tf_op jit(solution)/shard_map/attention_backward/pallas_call | solution.py:865
  47.3 0.7 sum_to_send.1.refs_5_
  48.0 1.7 %collective-permute-start.17 = (bf16[2,384,384]{2,1,0:T(8,128)(2,1)S(1)}, bf16[2,384,384]{2,1,0:T(8,128)(2,1)S(1)}, u32[]{:S(2)}, u32[]{:S(2)}) collective-permute-start(bf16[2,384,384]{2,1,0:T(8,128)(2,1)S(1)} %sum_to_send.1.refs_5_), channel_id=1, source_target_pairs={{0,8},{1,17},{2,10},{3,19},{4,12},{5,21},{6,14},{7,23},{8,0},{9,25... | collective-permute-start | bytes 1769480 | tf_op jit(solution)/shard_map/ppermute | solution.py:927
  49.7 5.0 %attention_backward.3 = (bf16[2,256,384]{2,1,0:T(8,128)(2,1)}, bf16[4,192,384]{2,1,0:T(8,128)(2,1)S(1)}, bf16[4,192,384]{2,1,0:T(8,128)(2,1)S(1)}, bf16[32,384]{1,0:T(8,128)(2,1)S(1)}) custom-call(s32[4]{0:T(128)S(1)} %pad_add_fusion.where, bf16[2,256,384]{2,1,0:T(8,128)(2,1)S(1)} %copy-done.13, ...), custom_call_target="tpu_custom_call", output_to_operand_aliasing={{0}: (15, {})} | custom-call | flops 4000000000 | bytes 8000000 | tf_op jit(solution)/shard_map/attention_backward/pallas_call | solution.py:865
  54.8 3.2 %collective-permute-done.17.arrived = bf16[2,384,384]{2,1,0:T(8,128)(2,1)S(1)} collective-permute-done((bf16[2,384,384]{2,1,0:T(8,128)(2,1)S(1)}, bf16[2,384,384]{2,1,0:T(8,128)(2,1)S(1)}, u32[]{:S(2)}, u32[]{:S(2)}) %collective-permute-start.17) | collective-permute-done | bytes 589856 | tf_op jit(solution)/shard_map/ppermute | solution.py:927
  57.9 0.7 sum_and_split.3
  58.7 1.1 collective-permute-start.18
  59.8 0.1 sum_and_split.2
  59.9 1.8 %collective-permute-start.16 = (bf16[2,192,384]{2,1,0:T(8,128)(2,1)S(1)}, bf16[2,192,384]{2,1,0:T(8,128)(2,1)S(1)}, u32[]{:S(2)}, u32[]{:S(2)}) collective-permute-start(bf16[2,192,384]{2,1,0:T(8,128)(2,1)S(1)} %get-tuple-element.102), channel_id=1, source_target_pairs={{0,8},{1,17},{2,10},{3,19},{4,12},{5,21},{6,14},{7,23},{8,0},{9,25... | collective-permute-start | bytes 884744 | tf_op jit(solution)/shard_map/ppermute | solution.py:927
  61.7 1.6 %collective-permute-start.19 = (bf16[32,384]{1,0:T(8,128)(2,1)S(1)}, bf16[32,384]{1,0:T(8,128)(2,1)S(1)}, u32[]{:S(2)}, u32[]{:S(2)}) collective-permute-start(bf16[32,384]{1,0:T(8,128)(2,1)S(1)} %get-tuple-element.105.small), channel_id=1, source_target_pairs={{0,2},{1,5},{2,0},{3,7},{4,6},{5,1},{6,4},{7,3},{8,10},{9,13},{10,... | collective-permute-start | bytes 73736 | tf_op jit(solution)/shard_map/ppermute | solution.py:917
  63.3 2.3 %collective-permute-done.19.small_in = bf16[32,384]{1,0:T(8,128)(2,1)S(1)} collective-permute-done((bf16[32,384]{1,0:T(8,128)(2,1)S(1)}, bf16[32,384]{1,0:T(8,128)(2,1)S(1)}, u32[]{:S(2)}, u32[]{:S(2)}) %collective-permute-start.19) | collective-permute-done | bytes 24608 | tf_op jit(solution)/shard_map/ppermute | solution.py:917
  65.5 2.9 %collective-permute-done.18.feed_in = bf16[384,384]{1,0:T(8,128)(2,1)S(1)} collective-permute-done((bf16[384,384]{1,0:T(8,128)(2,1)S(1)}, bf16[384,384]{1,0:T(8,128)(2,1)S(1)}, u32[]{:S(2)}, u32[]{:S(2)}) %collective-permute-start.18) | collective-permute-done | bytes 294944 | tf_op jit(solution)/shard_map/ppermute | solution.py:927
  68.5 0.7 step_1.1
  69.2 1.0 collective-permute-start.20
  70.3 2.0 %collective-permute-start.21 = (bf16[192,384]{1,0:T(8,128)(2,1)S(1)}, bf16[192,384]{1,0:T(8,128)(2,1)S(1)}, u32[]{:S(2)}, u32[]{:S(2)}) collective-permute-start(bf16[192,384]{1,0:T(8,128)(2,1)S(1)} %get-tuple-element.109), channel_id=1, source_target_pairs={{0,2},{1,5},{2,0},{3,7},{4,6},{5,1},{6,4},{7,3},{8,10},{9,13},{10,... | collective-permute-start | bytes 442376 | tf_op jit(solution)/shard_map/ppermute | solution.py:917
  72.3 2.6 %collective-permute-start.22 = (bf16[48,384]{1,0:T(8,128)(2,1)S(1)}, bf16[48,384]{1,0:T(8,128)(2,1)S(1)}, u32[]{:S(2)}, u32[]{:S(2)}) collective-permute-start(bf16[48,384]{1,0:T(8,128)(2,1)S(1)} %get-tuple-element.110.small), channel_id=1, source_target_pairs={{0,4},{1,3},{2,6},{3,1},{4,0},{5,7},{6,2},{7,5},{8,12},{9,11},{10,... | collective-permute-start | bytes 110600 | tf_op jit(solution)/shard_map/ppermute | solution.py:917
  74.9 2.3 %collective-permute-done.22.small_in = bf16[48,384]{1,0:T(8,128)(2,1)S(1)} collective-permute-done((bf16[48,384]{1,0:T(8,128)(2,1)S(1)}, bf16[48,384]{1,0:T(8,128)(2,1)S(1)}, u32[]{:S(2)}, u32[]{:S(2)}) %collective-permute-start.22) | collective-permute-done | bytes 36896 | tf_op jit(solution)/shard_map/ppermute | solution.py:917
  77.1 0.6 step_2.1
  77.7 2.7 %collective-permute-start.23 = (bf16[384,384]{1,0:T(8,128)(2,1)S(1)}, bf16[384,384]{1,0:T(8,128)(2,1)S(1)}, u32[]{:S(2)}, u32[]{:S(2)}) collective-permute-start(bf16[384,384]{1,0:T(8,128)(2,1)S(1)} %get-tuple-element.111.own), channel_id=1, source_target_pairs={{0,4},{1,3},{2,6},{3,1},{4,0},{5,7},{6,2},{7,5},{8,12},{9,11},{10,... | collective-permute-start | bytes 884744 | tf_op jit(solution)/shard_map/ppermute | solution.py:917
  80.4 1.2 %collective-permute-start.24 = (bf16[80,384]{1,0:T(8,128)(2,1)S(1)}, bf16[80,384]{1,0:T(8,128)(2,1)S(1)}, u32[]{:S(2)}, u32[]{:S(2)}) collective-permute-start(bf16[80,384]{1,0:T(8,128)(2,1)S(1)} %get-tuple-element.112.small), channel_id=1, source_target_pairs={{0,16},{1,9},{2,18},{3,11},{4,20},{5,13},{6,22},{7,15},{8,24},{9,1... | collective-permute-start | bytes 184328 | tf_op jit(solution)/shard_map/ppermute | solution.py:927
  81.6 3.0 %collective-permute-done.24.small_in = bf16[80,384]{1,0:T(8,128)(2,1)S(1)} collective-permute-done((bf16[80,384]{1,0:T(8,128)(2,1)S(1)}, bf16[80,384]{1,0:T(8,128)(2,1)S(1)}, u32[]{:S(2)}, u32[]{:S(2)}) %collective-permute-start.24) | collective-permute-done | bytes 61472 | tf_op jit(solution)/shard_map/ppermute | solution.py:927
  84.6 7.4 %collective-permute-done.23.arrived = bf16[384,384]{1,0:T(8,128)(2,1)S(1)} collective-permute-done((bf16[384,384]{1,0:T(8,128)(2,1)S(1)}, bf16[384,384]{1,0:T(8,128)(2,1)S(1)}, u32[]{:S(2)}, u32[]{:S(2)}) %collective-permute-start.23) | collective-permute-done | bytes 294944 | tf_op jit(solution)/shard_map/ppermute | solution.py:917
  92.1 0.6 step_3.1
  92.7 2.1 %collective-permute-start.25 = (bf16[384,384]{1,0:T(8,128)(2,1)S(1)}, bf16[384,384]{1,0:T(8,128)(2,1)S(1)}, u32[]{:S(2)}, u32[]{:S(2)}) collective-permute-start(bf16[384,384]{1,0:T(8,128)(2,1)S(1)} %get-tuple-element.113.own), channel_id=1, source_target_pairs={{0,2},{1,5},{2,0},{3,7},{4,6},{5,1},{6,4},{7,3},{8,10},{9,13},{10,... | collective-permute-start | bytes 884744 | tf_op jit(solution)/shard_map/ppermute | solution.py:917
  94.8 4.7 %collective-permute-done.26.small_in = bf16[144,384]{1,0:T(8,128)(2,1)S(1)} collective-permute-done((bf16[144,384]{1,0:T(8,128)(2,1)S(1)}, bf16[144,384]{1,0:T(8,128)(2,1)S(1)}, u32[]{:S(2)}, u32[]{:S(2)}) %collective-permute-start.26) | collective-permute-done | bytes 110624 | tf_op jit(solution)/shard_map/ppermute | solution.py:927
  99.5 0.9 step_4.1
  100.4 0.5 collective-permute-start.30
  101.0 0.1 collective-permute-start.28
  101.0 0.8 collective-permute-done.31
  101.9 0.8 fusion.21
  102.8 1.2 %fusion.16 = (f32[96,1152]{1,0:T(8,128)}, f32[96,1152]{1,0:T(8,128)}, f32[96,1152]{1,0:T(8,128)}) fusion(bf16[96,1152]{1,0:T(8,128)(2,1)S(1)} %copy-done.4, f32[96,384]{1,0:T(8,128)S(1)} %get-tuple-element.142, f32[96,384]{1,0:T(8,128)S(1)} %get-tuple-element.144, f32[96,384]{1,0:T(8,128)S(1)} %get-tuple-element.143, bf16[96,1152]{1,0:T(8,128)(2,1)S(1)} %copy-done.18, ...), kind=kLoop, calls=%fused_computation.24 | loop fusion | flops 2101248 | bytes 2433024 | tf_op jit(solution)/shard_map/sub | solution.py:57
  104.0 0.2 copy-done.6
  104.2 3.1 %modulation_update.1 = (f32[96,2304]{1,0:T(8,128)}, f32[96,2304]{1,0:T(8,128)}, f32[96,2304]{1,0:T(8,128)}, f32[14,96]{1,0:T(8,128)}, f32[14,96]{1,0:T(8,128)}, /*index=5*/f32[14,96]{1,0:T(8,128)}, f32[8,128]{1,0:T(8,128)S(1)}) custom-call(s32[4]{0:T(128)S(1)} %pad_add_fusion.where, bf16[272,384]{1,0:T(8,128)(2,1)S(1)} %get-tuple-element.117.near, ...), custom_call_target="tpu_custom_call" | custom-call | tf_op jit(solution)/shard_map/modulation_update/pallas_call | solution.py:678
  107.3 0.5 step_5.1
  107.8 0.9 collective-permute-start.29
  108.8 2.2 %fusion.11 = (f32[384,384]{1,0:T(8,128)}, f32[384,384]{1,0:T(8,128)}, f32[384,384]{1,0:T(8,128)}, f32[384,384]{1,0:T(8,128)}, f32[384,384]{1,0:T(8,128)}, /*index=5*/f32[384,384]{1,0:T(8,128)S(1)}) fusion(bf16[384,384]{1,0:T(8,128)(2,1)S(1)} %copy-done.3, bf16[384,384]{1,0:T(8,128)(2,1)S(1)} %collective-permute-done.30, ...), kind=kLoop, calls=%fused_computation.19 | loop fusion | flops 5603328 | bytes 5898241 | tf_op jit(solution)/shard_map/sub | solution.py:57
  110.9 0.6 collective-permute-done.29.refs_0_
  111.5 0.7 fusion.22
  (73 shorter events, 0.3 us)
Async XLA Ops:
  0.7 16.4 %copy-start.8 = (f32[2,384]{1,0:T(2,128)S(1)}, f32[2,384]{1,0:T(2,128)}, u32[]{:S(2)}) copy-start(f32[2,384]{1,0:T(2,128)} %condition.3) | copy-start | bytes 9220
  0.7 16.4 %copy-start.9 = (bf16[14,96]{1,0:T(8,128)(2,1)S(1)}, bf16[14,96]{1,0:T(8,128)(2,1)}, u32[]{:S(2)}) copy-start(bf16[14,96]{1,0:T(8,128)(2,1)} %bias.1) | copy-start | bytes 8068
  0.7 16.4 %copy-start = (bf16[96,2304]{1,0:T(8,128)(2,1)S(1)}, bf16[96,2304]{1,0:T(8,128)(2,1)}, u32[]{:S(2)}) copy-start(bf16[96,2304]{1,0:T(8,128)(2,1)} %weight.5) | copy-start | bytes 1327108
  3.5 24.4 %copy-start.4 = (bf16[96,1152]{1,0:T(8,128)(2,1)S(1)}, bf16[96,1152]{1,0:T(8,128)(2,1)}, u32[]{:S(2)}) copy-start(bf16[96,1152]{1,0:T(8,128)(2,1)} %own_att.1) | copy-start | bytes 663556
  3.5 24.4 %copy-start.7 = (bf16[96,384]{1,0:T(8,128)(2,1)S(1)}, bf16[96,384]{1,0:T(8,128)(2,1)}, u32[]{:S(2)}) copy-start(bf16[96,384]{1,0:T(8,128)(2,1)} %own_proj.1) | copy-start | bytes 221188
  3.5 24.4 %copy-start.13 = (bf16[2,256,384]{2,1,0:T(8,128)(2,1)S(1)}, bf16[2,256,384]{2,1,0:T(8,128)(2,1)}, u32[]{:S(2)}) copy-start(bf16[2,256,384]{2,1,0:T(8,128)(2,1)} %tokens.7) | copy-start | bytes 1179652
  3.5 7.7 %collective-permute-start = (bf16[208,384]{1,0:T(8,128)(2,1)}, bf16[208,384]{1,0:T(8,128)(2,1)S(1)}, u32[]{:S(2)}, u32[]{:S(2)}) collective-permute-start(bf16[208,384]{1,0:T(8,128)(2,1)} %get-tuple-element.74), channel_id=1, source_target_pairs={{0,8},{1,17},{2,10},{3,19},{4,12},{5,21},{6,14},{7,23},{8,0},{9,25... | collective-permute-start | bytes 479240 | tf_op jit(solution)/shard_map/ppermute | solution.py:927
  6.5 6.2 %collective-permute-start.1 = (bf16[208,384]{1,0:T(8,128)(2,1)}, bf16[208,384]{1,0:T(8,128)(2,1)S(1)}, u32[]{:S(2)}, u32[]{:S(2)}) collective-permute-start(bf16[208,384]{1,0:T(8,128)(2,1)} %get-tuple-element.74), channel_id=1, source_target_pairs={{0,16},{1,9},{2,18},{3,11},{4,20},{5,13},{6,22},{7,15},{8,24},{9,1... | collective-permute-start | bytes 479240 | tf_op jit(solution)/shard_map/ppermute | solution.py:927
  11.2 1.5 %collective-permute-start.4 = (bf16[208,384]{1,0:T(8,128)(2,1)S(1)}, bf16[208,384]{1,0:T(8,128)(2,1)S(1)}, u32[]{:S(2)}, u32[]{:S(2)}) collective-permute-start(bf16[208,384]{1,0:T(8,128)(2,1)S(1)} %collective-permute-done.first.n1), channel_id=1, source_target_pairs={{0,1},{1,0},{2,3},{3,2},{4,5},{5,4},{6,7},{7,6},{8,9},{9,8},{10,11... | collective-permute-start | bytes 479240 | tf_op jit(solution)/shard_map/ppermute | solution.py:79
  11.3 5.3 %collective-permute-start.2 = (bf16[208,384]{1,0:T(8,128)(2,1)S(1)}, bf16[208,384]{1,0:T(8,128)(2,1)S(1)}, u32[]{:S(2)}, u32[]{:S(2)}) collective-permute-start(bf16[208,384]{1,0:T(8,128)(2,1)S(1)} %collective-permute-done.first.n1), channel_id=1, source_target_pairs={{0,16},{1,9},{2,18},{3,11},{4,20},{5,13},{6,22},{7,15},{8,24},{9,1... | collective-permute-start | bytes 479240 | tf_op jit(solution)/shard_map/ppermute | solution.py:927
  12.7 10.8 %collective-permute-start.5 = (bf16[384,384]{1,0:T(8,128)(2,1)}, bf16[384,384]{1,0:T(8,128)(2,1)S(1)}, u32[]{:S(2)}, u32[]{:S(2)}) collective-permute-start(bf16[384,384]{1,0:T(8,128)(2,1)} %in_order.3), channel_id=1, source_target_pairs={{0,8},{1,17},{2,10},{3,19},{4,12},{5,21},{6,14},{7,23},{8,0},{9,25... | collective-permute-start | bytes 884744 | tf_op jit(solution)/shard_map/ppermute | solution.py:927
  15.0 11.1 %collective-permute-start.9 = (bf16[384,384]{1,0:T(8,128)(2,1)}, bf16[384,384]{1,0:T(8,128)(2,1)S(1)}, u32[]{:S(2)}, u32[]{:S(2)}) collective-permute-start(bf16[384,384]{1,0:T(8,128)(2,1)} %in_order.3), channel_id=1, source_target_pairs={{0,16},{1,9},{2,18},{3,11},{4,20},{5,13},{6,22},{7,15},{8,24},{9,1... | collective-permute-start | bytes 884744 | tf_op jit(solution)/shard_map/ppermute | solution.py:927
  16.4 9.7 %collective-permute-start.7 = (bf16[208,384]{1,0:T(8,128)(2,1)S(1)}, bf16[208,384]{1,0:T(8,128)(2,1)S(1)}, u32[]{:S(2)}, u32[]{:S(2)}) collective-permute-start(bf16[208,384]{1,0:T(8,128)(2,1)S(1)} %collective-permute-done.1.second.refs_2_.n2), channel_id=1, source_target_pairs={{0,1},{1,0},{2,3},{3,2},{4,5},{5,4},{6,7},{7,6},{8,9},{9,8},{10,11... | collective-permute-start | bytes 479240 | tf_op jit(solution)/shard_map/ppermute | solution.py:79
  16.5 10.1 %collective-permute-start.8 = (bf16[208,384]{1,0:T(8,128)(2,1)S(1)}, bf16[208,384]{1,0:T(8,128)(2,1)S(1)}, u32[]{:S(2)}, u32[]{:S(2)}) collective-permute-start(bf16[208,384]{1,0:T(8,128)(2,1)S(1)} %collective-permute-done.2.last.n3), channel_id=1, source_target_pairs={{0,1},{1,0},{2,3},{3,2},{4,5},{5,4},{6,7},{7,6},{8,9},{9,8},{10,11... | collective-permute-start | bytes 479240 | tf_op jit(solution)/shard_map/ppermute | solution.py:79
  18.1 5.4 %collective-permute-start.3 = (f32[4,2304]{1,0:T(4,128)S(1)}, f32[4,2304]{1,0:T(4,128)S(1)}, u32[]{:S(2)}, u32[]{:S(2)}) collective-permute-start(f32[4,2304]{1,0:T(4,128)S(1)} %get-tuple-element.76), channel_id=1, source_target_pairs={{0,8},{1,17},{2,10},{3,19},{4,12},{5,21},{6,14},{7,23},{8,0},{9,25... | collective-permute-start | bytes 110600 | tf_op jit(solution)/shard_map/ppermute | solution.py:927
  24.0 3.8 %collective-permute-start.6 = (f32[2,2304]{1,0:T(2,128)S(1)}, f32[2,2304]{1,0:T(2,128)S(1)}, u32[]{:S(2)}, u32[]{:S(2)}) collective-permute-start(f32[2,2304]{1,0:T(2,128)S(1)} %get-tuple-element.79), channel_id=1, source_target_pairs={{0,16},{1,9},{2,18},{3,11},{4,20},{5,13},{6,22},{7,15},{8,24},{9,1... | collective-permute-start | bytes 55304 | tf_op jit(solution)/shard_map/ppermute | solution.py:927
  25.1 6.7 %collective-permute-start.10 = (bf16[384,384]{1,0:T(8,128)(2,1)S(1)}, bf16[384,384]{1,0:T(8,128)(2,1)S(1)}, u32[]{:S(2)}, u32[]{:S(2)}) collective-permute-start(bf16[384,384]{1,0:T(8,128)(2,1)S(1)} %get-tuple-element.84.n1), channel_id=1, source_target_pairs={{0,16},{1,9},{2,18},{3,11},{4,20},{5,13},{6,22},{7,15},{8,24},{9,1... | collective-permute-start | bytes 884744 | tf_op jit(solution)/shard_map/ppermute | solution.py:927
  26.1 5.8 %collective-permute-start.11 = (bf16[384,384]{1,0:T(8,128)(2,1)S(1)}, bf16[384,384]{1,0:T(8,128)(2,1)S(1)}, u32[]{:S(2)}, u32[]{:S(2)}) collective-permute-start(bf16[384,384]{1,0:T(8,128)(2,1)S(1)} %get-tuple-element.84.n1), channel_id=1, source_target_pairs={{0,1},{1,0},{2,3},{3,2},{4,5},{5,4},{6,7},{7,6},{8,9},{9,8},{10,11... | collective-permute-start | bytes 884744 | tf_op jit(solution)/shard_map/ppermute | solution.py:79
  26.2 5.8 %collective-permute-start.12 = (bf16[384,384]{1,0:T(8,128)(2,1)S(1)}, bf16[384,384]{1,0:T(8,128)(2,1)S(1)}, u32[]{:S(2)}, u32[]{:S(2)}) collective-permute-start(bf16[384,384]{1,0:T(8,128)(2,1)S(1)} %collective-permute-done.9.n2), channel_id=1, source_target_pairs={{0,1},{1,0},{2,3},{3,2},{4,5},{5,4},{6,7},{7,6},{8,9},{9,8},{10,11... | collective-permute-start | bytes 884744 | tf_op jit(solution)/shard_map/ppermute | solution.py:79
  27.9 5.7 %copy-start.2 = (bf16[384,384]{1,0:T(8,128)(2,1)S(1)}, bf16[384,384]{1,0:T(8,128)(2,1)}, u32[]{:S(2)}) copy-start(bf16[384,384]{1,0:T(8,128)(2,1)} %own_expand.1) | copy-start | bytes 884740
  27.9 5.7 %copy-start.3 = (bf16[384,384]{1,0:T(8,128)(2,1)S(1)}, bf16[384,384]{1,0:T(8,128)(2,1)}, u32[]{:S(2)}) copy-start(bf16[384,384]{1,0:T(8,128)(2,1)} %own_contract.1) | copy-start | bytes 884740
  27.9 5.6 %copy-start.12 = (bf16[2,256,384]{2,1,0:T(8,128)(2,1)S(1)}, bf16[2,256,384]{2,1,0:T(8,128)(2,1)}, u32[]{:S(2)}) copy-start(bf16[2,256,384]{2,1,0:T(8,128)(2,1)} %cotangent.1) | copy-start | bytes 1179652
  31.9 1.6 %collective-permute-start.13 = (bf16[384,384]{1,0:T(8,128)(2,1)S(1)}, bf16[384,384]{1,0:T(8,128)(2,1)S(1)}, u32[]{:S(2)}, u32[]{:S(2)}) collective-permute-start(bf16[384,384]{1,0:T(8,128)(2,1)S(1)} %in_order.4.n3), channel_id=1, source_target_pairs={{0,1},{1,0},{2,3},{3,2},{4,5},{5,4},{6,7},{7,6},{8,9},{9,8},{10,11... | collective-permute-start | bytes 884744 | tf_op jit(solution)/shard_map/ppermute | solution.py:79
  43.1 4.2 %collective-permute-start.14 = (bf16[4,384,384]{2,1,0:T(8,128)(2,1)S(1)}, bf16[4,384,384]{2,1,0:T(8,128)(2,1)S(1)}, u32[]{:S(2)}, u32[]{:S(2)}) collective-permute-start(bf16[4,384,384]{2,1,0:T(8,128)(2,1)S(1)} %get-tuple-element.97), channel_id=1, source_target_pairs={{0,1},{1,0},{2,3},{3,2},{4,5},{5,4},{6,7},{7,6},{8,9},{9,8},{10,11... | collective-permute-start | bytes 3538952 | tf_op jit(solution)/shard_map/ppermute | solution.py:79
  48.0 9.9 %collective-permute-start.17 = (bf16[2,384,384]{2,1,0:T(8,128)(2,1)S(1)}, bf16[2,384,384]{2,1,0:T(8,128)(2,1)S(1)}, u32[]{:S(2)}, u32[]{:S(2)}) collective-permute-start(bf16[2,384,384]{2,1,0:T(8,128)(2,1)S(1)} %sum_to_send.1.refs_5_), channel_id=1, source_target_pairs={{0,8},{1,17},{2,10},{3,19},{4,12},{5,21},{6,14},{7,23},{8,0},{9,25... | collective-permute-start | bytes 1769480 | tf_op jit(solution)/shard_map/ppermute | solution.py:927
  54.8 5.0 %collective-permute-start.15 = (bf16[4,192,384]{2,1,0:T(8,128)(2,1)S(1)}, bf16[4,192,384]{2,1,0:T(8,128)(2,1)S(1)}, u32[]{:S(2)}, u32[]{:S(2)}) collective-permute-start(bf16[4,192,384]{2,1,0:T(8,128)(2,1)S(1)} %get-tuple-element.100), channel_id=1, source_target_pairs={{0,1},{1,0},{2,3},{3,2},{4,5},{5,4},{6,7},{7,6},{8,9},{9,8},{10,11... | collective-permute-start | bytes 1769480 | tf_op jit(solution)/shard_map/ppermute | solution.py:79
  58.7 9.8 %collective-permute-start.18 = (bf16[384,384]{1,0:T(8,128)(2,1)S(1)}, bf16[384,384]{1,0:T(8,128)(2,1)S(1)}, u32[]{:S(2)}, u32[]{:S(2)}) collective-permute-start(bf16[384,384]{1,0:T(8,128)(2,1)S(1)} %get-tuple-element.104), channel_id=1, source_target_pairs={{0,16},{1,9},{2,18},{3,11},{4,20},{5,13},{6,22},{7,15},{8,24},{9,1... | collective-permute-start | bytes 884744 | tf_op jit(solution)/shard_map/ppermute | solution.py:927
  59.9 8.6 %collective-permute-start.16 = (bf16[2,192,384]{2,1,0:T(8,128)(2,1)S(1)}, bf16[2,192,384]{2,1,0:T(8,128)(2,1)S(1)}, u32[]{:S(2)}, u32[]{:S(2)}) collective-permute-start(bf16[2,192,384]{2,1,0:T(8,128)(2,1)S(1)} %get-tuple-element.102), channel_id=1, source_target_pairs={{0,8},{1,17},{2,10},{3,19},{4,12},{5,21},{6,14},{7,23},{8,0},{9,25... | collective-permute-start | bytes 884744 | tf_op jit(solution)/shard_map/ppermute | solution.py:927
  61.7 3.8 %collective-permute-start.19 = (bf16[32,384]{1,0:T(8,128)(2,1)S(1)}, bf16[32,384]{1,0:T(8,128)(2,1)S(1)}, u32[]{:S(2)}, u32[]{:S(2)}) collective-permute-start(bf16[32,384]{1,0:T(8,128)(2,1)S(1)} %get-tuple-element.105.small), channel_id=1, source_target_pairs={{0,2},{1,5},{2,0},{3,7},{4,6},{5,1},{6,4},{7,3},{8,10},{9,13},{10,... | collective-permute-start | bytes 73736 | tf_op jit(solution)/shard_map/ppermute | solution.py:917
  69.2 7.9 %collective-permute-start.20 = (bf16[192,384]{1,0:T(8,128)(2,1)S(1)}, bf16[192,384]{1,0:T(8,128)(2,1)S(1)}, u32[]{:S(2)}, u32[]{:S(2)}) collective-permute-start(bf16[192,384]{1,0:T(8,128)(2,1)S(1)} %get-tuple-element.107), channel_id=1, source_target_pairs={{0,16},{1,9},{2,18},{3,11},{4,20},{5,13},{6,22},{7,15},{8,24},{9,1... | collective-permute-start | bytes 442376 | tf_op jit(solution)/shard_map/ppermute | solution.py:927
  70.3 6.9 %collective-permute-start.21 = (bf16[192,384]{1,0:T(8,128)(2,1)S(1)}, bf16[192,384]{1,0:T(8,128)(2,1)S(1)}, u32[]{:S(2)}, u32[]{:S(2)}) collective-permute-start(bf16[192,384]{1,0:T(8,128)(2,1)S(1)} %get-tuple-element.109), channel_id=1, source_target_pairs={{0,2},{1,5},{2,0},{3,7},{4,6},{5,1},{6,4},{7,3},{8,10},{9,13},{10,... | collective-permute-start | bytes 442376 | tf_op jit(solution)/shard_map/ppermute | solution.py:917
  72.3 4.9 %collective-permute-start.22 = (bf16[48,384]{1,0:T(8,128)(2,1)S(1)}, bf16[48,384]{1,0:T(8,128)(2,1)S(1)}, u32[]{:S(2)}, u32[]{:S(2)}) collective-permute-start(bf16[48,384]{1,0:T(8,128)(2,1)S(1)} %get-tuple-element.110.small), channel_id=1, source_target_pairs={{0,4},{1,3},{2,6},{3,1},{4,0},{5,7},{6,2},{7,5},{8,12},{9,11},{10,... | collective-permute-start | bytes 110600 | tf_op jit(solution)/shard_map/ppermute | solution.py:917
  77.7 14.3 %collective-permute-start.23 = (bf16[384,384]{1,0:T(8,128)(2,1)S(1)}, bf16[384,384]{1,0:T(8,128)(2,1)S(1)}, u32[]{:S(2)}, u32[]{:S(2)}) collective-permute-start(bf16[384,384]{1,0:T(8,128)(2,1)S(1)} %get-tuple-element.111.own), channel_id=1, source_target_pairs={{0,4},{1,3},{2,6},{3,1},{4,0},{5,7},{6,2},{7,5},{8,12},{9,11},{10,... | collective-permute-start | bytes 884744 | tf_op jit(solution)/shard_map/ppermute | solution.py:917
  80.4 4.2 %collective-permute-start.24 = (bf16[80,384]{1,0:T(8,128)(2,1)S(1)}, bf16[80,384]{1,0:T(8,128)(2,1)S(1)}, u32[]{:S(2)}, u32[]{:S(2)}) collective-permute-start(bf16[80,384]{1,0:T(8,128)(2,1)S(1)} %get-tuple-element.112.small), channel_id=1, source_target_pairs={{0,16},{1,9},{2,18},{3,11},{4,20},{5,13},{6,22},{7,15},{8,24},{9,1... | collective-permute-start | bytes 184328 | tf_op jit(solution)/shard_map/ppermute | solution.py:927
  92.7 6.9 %collective-permute-start.25 = (bf16[384,384]{1,0:T(8,128)(2,1)S(1)}, bf16[384,384]{1,0:T(8,128)(2,1)S(1)}, u32[]{:S(2)}, u32[]{:S(2)}) collective-permute-start(bf16[384,384]{1,0:T(8,128)(2,1)S(1)} %get-tuple-element.113.own), channel_id=1, source_target_pairs={{0,2},{1,5},{2,0},{3,7},{4,6},{5,1},{6,4},{7,3},{8,10},{9,13},{10,... | collective-permute-start | bytes 884744 | tf_op jit(solution)/shard_map/ppermute | solution.py:917
  94.8 7.1 %copy-start.20 = (bf16[96,384]{1,0:T(8,128)(2,1)S(1)}, bf16[96,384]{1,0:T(8,128)(2,1)}, u32[]{:S(2)}) copy-start(bf16[96,384]{1,0:T(8,128)(2,1)} %param.34) | copy-start | bytes 221188
  94.8 7.1 %copy-start.21 = (bf16[96,384]{1,0:T(8,128)(2,1)S(1)}, bf16[96,384]{1,0:T(8,128)(2,1)}, u32[]{:S(2)}) copy-start(bf16[96,384]{1,0:T(8,128)(2,1)} %param.40) | copy-start | bytes 221188
  94.8 4.7 %collective-permute-start.26 = (bf16[144,384]{1,0:T(8,128)(2,1)S(1)}, bf16[144,384]{1,0:T(8,128)(2,1)S(1)}, u32[]{:S(2)}, u32[]{:S(2)}) collective-permute-start(bf16[144,384]{1,0:T(8,128)(2,1)S(1)} %get-tuple-element.114.small), channel_id=1, source_target_pairs={{0,8},{1,17},{2,10},{3,19},{4,12},{5,21},{6,14},{7,23},{8,0},{9,25... | collective-permute-start | bytes 331784 | tf_op jit(solution)/shard_map/ppermute | solution.py:927
  100.4 1.4 %collective-permute-start.31 = (bf16[192,384]{1,0:T(8,128)(2,1)S(1)}, bf16[192,384]{1,0:T(8,128)(2,1)S(1)}, u32[]{:S(2)}, u32[]{:S(2)}) collective-permute-start(bf16[192,384]{1,0:T(8,128)(2,1)S(1)} %get-tuple-element.121), channel_id=1, source_target_pairs={{0,1},{1,0},{2,3},{3,2},{4,5},{5,4},{6,7},{7,6},{8,9},{9,8},{10,11... | collective-permute-start | bytes 442376 | tf_op jit(solution)/shard_map/ppermute | solution.py:79
  100.4 8.3 %collective-permute-start.30 = (bf16[384,384]{1,0:T(8,128)(2,1)S(1)}, bf16[384,384]{1,0:T(8,128)(2,1)S(1)}, u32[]{:S(2)}, u32[]{:S(2)}) collective-permute-start(bf16[384,384]{1,0:T(8,128)(2,1)S(1)} %get-tuple-element.119), channel_id=1, source_target_pairs={{0,1},{1,0},{2,3},{3,2},{4,5},{5,4},{6,7},{7,6},{8,9},{9,8},{10,11... | collective-permute-start | bytes 884744 | tf_op jit(solution)/shard_map/ppermute | solution.py:79
  101.0 3.0 %collective-permute-start.28 = (bf16[272,384]{1,0:T(8,128)(2,1)S(1)}, bf16[272,384]{1,0:T(8,128)(2,1)S(1)}, u32[]{:S(2)}, u32[]{:S(2)}) collective-permute-start(bf16[272,384]{1,0:T(8,128)(2,1)S(1)} %get-tuple-element.117.near), channel_id=1, source_target_pairs={{0,1},{1,0},{2,3},{3,2},{4,5},{5,4},{6,7},{7,6},{8,9},{9,8},{10,11... | collective-permute-start | bytes 626696 | tf_op jit(solution)/shard_map/ppermute | solution.py:79
  101.0 1.7 %copy-start.18 = (bf16[96,1152]{1,0:T(8,128)(2,1)S(1)}, bf16[96,1152]{1,0:T(8,128)(2,1)}, u32[]{:S(2)}) copy-start(bf16[96,1152]{1,0:T(8,128)(2,1)} %param.33) | copy-start | bytes 663556
  101.0 1.7 %copy-start.19 = (bf16[96,1152]{1,0:T(8,128)(2,1)S(1)}, bf16[96,1152]{1,0:T(8,128)(2,1)}, u32[]{:S(2)}) copy-start(bf16[96,1152]{1,0:T(8,128)(2,1)} %param.39) | copy-start | bytes 663556
  101.0 6.3 %collective-permute-start.27 = (f32[8,128]{1,0:T(8,128)S(1)}, f32[8,128]{1,0:T(8,128)S(1)}, u32[]{:S(2)}, u32[]{:S(2)}) collective-permute-start(f32[8,128]{1,0:T(8,128)S(1)} %get-tuple-element.116), channel_id=1, source_target_pairs={{0,8},{1,17},{2,10},{3,19},{4,12},{5,21},{6,14},{7,23},{8,0},{9,25... | collective-permute-start | bytes 12296 | tf_op jit(solution)/shard_map/ppermute | solution.py:927
  102.7 1.3 %copy-start.5 = (bf16[96,2304]{1,0:T(8,128)(2,1)S(1)}, bf16[96,2304]{1,0:T(8,128)(2,1)}, u32[]{:S(2)}) copy-start(bf16[96,2304]{1,0:T(8,128)(2,1)} %mean.1) | copy-start | bytes 1327108
  102.7 1.5 %copy-start.6 = (bf16[96,2304]{1,0:T(8,128)(2,1)S(1)}, bf16[96,2304]{1,0:T(8,128)(2,1)}, u32[]{:S(2)}) copy-start(bf16[96,2304]{1,0:T(8,128)(2,1)} %square.1) | copy-start | bytes 1327108
  102.7 1.4 %copy-start.10 = (bf16[14,96]{1,0:T(8,128)(2,1)S(1)}, bf16[14,96]{1,0:T(8,128)(2,1)}, u32[]{:S(2)}) copy-start(bf16[14,96]{1,0:T(8,128)(2,1)} %bias_mean.1) | copy-start | bytes 8068
  102.7 1.4 %copy-start.11 = (bf16[14,96]{1,0:T(8,128)(2,1)S(1)}, bf16[14,96]{1,0:T(8,128)(2,1)}, u32[]{:S(2)}) copy-start(bf16[14,96]{1,0:T(8,128)(2,1)} %bias_square.1) | copy-start | bytes 8068
  104.0 4.8 %copy-start.14 = (bf16[384,384]{1,0:T(8,128)(2,1)S(1)}, bf16[384,384]{1,0:T(8,128)(2,1)}, u32[]{:S(2)}) copy-start(bf16[384,384]{1,0:T(8,128)(2,1)} %param.36) | copy-start | bytes 884740
  104.0 4.8 %copy-start.15 = (bf16[384,384]{1,0:T(8,128)(2,1)S(1)}, bf16[384,384]{1,0:T(8,128)(2,1)}, u32[]{:S(2)}) copy-start(bf16[384,384]{1,0:T(8,128)(2,1)} %param.42) | copy-start | bytes 884740
  104.0 4.8 %copy-start.16 = (bf16[384,384]{1,0:T(8,128)(2,1)S(1)}, bf16[384,384]{1,0:T(8,128)(2,1)}, u32[]{:S(2)}) copy-start(bf16[384,384]{1,0:T(8,128)(2,1)} %param.41) | copy-start | bytes 884740
  104.0 4.8 %copy-start.17 = (bf16[384,384]{1,0:T(8,128)(2,1)S(1)}, bf16[384,384]{1,0:T(8,128)(2,1)}, u32[]{:S(2)}) copy-start(bf16[384,384]{1,0:T(8,128)(2,1)} %param.35) | copy-start | bytes 884740
  107.8 3.7 %collective-permute-start.29 = (f32[8,128]{1,0:T(8,128)S(1)}, f32[8,128]{1,0:T(8,128)S(1)}, u32[]{:S(2)}, u32[]{:S(2)}) collective-permute-start(f32[8,128]{1,0:T(8,128)S(1)} %step_5.1), channel_id=1, source_target_pairs={{0,16},{1,9},{2,18},{3,11},{4,20},{5,13},{6,22},{7,15},{8,24},{9,1... | collective-permute-start | bytes 12296 | tf_op jit(solution)/shard_map/ppermute | solution.py:927
  110.9 1.3 %copy-start.1 = (f32[384,384]{1,0:T(8,128)}, f32[384,384]{1,0:T(8,128)S(1)}, u32[]{:S(2)}) copy-start(f32[384,384]{1,0:T(8,128)S(1)} %get-tuple-element.141.refs_1_) | copy-start | bytes 1769476
